TPU v7x, 512 devices: a whole 4x8x8 slice. The times are simulated.
512 devices in a mesh: grp: 4 (over x), seq: 16 (over z, y_lo), dp: 8 (over y_hi, core).
Axes of the slice: x: 4, y: 8 (y_hi: 4, y_lo: 2; y = y_hi * 2 + y_lo), z: 8, core: 2. Of those that a mesh axis runs over, the one named last changes fastest.
Arguments:
- video: bfloat16 [8, 128, 256, 512], P('dp', 'seq', 'grp'), may hold values from -7 to 7
- conv_weight: bfloat16 [3, 128, 128], replicated, may hold values from -0.3125 to 0.3125
- latent_weight: bfloat16 [512, 64], replicated, may hold values from -0.25 to 0.25
- assign: int32 [8, 128, 256], P('dp', 'seq', 'grp'), may hold values from 0 to 1023, as said below
- embed_weight: bfloat16 [64, 3072], replicated, may hold values from -0.75 to 0.75
- norm_gain: float32 [3072], replicated, may hold values from 0.1 to 1.9
- qkv_weight: bfloat16 [3, 3072, 2048], P(None, None, 'seq'), may hold values from -6 to 6
- q_gain: float32 [128], replicated, may hold values from 0.5 to 5
- k_gain: float32 [128], replicated, may hold values from 0.5 to 5
- out_weight: bfloat16 [2048, 3072], P('seq'), may hold values from -2.390625 to 2.390625
- cotangent: bfloat16 [8, 1024, 3072], P('dp', ('grp', 'seq')), may hold values from -6 to 6
Outputs:
- attended: bfloat16 [8, 1024, 3072], P('dp', ('grp', 'seq'))
- out_grad: bfloat16 [2048, 3072], P('seq')
Inputs may be any that keep to these rules, and one draw needn't show every extreme that they name: `assign`: every one of the 1024 merged groups of a clip receives at least one token.
All inputs are finite; a program needn't handle non-finite values.
Results may differ from a plain program's by a relative error of at most 0.04.
The roundings to bfloat16 on the way count: a program that leaves them out, or rounds other values in their place, can miss the bound.
Values may be sent and summed in bfloat16 or wider, within the bound.
No kernel may reach another device: no remote copies, remote signals or barrier semaphores. Data moves between devices by JAX's collectives and lax.ppermute only.
A program may use at most 64 MiB of HBM per device.

v0:
```python
import math

import jax
import jax.numpy as jnp
from jax import lax
from jax.sharding import PartitionSpec as P


def passed_along(block, axis, distance):
    devices = range(lax.axis_size(axis))
    route = [(i - distance, i) for i in devices if i - distance in devices]
    return lax.ppermute(block, axis, route)


def embed_norm(merged_rows, embed_weight, norm_gain):
    embedded = jnp.dot(merged_rows, embed_weight, preferred_element_type=jnp.float32)
    center = embedded - jnp.mean(embedded, axis=-1, keepdims=True)
    spread = jnp.mean(center * center, axis=-1, keepdims=True)
    return (center * lax.rsqrt(spread + 1e-06) * norm_gain).astype(jnp.bfloat16)


def head_norm(projected_part, gain_vector):
    square_mean = jnp.mean(projected_part * projected_part, axis=-1, keepdims=True)
    return (projected_part * lax.rsqrt(square_mean + 1e-06) * gain_vector).astype(jnp.bfloat16)


def shards(
    video,
    conv_weight,
    latent_weight,
    assign,
    embed_weight,
    norm_gain,
    qkv_weight,
    q_gain,
    k_gain,
    out_weight,
    cotangent,
):
    frames = video[0]
    frame_count, tokens_frame, feature_width = frames.shape
    channels = conv_weight.shape[1]
    earlier = passed_along(frames[frame_count - 2 :], "seq", 1)
    pixels = jnp.concatenate([earlier, frames], axis=0).reshape(frame_count + 2, -1, channels)
    preact = jnp.zeros((frame_count * pixels.shape[1], channels), jnp.float32)
    for offset in range(3):
        window = pixels[2 - offset : 2 - offset + frame_count].reshape(-1, channels)
        preact = preact + jnp.dot(window, conv_weight[offset], preferred_element_type=jnp.float32)
    own_pixels = pixels[2:].reshape(-1, channels).astype(jnp.float32)
    hidden = (
        (own_pixels + jax.nn.silu(preact))
        .astype(jnp.bfloat16)
        .reshape(frame_count * tokens_frame, feature_width)
    )
    latent = jnp.dot(hidden, latent_weight, preferred_element_type=jnp.float32).astype(jnp.bfloat16)
    labels = assign[0].reshape(-1)
    group_rows = cotangent.shape[1]
    all_groups = group_rows * lax.axis_size("grp") * lax.axis_size("seq")
    member = labels[None, :] == jnp.arange(all_groups, dtype=jnp.int32)[:, None]
    member_sums = jnp.dot(member.astype(jnp.bfloat16), latent, preferred_element_type=jnp.float32)
    member_counts = jnp.sum(member.astype(jnp.float32), axis=1)
    latent_sums, counts = (
        lax.psum_scatter(member_sums, ("grp", "seq"), scatter_dimension=0, tiled=True),
        lax.psum_scatter(member_counts, ("grp", "seq"), scatter_dimension=0, tiled=True),
    )
    merged = (latent_sums / counts[:, None]).astype(jnp.bfloat16)
    count_marks = counts.astype(jnp.bfloat16)
    heads_width = qkv_weight.shape[2]
    head_size = q_gain.shape[0]
    heads_local = heads_width // head_size
    slice_rows = group_rows * lax.axis_size("seq")
    normed = embed_norm(merged, embed_weight, norm_gain)
    projected = jnp.einsum(
        "rd,kdc->rkc",
        lax.all_gather(normed, "seq", axis=0, tiled=True),
        qkv_weight,
        preferred_element_type=jnp.float32,
    )
    placed_counts = lax.all_gather(count_marks, "seq", axis=0, tiled=True)
    head_parts = projected.reshape(slice_rows, 3, heads_local, head_size)
    queries = head_norm(head_parts[:, 0], q_gain)
    key_rows = head_norm(head_parts[:, 1], k_gain)
    value_rows = head_parts[:, 2].astype(jnp.bfloat16)
    score_scale = 1.0 / math.sqrt(head_size)
    row_top = jnp.full((heads_local, slice_rows), -jnp.inf, jnp.float32)
    denominator = jnp.zeros((heads_local, slice_rows), jnp.float32)
    running = jnp.zeros((heads_local, slice_rows, head_size), jnp.float32)
    remote_keys = lax.all_gather(key_rows, "grp", axis=0, tiled=True)
    remote_values = lax.all_gather(value_rows, "grp", axis=0, tiled=True)
    remote_counts = lax.all_gather(placed_counts, "grp", axis=0, tiled=True)
    key_bias = jnp.log(remote_counts.astype(jnp.float32))
    scores = (
        jnp.einsum("qhc,khc->hqk", queries, remote_keys, preferred_element_type=jnp.float32)
        * score_scale
        + key_bias[None, None, :]
    )
    new_top = jnp.max(scores, axis=-1)
    rescale = jnp.exp(row_top - new_top)
    weights = jnp.exp(scores - new_top[:, :, None])
    denominator = denominator * rescale + jnp.sum(weights, axis=-1)
    mixed = jnp.einsum(
        "hqk,khc->hqc",
        weights.astype(jnp.bfloat16),
        remote_values,
        preferred_element_type=jnp.float32,
    )
    running = running * rescale[:, :, None] + mixed
    row_top, denominator, running = (new_top, denominator, running)
    head_out = (
        (running / denominator[:, :, None])
        .astype(jnp.bfloat16)
        .transpose(1, 0, 2)
        .reshape(slice_rows, heads_width)
    )
    head_rows = head_out
    attended = lax.psum_scatter(
        jnp.dot(head_rows, out_weight, preferred_element_type=jnp.float32),
        "seq",
        scatter_dimension=0,
        tiled=True,
    ).astype(jnp.bfloat16)
    head_rows = head_out
    local_grad = jnp.einsum(
        "rc,rd->cd",
        head_rows,
        lax.all_gather(cotangent[0], "seq", axis=0, tiled=True),
        preferred_element_type=jnp.float32,
    )
    out_grad = lax.psum(local_grad, ("grp", "dp")).astype(jnp.bfloat16)
    return (attended[None], out_grad)


def solution(mesh):
    placed = (
        P("dp", "seq", "grp", None),
        P(),
        P(),
        P("dp", "seq", "grp"),
        P(),
        P(),
        P(None, None, "seq"),
        P(),
        P(),
        P("seq", None),
        P("dp", ("grp", "seq"), None),
    )
    return jax.shard_map(
        shards,
        mesh=mesh,
        in_specs=placed,
        out_specs=(P("dp", ("grp", "seq"), None), P("seq", None)),
        check_vma=False,
    )
```

profile of v0, /device:TPU:1, one launch (start us, length us, event | category | flops | bytes accessed | tf_op | source)
XLA Modules:
  0.0 673.6 jit_solution(6495557382712274800)
XLA Ops:
  7.2 0.0 copy-start
  7.2 0.0 copy-start.1
  7.2 0.0 reduce-scatter.3.cloned.1.call-start
  7.2 1.0 slice_bitcast_fusion.1
  8.3 4.0 collective-permute-start
  12.3 1.4 reshape.243
  13.7 1.0 fusion.20
  14.7 0.1 eq.15
  14.8 0.9 pad_maximum_fusion
  15.7 1.4 reshape.244
  17.0 1.1 reshape.245
  18.1 1.1 convolution_add_fusion.1
  19.2 2.0 add_convert_fusion
  21.3 2.3 reshape.246
  23.6 2.5 fusion
  26.1 0.0 reduce-scatter.3.cloned.1.call-update
  26.1 0.0 all-gather.6.cloned.1.call-start
  26.2 1.3 dynamic-slice.1
  28.0 1.0 convert_reduce_fusion
  29.0 141.2 %all-reduce.1 = f32[1024]{0:T(1024)} all-reduce(f32[1024]{0:T(1024)S(1)} %convert_reduce_fusion), channel_id=5, replica_groups=mesh['grp'=4,'seq'=16,'dp'=8] {'grp','seq'}, use_global_device_ids=true, to_apply=%region_2.3.clone | all-reduce | flops 1024 | bytes 8192
  170.2 1.2 fusion.28
  171.4 129.6 %reduce-scatter.3.cloned.1.call-done = f32[16,64]{1,0:T(8,128)} async-done(((f32[1024,64]{1,0:T(8,128)}), f32[16,64]{1,0:T(8,128)}) %reduce-scatter.3.cloned.1.call-update) | async-done | bytes 4112 | tf_op jit(solution)/shard_map/reduce_scatter | solution.py:63
  301.0 1.0 fusion.29
  302.0 0.2 multiply_reduce_fusion
  302.2 0.7 multiply_convert_fusion
  303.0 0.0 all-gather.6.cloned.1.call-update
  303.0 0.0 all-gather.8.cloned.1.call-start
  303.1 0.7 all-gather.8.cloned.1.call-update
  303.7 0.0 reduce-scatter.5.cloned.1.call-start
  303.8 1.3 dynamic-slice
  305.7 0.8 dynamic-update-slice
  306.5 25.1 %all-reduce = bf16[256]{0:T(256)(128)(2,1)S(1)} all-reduce(bf16[256]{0:T(256)(128)(2,1)S(1)} %dynamic-update-slice), channel_id=1, replica_groups=mesh['grp'=4,'seq'=16,'dp'=8] {'seq'}, use_global_device_ids=true, to_apply=%add | all-reduce | flops 256 | bytes 1024
  331.6 2.4 copy.15
  334.0 6.4 all-gather.2
  340.4 75.6 %all-gather.6.cloned.1.call-done = bf16[256,3072]{1,0:T(8,128)(2,1)} async-done(((bf16[16,3072]{1,0:T(8,128)(2,1)}), bf16[256,3072]{1,0:T(8,128)(2,1)}) %all-gather.6.cloned.1.call-update) | async-done | bytes 1572880 | tf_op jit(solution)/shard_map/all_gather | solution.py:75
  416.1 3.0 fusion.31
  419.1 0.1 multiply_convert_fusion.1
  419.2 9.8 %all_gather.19 = bf16[1024,1,128]{0,2,1:T(8,128)(2,1)S(1)} all-gather(bf16[256,1,128]{0,2,1:T(8,128)(2,1)S(1)} %multiply_convert_fusion.1), channel_id=1, replica_groups=mesh['grp'=4,'seq'=16,'dp'=8] {'grp'}, dimensions={0}, use_global_device_ids=true | all-gather | bytes 327680 | tf_op jit(solution)/shard_map/all_gather | solution.py:88
  429.0 9.6 %all-gather = bf16[1024,1,1,128]{0,3,1,2:T(8,128)(2,1)S(1)} all-gather(bf16[256,1,1,128]{0,3,1,2:T(8,128)(2,1)S(1)} %slice.81), channel_id=2, replica_groups=mesh['grp'=4,'seq'=16,'dp'=8] {'grp'}, dimensions={0}, use_global_device_ids=true | all-gather | bytes 327680 | tf_op jit(solution)/shard_map/all_gather | solution.py:89
  438.7 0.5 fusion.30
  439.1 0.3 fusion.7
  439.5 0.4 fusion.5
  439.8 2.2 fusion.32
  442.0 0.0 reduce-scatter.5.cloned.1.call-update
  442.0 52.5 %all-gather.8.cloned.1.call-done = bf16[1,256,3072]{2,1,0:T(8,128)(2,1)} async-done(((bf16[1,16,3072]{2,1,0:T(8,128)(2,1)}), bf16[1,256,3072]{2,1,0:T(8,128)(2,1)}) %all-gather.8.cloned.1.call-update) | async-done | bytes 1572880 | tf_op jit(solution)/shard_map/all_gather | solution.py:126
  494.5 1.8 fusion.1
  496.3 169.2 %all-reduce.3 = bf16[128,3072]{1,0:T(8,128)(2,1)} all-reduce(f32[128,3072]{1,0:T(8,128)S(1)} %fusion.1), channel_id=1, replica_groups=mesh['grp'=4,'seq'=16,'dp'=8] {'grp','dp'}, use_global_device_ids=true, to_apply=%region_10.11 | all-reduce | flops 393216 | bytes 2359296 | tf_op jit(solution)/shard_map/psum | solution.py:129
  665.5 1.6 convert_bitcast_fusion
  (31 shorter events, 0.2 us)
Async XLA Ops:
  7.2 432.6 %copy-start = (bf16[128,3072]{1,0:T(8,128)(2,1)S(1)}, bf16[128,3072]{1,0:T(8,128)(2,1)}, u32[]{:S(2)}) copy-start(bf16[128,3072]{1,0:T(8,128)(2,1)} %param.20) | copy-start | bytes 2359300
  7.2 7.6 %copy-start.1 = (bf16[1,8,64,512]{3,2,1,0:T(8,128)(2,1)S(1)}, bf16[1,8,64,512]{3,2,1,0:T(8,128)(2,1)}, u32[]{:S(2)}) copy-start(bf16[1,8,64,512]{3,2,1,0:T(8,128)(2,1)} %param.11) | copy-start | bytes 1572868
  7.2 7.5 %copy-start.7 = (s32[1,8,64]{2,1,0:T(8,128)S(1)}, s32[1,8,64]{2,1,0:T(8,128)}, u32[]{:S(2)}) copy-start(s32[1,8,64]{2,1,0:T(8,128)} %param.14) | copy-start | bytes 6148
  7.2 293.8 %reduce-scatter.3.cloned.1.call-start = ((), (), s32[]{:S(2)}) async-start(), calls=%async_computation.2 | async-start | bytes 532480 | tf_op jit(solution)/shard_map/reduce_scatter | solution.py:63
  8.3 6.5 collective-permute-start
  14.8 8.8 %copy-start.6 = (s32[512]{0:T(512)}, s32[512]{0:T(512)S(1)}, u32[]{:S(2)}) copy-start(s32[512]{0:T(512)S(1)} %eq.15) | copy-start | bytes 6148
  18.1 1.1 copy-start.3
  21.3 279.7 %copy-start.4 = (bf16[64,3072]{1,0:T(8,128)(2,1)S(1)}, bf16[64,3072]{1,0:T(8,128)(2,1)}, u32[]{:S(2)}) copy-start(bf16[64,3072]{1,0:T(8,128)(2,1)} %param.15) | copy-start | bytes 1179652
  21.3 281.0 %copy-start.5 = (f32[3072]{0:T(1024)S(1)}, f32[3072]{0:T(1024)}, u32[]{:S(2)}) copy-start(f32[3072]{0:T(1024)} %param.16) | copy-start | bytes 36868
  21.3 310.3 %copy-start.2 = (bf16[3,3072,128]{2,1,0:T(8,128)(2,1)S(1)}, bf16[3,3072,128]{2,1,0:T(8,128)(2,1)}, u32[]{:S(2)}) copy-start(bf16[3,3072,128]{2,1,0:T(8,128)(2,1)} %param.17) | copy-start | bytes 7077892
  26.1 389.9 %all-gather.6.cloned.1.call-start = ((), (), s32[]{:S(2)}) async-start(), calls=%async_computation.3 | async-start | bytes 1671168 | tf_op jit(solution)/shard_map/all_gather | solution.py:75
  303.0 191.5 %all-gather.8.cloned.1.call-start = ((), (), s32[]{:S(2)}) async-start(), calls=%async_computation.5 | async-start | bytes 1671168 | tf_op jit(solution)/shard_map/all_gather | solution.py:126
  303.7 361.8 %reduce-scatter.5.cloned.1.call-start = ((), (), s32[]{:S(2)}) async-start(), calls=%async_computation.4 | async-start | bytes 3342336 | tf_op jit(solution)/shard_map/reduce_scatter | solution.py:116
  416.1 3.1 copy-start.8
  416.1 22.6 %copy-start.9 = (f32[128]{0:T(128)S(1)}, f32[128]{0:T(128)}, u32[]{:S(2)}) copy-start(f32[128]{0:T(128)} %param.18) | copy-start | bytes 1540
Sparse Core Ops, SparseCore 0:
  26.3 274.6 reduce-scatter.2
  303.8 112.2 all-gather.5
  418.4 76.0 all-gather.7
  497.4 106.9 reduce-scatter.4
where the time goes:
time: 680 us; the launch traced here: 674 us
  blocking collectives  361 us (53%)
  waiting for transfers between devices  258 us (38%)
  matrix products  15.5 us (2%)
  between operations  15.2 us (2%)
  local copies, waits for them, and re-layouts  13 us (2%)
    psum x1, blocking collectives, shards(): out_grad = lax.psum(local_grad, ('grp', 'dp')).astype(jnp.bfloat16)  169 us
    unnamed x2, blocking collectives  166 us
    reduce_scatter x1, waiting for transfers between devices, shards(): lax.psum_scatter(member_sums, ('grp', 'seq'), scatter_dimension=0, tiled=...  130 us
    all_gather x1, waiting for transfers between devices, shards(): lax.all_gather(normed, 'seq', axis=0, tiled=True)  75.6 us
    all_gather x1, waiting for transfers between devices, shards(): lax.all_gather(cotangent[0], 'seq', axis=0, tiled=True)  52.5 us
  transfers between devices with their start and end apart: 5, of which 3 were waited for; matrix products, arithmetic and copies ran while one was open for 3% of the time, Pallas kernels for 0%

commit v1 on v0

v1 whole, which is shorter than its diff:
```python
import functools
import math

import jax
import jax.numpy as jnp
from jax import lax
from jax.experimental import pallas as pl
from jax.experimental.pallas import tpu as pltpu
from jax.sharding import PartitionSpec as P

F32 = jnp.float32
BF16 = jnp.bfloat16
LANES = 128
HALF = 64
NT = (((1,), (1,)), ((), ()))
TN = (((0,), (0,)), ((), ()))


def shifted_frames(block, axis, distance):
    devices = range(lax.axis_size(axis))
    route = [(i - distance, i) for i in devices if i - distance in devices]
    return lax.ppermute(block, axis, route)


def xor_swap(block, axis, mask):
    route = [(i, i ^ mask) for i in range(lax.axis_size(axis))]
    return lax.ppermute(block, axis, route)


def lane_index(rows):
    return lax.broadcasted_iota(jnp.int32, (rows, LANES), 1)


def split_pairs(sums):
    lane = lane_index(sums.shape[0])
    high = sums.astype(BF16).astype(F32)
    keep = jnp.logical_or(lane < HALF, lane == LANES - 2)
    return jnp.where(keep, high, sums - high).astype(BF16)


def join_pairs(pairs):
    lane = lane_index(pairs.shape[0])
    total = pairs + jnp.where(lane < HALF - 2, pltpu.roll(pairs, HALF, 1), 0.0)
    counts = pairs[:, LANES - 2 : LANES - 1] + pairs[:, LANES - 1 :]
    return total, counts


def latent_rows(windows, conv_ref, latent_ref):
    channels = conv_ref.shape[1]
    taps = conv_ref[...].reshape(3 * channels, channels)
    weights = jnp.concatenate([latent_ref[...], latent_ref[...]], axis=0)
    latent = None
    for part, views in enumerate(windows):
        cols = slice(part * channels, (part + 1) * channels)
        preact = jnp.dot(jnp.concatenate(views, axis=1), taps, preferred_element_type=F32)
        hidden = (views[0].astype(F32) + preact / (1.0 + jnp.exp(-preact))).astype(BF16)
        term = lax.dot_general(hidden, weights[:, cols], NT, preferred_element_type=F32)
        latent = term if latent is None else latent + term
    return jnp.where(lane_index(latent.shape[0]) < LANES - 2, latent, 1.0).astype(BF16)


def late_kernel(video_ref, conv_ref, latent_ref, out_ref):
    frame_count, tokens, width = video_ref.shape
    channels = conv_ref.shape[1]
    windows = []
    for start in range(0, width, channels):
        cols = slice(start, start + channels)
        windows.append([
            video_ref[2 - k : frame_count - k, :, cols].reshape(-1, channels) for k in range(3)
        ])
    out_ref[...] = latent_rows(windows, conv_ref, latent_ref)


def sums_kernel(
    video_ref, earlier_ref, conv_ref, latent_ref, late_ref, labels_ref, out_ref, *, grp, seq,
):
    channels = conv_ref.shape[1]
    width = video_ref.shape[2]
    windows = []
    for start in range(0, width, channels):
        cols = slice(start, start + channels)
        padded = jnp.concatenate([earlier_ref[:, :, cols], video_ref[:2, :, cols]], axis=0)
        windows.append([padded[2 - k : 4 - k].reshape(-1, channels) for k in range(3)])
    first = latent_rows(windows, conv_ref, latent_ref)
    rows = jnp.concatenate([first, late_ref[...]], axis=0)
    labels = labels_ref[...]
    total = out_ref.shape[0]
    block = total // (grp * seq)
    step = 256
    for start in range(0, total, step):
        place = lax.broadcasted_iota(jnp.int32, (step, labels.shape[1]), 0) + start
        inner = place & (block - 1)
        column = (place >> (block.bit_length() - 1)) & (grp - 1)
        slab = place >> ((block * grp).bit_length() - 1)
        member = (labels == (column * seq + slab) * block + inner).astype(F32).astype(BF16)
        out_ref[start : start + step, :] = split_pairs(
            jnp.dot(member, rows, preferred_element_type=F32)
        )


def add_up(parts_ref):
    total = parts_ref[0].astype(F32)
    for i in range(1, parts_ref.shape[0]):
        total = total + parts_ref[i].astype(F32)
    return total


def resplit_kernel(parts_ref, out_ref):
    total, counts = join_pairs(add_up(parts_ref))
    lane = lane_index(total.shape[0])
    doubled = jnp.where(lane < HALF, total, pltpu.roll(total, HALF, 1))
    pairs = split_pairs(jnp.where(lane < LANES - 2, doubled, counts))
    for i in range(out_ref.shape[0]):
        out_ref[i] = pairs


def merge_kernel(parts_ref, out_ref):
    total, counts = join_pairs(add_up(parts_ref))
    lane = lane_index(total.shape[0])
    merged = jnp.where(lane < HALF, total / counts, 0.0)
    high = counts.astype(BF16).astype(F32)
    marks = jnp.where(lane == LANES - 2, high, counts - high)
    rows = jnp.where(lane < LANES - 2, merged, marks).astype(BF16)
    for i in range(out_ref.shape[0]):
        out_ref[i] = rows


def spread_kernel(parts_ref, out_ref):
    total = add_up(parts_ref).astype(BF16)
    for i in range(out_ref.shape[0]):
        out_ref[i] = total


def head_norm(projected, gain):
    square_mean = jnp.mean(projected * projected, axis=-1, keepdims=True)
    return (projected * lax.rsqrt(square_mean + 1e-06) * gain).astype(BF16)


def attend_kernel(
    merged_ref, embed_ref, norm_ref, qkv_ref, qgain_ref, kgain_ref, out_ref,
    kv_ref, q_ref, k_ref, v_ref,
):
    latents, width = embed_ref.shape
    head = q_ref.shape[1]
    total = out_ref.shape[0]
    step = 256
    kv_ref[:, :head] = qkv_ref[1]
    kv_ref[:, head:] = qkv_ref[2]
    pick = (lane_index(16) >= LANES - 2).astype(F32).astype(BF16)
    count_row = lax.dot_general(pick, merged_ref[...], NT, preferred_element_type=F32)[0:1, :]
    bias = jnp.log(count_row)
    ones = jnp.ones((16, width), BF16)
    embed_mean = lax.dot_general(ones, embed_ref[...], NT, preferred_element_type=F32)
    embed_mean = embed_mean[0:1, :] * (1.0 / width)
    embed = jnp.concatenate([embed_ref[...], jnp.ones((LANES - latents, width), BF16)], axis=0)
    lane = lane_index(step)
    for start in range(0, total, step):
        here = slice(start, start + step)
        rows = merged_ref[here, :].astype(F32)
        mean = -jnp.sum(rows[:, :latents] * embed_mean, axis=-1, keepdims=True)
        high = mean.astype(BF16).astype(F32)
        middle = (mean - high).astype(BF16).astype(F32)
        low = mean - high - middle
        tail = jnp.where(lane == latents, high, 0.0)
        tail = jnp.where(lane == latents + 1, middle, tail)
        tail = jnp.where(lane == latents + 2, low, tail)
        factors = jnp.where(lane < latents, rows, tail).astype(BF16)
        center = jnp.dot(factors, embed, preferred_element_type=F32)
        spread = jnp.mean(center * center, axis=-1, keepdims=True)
        normed = (center * lax.rsqrt(spread + 1e-06) * norm_ref[...]).astype(BF16)
        q_part = jnp.dot(normed, qkv_ref[0], preferred_element_type=F32)
        kv_part = jnp.dot(normed, kv_ref[...], preferred_element_type=F32)
        q_ref[here, :] = head_norm(q_part, qgain_ref[...])
        k_ref[here, :] = head_norm(kv_part[:, :head], kgain_ref[...])
        v_ref[here, :] = kv_part[:, head:].astype(BF16)
    scale = 1.0 / math.sqrt(head)
    for start in range(0, total, step):
        here = slice(start, start + step)
        scores = lax.dot_general(
            q_ref[here, :], k_ref[...], NT, preferred_element_type=F32
        ) * scale + bias
        top = jnp.max(scores, axis=-1, keepdims=True)
        weights = jnp.exp(scores - top)
        denominator = jnp.sum(weights, axis=-1, keepdims=True)
        mixed = jnp.dot(weights.astype(BF16), v_ref[...], preferred_element_type=F32)
        out_ref[here, :] = (mixed / denominator).astype(BF16)


def call(body, shape, dtype, *args, name, scratch=(), flops=10**8, moved=10**6):
    return pl.pallas_call(
        body,
        out_shape=jax.ShapeDtypeStruct(shape, dtype),
        in_specs=[pl.BlockSpec(memory_space=pltpu.VMEM)] * len(args),
        out_specs=pl.BlockSpec(memory_space=pltpu.VMEM),
        scratch_shapes=list(scratch),
        cost_estimate=pl.CostEstimate(flops=flops, bytes_accessed=moved, transcendentals=0),
        compiler_params=pltpu.CompilerParams(vmem_limit_bytes=48 * 2**20),
        name=name,
    )(*args)


def shards(
    video, conv_weight, latent_weight, assign, embed_weight, norm_gain, qkv_weight, q_gain, k_gain,
    out_weight, cotangent,
):
    grp_size, seq_size, dp_size = (lax.axis_size(a) for a in ("grp", "seq", "dp"))
    slabs = seq_size // 2
    owners = grp_size * seq_size
    block, width = cotangent.shape[1:]
    head = q_gain.shape[0]
    groups = block * owners
    columns = width // grp_size
    grp = lax.axis_index("grp")
    seq = lax.axis_index("seq")
    same_side = [list(range(k, seq_size, 2)) for k in range(2)]

    frames = video[0]
    frame_count, tokens = frames.shape[:2]
    earlier = shifted_frames(frames[frame_count - 2 :], "seq", 1)
    latent_t = latent_weight.T
    labels = assign[0].reshape(1, -1)
    late = call(
        late_kernel, ((frame_count - 2) * tokens, LANES), BF16, frames, conv_weight, latent_t,
        name="late_frames", flops=10**9,
    )
    sums = call(
        functools.partial(sums_kernel, grp=grp_size, seq=seq_size), (groups, LANES), BF16,
        frames, earlier, conv_weight, latent_t, late, labels, name="group_sums", flops=10**9,
    )

    shared = block * grp_size
    parts = lax.all_to_all(sums.reshape(seq_size, shared, LANES), "seq", 0, 0, tiled=True)
    slab_sums = call(resplit_kernel, (grp_size, shared, LANES), BF16, parts, name="slab_sums")
    slab_parts = lax.all_to_all(slab_sums, "grp", 0, 0, tiled=True)
    merged = call(merge_kernel, (seq_size, shared, LANES), BF16, slab_parts, name="merged")
    merged = lax.all_to_all(merged, "seq", 0, 0, tiled=True).reshape(groups, LANES)

    cot, _ = lax.optimization_barrier((cotangent, sums))
    by_column = cot[0].reshape(block, grp_size, columns).transpose(1, 0, 2)
    by_column = jnp.broadcast_to(by_column[None], (2,) + by_column.shape)
    corners = [
        [g * seq_size + 2 * z + y for y in range(2) for g in range(grp_size)] for z in range(slabs)
    ]
    near = lax.all_to_all(
        by_column.reshape(2 * grp_size, block, columns), ("grp", "seq"), 0, 0,
        axis_index_groups=corners, tiled=True,
    ).reshape(2 * shared, columns)
    far = lax.all_to_all(
        jnp.broadcast_to(near[None], (slabs,) + near.shape), "seq", 0, 0,
        axis_index_groups=same_side, tiled=True,
    )
    grad_rows = far.reshape(groups, columns)

    late_weight, _ = lax.optimization_barrier((out_weight, slab_parts))
    weight_pair = xor_swap(late_weight, "seq", 1)

    head_out = call(
        attend_kernel, (groups, head), BF16, merged, embed_weight, norm_gain[None], qkv_weight,
        q_gain[None], k_gain[None], name="attend", flops=8 * 10**9,
        scratch=[pltpu.VMEM((width, 2 * head), BF16)] + [pltpu.VMEM((groups, head), BF16)] * 3,
    )

    side = seq % 2
    by_owner = lax.dynamic_index_in_dim(
        head_out.reshape(slabs, 2, grp_size, block, head), grp, 2, keepdims=False
    )
    mine = lax.dynamic_index_in_dim(by_owner, side, 1, keepdims=False)
    theirs = xor_swap(lax.dynamic_index_in_dim(by_owner, 1 - side, 1, keepdims=False), "seq", 1)

    local_grad = lax.dot_general(
        head_out, grad_rows, TN, preferred_element_type=F32
    ).astype(BF16)
    grad_parts = lax.all_to_all(
        local_grad.reshape(dp_size, head // dp_size, columns), "dp", 0, 0, tiled=True
    )

    both = jnp.concatenate([mine, theirs], axis=2).reshape(-1, 2 * head)
    both_weights = jnp.concatenate([out_weight, weight_pair], axis=0)
    partial = jnp.dot(both, both_weights, preferred_element_type=F32).astype(BF16)
    out_parts = lax.all_to_all(
        partial.reshape(slabs, block, width), "seq", 0, 0, axis_index_groups=same_side, tiled=True
    )

    grad_block = call(
        spread_kernel, (dp_size, head // dp_size, columns), BF16, grad_parts, name="grad_block"
    )
    grad_cols = lax.all_to_all(grad_block, "dp", 0, 0, tiled=True).reshape(head, columns)
    out_grad = lax.all_to_all(
        jnp.broadcast_to(grad_cols[None], (grp_size, head, columns)), "grp", 0, 0, tiled=True
    )
    out_grad = out_grad.transpose(1, 0, 2).reshape(head, width)
    attended = jnp.sum(out_parts.astype(F32), axis=0).astype(BF16)
    return (attended[None], out_grad)


def solution(mesh):
    placed = (
        P("dp", "seq", "grp", None), P(), P(), P("dp", "seq", "grp"), P(), P(),
        P(None, None, "seq"), P(), P(), P("seq", None), P("dp", ("grp", "seq"), None),
    )
    return jax.shard_map(
        shards,
        mesh=mesh,
        in_specs=placed,
        out_specs=(P("dp", ("grp", "seq"), None), P("seq", None)),
        check_vma=False,
    )
```

time: 680 us -> 190 us (0.28)
  blocking collectives: 361 us -> 48.2 us
  waiting for transfers between devices: 258 us -> 68.2 us
  starting transfers between devices: 4.2 us -> 43.1 us
  between operations: 15.2 us -> 0.83 us
  Pallas kernels: 0 us -> 12.1 us
  matrix products: 15.5 us -> 4.89 us
    psum x1 -> x0, blocking collectives: 169 us -> none  [shards(): out_grad = lax.psum(local_grad, ('grp', 'dp')).astype(jnp.bfloat16)]
    unnamed x2 -> x0, blocking collectives: 166 us -> none
    reduce_scatter x2 -> x0, waiting for transfers between devices: 130 us -> none  [the longest x1 130 us: shards(): lax.psum_scatter(member_sums, ('grp', 'seq'), scatter_dimension=0, tiled=...]
    all_gather x2 -> x0, waiting for transfers between devices: 128 us -> none  [the longest x1 75.6 us: shards(): lax.all_gather(normed, 'seq', axis=0, tiled=True)]
    all_to_all x0 -> x6, waiting for transfers between devices: none -> 64.3 us  [the longest x1 23.1 us: shards(): lax.all_to_all(jnp.broadcast_to(near[None], (slabs,) + near.shape), 'seq'...]
    all_to_all x0 -> x3, blocking collectives: none -> 48.2 us  [the longest x1 19.7 us: shards(): lax.all_to_all(sums.reshape(seq_size, shared, LANES), 'seq', 0, 0, tiled=...]
    all_to_all x0 -> x6, starting transfers between devices: none -> 32.1 us  [the longest x1 12.1 us: shards(): lax.all_to_all(local_grad.reshape(dp_size, head // dp_size, columns), 'dp...]
    all_gather x3 -> x0, blocking collectives: 25.8 us -> none  [the longest x1 9.77 us: shards(): remote_keys = lax.all_gather(key_rows, 'grp', axis=0, tiled=True)]
  transfers between devices with their start and end apart: 5 -> 9, of which waited for: 3 -> 6; matrix products, arithmetic and copies ran while one was open for 3% -> 3% of each run, Pallas kernels for 0% -> 6%
where the time goes in v1:
time: 190 us; the launch traced here: 187 us
  waiting for transfers between devices  68.2 us (36%)
  blocking collectives  48.2 us (25%)
  starting transfers between devices  43.1 us (23%)
  Pallas kernels  12.1 us (6%)
  local copies, waits for them, and re-layouts  8.96 us (5%)
  matrix products  4.89 us (3%)
    all_to_all x1, waiting for transfers between devices, shards(): lax.all_to_all(jnp.broadcast_to(near[None], (slabs,) + near.shape), 'seq'...  23.1 us
    all_to_all x1, waiting for transfers between devices, shards(): lax.all_to_all(partial.reshape(slabs, block, width), 'seq', 0, 0, axis_in...  22.3 us
    all_to_all x1, blocking collectives, shards(): lax.all_to_all(sums.reshape(seq_size, shared, LANES), 'seq', 0, 0, tiled=...  19.7 us
    all_to_all x1, blocking collectives, shards(): lax.all_to_all(grad_block, 'dp', 0, 0, tiled=True).reshape(head, columns)  16.4 us
    all_to_all x1, starting transfers between devices, shards(): lax.all_to_all(local_grad.reshape(dp_size, head // dp_size, columns), 'dp...  12.1 us
    all_to_all x1, blocking collectives, shards(): lax.all_to_all(merged, 'seq', 0, 0, tiled=True).reshape(groups, LANES)  12.1 us
    pallas_call x6, Pallas kernels, call(): pl.pallas_call(body, out_shape=jax.ShapeDtypeStruct(shape, dtype), in_spe...  12.1 us
    all_to_all x1, waiting for transfers between devices, shards(): lax.all_to_all(jnp.broadcast_to(grad_cols[None], (grp_size, head, columns...  8.88 us
  transfers between devices with their start and end apart: 9, of which 6 were waited for; matrix products, arithmetic and copies ran while one was open for 3% of the time, Pallas kernels for 6%

profile of v1, /device:TPU:1, one launch (start us, length us, event | category | flops | bytes accessed | tf_op | source)
XLA Modules:
  0.0 187.1 jit_solution(13917160454540629114)
XLA Ops:
  0.6 0.9 slice_bitcast_fusion
  1.5 4.0 %collective-permute-start = (bf16[2,64,512]{2,1,0:T(8,128)(2,1)S(1)}, bf16[2,64,512]{2,1,0:T(8,128)(2,1)S(1)}, u32[]{:S(2)}, u32[]{:S(2)}) collective-permute-start(bf16[2,64,512]{2,1,0:T(8,128)(2,1)S(1)} %slice_bitcast_fusion), channel_id=1, source_target_pairs={{0,8},{8,16},{16,24},{24,32},{32,40},{40,48},{48,56},{56,64},{64,7... | collective-permute-start | bytes 393224 | tf_op jit(solution)/shard_map/ppermute | solution.py:22
  5.6 0.8 reshape_squeeze.6.labels_ref
  6.4 1.0 copy-done
  7.4 0.9 copy-done.3
  8.3 0.8 copy-done.4
  9.1 1.0 late_frames.1.late_ref
  10.1 0.0 copy-start.8
  10.1 0.0 collective-permute-done.earlier_ref
  10.1 0.9 group_sums.1
  11.0 19.7 %all_to_all.45.parts_ref = bf16[16,64,128]{2,1,0:T(8,128)(2,1)S(1)} all-to-all(bf16[16,64,128]{2,1,0:T(8,128)(2,1)S(1)} %bitcast.29), channel_id=1, replica_groups=mesh['grp'=4,'seq'=16,'dp'=8] {'seq'}, dimensions={0} | all-to-all | bytes 524288 | tf_op jit(solution)/shard_map/all_to_all | solution.py:232
  30.7 0.8 slab_sums.1
  31.6 4.0 %all-to-all-start.1 = ((bf16[4,64,128]{2,1,0:T(8,128)(2,1)}), bf16[4,64,128]{2,1,0:T(8,128)(2,1)S(1)}, u32[]{:S(2)}, u32[]{:S(2)}) async-start(bf16[4,64,128]{2,1,0:T(8,128)(2,1)} %slab_sums.1), calls=%async_computation.1 | async-start | bytes 131072 | tf_op jit(solution)/shard_map/all_to_all | solution.py:234
  35.6 0.0 copy-done.8
  35.7 4.4 %all-to-all-done.1.parts_ref = bf16[4,64,128]{2,1,0:T(8,128)(2,1)S(1)} async-done(((bf16[4,64,128]{2,1,0:T(8,128)(2,1)}), bf16[4,64,128]{2,1,0:T(8,128)(2,1)S(1)}, u32[]{:S(2)}, u32[]{:S(2)}) %all-to-all-start.1) | async-done | bytes 65568 | tf_op jit(solution)/shard_map/all_to_all | solution.py:234
  40.1 0.7 broadcast_in_dim.36
  40.8 4.3 %all-to-all-start.4 = ((bf16[8,16,768]{2,1,0:T(8,128)(2,1)}), bf16[8,16,768]{2,1,0:T(8,128)(2,1)S(1)}, u32[]{:S(2)}, u32[]{:S(2)}) async-start(bf16[8,16,768]{2,1,0:T(8,128)(2,1)} %bitcast.15), calls=%async_computation.4 | async-start | bytes 393216 | tf_op jit(solution)/shard_map/all_to_all | solution.py:244
  45.1 0.2 merged.1
  45.3 5.6 %all-to-all-done.4 = bf16[8,16,768]{2,1,0:T(8,128)(2,1)S(1)} async-done(((bf16[8,16,768]{2,1,0:T(8,128)(2,1)}), bf16[8,16,768]{2,1,0:T(8,128)(2,1)S(1)}, u32[]{:S(2)}, u32[]{:S(2)}) %all-to-all-start.4) | async-done | bytes 196640 | tf_op jit(solution)/shard_map/all_to_all | solution.py:244
  50.9 12.1 %all_to_all.46 = bf16[16,64,128]{2,1,0:T(8,128)(2,1)S(1)} all-to-all(bf16[16,64,128]{2,1,0:T(8,128)(2,1)S(1)} %merged.1), channel_id=1, replica_groups=mesh['grp'=4,'seq'=16,'dp'=8] {'seq'}, dimensions={0} | all-to-all | bytes 524288 | tf_op jit(solution)/shard_map/all_to_all | solution.py:236
  63.0 1.2 broadcast_in_dim.38
  64.2 0.0 copy-start.7
  64.2 4.6 %all-to-all-start.5 = ((bf16[8,128,768]{2,1,0:T(8,128)(2,1)}), bf16[8,128,768]{2,1,0:T(8,128)(2,1)}, u32[]{:S(2)}, u32[]{:S(2)}) async-start(bf16[8,128,768]{2,1,0:T(8,128)(2,1)} %broadcast_in_dim.38), calls=%async_computation.5 | async-start | bytes 3145728 | tf_op jit(solution)/shard_map/all_to_all | solution.py:248
  68.8 3.6 %collective-permute-start.2 = (bf16[128,3072]{1,0:T(8,128)(2,1)}, bf16[128,3072]{1,0:T(8,128)(2,1)}, u32[]{:S(2)}, u32[]{:S(2)}) collective-permute-start(bf16[128,3072]{1,0:T(8,128)(2,1)} %param.20), channel_id=1, source_target_pairs={{0,8},{8,0},{16,24},{24,16},{32,40},{40,32},{48,56},{56,48},{64,72... | collective-permute-start | bytes 2359304 | tf_op jit(solution)/shard_map/ppermute | solution.py:27
  72.4 0.0 copy-done.1
  72.4 0.0 copy-done.2
  72.4 0.0 copy-done.5
  72.4 0.0 copy-done.6
  72.5 0.0 copy-done.7
  72.5 9.2 %attend.1 = bf16[1024,128]{1,0:T(8,128)(2,1)S(1)} custom-call(bf16[1024,128]{1,0:T(8,128)(2,1)S(1)} %bitcast.28, bf16[64,3072]{1,0:T(8,128)(2,1)S(1)} %copy-done.2, f32[1,3072]{1,0:T(1,128)S(1)} %bitcast.34, bf16[3,3072,128]{2,1,0:T(8,128)(2,1)S(1)} %copy-done.1, f32[1,128]{1,0:T(1,128)S(1)} %bitcast.35, f32[1,128]{1,0:T(1,128)S(1)} %bitcast.36), custom_call_target="tpu_custom_call" | custom-call | flops 8000000000 | bytes 1000000 | tf_op jit(solution)/shard_map/attend/pallas_call | solution.py:190
  81.7 0.0 copy-start.9
  81.7 23.1 %all-to-all-done.5 = bf16[8,128,768]{2,1,0:T(8,128)(2,1)} async-done(((bf16[8,128,768]{2,1,0:T(8,128)(2,1)}), bf16[8,128,768]{2,1,0:T(8,128)(2,1)}, u32[]{:S(2)}, u32[]{:S(2)}) %all-to-all-start.5) | async-done | bytes 1572896 | tf_op jit(solution)/shard_map/all_to_all | solution.py:248
  104.7 2.5 %convolution_convert_fusion.1 = bf16[128,768]{1,0:T(8,128)(2,1)} fusion(bf16[1024,128]{1,0:T(8,128)(2,1)S(1)} %attend.1, bf16[1024,768]{1,0:T(8,128)(2,1)} %bitcast.17), kind=kOutput, calls=%fused_computation.4 | convolution fusion | flops 201424896 | bytes 2031616 | tf_op jit(solution)/shard_map/dot_general | solution.py:270
  107.2 12.1 %all-to-all-start.6 = ((bf16[8,16,768]{2,1,0:T(8,128)(2,1)}), bf16[8,16,768]{2,1,0:T(8,128)(2,1)S(1)}, u32[]{:S(2)}, u32[]{:S(2)}) async-start(bf16[8,16,768]{2,1,0:T(8,128)(2,1)} %bitcast.18), calls=%async_computation.6 | async-start | bytes 393216 | tf_op jit(solution)/shard_map/all_to_all | solution.py:273
  119.4 3.4 %collective-permute-start.1 = (bf16[8,16,128]{2,1,0:T(8,128)(2,1)S(1)}, bf16[8,16,128]{2,1,0:T(8,128)(2,1)S(1)}, u32[]{:S(2)}, u32[]{:S(2)}) collective-permute-start(bf16[8,16,128]{2,1,0:T(8,128)(2,1)S(1)} %get-tuple-element.9), channel_id=1, source_target_pairs={{0,8},{8,0},{16,24},{24,16},{32,40},{40,32},{48,56},{56,48},{64,72... | collective-permute-start | bytes 98312 | tf_op jit(solution)/shard_map/ppermute | solution.py:27
  122.8 4.0 %collective-permute-done.1 = bf16[8,16,128]{2,1,0:T(8,128)(2,1)S(1)} collective-permute-done((bf16[8,16,128]{2,1,0:T(8,128)(2,1)S(1)}, bf16[8,16,128]{2,1,0:T(8,128)(2,1)S(1)}, u32[]{:S(2)}, u32[]{:S(2)}) %collective-permute-start.1) | collective-permute-done | bytes 32800 | tf_op jit(solution)/shard_map/ppermute | solution.py:27
  126.7 0.0 collective-permute-done.2
  126.7 2.4 %convolution_convert_fusion = bf16[128,3072]{1,0:T(8,128)(2,1)} fusion(bf16[128,3072]{1,0:T(8,128)(2,1)} %collective-permute-done.2, bf16[128,3072]{1,0:T(8,128)(2,1)S(1)} %copy-done.9, bf16[128,128]{1,0:T(8,128)(2,1)S(1)} %bitcast.43, bf16[128,128]{1,0:T(8,128)(2,1)S(1)} %bitcast.42), kind=kOutput, calls=%fused_computation | convolution fusion | flops 204996608 | bytes 2424832 | tf_op jit(solution)/shard_map/dot_general | solution.py:279
  129.1 0.0 all-to-all-done.6.parts_ref
  129.1 3.5 %all-to-all-start.3 = ((bf16[8,16,3072]{2,1,0:T(8,128)(2,1)}), bf16[8,16,3072]{2,1,0:T(8,128)(2,1)S(1)}, u32[]{:S(2)}, u32[]{:S(2)}) async-start(bf16[8,16,3072]{2,1,0:T(8,128)(2,1)} %bitcast.12), calls=%async_computation.3 | async-start | bytes 1572864 | tf_op jit(solution)/shard_map/all_to_all | solution.py:280
  132.7 22.3 %all-to-all-done.3 = bf16[8,16,3072]{2,1,0:T(8,128)(2,1)S(1)} async-done(((bf16[8,16,3072]{2,1,0:T(8,128)(2,1)}), bf16[8,16,3072]{2,1,0:T(8,128)(2,1)S(1)}, u32[]{:S(2)}, u32[]{:S(2)}) %all-to-all-start.3) | async-done | bytes 786464 | tf_op jit(solution)/shard_map/all_to_all | solution.py:280
  155.1 16.4 %all_to_all.47 = bf16[8,16,768]{2,1,0:T(8,128)(2,1)S(1)} all-to-all(bf16[8,16,768]{2,1,0:T(8,128)(2,1)S(1)} %grad_block.1), channel_id=1, replica_groups=mesh['grp'=4,'seq'=16,'dp'=8] {'dp'}, dimensions={0} | all-to-all | bytes 393216 | tf_op jit(solution)/shard_map/all_to_all | solution.py:287
  171.4 0.9 broadcast_in_dim.40
  172.4 3.5 %all-to-all-start.8 = ((bf16[4,128,768]{2,1,0:T(8,128)(2,1)}), bf16[4,128,768]{2,1,0:T(8,128)(2,1)S(1)}, u32[]{:S(2)}, u32[]{:S(2)}) async-start(bf16[4,128,768]{2,1,0:T(8,128)(2,1)} %broadcast_in_dim.40), calls=%async_computation.8 | async-start | bytes 1572864 | tf_op jit(solution)/shard_map/all_to_all | solution.py:288
  175.9 0.8 reduce_sum.12
  176.6 8.9 %all-to-all-done.8 = bf16[4,128,768]{2,1,0:T(8,128)(2,1)S(1)} async-done(((bf16[4,128,768]{2,1,0:T(8,128)(2,1)}), bf16[4,128,768]{2,1,0:T(8,128)(2,1)S(1)}, u32[]{:S(2)}, u32[]{:S(2)}) %all-to-all-start.8) | async-done | bytes 786464 | tf_op jit(solution)/shard_map/all_to_all | solution.py:288
  185.5 0.4 copy.16
  185.9 1.2 copy.17
  (12 shorter events, 0.1 us)
Async XLA Ops:
  1.5 8.6 %collective-permute-start = (bf16[2,64,512]{2,1,0:T(8,128)(2,1)S(1)}, bf16[2,64,512]{2,1,0:T(8,128)(2,1)S(1)}, u32[]{:S(2)}, u32[]{:S(2)}) collective-permute-start(bf16[2,64,512]{2,1,0:T(8,128)(2,1)S(1)} %slice_bitcast_fusion), channel_id=1, source_target_pairs={{0,8},{8,16},{16,24},{24,32},{32,40},{40,48},{48,56},{56,64},{64,7... | collective-permute-start | bytes 393224 | tf_op jit(solution)/shard_map/ppermute | solution.py:22
  6.4 1.0 copy-start
  7.4 0.9 copy-start.3
  8.3 0.8 copy-start.4
  10.1 25.5 %copy-start.8 = (bf16[1,16,3072]{2,1,0:T(8,128)(2,1)S(1)}, bf16[1,16,3072]{2,1,0:T(8,128)(2,1)}, u32[]{:S(2)}) copy-start(bf16[1,16,3072]{2,1,0:T(8,128)(2,1)} %param.21) | copy-start | bytes 294916
  31.6 8.5 %all-to-all-start.1 = ((bf16[4,64,128]{2,1,0:T(8,128)(2,1)}), bf16[4,64,128]{2,1,0:T(8,128)(2,1)S(1)}, u32[]{:S(2)}, u32[]{:S(2)}) async-start(bf16[4,64,128]{2,1,0:T(8,128)(2,1)} %slab_sums.1), calls=%async_computation.1 | async-start | bytes 131072 | tf_op jit(solution)/shard_map/all_to_all | solution.py:234
  40.8 10.1 %all-to-all-start.4 = ((bf16[8,16,768]{2,1,0:T(8,128)(2,1)}), bf16[8,16,768]{2,1,0:T(8,128)(2,1)S(1)}, u32[]{:S(2)}, u32[]{:S(2)}) async-start(bf16[8,16,768]{2,1,0:T(8,128)(2,1)} %bitcast.15), calls=%async_computation.4 | async-start | bytes 393216 | tf_op jit(solution)/shard_map/all_to_all | solution.py:244
  64.2 8.2 %copy-start.1 = (bf16[3,3072,128]{2,1,0:T(8,128)(2,1)S(1)}, bf16[3,3072,128]{2,1,0:T(8,128)(2,1)}, u32[]{:S(2)}) copy-start(bf16[3,3072,128]{2,1,0:T(8,128)(2,1)} %qkv_ref.1) | copy-start | bytes 7077892
  64.2 8.2 %copy-start.2 = (bf16[64,3072]{1,0:T(8,128)(2,1)S(1)}, bf16[64,3072]{1,0:T(8,128)(2,1)}, u32[]{:S(2)}) copy-start(bf16[64,3072]{1,0:T(8,128)(2,1)} %embed_ref.1) | copy-start | bytes 1179652
  64.2 8.2 %copy-start.5 = (f32[3072]{0:T(1024)S(1)}, f32[3072]{0:T(1024)}, u32[]{:S(2)}) copy-start(f32[3072]{0:T(1024)} %param.16) | copy-start | bytes 36868
  64.2 8.2 %copy-start.6 = (f32[128]{0:T(128)S(1)}, f32[128]{0:T(128)}, u32[]{:S(2)}) copy-start(f32[128]{0:T(128)} %param.18) | copy-start | bytes 1540
  64.2 8.2 %copy-start.7 = (f32[128]{0:T(128)S(1)}, f32[128]{0:T(128)}, u32[]{:S(2)}) copy-start(f32[128]{0:T(128)} %param.19) | copy-start | bytes 1540
  64.2 40.5 %all-to-all-start.5 = ((bf16[8,128,768]{2,1,0:T(8,128)(2,1)}), bf16[8,128,768]{2,1,0:T(8,128)(2,1)}, u32[]{:S(2)}, u32[]{:S(2)}) async-start(bf16[8,128,768]{2,1,0:T(8,128)(2,1)} %broadcast_in_dim.38), calls=%async_computation.5 | async-start | bytes 3145728 | tf_op jit(solution)/shard_map/all_to_all | solution.py:248
  68.8 57.9 %collective-permute-start.2 = (bf16[128,3072]{1,0:T(8,128)(2,1)}, bf16[128,3072]{1,0:T(8,128)(2,1)}, u32[]{:S(2)}, u32[]{:S(2)}) collective-permute-start(bf16[128,3072]{1,0:T(8,128)(2,1)} %param.20), channel_id=1, source_target_pairs={{0,8},{8,0},{16,24},{24,16},{32,40},{40,32},{48,56},{56,48},{64,72... | collective-permute-start | bytes 2359304 | tf_op jit(solution)/shard_map/ppermute | solution.py:27
  81.7 45.1 %copy-start.9 = (bf16[128,3072]{1,0:T(8,128)(2,1)S(1)}, bf16[128,3072]{1,0:T(8,128)(2,1)}, u32[]{:S(2)}) copy-start(bf16[128,3072]{1,0:T(8,128)(2,1)} %param.20) | copy-start | bytes 2359300
  107.2 21.9 %all-to-all-start.6 = ((bf16[8,16,768]{2,1,0:T(8,128)(2,1)}), bf16[8,16,768]{2,1,0:T(8,128)(2,1)S(1)}, u32[]{:S(2)}, u32[]{:S(2)}) async-start(bf16[8,16,768]{2,1,0:T(8,128)(2,1)} %bitcast.18), calls=%async_computation.6 | async-start | bytes 393216 | tf_op jit(solution)/shard_map/all_to_all | solution.py:273
  119.4 7.4 %collective-permute-start.1 = (bf16[8,16,128]{2,1,0:T(8,128)(2,1)S(1)}, bf16[8,16,128]{2,1,0:T(8,128)(2,1)S(1)}, u32[]{:S(2)}, u32[]{:S(2)}) collective-permute-start(bf16[8,16,128]{2,1,0:T(8,128)(2,1)S(1)} %get-tuple-element.9), channel_id=1, source_target_pairs={{0,8},{8,0},{16,24},{24,16},{32,40},{40,32},{48,56},{56,48},{64,72... | collective-permute-start | bytes 98312 | tf_op jit(solution)/shard_map/ppermute | solution.py:27
  129.1 25.9 %all-to-all-start.3 = ((bf16[8,16,3072]{2,1,0:T(8,128)(2,1)}), bf16[8,16,3072]{2,1,0:T(8,128)(2,1)S(1)}, u32[]{:S(2)}, u32[]{:S(2)}) async-start(bf16[8,16,3072]{2,1,0:T(8,128)(2,1)} %bitcast.12), calls=%async_computation.3 | async-start | bytes 1572864 | tf_op jit(solution)/shard_map/all_to_all | solution.py:280
  172.4 13.1 %all-to-all-start.8 = ((bf16[4,128,768]{2,1,0:T(8,128)(2,1)}), bf16[4,128,768]{2,1,0:T(8,128)(2,1)S(1)}, u32[]{:S(2)}, u32[]{:S(2)}) async-start(bf16[4,128,768]{2,1,0:T(8,128)(2,1)} %broadcast_in_dim.40), calls=%async_computation.8 | async-start | bytes 1572864 | tf_op jit(solution)/shard_map/all_to_all | solution.py:288

commit v2 on v1

--- a/solution.py
+++ b/solution.py
@@ -59,7 +59,17 @@
     return jnp.where(lane_index(latent.shape[0]) < LANES - 2, latent, 1.0).astype(BF16)
 
 
-def late_kernel(video_ref, conv_ref, latent_ref, out_ref):
+def late_kernel(video_hbm, conv_hbm, latent_hbm, out_ref, video_ref, conv_ref, latent_ref, sems):
+    copies = [
+        pltpu.make_async_copy(src, dst, sems.at[i])
+        for i, (src, dst) in enumerate(
+            [(video_hbm, video_ref), (conv_hbm, conv_ref), (latent_hbm, latent_ref)]
+        )
+    ]
+    for copy in copies:
+        copy.start()
+    for copy in copies:
+        copy.wait()
     frame_count, tokens, width = video_ref.shape
     channels = conv_ref.shape[1]
     windows = []
@@ -131,14 +141,52 @@
         out_ref[i] = total
 
 
+def grad_kernel(place_ref, head_ref, first_ref, second_ref, out_ref, rows_ref, *, masks):
+    seq = place_ref[1]
+    half = first_ref.shape[0]
+    part = rows_ref.shape[0] >> len(masks)
+    for slot in range(1 << len(masks)):
+        mask = sum(m for bit, m in enumerate(masks) if slot >> bit & 1)
+        start = pl.multiple_of((seq ^ mask) * part, part)
+        rows_ref[slot * part : (slot + 1) * part, :] = head_ref[pl.ds(start, part), :]
+    out_ref[...] = (
+        lax.dot_general(rows_ref[:half, :], first_ref[...], TN, preferred_element_type=F32)
+        + lax.dot_general(rows_ref[half:, :], second_ref[...], TN, preferred_element_type=F32)
+    ).astype(BF16)
+
+
+def project_kernel(place_ref, heads_ref, weight_ref, out_ref):
+    member = place_ref[1] & 3
+    heads = jnp.concatenate([heads_ref[member ^ k] for k in range(4)], axis=1)
+    out_ref[...] = jnp.dot(heads, weight_ref[...], preferred_element_type=F32).astype(BF16)
+
+
+def attended_kernel(parts_ref, out_ref):
+    columns = parts_ref.shape[2]
+    for t in range(4):
+        total = parts_ref[t].astype(F32)
+        for i in range(t + 4, parts_ref.shape[0], 4):
+            total = total + parts_ref[i].astype(F32)
+        start = (2 * (t & 1) + (t >> 1)) * columns
+        out_ref[:, start : start + columns] = total.astype(BF16)
+
+
+def columns_kernel(place_ref, *refs):
+    out_ref = refs[-1]
+    columns = refs[0].shape[1]
+    for k, ref in enumerate(refs[:-1]):
+        start = pl.multiple_of((place_ref[0] ^ k) * columns, columns)
+        out_ref[:, pl.ds(start, columns)] = ref[...]
+
+
 def head_norm(projected, gain):
     square_mean = jnp.mean(projected * projected, axis=-1, keepdims=True)
     return (projected * lax.rsqrt(square_mean + 1e-06) * gain).astype(BF16)
 
 
 def attend_kernel(
-    merged_ref, embed_ref, norm_ref, qkv_ref, qgain_ref, kgain_ref, out_ref,
-    kv_ref, q_ref, k_ref, v_ref,
+    place_ref, merged_ref, embed_ref, norm_ref, qkv_ref, qgain_ref, kgain_ref, out_ref, own_ref,
+    kv_ref, q_ref, k_ref, v_ref, *, grp_size, block,
 ):
     latents, width = embed_ref.shape
     head = q_ref.shape[1]
@@ -184,19 +232,32 @@
         denominator = jnp.sum(weights, axis=-1, keepdims=True)
         mixed = jnp.dot(weights.astype(BF16), v_ref[...], preferred_element_type=F32)
         out_ref[here, :] = (mixed / denominator).astype(BF16)
-
-
-def call(body, shape, dtype, *args, name, scratch=(), flops=10**8, moved=10**6):
-    return pl.pallas_call(
+    grp = place_ref[0]
+    for i in range(total // (block * grp_size)):
+        start = pl.multiple_of((i * grp_size + grp) * block, block)
+        mine = out_ref[pl.ds(start, block), :]
+        for j in range(own_ref.shape[0]):
+            own_ref[j, i * block : (i + 1) * block, :] = mine
+
+
+def call(body, shapes, *args, name, scratch=(), places=(), flops=10**8, moved=10**6):
+    spaces = {"smem": pltpu.SMEM, "any": pl.ANY}
+    outs = tuple(jax.ShapeDtypeStruct(shape, BF16) for shape in shapes)
+    whole = pl.BlockSpec(memory_space=pltpu.VMEM)
+    in_specs = [whole] * len(args)
+    for i, place in enumerate(places):
+        in_specs[i] = pl.BlockSpec(memory_space=spaces[place])
+    result = pl.pallas_call(
         body,
-        out_shape=jax.ShapeDtypeStruct(shape, dtype),
-        in_specs=[pl.BlockSpec(memory_space=pltpu.VMEM)] * len(args),
-        out_specs=pl.BlockSpec(memory_space=pltpu.VMEM),
+        out_shape=outs,
+        in_specs=in_specs,
+        out_specs=(whole,) * len(outs),
         scratch_shapes=list(scratch),
         cost_estimate=pl.CostEstimate(flops=flops, bytes_accessed=moved, transcendentals=0),
         compiler_params=pltpu.CompilerParams(vmem_limit_bytes=48 * 2**20),
         name=name,
     )(*args)
+    return result[0] if len(outs) == 1 else result
 
 
 def shards(
@@ -204,15 +265,16 @@
     out_weight, cotangent,
 ):
     grp_size, seq_size, dp_size = (lax.axis_size(a) for a in ("grp", "seq", "dp"))
-    slabs = seq_size // 2
     owners = grp_size * seq_size
     block, width = cotangent.shape[1:]
     head = q_gain.shape[0]
     groups = block * owners
     columns = width // grp_size
+    shared = block * grp_size
+    rows = block * seq_size
     grp = lax.axis_index("grp")
     seq = lax.axis_index("seq")
-    same_side = [list(range(k, seq_size, 2)) for k in range(2)]
+    place = jnp.stack([grp, seq]).astype(jnp.int32)
 
     frames = video[0]
     frame_count, tokens = frames.shape[:2]
@@ -220,76 +282,80 @@
     latent_t = latent_weight.T
     labels = assign[0].reshape(1, -1)
     late = call(
-        late_kernel, ((frame_count - 2) * tokens, LANES), BF16, frames, conv_weight, latent_t,
-        name="late_frames", flops=10**9,
+        late_kernel, [((frame_count - 2) * tokens, LANES)], frames, conv_weight, latent_t,
+        name="late_frames", flops=10**9, places=["any"] * 3,
+        scratch=[
+            pltpu.VMEM(x.shape, BF16) for x in (frames, conv_weight, latent_t)
+        ] + [pltpu.SemaphoreType.DMA((3,))],
     )
     sums = call(
-        functools.partial(sums_kernel, grp=grp_size, seq=seq_size), (groups, LANES), BF16,
+        functools.partial(sums_kernel, grp=grp_size, seq=seq_size), [(groups, LANES)],
         frames, earlier, conv_weight, latent_t, late, labels, name="group_sums", flops=10**9,
     )
 
-    shared = block * grp_size
+    by_column = jnp.concatenate(
+        [cotangent[0, :, g * columns : (g + 1) * columns] for g in range(grp_size)], axis=0
+    ).reshape(grp_size, block, columns)
+    near = lax.all_to_all(by_column, "grp", 0, 0, tiled=True).reshape(shared, columns)
+
     parts = lax.all_to_all(sums.reshape(seq_size, shared, LANES), "seq", 0, 0, tiled=True)
-    slab_sums = call(resplit_kernel, (grp_size, shared, LANES), BF16, parts, name="slab_sums")
+    slab_sums = call(resplit_kernel, [(grp_size, shared, LANES)], parts, name="slab_sums")
     slab_parts = lax.all_to_all(slab_sums, "grp", 0, 0, tiled=True)
-    merged = call(merge_kernel, (seq_size, shared, LANES), BF16, slab_parts, name="merged")
+    merged = call(merge_kernel, [(seq_size, shared, LANES)], slab_parts, name="merged")
     merged = lax.all_to_all(merged, "seq", 0, 0, tiled=True).reshape(groups, LANES)
 
-    cot, _ = lax.optimization_barrier((cotangent, sums))
-    by_column = cot[0].reshape(block, grp_size, columns).transpose(1, 0, 2)
-    by_column = jnp.broadcast_to(by_column[None], (2,) + by_column.shape)
-    corners = [
-        [g * seq_size + 2 * z + y for y in range(2) for g in range(grp_size)] for z in range(slabs)
-    ]
-    near = lax.all_to_all(
-        by_column.reshape(2 * grp_size, block, columns), ("grp", "seq"), 0, 0,
-        axis_index_groups=corners, tiled=True,
-    ).reshape(2 * shared, columns)
-    far = lax.all_to_all(
-        jnp.broadcast_to(near[None], (slabs,) + near.shape), "seq", 0, 0,
-        axis_index_groups=same_side, tiled=True,
-    )
-    grad_rows = far.reshape(groups, columns)
-
-    late_weight, _ = lax.optimization_barrier((out_weight, slab_parts))
-    weight_pair = xor_swap(late_weight, "seq", 1)
-
-    head_out = call(
-        attend_kernel, (groups, head), BF16, merged, embed_weight, norm_gain[None], qkv_weight,
-        q_gain[None], k_gain[None], name="attend", flops=8 * 10**9,
+    masks = (8, 4, 1, 2)
+    for mask in masks[:-1]:
+        near = jnp.concatenate([near, xor_swap(near, "seq", mask)], axis=0)
+    far = xor_swap(near, "seq", masks[-1])
+
+    side = seq & 1
+    depth = (seq >> 1) & 1
+
+    def halved(block, choice, mask):
+        size = block.shape[1] // 2
+        kept = lax.dynamic_slice_in_dim(block, choice * size, size, 1)
+        given = lax.dynamic_slice_in_dim(block, (1 - choice) * size, size, 1)
+        return jnp.concatenate([kept, xor_swap(given, "seq", mask)], axis=0)
+
+    weight, _ = lax.optimization_barrier((out_weight, slab_sums))
+    weight_quad = halved(halved(weight, side, 1), depth, 2)
+
+    head_out, own_rows = call(
+        functools.partial(attend_kernel, grp_size=grp_size, block=block),
+        [(groups, head), (4, rows, head)], place, merged, embed_weight, norm_gain[None],
+        qkv_weight, q_gain[None], k_gain[None], name="attend", flops=8 * 10**9, places=["smem"],
         scratch=[pltpu.VMEM((width, 2 * head), BF16)] + [pltpu.VMEM((groups, head), BF16)] * 3,
     )
 
-    side = seq % 2
-    by_owner = lax.dynamic_index_in_dim(
-        head_out.reshape(slabs, 2, grp_size, block, head), grp, 2, keepdims=False
-    )
-    mine = lax.dynamic_index_in_dim(by_owner, side, 1, keepdims=False)
-    theirs = xor_swap(lax.dynamic_index_in_dim(by_owner, 1 - side, 1, keepdims=False), "seq", 1)
-
-    local_grad = lax.dot_general(
-        head_out, grad_rows, TN, preferred_element_type=F32
-    ).astype(BF16)
+    quads = [list(range(k, k + 4)) for k in range(0, seq_size, 4)]
+    quad_heads = lax.all_to_all(own_rows, "seq", 0, 0, axis_index_groups=quads, tiled=True)
+    local_grad = call(
+        functools.partial(grad_kernel, masks=masks), [(head, columns)], place, head_out, near, far,
+        name="local_grad", places=["smem"], scratch=[pltpu.VMEM((groups, head), BF16)],
+        flops=10**9,
+    )
     grad_parts = lax.all_to_all(
         local_grad.reshape(dp_size, head // dp_size, columns), "dp", 0, 0, tiled=True
     )
-
-    both = jnp.concatenate([mine, theirs], axis=2).reshape(-1, 2 * head)
-    both_weights = jnp.concatenate([out_weight, weight_pair], axis=0)
-    partial = jnp.dot(both, both_weights, preferred_element_type=F32).astype(BF16)
+    grad_block = call(
+        spread_kernel, [(dp_size, head // dp_size, columns)], grad_parts, name="grad_block"
+    )
+    grad_cols = lax.all_to_all(grad_block, "dp", 0, 0, tiled=True).reshape(head, columns)
+
+    partial = call(
+        project_kernel, [(rows, columns)], place, quad_heads, weight_quad, name="project",
+        places=["smem"], flops=10**9,
+    )
+    partial, _ = lax.optimization_barrier((partial, grad_cols))
     out_parts = lax.all_to_all(
-        partial.reshape(slabs, block, width), "seq", 0, 0, axis_index_groups=same_side, tiled=True
-    )
-
-    grad_block = call(
-        spread_kernel, (dp_size, head // dp_size, columns), BF16, grad_parts, name="grad_block"
-    )
-    grad_cols = lax.all_to_all(grad_block, "dp", 0, 0, tiled=True).reshape(head, columns)
-    out_grad = lax.all_to_all(
-        jnp.broadcast_to(grad_cols[None], (grp_size, head, columns)), "grp", 0, 0, tiled=True
-    )
-    out_grad = out_grad.transpose(1, 0, 2).reshape(head, width)
-    attended = jnp.sum(out_parts.astype(F32), axis=0).astype(BF16)
+        partial.reshape(seq_size, block, columns), "seq", 0, 0, tiled=True
+    )
+    gathered = [grad_cols] + [xor_swap(grad_cols, "grp", k) for k in range(1, grp_size)]
+    out_grad = call(
+        columns_kernel, [(head, width)], place, *gathered, name="grad_columns", places=["smem"]
+    )
+    attended = call(attended_kernel, [(block, width)], out_parts, name="attended")
     return (attended[None], out_grad)
 
 

time: 190 us -> 160 us (0.84)
  blocking collectives: 48.2 us -> 9.29 us
  starting transfers between devices: 43.1 us -> 77.8 us
  waiting for transfers between devices: 68.2 us -> 38.3 us
  Pallas kernels: 12.1 us -> 22 us
  matrix products: 4.89 us -> 0 us
    all_to_all x4 -> x5, waiting for transfers between devices: 59.9 us -> 7.94 us  [the longest x1 4.65 us: shards(): lax.all_to_all(grad_block, 'dp', 0, 0, tiled=True).reshape(head, columns)]
    all_to_all x3 -> x1, blocking collectives: 48.2 us -> 9.29 us  [shards(): lax.all_to_all(by_column, 'grp', 0, 0, tiled=True).reshape(shared, columns)]
    ppermute x2 -> x9, starting transfers between devices: 7 us -> 37.1 us  [xor_swap(): return lax.ppermute(block, axis, route)]
    ppermute x2 -> x9, waiting for transfers between devices: 3.96 us -> 17 us  [xor_swap(): return lax.ppermute(block, axis, route)]
    pallas_call x6 -> x10, Pallas kernels: 12.1 us -> 22 us  [call(): pl.pallas_call(body, out_shape=outs, in_specs=in_specs, out_specs=(whole,...]
    all_to_all x4 -> x5, starting transfers between devices: 15.9 us -> 25.9 us  [the longest x1 6.91 us: shards(): lax.all_to_all(partial.reshape(seq_size, block, columns), 'seq', 0, 0, ti...]
    all_to_all x1, waiting for transfers between devices: 0.01 us -> 8.93 us  [shards(): lax.all_to_all(local_grad.reshape(dp_size, head // dp_size, columns), 'dp...]
    dot_general x2 -> x0, matrix products: 4.89 us -> none  [the longest x1 2.49 us: shards(): lax.dot_general(head_out, grad_rows, TN, preferred_element_type=F32)]
  transfers between devices with their start and end apart: 9 -> 17, of which waited for: 6 -> 9; matrix products, arithmetic and copies ran while one was open for 3% -> 4% of each run, Pallas kernels for 6% -> 13%
where the time goes in v2:
time: 160 us; the launch traced here: 159 us
  starting transfers between devices  77.8 us (49%)
  waiting for transfers between devices  38.3 us (24%)
  Pallas kernels  22 us (14%)
  blocking collectives  9.29 us (6%)
  local copies, waits for them, and re-layouts  7.64 us (5%)
  other arithmetic  2.57 us (2%)
    ppermute x9, starting transfers between devices, xor_swap(): return lax.ppermute(block, axis, route)  37.1 us
    pallas_call x10, Pallas kernels, call(): pl.pallas_call(body, out_shape=outs, in_specs=in_specs, out_specs=(whole,...  22 us
    ppermute x9, waiting for transfers between devices, xor_swap(): return lax.ppermute(block, axis, route)  17 us
    all_to_all x1, blocking collectives, shards(): lax.all_to_all(by_column, 'grp', 0, 0, tiled=True).reshape(shared, columns)  9.29 us
    all_to_all x1, waiting for transfers between devices, shards(): lax.all_to_all(local_grad.reshape(dp_size, head // dp_size, columns), 'dp...  8.93 us
    all_to_all x1, starting transfers between devices, shards(): lax.all_to_all(local_grad.reshape(dp_size, head // dp_size, columns), 'dp...  8.42 us
    all_to_all x1, starting transfers between devices, shards(): lax.all_to_all(partial.reshape(seq_size, block, columns), 'seq', 0, 0, ti...  6.91 us
    all_to_all x1, starting transfers between devices, shards(): lax.all_to_all(grad_block, 'dp', 0, 0, tiled=True).reshape(head, columns)  6.22 us
  transfers between devices with their start and end apart: 17, of which 9 were waited for; matrix products, arithmetic and copies ran while one was open for 4% of the time, Pallas kernels for 13%

profile of v2, /device:TPU:1, one launch (start us, length us, event | category | flops | bytes accessed | tf_op | source)
XLA Modules:
  0.0 158.6 jit_solution(11992422055932011667)
XLA Ops:
  0.6 0.8 slice_bitcast_fusion.4
  1.4 9.3 %all_to_all.40 = bf16[4,16,768]{2,1,0:T(8,128)(2,1)S(1)} all-to-all(bf16[4,16,768]{2,1,0:T(8,128)(2,1)S(1)} %bitcast.41), channel_id=1, replica_groups=mesh['grp'=4,'seq'=16,'dp'=8] {'grp'}, dimensions={0} | all-to-all | bytes 196608 | tf_op jit(solution)/shard_map/all_to_all | solution.py:299
  10.7 10.6 %collective-permute-start.3 = (bf16[64,768]{1,0:T(8,128)(2,1)S(1)}, bf16[64,768]{1,0:T(8,128)(2,1)S(1)}, u32[]{:S(2)}, u32[]{:S(2)}) collective-permute-start(bf16[64,768]{1,0:T(8,128)(2,1)S(1)} %bitcast.37), channel_id=1, source_target_pairs={{0,64},{8,72},{16,80},{24,88},{32,96},{40,104},{48,112},{56,120},{... | collective-permute-start | bytes 294920 | tf_op jit(solution)/shard_map/ppermute | solution.py:27
  21.4 0.9 slice_bitcast_fusion
  22.3 3.2 %collective-permute-start = (bf16[2,64,512]{2,1,0:T(8,128)(2,1)S(1)}, bf16[2,64,512]{2,1,0:T(8,128)(2,1)S(1)}, u32[]{:S(2)}, u32[]{:S(2)}) collective-permute-start(bf16[2,64,512]{2,1,0:T(8,128)(2,1)S(1)} %slice_bitcast_fusion), channel_id=1, source_target_pairs={{0,8},{8,16},{16,24},{24,32},{32,40},{40,48},{48,56},{56,64},{64,7... | collective-permute-start | bytes 393224 | tf_op jit(solution)/shard_map/ppermute | solution.py:22
  25.5 1.0 copy-done
  26.6 0.9 copy-done.4
  27.4 0.8 copy-done.6
  28.3 1.2 late_frames.1.late_ref
  29.5 0.1 reshape_squeeze.3.labels_ref
  29.6 4.0 %collective-permute-start.4 = (bf16[128,768]{1,0:T(8,128)(2,1)S(1)}, bf16[128,768]{1,0:T(8,128)(2,1)S(1)}, u32[]{:S(2)}, u32[]{:S(2)}) collective-permute-start(bf16[128,768]{1,0:T(8,128)(2,1)S(1)} %pad_maximum_fusion.3), channel_id=1, source_target_pairs={{0,32},{8,40},{16,48},{24,56},{32,0},{40,8},{48,16},{56,24},{64,96... | collective-permute-start | bytes 589832 | tf_op jit(solution)/shard_map/ppermute | solution.py:27
  33.7 1.6 %group_sums.1 = bf16[1024,128]{1,0:T(8,128)(2,1)} custom-call(bf16[8,64,512]{2,1,0:T(8,128)(2,1)S(1)} %bitcast.31, bf16[2,64,512]{2,1,0:T(8,128)(2,1)S(1)} %collective-permute-done.earlier_ref, bf16[3,128,128]{2,1,0:T(8,128)(2,1)S(1)} %copy-done.5, bf16[64,512]{1,0:T(8,128)(2,1)S(1)} %bitcast.33, bf16[384,128]{1,0:T(8,128)(2,1)S(1)} %late_frames.1.late_ref, ...), custom_call_target="tpu_custom_call" | custom-call | flops 1000000000 | bytes 1000000 | tf_op jit(solution)/shard_map/group_sums/pallas_call | solution.py:250
  35.3 3.5 %all-to-all-start = ((bf16[16,64,128]{2,1,0:T(8,128)(2,1)}), bf16[16,64,128]{2,1,0:T(8,128)(2,1)S(1)}, u32[]{:S(2)}, u32[]{:S(2)}) async-start(bf16[16,64,128]{2,1,0:T(8,128)(2,1)} %bitcast.5), calls=%async_computation | async-start | bytes 524288 | tf_op jit(solution)/shard_map/all_to_all | solution.py:301
  38.8 3.6 %collective-permute-done.4 = bf16[128,768]{1,0:T(8,128)(2,1)S(1)} collective-permute-done((bf16[128,768]{1,0:T(8,128)(2,1)S(1)}, bf16[128,768]{1,0:T(8,128)(2,1)S(1)}, u32[]{:S(2)}, u32[]{:S(2)}) %collective-permute-start.4) | collective-permute-done | bytes 196640 | tf_op jit(solution)/shard_map/ppermute | solution.py:27
  42.5 3.0 %collective-permute-start.5 = (bf16[256,768]{1,0:T(8,128)(2,1)S(1)}, bf16[256,768]{1,0:T(8,128)(2,1)}, u32[]{:S(2)}, u32[]{:S(2)}) collective-permute-start(bf16[256,768]{1,0:T(8,128)(2,1)S(1)} %pad_maximum_fusion.2), channel_id=1, source_target_pairs={{0,8},{8,0},{16,24},{24,16},{32,40},{40,32},{48,56},{56,48},{64,72... | collective-permute-start | bytes 1179656 | tf_op jit(solution)/shard_map/ppermute | solution.py:27
  45.5 3.3 %all-to-all-done.parts_ref = bf16[16,64,128]{2,1,0:T(8,128)(2,1)S(1)} async-done(((bf16[16,64,128]{2,1,0:T(8,128)(2,1)}), bf16[16,64,128]{2,1,0:T(8,128)(2,1)S(1)}, u32[]{:S(2)}, u32[]{:S(2)}) %all-to-all-start) | async-done | bytes 262176 | tf_op jit(solution)/shard_map/all_to_all | solution.py:301
  48.8 0.8 slab_sums.1
  49.6 3.3 %all-to-all-start.1 = ((bf16[4,64,128]{2,1,0:T(8,128)(2,1)}), bf16[4,64,128]{2,1,0:T(8,128)(2,1)S(1)}, u32[]{:S(2)}, u32[]{:S(2)}) async-start(bf16[4,64,128]{2,1,0:T(8,128)(2,1)} %slab_sums.1), calls=%async_computation.1 | async-start | bytes 131072 | tf_op jit(solution)/shard_map/all_to_all | solution.py:303
  52.9 4.4 %all-to-all-done.1.parts_ref = bf16[4,64,128]{2,1,0:T(8,128)(2,1)S(1)} async-done(((bf16[4,64,128]{2,1,0:T(8,128)(2,1)}), bf16[4,64,128]{2,1,0:T(8,128)(2,1)S(1)}, u32[]{:S(2)}, u32[]{:S(2)}) %all-to-all-start.1) | async-done | bytes 65568 | tf_op jit(solution)/shard_map/all_to_all | solution.py:303
  57.4 0.9 merged.1
  58.2 5.8 %all-to-all-start.2 = ((bf16[16,64,128]{2,1,0:T(8,128)(2,1)}), bf16[16,64,128]{2,1,0:T(8,128)(2,1)S(1)}, u32[]{:S(2)}, u32[]{:S(2)}) async-start(bf16[16,64,128]{2,1,0:T(8,128)(2,1)} %merged.1), calls=%async_computation.2 | async-start | bytes 524288 | tf_op jit(solution)/shard_map/all_to_all | solution.py:305
  64.0 0.1 pad_add_fusion.place_ref
  64.1 1.3 pad_maximum_fusion.1.first_ref
  65.5 3.3 %collective-permute-start.6 = (bf16[512,768]{1,0:T(8,128)(2,1)S(1)}, bf16[512,768]{1,0:T(8,128)(2,1)}, u32[]{:S(2)}, u32[]{:S(2)}) collective-permute-start(bf16[512,768]{1,0:T(8,128)(2,1)S(1)} %pad_maximum_fusion.1.first_ref), channel_id=1, source_target_pairs={{0,16},{8,24},{16,0},{24,8},{32,48},{40,56},{48,32},{56,40},{64,80... | collective-permute-start | bytes 2359304 | tf_op jit(solution)/shard_map/ppermute | solution.py:27
  68.7 2.1 %constant_dynamic-slice_fusion = (bf16[128,1536]{1,0:T(8,128)(2,1)}, bf16[128,1536]{1,0:T(8,128)(2,1)}) fusion(bf16[128,3072]{1,0:T(8,128)(2,1)} %param.20, s32[]{:T(128)S(6)} %select_n.13, s32[]{:T(128)S(6)} %select_n.12), kind=kLoop, calls=%fused_computation.16 | loop fusion | bytes 1572872 | tf_op jit(solution)/shard_map/dynamic_slice | solution.py:318
  70.8 3.3 %collective-permute-start.1 = (bf16[128,1536]{1,0:T(8,128)(2,1)}, bf16[128,1536]{1,0:T(8,128)(2,1)}, u32[]{:S(2)}, u32[]{:S(2)}) collective-permute-start(bf16[128,1536]{1,0:T(8,128)(2,1)} %get-tuple-element.12), channel_id=1, source_target_pairs={{0,8},{8,0},{16,24},{24,16},{32,40},{40,32},{48,56},{56,48},{64,72... | collective-permute-start | bytes 1179656 | tf_op jit(solution)/shard_map/ppermute | solution.py:27
  74.1 1.0 copy-done.3
  75.1 10.6 %attend.1 = (bf16[1024,128]{1,0:T(8,128)(2,1)S(1)}, bf16[4,256,128]{2,1,0:T(8,128)(2,1)}) custom-call(s32[2]{0:T(128)S(1)} %pad_add_fusion.place_ref, bf16[1024,128]{1,0:T(8,128)(2,1)S(1)} %bitcast.29, bf16[64,3072]{1,0:T(8,128)(2,1)S(1)} %copy-done.3, f32[1,3072]{1,0:T(1,128)S(1)} %bitcast.34, bf16[3,3072,128]{2,1,0:T(8,128)(2,1)S(1)} %copy-done.2, ...), custom_call_target="tpu_custom_call" | custom-call | flops 8000000000 | bytes 1000000 | tf_op jit(solution)/shard_map/attend/pallas_call | solution.py:250
  85.7 3.1 %collective-permute-done.6.second_ref = bf16[512,768]{1,0:T(8,128)(2,1)} collective-permute-done((bf16[512,768]{1,0:T(8,128)(2,1)S(1)}, bf16[512,768]{1,0:T(8,128)(2,1)}, u32[]{:S(2)}, u32[]{:S(2)}) %collective-permute-start.6) | collective-permute-done | bytes 786464 | tf_op jit(solution)/shard_map/ppermute | solution.py:27
  88.8 2.3 %local_grad.1 = bf16[128,768]{1,0:T(8,128)(2,1)} custom-call(s32[2]{0:T(128)S(1)} %pad_add_fusion.place_ref, bf16[1024,128]{1,0:T(8,128)(2,1)S(1)} %get-tuple-element.8.head_ref, bf16[512,768]{1,0:T(8,128)(2,1)S(1)} %pad_maximum_fusion.1.first_ref, bf16[512,768]{1,0:T(8,128)(2,1)} %collective-permute-done.6.second_ref), custom_call_target="tpu_custom_call" | custom-call | flops 1000000000 | bytes 1000000 | tf_op jit(solution)/shard_map/local_grad/pallas_call | solution.py:250
  91.1 8.4 %all-to-all-start.5 = ((bf16[8,16,768]{2,1,0:T(8,128)(2,1)}), bf16[8,16,768]{2,1,0:T(8,128)(2,1)S(1)}, u32[]{:S(2)}, u32[]{:S(2)}) async-start(bf16[8,16,768]{2,1,0:T(8,128)(2,1)} %bitcast.16), calls=%async_computation.5 | async-start | bytes 393216 | tf_op jit(solution)/shard_map/all_to_all | solution.py:338
  99.5 8.9 %all-to-all-done.5.parts_ref = bf16[8,16,768]{2,1,0:T(8,128)(2,1)S(1)} async-done(((bf16[8,16,768]{2,1,0:T(8,128)(2,1)}), bf16[8,16,768]{2,1,0:T(8,128)(2,1)S(1)}, u32[]{:S(2)}, u32[]{:S(2)}) %all-to-all-start.5) | async-done | bytes 196640 | tf_op jit(solution)/shard_map/all_to_all | solution.py:338
  108.4 3.4 %all-to-all-start.3 = ((bf16[4,256,128]{2,1,0:T(8,128)(2,1)}), bf16[4,256,128]{2,1,0:T(8,128)(2,1)S(1)}, u32[]{:S(2)}, u32[]{:S(2)}) async-start(bf16[4,256,128]{2,1,0:T(8,128)(2,1)} %get-tuple-element.6), calls=%async_computation.3 | async-start | bytes 524288 | tf_op jit(solution)/shard_map/all_to_all | solution.py:332
  111.9 1.1 fusion.1
  113.0 3.3 %collective-permute-start.2 = (bf16[256,768]{1,0:T(8,128)(2,1)S(1)}, bf16[256,768]{1,0:T(8,128)(2,1)S(1)}, u32[]{:S(2)}, u32[]{:S(2)}) collective-permute-start(bf16[256,768]{1,0:T(8,128)(2,1)S(1)} %get-tuple-element.11), channel_id=1, source_target_pairs={{0,16},{8,24},{16,0},{24,8},{32,48},{40,56},{48,32},{56,40},{64,80... | collective-permute-start | bytes 1179656 | tf_op jit(solution)/shard_map/ppermute | solution.py:27
  116.3 0.7 grad_block.1
  117.0 6.2 %all-to-all-start.6 = ((bf16[8,16,768]{2,1,0:T(8,128)(2,1)}), bf16[8,16,768]{2,1,0:T(8,128)(2,1)S(1)}, u32[]{:S(2)}, u32[]{:S(2)}) async-start(bf16[8,16,768]{2,1,0:T(8,128)(2,1)} %grad_block.1), calls=%async_computation.6 | async-start | bytes 393216 | tf_op jit(solution)/shard_map/all_to_all | solution.py:344
  123.2 2.6 %collective-permute-done.2 = bf16[256,768]{1,0:T(8,128)(2,1)S(1)} collective-permute-done((bf16[256,768]{1,0:T(8,128)(2,1)S(1)}, bf16[256,768]{1,0:T(8,128)(2,1)S(1)}, u32[]{:S(2)}, u32[]{:S(2)}) %collective-permute-start.2) | collective-permute-done | bytes 393248 | tf_op jit(solution)/shard_map/ppermute | solution.py:27
  125.9 1.7 %project.1 = bf16[256,768]{1,0:T(8,128)(2,1)} custom-call(s32[2]{0:T(128)S(1)} %pad_add_fusion.place_ref, bf16[4,256,128]{2,1,0:T(8,128)(2,1)S(1)} %all-to-all-done.3.heads_ref, bf16[512,768]{1,0:T(8,128)(2,1)S(1)} %pad_maximum_fusion.weight_ref), custom_call_target="tpu_custom_call" | custom-call | flops 1000000000 | bytes 1000000 | tf_op jit(solution)/shard_map/project/pallas_call | solution.py:250
  127.6 4.7 %all-to-all-done.6 = bf16[8,16,768]{2,1,0:T(8,128)(2,1)S(1)} async-done(((bf16[8,16,768]{2,1,0:T(8,128)(2,1)}), bf16[8,16,768]{2,1,0:T(8,128)(2,1)S(1)}, u32[]{:S(2)}, u32[]{:S(2)}) %all-to-all-start.6) | async-done | bytes 196640 | tf_op jit(solution)/shard_map/all_to_all | solution.py:344
  132.2 6.9 %all-to-all-start.7 = ((bf16[16,16,768]{2,1,0:T(8,128)(2,1)}), bf16[16,16,768]{2,1,0:T(8,128)(2,1)S(1)}, u32[]{:S(2)}, u32[]{:S(2)}) async-start(bf16[16,16,768]{2,1,0:T(8,128)(2,1)} %bitcast.18), calls=%async_computation.7 | async-start | bytes 786432 | tf_op jit(solution)/shard_map/all_to_all | solution.py:351
  139.1 2.2 %collective-permute-start.7 = (bf16[128,768]{1,0:T(8,128)(2,1)S(1)}, bf16[128,768]{1,0:T(8,128)(2,1)S(1)}, u32[]{:S(2)}, u32[]{:S(2)}) collective-permute-start(bf16[128,768]{1,0:T(8,128)(2,1)S(1)} %bitcast.25), channel_id=1, source_target_pairs={{0,128},{128,0},{256,384},{384,256},{1,129},{129,1},{257,385},{385... | collective-permute-start | bytes 589832 | tf_op jit(solution)/shard_map/ppermute | solution.py:27
  141.3 3.7 %collective-permute-start.8 = (bf16[128,768]{1,0:T(8,128)(2,1)S(1)}, bf16[128,768]{1,0:T(8,128)(2,1)S(1)}, u32[]{:S(2)}, u32[]{:S(2)}) collective-permute-start(bf16[128,768]{1,0:T(8,128)(2,1)S(1)} %bitcast.26), channel_id=1, source_target_pairs={{0,256},{128,384},{256,0},{384,128},{1,257},{129,385},{257,1},{385... | collective-permute-start | bytes 589832 | tf_op jit(solution)/shard_map/ppermute | solution.py:27
  145.0 3.7 %collective-permute-start.9 = (bf16[128,768]{1,0:T(8,128)(2,1)S(1)}, bf16[128,768]{1,0:T(8,128)(2,1)S(1)}, u32[]{:S(2)}, u32[]{:S(2)}) collective-permute-start(bf16[128,768]{1,0:T(8,128)(2,1)S(1)} %bitcast.27), channel_id=1, source_target_pairs={{0,384},{128,256},{256,128},{384,0},{1,385},{129,257},{257,129},{3... | collective-permute-start | bytes 589832 | tf_op jit(solution)/shard_map/ppermute | solution.py:27
  148.7 2.9 %collective-permute-done.8.refs_2_ = bf16[128,768]{1,0:T(8,128)(2,1)S(1)} collective-permute-done((bf16[128,768]{1,0:T(8,128)(2,1)S(1)}, bf16[128,768]{1,0:T(8,128)(2,1)S(1)}, u32[]{:S(2)}, u32[]{:S(2)}) %collective-permute-start.8) | collective-permute-done | bytes 196640 | tf_op jit(solution)/shard_map/ppermute | solution.py:27
  151.7 4.7 %collective-permute-done.9.refs_3_ = bf16[128,768]{1,0:T(8,128)(2,1)S(1)} collective-permute-done((bf16[128,768]{1,0:T(8,128)(2,1)S(1)}, bf16[128,768]{1,0:T(8,128)(2,1)S(1)}, u32[]{:S(2)}, u32[]{:S(2)}) %collective-permute-start.9) | collective-permute-done | bytes 196640 | tf_op jit(solution)/shard_map/ppermute | solution.py:27
  156.4 1.5 grad_columns.1
  157.9 0.7 attended.1
  (38 shorter events, 0.2 us)
Async XLA Ops:
  10.7 18.9 %collective-permute-start.3 = (bf16[64,768]{1,0:T(8,128)(2,1)S(1)}, bf16[64,768]{1,0:T(8,128)(2,1)S(1)}, u32[]{:S(2)}, u32[]{:S(2)}) collective-permute-start(bf16[64,768]{1,0:T(8,128)(2,1)S(1)} %bitcast.37), channel_id=1, source_target_pairs={{0,64},{8,72},{16,80},{24,88},{32,96},{40,104},{48,112},{56,120},{... | collective-permute-start | bytes 294920 | tf_op jit(solution)/shard_map/ppermute | solution.py:27
  22.3 11.4 %collective-permute-start = (bf16[2,64,512]{2,1,0:T(8,128)(2,1)S(1)}, bf16[2,64,512]{2,1,0:T(8,128)(2,1)S(1)}, u32[]{:S(2)}, u32[]{:S(2)}) collective-permute-start(bf16[2,64,512]{2,1,0:T(8,128)(2,1)S(1)} %slice_bitcast_fusion), channel_id=1, source_target_pairs={{0,8},{8,16},{16,24},{24,32},{32,40},{40,48},{48,56},{56,64},{64,7... | collective-permute-start | bytes 393224 | tf_op jit(solution)/shard_map/ppermute | solution.py:22
  25.5 1.0 copy-start
  26.6 0.9 copy-start.4
  27.4 0.8 copy-start.6
  28.3 1.2 copy-start.14
  28.3 5.4 %copy-start.1 = (bf16[1,8,64,512]{3,2,1,0:T(8,128)(2,1)S(1)}, bf16[1,8,64,512]{3,2,1,0:T(8,128)(2,1)}, u32[]{:S(2)}) copy-start(bf16[1,8,64,512]{3,2,1,0:T(8,128)(2,1)} %param.11) | copy-start | bytes 1572868
  28.3 5.4 %copy-start.5 = (bf16[3,128,128]{2,1,0:T(8,128)(2,1)S(1)}, bf16[3,128,128]{2,1,0:T(8,128)(2,1)}, u32[]{:S(2)}) copy-start(bf16[3,128,128]{2,1,0:T(8,128)(2,1)} %conv_ref.1) | copy-start | bytes 294916
  28.3 5.4 %copy-start.7 = (bf16[512,64]{0,1:T(8,128)(2,1)S(1)}, bf16[512,64]{0,1:T(8,128)(2,1)}, u32[]{:S(2)}) copy-start(bf16[512,64]{0,1:T(8,128)(2,1)} %param.13) | copy-start | bytes 196612
  29.6 12.9 %copy-start.12 = (bf16[64,768]{1,0:T(8,128)(2,1)}, bf16[64,768]{1,0:T(8,128)(2,1)S(1)}, u32[]{:S(2)}) copy-start(bf16[64,768]{1,0:T(8,128)(2,1)S(1)} %collective-permute-done.3) | copy-start | bytes 294916
  29.6 12.8 %collective-permute-start.4 = (bf16[128,768]{1,0:T(8,128)(2,1)S(1)}, bf16[128,768]{1,0:T(8,128)(2,1)S(1)}, u32[]{:S(2)}, u32[]{:S(2)}) collective-permute-start(bf16[128,768]{1,0:T(8,128)(2,1)S(1)} %pad_maximum_fusion.3), channel_id=1, source_target_pairs={{0,32},{8,40},{16,48},{24,56},{32,0},{40,8},{48,16},{56,24},{64,96... | collective-permute-start | bytes 589832 | tf_op jit(solution)/shard_map/ppermute | solution.py:27
  35.3 13.5 %all-to-all-start = ((bf16[16,64,128]{2,1,0:T(8,128)(2,1)}), bf16[16,64,128]{2,1,0:T(8,128)(2,1)S(1)}, u32[]{:S(2)}, u32[]{:S(2)}) async-start(bf16[16,64,128]{2,1,0:T(8,128)(2,1)} %bitcast.5), calls=%async_computation | async-start | bytes 524288 | tf_op jit(solution)/shard_map/all_to_all | solution.py:301
  42.5 21.6 %copy-start.13 = (bf16[128,768]{1,0:T(8,128)(2,1)}, bf16[128,768]{1,0:T(8,128)(2,1)S(1)}, u32[]{:S(2)}) copy-start(bf16[128,768]{1,0:T(8,128)(2,1)S(1)} %collective-permute-done.4) | copy-start | bytes 589828
  42.5 21.6 %collective-permute-start.5 = (bf16[256,768]{1,0:T(8,128)(2,1)S(1)}, bf16[256,768]{1,0:T(8,128)(2,1)}, u32[]{:S(2)}, u32[]{:S(2)}) collective-permute-start(bf16[256,768]{1,0:T(8,128)(2,1)S(1)} %pad_maximum_fusion.2), channel_id=1, source_target_pairs={{0,8},{8,0},{16,24},{24,16},{32,40},{40,32},{48,56},{56,48},{64,72... | collective-permute-start | bytes 1179656 | tf_op jit(solution)/shard_map/ppermute | solution.py:27
  49.6 7.7 %all-to-all-start.1 = ((bf16[4,64,128]{2,1,0:T(8,128)(2,1)}), bf16[4,64,128]{2,1,0:T(8,128)(2,1)S(1)}, u32[]{:S(2)}, u32[]{:S(2)}) async-start(bf16[4,64,128]{2,1,0:T(8,128)(2,1)} %slab_sums.1), calls=%async_computation.1 | async-start | bytes 131072 | tf_op jit(solution)/shard_map/all_to_all | solution.py:303
  58.2 15.8 %all-to-all-start.2 = ((bf16[16,64,128]{2,1,0:T(8,128)(2,1)}), bf16[16,64,128]{2,1,0:T(8,128)(2,1)S(1)}, u32[]{:S(2)}, u32[]{:S(2)}) async-start(bf16[16,64,128]{2,1,0:T(8,128)(2,1)} %merged.1), calls=%async_computation.2 | async-start | bytes 524288 | tf_op jit(solution)/shard_map/all_to_all | solution.py:305
  64.1 9.9 %copy-start.2 = (bf16[3,3072,128]{2,1,0:T(8,128)(2,1)S(1)}, bf16[3,3072,128]{2,1,0:T(8,128)(2,1)}, u32[]{:S(2)}) copy-start(bf16[3,3072,128]{2,1,0:T(8,128)(2,1)} %qkv_ref.1) | copy-start | bytes 7077892
  64.1 10.0 %copy-start.8 = (f32[3072]{0:T(1024)S(1)}, f32[3072]{0:T(1024)}, u32[]{:S(2)}) copy-start(f32[3072]{0:T(1024)} %param.16) | copy-start | bytes 36868
  64.1 10.0 %copy-start.9 = (f32[128]{0:T(128)S(1)}, f32[128]{0:T(128)}, u32[]{:S(2)}) copy-start(f32[128]{0:T(128)} %param.18) | copy-start | bytes 1540
  64.1 10.0 %copy-start.10 = (f32[128]{0:T(128)S(1)}, f32[128]{0:T(128)}, u32[]{:S(2)}) copy-start(f32[128]{0:T(128)} %param.19) | copy-start | bytes 1540
  65.5 23.3 %collective-permute-start.6 = (bf16[512,768]{1,0:T(8,128)(2,1)S(1)}, bf16[512,768]{1,0:T(8,128)(2,1)}, u32[]{:S(2)}, u32[]{:S(2)}) collective-permute-start(bf16[512,768]{1,0:T(8,128)(2,1)S(1)} %pad_maximum_fusion.1.first_ref), channel_id=1, source_target_pairs={{0,16},{8,24},{16,0},{24,8},{32,48},{40,56},{48,32},{56,40},{64,80... | collective-permute-start | bytes 2359304 | tf_op jit(solution)/shard_map/ppermute | solution.py:27
  70.8 41.1 %collective-permute-start.1 = (bf16[128,1536]{1,0:T(8,128)(2,1)}, bf16[128,1536]{1,0:T(8,128)(2,1)}, u32[]{:S(2)}, u32[]{:S(2)}) collective-permute-start(bf16[128,1536]{1,0:T(8,128)(2,1)} %get-tuple-element.12), channel_id=1, source_target_pairs={{0,8},{8,0},{16,24},{24,16},{32,40},{40,32},{48,56},{56,48},{64,72... | collective-permute-start | bytes 1179656 | tf_op jit(solution)/shard_map/ppermute | solution.py:27
  74.1 1.0 copy-start.3
  88.8 23.1 %copy-start.11 = (bf16[128,1536]{1,0:T(8,128)(2,1)S(1)}, bf16[128,1536]{1,0:T(8,128)(2,1)}, u32[]{:S(2)}) copy-start(bf16[128,1536]{1,0:T(8,128)(2,1)} %get-tuple-element.13) | copy-start | bytes 1179652
  91.1 17.4 %all-to-all-start.5 = ((bf16[8,16,768]{2,1,0:T(8,128)(2,1)}), bf16[8,16,768]{2,1,0:T(8,128)(2,1)S(1)}, u32[]{:S(2)}, u32[]{:S(2)}) async-start(bf16[8,16,768]{2,1,0:T(8,128)(2,1)} %bitcast.16), calls=%async_computation.5 | async-start | bytes 393216 | tf_op jit(solution)/shard_map/all_to_all | solution.py:338
  108.4 8.6 %all-to-all-start.3 = ((bf16[4,256,128]{2,1,0:T(8,128)(2,1)}), bf16[4,256,128]{2,1,0:T(8,128)(2,1)S(1)}, u32[]{:S(2)}, u32[]{:S(2)}) async-start(bf16[4,256,128]{2,1,0:T(8,128)(2,1)} %get-tuple-element.6), calls=%async_computation.3 | async-start | bytes 524288 | tf_op jit(solution)/shard_map/all_to_all | solution.py:332
  113.0 12.9 %collective-permute-start.2 = (bf16[256,768]{1,0:T(8,128)(2,1)S(1)}, bf16[256,768]{1,0:T(8,128)(2,1)S(1)}, u32[]{:S(2)}, u32[]{:S(2)}) collective-permute-start(bf16[256,768]{1,0:T(8,128)(2,1)S(1)} %get-tuple-element.11), channel_id=1, source_target_pairs={{0,16},{8,24},{16,0},{24,8},{32,48},{40,56},{48,32},{56,40},{64,80... | collective-permute-start | bytes 1179656 | tf_op jit(solution)/shard_map/ppermute | solution.py:27
  117.0 15.2 %all-to-all-start.6 = ((bf16[8,16,768]{2,1,0:T(8,128)(2,1)}), bf16[8,16,768]{2,1,0:T(8,128)(2,1)S(1)}, u32[]{:S(2)}, u32[]{:S(2)}) async-start(bf16[8,16,768]{2,1,0:T(8,128)(2,1)} %grad_block.1), calls=%async_computation.6 | async-start | bytes 393216 | tf_op jit(solution)/shard_map/all_to_all | solution.py:344
  132.2 25.7 %all-to-all-start.7 = ((bf16[16,16,768]{2,1,0:T(8,128)(2,1)}), bf16[16,16,768]{2,1,0:T(8,128)(2,1)S(1)}, u32[]{:S(2)}, u32[]{:S(2)}) async-start(bf16[16,16,768]{2,1,0:T(8,128)(2,1)} %bitcast.18), calls=%async_computation.7 | async-start | bytes 786432 | tf_op jit(solution)/shard_map/all_to_all | solution.py:351
  139.1 9.6 %collective-permute-start.7 = (bf16[128,768]{1,0:T(8,128)(2,1)S(1)}, bf16[128,768]{1,0:T(8,128)(2,1)S(1)}, u32[]{:S(2)}, u32[]{:S(2)}) collective-permute-start(bf16[128,768]{1,0:T(8,128)(2,1)S(1)} %bitcast.25), channel_id=1, source_target_pairs={{0,128},{128,0},{256,384},{384,256},{1,129},{129,1},{257,385},{385... | collective-permute-start | bytes 589832 | tf_op jit(solution)/shard_map/ppermute | solution.py:27
  141.3 10.4 %collective-permute-start.8 = (bf16[128,768]{1,0:T(8,128)(2,1)S(1)}, bf16[128,768]{1,0:T(8,128)(2,1)S(1)}, u32[]{:S(2)}, u32[]{:S(2)}) collective-permute-start(bf16[128,768]{1,0:T(8,128)(2,1)S(1)} %bitcast.26), channel_id=1, source_target_pairs={{0,256},{128,384},{256,0},{384,128},{1,257},{129,385},{257,1},{385... | collective-permute-start | bytes 589832 | tf_op jit(solution)/shard_map/ppermute | solution.py:27
  145.0 11.4 %collective-permute-start.9 = (bf16[128,768]{1,0:T(8,128)(2,1)S(1)}, bf16[128,768]{1,0:T(8,128)(2,1)S(1)}, u32[]{:S(2)}, u32[]{:S(2)}) collective-permute-start(bf16[128,768]{1,0:T(8,128)(2,1)S(1)} %bitcast.27), channel_id=1, source_target_pairs={{0,384},{128,256},{256,128},{384,0},{1,385},{129,257},{257,129},{3... | collective-permute-start | bytes 589832 | tf_op jit(solution)/shard_map/ppermute | solution.py:27

commit v3 on v2

--- a/solution.py
+++ b/solution.py
@@ -59,12 +59,15 @@
     return jnp.where(lane_index(latent.shape[0]) < LANES - 2, latent, 1.0).astype(BF16)
 
 
-def late_kernel(video_hbm, conv_hbm, latent_hbm, out_ref, video_ref, conv_ref, latent_ref, sems):
+def late_kernel(
+    video_hbm, conv_hbm, latent_hbm, out_ref, first_ref, conv_ref, latent_ref, video_ref, sems,
+):
     copies = [
         pltpu.make_async_copy(src, dst, sems.at[i])
-        for i, (src, dst) in enumerate(
-            [(video_hbm, video_ref), (conv_hbm, conv_ref), (latent_hbm, latent_ref)]
-        )
+        for i, (src, dst) in enumerate([
+            (video_hbm, video_ref), (conv_hbm, conv_ref), (latent_hbm, latent_ref),
+            (video_hbm.at[: first_ref.shape[0]], first_ref),
+        ])
     ]
     for copy in copies:
         copy.start()
@@ -89,7 +92,7 @@
     windows = []
     for start in range(0, width, channels):
         cols = slice(start, start + channels)
-        padded = jnp.concatenate([earlier_ref[:, :, cols], video_ref[:2, :, cols]], axis=0)
+        padded = jnp.concatenate([earlier_ref[:, :, cols], video_ref[:, :, cols]], axis=0)
         windows.append([padded[2 - k : 4 - k].reshape(-1, channels) for k in range(3)])
     first = latent_rows(windows, conv_ref, latent_ref)
     rows = jnp.concatenate([first, late_ref[...]], axis=0)
@@ -155,9 +158,8 @@
     ).astype(BF16)
 
 
-def project_kernel(place_ref, heads_ref, weight_ref, out_ref):
-    member = place_ref[1] & 3
-    heads = jnp.concatenate([heads_ref[member ^ k] for k in range(4)], axis=1)
+def project_kernel(near_ref, far_ref, weight_ref, out_ref):
+    heads = jnp.concatenate([near_ref[0], near_ref[1], far_ref[0], far_ref[1]], axis=1)
     out_ref[...] = jnp.dot(heads, weight_ref[...], preferred_element_type=F32).astype(BF16)
 
 
@@ -235,13 +237,11 @@
     grp = place_ref[0]
     for i in range(total // (block * grp_size)):
         start = pl.multiple_of((i * grp_size + grp) * block, block)
-        mine = out_ref[pl.ds(start, block), :]
-        for j in range(own_ref.shape[0]):
-            own_ref[j, i * block : (i + 1) * block, :] = mine
+        own_ref[i * block : (i + 1) * block, :] = out_ref[pl.ds(start, block), :]
 
 
 def call(body, shapes, *args, name, scratch=(), places=(), flops=10**8, moved=10**6):
-    spaces = {"smem": pltpu.SMEM, "any": pl.ANY}
+    spaces = {"smem": pltpu.SMEM, "hbm": pltpu.HBM}
     outs = tuple(jax.ShapeDtypeStruct(shape, BF16) for shape in shapes)
     whole = pl.BlockSpec(memory_space=pltpu.VMEM)
     in_specs = [whole] * len(args)
@@ -281,21 +281,22 @@
     earlier = shifted_frames(frames[frame_count - 2 :], "seq", 1)
     latent_t = latent_weight.T
     labels = assign[0].reshape(1, -1)
-    late = call(
-        late_kernel, [((frame_count - 2) * tokens, LANES)], frames, conv_weight, latent_t,
-        name="late_frames", flops=10**9, places=["any"] * 3,
-        scratch=[
-            pltpu.VMEM(x.shape, BF16) for x in (frames, conv_weight, latent_t)
-        ] + [pltpu.SemaphoreType.DMA((3,))],
+    late, first, taps, latent_rhs = call(
+        late_kernel,
+        [((frame_count - 2) * tokens, LANES), (2,) + frames.shape[1:], conv_weight.shape,
+         latent_t.shape],
+        frames, conv_weight, latent_t, name="late_frames", flops=10**9, places=["hbm"] * 3,
+        scratch=[pltpu.VMEM(frames.shape, BF16), pltpu.SemaphoreType.DMA((4,))],
     )
     sums = call(
         functools.partial(sums_kernel, grp=grp_size, seq=seq_size), [(groups, LANES)],
-        frames, earlier, conv_weight, latent_t, late, labels, name="group_sums", flops=10**9,
+        first, earlier, taps, latent_rhs, late, labels, name="group_sums", flops=10**9,
     )
 
     by_column = jnp.concatenate(
         [cotangent[0, :, g * columns : (g + 1) * columns] for g in range(grp_size)], axis=0
     ).reshape(grp_size, block, columns)
+    by_column, _ = lax.optimization_barrier((by_column, earlier))
     near = lax.all_to_all(by_column, "grp", 0, 0, tiled=True).reshape(shared, columns)
 
     parts = lax.all_to_all(sums.reshape(seq_size, shared, LANES), "seq", 0, 0, tiled=True)
@@ -319,22 +320,26 @@
         return jnp.concatenate([kept, xor_swap(given, "seq", mask)], axis=0)
 
     weight, _ = lax.optimization_barrier((out_weight, slab_sums))
-    weight_quad = halved(halved(weight, side, 1), depth, 2)
+    weight_pair = halved(weight, side, 1)
 
     head_out, own_rows = call(
         functools.partial(attend_kernel, grp_size=grp_size, block=block),
-        [(groups, head), (4, rows, head)], place, merged, embed_weight, norm_gain[None],
+        [(groups, head), (rows, head)], place, merged, embed_weight, norm_gain[None],
         qkv_weight, q_gain[None], k_gain[None], name="attend", flops=8 * 10**9, places=["smem"],
         scratch=[pltpu.VMEM((width, 2 * head), BF16)] + [pltpu.VMEM((groups, head), BF16)] * 3,
     )
 
-    quads = [list(range(k, k + 4)) for k in range(0, seq_size, 4)]
-    quad_heads = lax.all_to_all(own_rows, "seq", 0, 0, axis_index_groups=quads, tiled=True)
+    other_rows = xor_swap(own_rows, "seq", 1)
     local_grad = call(
         functools.partial(grad_kernel, masks=masks), [(head, columns)], place, head_out, near, far,
         name="local_grad", places=["smem"], scratch=[pltpu.VMEM((groups, head), BF16)],
         flops=10**9,
     )
+    pair_heads, weight_pair, _ = lax.optimization_barrier(
+        (jnp.stack([own_rows, other_rows]), weight_pair, local_grad)
+    )
+    quad_heads = (pair_heads, xor_swap(pair_heads, "seq", 2))
+    weight_quad = halved(weight_pair, depth, 2)
     grad_parts = lax.all_to_all(
         local_grad.reshape(dp_size, head // dp_size, columns), "dp", 0, 0, tiled=True
     )
@@ -344,8 +349,7 @@
     grad_cols = lax.all_to_all(grad_block, "dp", 0, 0, tiled=True).reshape(head, columns)
 
     partial = call(
-        project_kernel, [(rows, columns)], place, quad_heads, weight_quad, name="project",
-        places=["smem"], flops=10**9,
+        project_kernel, [(rows, columns)], *quad_heads, weight_quad, name="project", flops=10**9,
     )
     partial, _ = lax.optimization_barrier((partial, grad_cols))
     out_parts = lax.all_to_all(

time: 160 us -> 155 us (0.969)
  blocking collectives: 9.29 us -> 0 us
  starting transfers between devices: 77.8 us -> 83.5 us
  waiting for transfers between devices: 38.3 us -> 35.2 us
    all_to_all x1 -> x0, blocking collectives: 9.29 us -> none  [shards(): lax.all_to_all(by_column, 'grp', 0, 0, tiled=True).reshape(shared, columns)]
    ppermute x9 -> x11, waiting for transfers between devices: 17 us -> 25 us  [xor_swap(): return lax.ppermute(block, axis, route)]
    all_to_all x1, starting transfers between devices: 3.53 us -> 10.9 us  [shards(): lax.all_to_all(sums.reshape(seq_size, shared, LANES), 'seq', 0, 0, tiled=...]
    all_to_all x1, waiting for transfers between devices: 4.43 us -> 0.01 us  [shards(): slab_parts = lax.all_to_all(slab_sums, 'grp', 0, 0, tiled=True)]
    all_to_all x1, waiting for transfers between devices: 4.65 us -> 0.72 us  [shards(): lax.all_to_all(grad_block, 'dp', 0, 0, tiled=True).reshape(head, columns)]
    all_to_all x1, waiting for transfers between devices: 3.28 us -> 0.01 us  [shards(): lax.all_to_all(sums.reshape(seq_size, shared, LANES), 'seq', 0, 0, tiled=...]
    all_to_all x1, waiting for transfers between devices: 0.01 us -> 3.07 us  [shards(): lax.all_to_all(by_column, 'grp', 0, 0, tiled=True).reshape(shared, columns)]
    ppermute x9 -> x11, starting transfers between devices: 37.1 us -> 34.4 us  [xor_swap(): return lax.ppermute(block, axis, route)]
  transfers between devices with their start and end apart: 17 -> 19, of which waited for: 9 -> 8; matrix products, arithmetic and copies ran while one was open for 4% -> 5% of each run, Pallas kernels for 13% -> 12%
where the time goes in v3:
time: 155 us; the launch traced here: 152 us
  starting transfers between devices  83.5 us (54%)
  waiting for transfers between devices  35.2 us (23%)
  Pallas kernels  20.8 us (13%)
  local copies, waits for them, and re-layouts  7.84 us (5%)
  other arithmetic  3.86 us (2%)
    ppermute x11, starting transfers between devices, xor_swap(): return lax.ppermute(block, axis, route)  34.4 us
    ppermute x11, waiting for transfers between devices, xor_swap(): return lax.ppermute(block, axis, route)  25 us
    pallas_call x10, Pallas kernels, call(): pl.pallas_call(body, out_shape=outs, in_specs=in_specs, out_specs=(whole,...  20.8 us
    all_to_all x1, starting transfers between devices, shards(): lax.all_to_all(local_grad.reshape(dp_size, head // dp_size, columns), 'dp...  11 us
    all_to_all x1, starting transfers between devices, shards(): lax.all_to_all(sums.reshape(seq_size, shared, LANES), 'seq', 0, 0, tiled=...  10.9 us
    all_to_all x1, starting transfers between devices, shards(): lax.all_to_all(partial.reshape(seq_size, block, columns), 'seq', 0, 0, ti...  6.64 us
    all_to_all x1, waiting for transfers between devices, shards(): lax.all_to_all(local_grad.reshape(dp_size, head // dp_size, columns), 'dp...  6.41 us
    all_to_all x1, starting transfers between devices, shards(): lax.all_to_all(grad_block, 'dp', 0, 0, tiled=True).reshape(head, columns)  5.69 us
  transfers between devices with their start and end apart: 19, of which 8 were waited for; matrix products, arithmetic and copies ran while one was open for 5% of the time, Pallas kernels for 12%

profile of v3, /device:TPU:1, one launch (start us, length us, event | category | flops | bytes accessed | tf_op | source)
XLA Modules:
  0.0 152.1 jit_solution(16208587503458307939)
XLA Ops:
  0.6 0.9 slice_bitcast_fusion
  1.5 4.0 %collective-permute-start = (bf16[2,64,512]{2,1,0:T(8,128)(2,1)S(1)}, bf16[2,64,512]{2,1,0:T(8,128)(2,1)S(1)}, u32[]{:S(2)}, u32[]{:S(2)}) collective-permute-start(bf16[2,64,512]{2,1,0:T(8,128)(2,1)S(1)} %slice_bitcast_fusion), channel_id=1, source_target_pairs={{0,8},{8,16},{16,24},{24,32},{32,40},{40,48},{48,56},{56,64},{64,7... | collective-permute-start | bytes 393224 | tf_op jit(solution)/shard_map/ppermute | solution.py:22
  5.6 0.8 slice_bitcast_fusion.4
  6.4 1.0 copy-done
  7.4 0.9 copy-done.3
  8.3 0.8 copy-done.4
  9.2 1.4 late_frames.1
  10.7 0.6 pad_maximum_fusion.6
  11.3 4.0 %all-to-all-start.3 = ((bf16[4,16,768]{2,1,0:T(8,128)(2,1)}), bf16[4,16,768]{2,1,0:T(8,128)(2,1)S(1)}, u32[]{:S(2)}, u32[]{:S(2)}) async-start(bf16[4,16,768]{2,1,0:T(8,128)(2,1)} %bitcast.16), calls=%async_computation.3 | async-start | bytes 196608 | tf_op jit(solution)/shard_map/all_to_all | solution.py:300
  15.3 1.6 %group_sums.1 = bf16[1024,128]{1,0:T(8,128)(2,1)} custom-call(bf16[2,64,512]{2,1,0:T(8,128)(2,1)S(1)} %get-tuple-element.13.video_ref, bf16[2,64,512]{2,1,0:T(8,128)(2,1)S(1)} %collective-permute-done.earlier_ref, bf16[3,128,128]{2,1,0:T(8,128)(2,1)S(1)} %get-tuple-element.14.conv_ref, bf16[64,512]{1,0:T(8,128)(2,1)S(1)} %get-tuple-element.15.latent_ref, ...), custom_call_target="tpu_custom_call" | custom-call | flops 1000000000 | bytes 1000000 | tf_op jit(solution)/shard_map/group_sums/pallas_call | solution.py:250
  16.9 3.1 %all-to-all-done.3 = bf16[4,16,768]{2,1,0:T(8,128)(2,1)S(1)} async-done(((bf16[4,16,768]{2,1,0:T(8,128)(2,1)}), bf16[4,16,768]{2,1,0:T(8,128)(2,1)S(1)}, u32[]{:S(2)}, u32[]{:S(2)}) %all-to-all-start.3) | async-done | bytes 98336 | tf_op jit(solution)/shard_map/all_to_all | solution.py:300
  20.0 10.9 %all-to-all-start = ((bf16[16,64,128]{2,1,0:T(8,128)(2,1)}), bf16[16,64,128]{2,1,0:T(8,128)(2,1)S(1)}, u32[]{:S(2)}, u32[]{:S(2)}) async-start(bf16[16,64,128]{2,1,0:T(8,128)(2,1)} %bitcast.5), calls=%async_computation | async-start | bytes 524288 | tf_op jit(solution)/shard_map/all_to_all | solution.py:302
  30.9 7.2 %collective-permute-start.3 = (bf16[64,768]{1,0:T(8,128)(2,1)S(1)}, bf16[64,768]{1,0:T(8,128)(2,1)S(1)}, u32[]{:S(2)}, u32[]{:S(2)}) collective-permute-start(bf16[64,768]{1,0:T(8,128)(2,1)S(1)} %bitcast.38), channel_id=1, source_target_pairs={{0,64},{8,72},{16,80},{24,88},{32,96},{40,104},{48,112},{56,120},{... | collective-permute-start | bytes 294920 | tf_op jit(solution)/shard_map/ppermute | solution.py:27
  38.1 6.9 %collective-permute-done.3 = bf16[64,768]{1,0:T(8,128)(2,1)S(1)} collective-permute-done((bf16[64,768]{1,0:T(8,128)(2,1)S(1)}, bf16[64,768]{1,0:T(8,128)(2,1)S(1)}, u32[]{:S(2)}, u32[]{:S(2)}) %collective-permute-start.3) | collective-permute-done | bytes 98336 | tf_op jit(solution)/shard_map/ppermute | solution.py:27
  45.1 2.6 %collective-permute-start.4 = (bf16[128,768]{1,0:T(8,128)(2,1)S(1)}, bf16[128,768]{1,0:T(8,128)(2,1)S(1)}, u32[]{:S(2)}, u32[]{:S(2)}) collective-permute-start(bf16[128,768]{1,0:T(8,128)(2,1)S(1)} %pad_maximum_fusion.4), channel_id=1, source_target_pairs={{0,32},{8,40},{16,48},{24,56},{32,0},{40,8},{48,16},{56,24},{64,96... | collective-permute-start | bytes 589832 | tf_op jit(solution)/shard_map/ppermute | solution.py:27
  47.7 0.8 slab_sums.1
  48.5 3.3 %all-to-all-start.1 = ((bf16[4,64,128]{2,1,0:T(8,128)(2,1)}), bf16[4,64,128]{2,1,0:T(8,128)(2,1)S(1)}, u32[]{:S(2)}, u32[]{:S(2)}) async-start(bf16[4,64,128]{2,1,0:T(8,128)(2,1)} %slab_sums.1), calls=%async_computation.1 | async-start | bytes 131072 | tf_op jit(solution)/shard_map/all_to_all | solution.py:304
  51.8 5.9 %collective-permute-done.4 = bf16[128,768]{1,0:T(8,128)(2,1)S(1)} collective-permute-done((bf16[128,768]{1,0:T(8,128)(2,1)S(1)}, bf16[128,768]{1,0:T(8,128)(2,1)S(1)}, u32[]{:S(2)}, u32[]{:S(2)}) %collective-permute-start.4) | collective-permute-done | bytes 196640 | tf_op jit(solution)/shard_map/ppermute | solution.py:27
  57.7 0.8 pad_maximum_fusion.3
  58.6 3.1 %collective-permute-start.5 = (bf16[256,768]{1,0:T(8,128)(2,1)}, bf16[256,768]{1,0:T(8,128)(2,1)}, u32[]{:S(2)}, u32[]{:S(2)}) collective-permute-start(bf16[256,768]{1,0:T(8,128)(2,1)} %pad_maximum_fusion.3), channel_id=1, source_target_pairs={{0,8},{8,0},{16,24},{24,16},{32,40},{40,32},{48,56},{56,48},{64,72... | collective-permute-start | bytes 1179656 | tf_op jit(solution)/shard_map/ppermute | solution.py:27
  61.7 0.9 merged.1
  62.6 3.5 %all-to-all-start.2 = ((bf16[16,64,128]{2,1,0:T(8,128)(2,1)}), bf16[16,64,128]{2,1,0:T(8,128)(2,1)S(1)}, u32[]{:S(2)}, u32[]{:S(2)}) async-start(bf16[16,64,128]{2,1,0:T(8,128)(2,1)} %merged.1), calls=%async_computation.2 | async-start | bytes 524288 | tf_op jit(solution)/shard_map/all_to_all | solution.py:306
  66.2 2.2 %constant_dynamic-slice_fusion.3 = (bf16[128,1536]{1,0:T(8,128)(2,1)}, bf16[128,1536]{1,0:T(8,128)(2,1)}) fusion(bf16[128,3072]{1,0:T(8,128)(2,1)} %param.20, s32[]{:T(128)S(6)} %select_n.12, s32[]{:T(128)S(6)} %select_n.13), kind=kLoop, calls=%fused_computation.15 | loop fusion | bytes 1572872 | tf_op jit(solution)/shard_map/dynamic_slice | solution.py:318
  68.4 3.1 %collective-permute-start.2 = (bf16[128,1536]{1,0:T(8,128)(2,1)}, bf16[128,1536]{1,0:T(8,128)(2,1)}, u32[]{:S(2)}, u32[]{:S(2)}) collective-permute-start(bf16[128,1536]{1,0:T(8,128)(2,1)} %get-tuple-element.27), channel_id=1, source_target_pairs={{0,8},{8,0},{16,24},{24,16},{32,40},{40,32},{48,56},{56,48},{64,72... | collective-permute-start | bytes 1179656 | tf_op jit(solution)/shard_map/ppermute | solution.py:27
  71.6 1.2 pad_maximum_fusion.1.first_ref
  72.8 3.1 %collective-permute-start.6 = (bf16[512,768]{1,0:T(8,128)(2,1)S(1)}, bf16[512,768]{1,0:T(8,128)(2,1)}, u32[]{:S(2)}, u32[]{:S(2)}) collective-permute-start(bf16[512,768]{1,0:T(8,128)(2,1)S(1)} %pad_maximum_fusion.1.first_ref), channel_id=1, source_target_pairs={{0,16},{8,24},{16,0},{24,8},{32,48},{40,56},{48,32},{56,40},{64,80... | collective-permute-start | bytes 2359304 | tf_op jit(solution)/shard_map/ppermute | solution.py:27
  75.9 1.0 copy-done.2
  76.9 9.9 %attend.1 = (bf16[1024,128]{1,0:T(8,128)(2,1)S(1)}, bf16[256,128]{1,0:T(8,128)(2,1)S(1)}) custom-call(s32[2]{0:T(128)S(1)} %pad_add_fusion.place_ref, bf16[1024,128]{1,0:T(8,128)(2,1)S(1)} %bitcast.31, bf16[64,3072]{1,0:T(8,128)(2,1)S(1)} %copy-done.2, f32[1,3072]{1,0:T(1,128)S(1)} %bitcast.35, bf16[3,3072,128]{2,1,0:T(8,128)(2,1)S(1)} %copy-done.1, ...), custom_call_target="tpu_custom_call" | custom-call | flops 8000000000 | bytes 1000000 | tf_op jit(solution)/shard_map/attend/pallas_call | solution.py:250
  86.8 2.7 %collective-permute-start.1 = (bf16[256,128]{1,0:T(8,128)(2,1)S(1)}, bf16[256,128]{1,0:T(8,128)(2,1)S(1)}, u32[]{:S(2)}, u32[]{:S(2)}) collective-permute-start(bf16[256,128]{1,0:T(8,128)(2,1)S(1)} %get-tuple-element.17), channel_id=1, source_target_pairs={{0,8},{8,0},{16,24},{24,16},{32,40},{40,32},{48,56},{56,48},{64,72... | collective-permute-start | bytes 196616 | tf_op jit(solution)/shard_map/ppermute | solution.py:27
  89.6 1.0 pad_maximum_fusion
  90.6 1.6 %collective-permute-done.1 = bf16[256,128]{1,0:T(8,128)(2,1)S(1)} collective-permute-done((bf16[256,128]{1,0:T(8,128)(2,1)S(1)}, bf16[256,128]{1,0:T(8,128)(2,1)S(1)}, u32[]{:S(2)}, u32[]{:S(2)}) %collective-permute-start.1) | collective-permute-done | bytes 65568 | tf_op jit(solution)/shard_map/ppermute | solution.py:27
  92.3 2.3 %local_grad.1 = bf16[128,768]{1,0:T(8,128)(2,1)} custom-call(s32[2]{0:T(128)S(1)} %pad_add_fusion.place_ref, bf16[1024,128]{1,0:T(8,128)(2,1)S(1)} %get-tuple-element.19.head_ref, bf16[512,768]{1,0:T(8,128)(2,1)S(1)} %pad_maximum_fusion.1.first_ref, bf16[512,768]{1,0:T(8,128)(2,1)} %collective-permute-done.6.second_ref), custom_call_target="tpu_custom_call" | custom-call | flops 1000000000 | bytes 1000000 | tf_op jit(solution)/shard_map/local_grad/pallas_call | solution.py:250
  94.5 11.0 %all-to-all-start.4 = ((bf16[8,16,768]{2,1,0:T(8,128)(2,1)}), bf16[8,16,768]{2,1,0:T(8,128)(2,1)S(1)}, u32[]{:S(2)}, u32[]{:S(2)}) async-start(bf16[8,16,768]{2,1,0:T(8,128)(2,1)} %bitcast.18), calls=%async_computation.4 | async-start | bytes 393216 | tf_op jit(solution)/shard_map/all_to_all | solution.py:343
  105.6 2.2 %collective-permute-start.8 = (bf16[256,768]{1,0:T(8,128)(2,1)S(1)}, bf16[256,768]{1,0:T(8,128)(2,1)S(1)}, u32[]{:S(2)}, u32[]{:S(2)}) collective-permute-start(bf16[256,768]{1,0:T(8,128)(2,1)S(1)} %get-tuple-element.25), channel_id=1, source_target_pairs={{0,16},{8,24},{16,0},{24,8},{32,48},{40,56},{48,32},{56,40},{64,80... | collective-permute-start | bytes 1179656 | tf_op jit(solution)/shard_map/ppermute | solution.py:27
  107.8 6.4 %all-to-all-done.4.parts_ref = bf16[8,16,768]{2,1,0:T(8,128)(2,1)S(1)} async-done(((bf16[8,16,768]{2,1,0:T(8,128)(2,1)}), bf16[8,16,768]{2,1,0:T(8,128)(2,1)S(1)}, u32[]{:S(2)}, u32[]{:S(2)}) %all-to-all-start.4) | async-done | bytes 196640 | tf_op jit(solution)/shard_map/all_to_all | solution.py:343
  114.2 0.7 grad_block.1
  114.9 5.7 %all-to-all-start.5 = ((bf16[8,16,768]{2,1,0:T(8,128)(2,1)}), bf16[8,16,768]{2,1,0:T(8,128)(2,1)S(1)}, u32[]{:S(2)}, u32[]{:S(2)}) async-start(bf16[8,16,768]{2,1,0:T(8,128)(2,1)} %grad_block.1), calls=%async_computation.5 | async-start | bytes 393216 | tf_op jit(solution)/shard_map/all_to_all | solution.py:349
  120.6 1.9 %collective-permute-start.7 = (bf16[2,256,128]{2,1,0:T(8,128)(2,1)S(1)}, bf16[2,256,128]{2,1,0:T(8,128)(2,1)S(1)}, u32[]{:S(2)}, u32[]{:S(2)}) collective-permute-start(bf16[2,256,128]{2,1,0:T(8,128)(2,1)S(1)} %pad_maximum_fusion.5.near_ref), channel_id=1, source_target_pairs={{0,16},{8,24},{16,0},{24,8},{32,48},{40,56},{48,32},{56,40},{64,80... | collective-permute-start | bytes 393224 | tf_op jit(solution)/shard_map/ppermute | solution.py:27
  122.5 4.9 %collective-permute-done.7.far_ref = bf16[2,256,128]{2,1,0:T(8,128)(2,1)S(1)} collective-permute-done((bf16[2,256,128]{2,1,0:T(8,128)(2,1)S(1)}, bf16[2,256,128]{2,1,0:T(8,128)(2,1)S(1)}, u32[]{:S(2)}, u32[]{:S(2)}) %collective-permute-start.7) | collective-permute-done | bytes 131104 | tf_op jit(solution)/shard_map/ppermute | solution.py:27
  127.4 1.1 project.1
  128.5 0.7 all-to-all-done.5
  129.2 6.6 %all-to-all-start.6 = ((bf16[16,16,768]{2,1,0:T(8,128)(2,1)}), bf16[16,16,768]{2,1,0:T(8,128)(2,1)S(1)}, u32[]{:S(2)}, u32[]{:S(2)}) async-start(bf16[16,16,768]{2,1,0:T(8,128)(2,1)} %bitcast.20), calls=%async_computation.6 | async-start | bytes 786432 | tf_op jit(solution)/shard_map/all_to_all | solution.py:355
  135.9 2.5 %collective-permute-start.10 = (bf16[128,768]{1,0:T(8,128)(2,1)S(1)}, bf16[128,768]{1,0:T(8,128)(2,1)S(1)}, u32[]{:S(2)}, u32[]{:S(2)}) collective-permute-start(bf16[128,768]{1,0:T(8,128)(2,1)S(1)} %bitcast.27), channel_id=1, source_target_pairs={{0,256},{128,384},{256,0},{384,128},{1,257},{129,385},{257,1},{385... | collective-permute-start | bytes 589832 | tf_op jit(solution)/shard_map/ppermute | solution.py:27
  138.4 4.0 %collective-permute-start.11 = (bf16[128,768]{1,0:T(8,128)(2,1)S(1)}, bf16[128,768]{1,0:T(8,128)(2,1)S(1)}, u32[]{:S(2)}, u32[]{:S(2)}) collective-permute-start(bf16[128,768]{1,0:T(8,128)(2,1)S(1)} %bitcast.28), channel_id=1, source_target_pairs={{0,384},{128,256},{256,128},{384,0},{1,385},{129,257},{257,129},{3... | collective-permute-start | bytes 589832 | tf_op jit(solution)/shard_map/ppermute | solution.py:27
  142.4 1.9 %collective-permute-start.9 = (bf16[128,768]{1,0:T(8,128)(2,1)S(1)}, bf16[128,768]{1,0:T(8,128)(2,1)S(1)}, u32[]{:S(2)}, u32[]{:S(2)}) collective-permute-start(bf16[128,768]{1,0:T(8,128)(2,1)S(1)} %bitcast.29), channel_id=1, source_target_pairs={{0,128},{128,0},{256,384},{384,256},{1,129},{129,1},{257,385},{385... | collective-permute-start | bytes 589832 | tf_op jit(solution)/shard_map/ppermute | solution.py:27
  144.3 5.6 %collective-permute-done.11.refs_3_ = bf16[128,768]{1,0:T(8,128)(2,1)S(1)} collective-permute-done((bf16[128,768]{1,0:T(8,128)(2,1)S(1)}, bf16[128,768]{1,0:T(8,128)(2,1)S(1)}, u32[]{:S(2)}, u32[]{:S(2)}) %collective-permute-start.11) | collective-permute-done | bytes 196640 | tf_op jit(solution)/shard_map/ppermute | solution.py:27
  150.0 1.5 grad_columns.1
  151.5 0.7 attended.1
  (37 shorter events, 0.4 us)
Async XLA Ops:
  1.5 9.8 %collective-permute-start = (bf16[2,64,512]{2,1,0:T(8,128)(2,1)S(1)}, bf16[2,64,512]{2,1,0:T(8,128)(2,1)S(1)}, u32[]{:S(2)}, u32[]{:S(2)}) collective-permute-start(bf16[2,64,512]{2,1,0:T(8,128)(2,1)S(1)} %slice_bitcast_fusion), channel_id=1, source_target_pairs={{0,8},{8,16},{16,24},{24,32},{32,40},{40,48},{48,56},{56,64},{64,7... | collective-permute-start | bytes 393224 | tf_op jit(solution)/shard_map/ppermute | solution.py:22
  6.4 1.0 copy-start
  7.4 0.9 copy-start.3
  8.3 0.8 copy-start.4
  9.2 1.4 copy-start.11
  11.3 8.7 %all-to-all-start.3 = ((bf16[4,16,768]{2,1,0:T(8,128)(2,1)}), bf16[4,16,768]{2,1,0:T(8,128)(2,1)S(1)}, u32[]{:S(2)}, u32[]{:S(2)}) async-start(bf16[4,16,768]{2,1,0:T(8,128)(2,1)} %bitcast.16), calls=%async_computation.3 | async-start | bytes 196608 | tf_op jit(solution)/shard_map/all_to_all | solution.py:300
  20.0 27.7 %all-to-all-start = ((bf16[16,64,128]{2,1,0:T(8,128)(2,1)}), bf16[16,64,128]{2,1,0:T(8,128)(2,1)S(1)}, u32[]{:S(2)}, u32[]{:S(2)}) async-start(bf16[16,64,128]{2,1,0:T(8,128)(2,1)} %bitcast.5), calls=%async_computation | async-start | bytes 524288 | tf_op jit(solution)/shard_map/all_to_all | solution.py:302
  30.9 14.1 %collective-permute-start.3 = (bf16[64,768]{1,0:T(8,128)(2,1)S(1)}, bf16[64,768]{1,0:T(8,128)(2,1)S(1)}, u32[]{:S(2)}, u32[]{:S(2)}) collective-permute-start(bf16[64,768]{1,0:T(8,128)(2,1)S(1)} %bitcast.38), channel_id=1, source_target_pairs={{0,64},{8,72},{16,80},{24,88},{32,96},{40,104},{48,112},{56,120},{... | collective-permute-start | bytes 294920 | tf_op jit(solution)/shard_map/ppermute | solution.py:27
  45.0 26.5 %copy-start.9 = (bf16[64,768]{1,0:T(8,128)(2,1)}, bf16[64,768]{1,0:T(8,128)(2,1)S(1)}, u32[]{:S(2)}) copy-start(bf16[64,768]{1,0:T(8,128)(2,1)S(1)} %collective-permute-done.3) | copy-start | bytes 294916
  45.1 12.7 %collective-permute-start.4 = (bf16[128,768]{1,0:T(8,128)(2,1)S(1)}, bf16[128,768]{1,0:T(8,128)(2,1)S(1)}, u32[]{:S(2)}, u32[]{:S(2)}) collective-permute-start(bf16[128,768]{1,0:T(8,128)(2,1)S(1)} %pad_maximum_fusion.4), channel_id=1, source_target_pairs={{0,32},{8,40},{16,48},{24,56},{32,0},{40,8},{48,16},{56,24},{64,96... | collective-permute-start | bytes 589832 | tf_op jit(solution)/shard_map/ppermute | solution.py:27
  48.5 13.2 %all-to-all-start.1 = ((bf16[4,64,128]{2,1,0:T(8,128)(2,1)}), bf16[4,64,128]{2,1,0:T(8,128)(2,1)S(1)}, u32[]{:S(2)}, u32[]{:S(2)}) async-start(bf16[4,64,128]{2,1,0:T(8,128)(2,1)} %slab_sums.1), calls=%async_computation.1 | async-start | bytes 131072 | tf_op jit(solution)/shard_map/all_to_all | solution.py:304
  57.7 13.8 %copy-start.10 = (bf16[128,768]{1,0:T(8,128)(2,1)}, bf16[128,768]{1,0:T(8,128)(2,1)S(1)}, u32[]{:S(2)}) copy-start(bf16[128,768]{1,0:T(8,128)(2,1)S(1)} %collective-permute-done.4) | copy-start | bytes 589828
  58.6 13.0 %collective-permute-start.5 = (bf16[256,768]{1,0:T(8,128)(2,1)}, bf16[256,768]{1,0:T(8,128)(2,1)}, u32[]{:S(2)}, u32[]{:S(2)}) collective-permute-start(bf16[256,768]{1,0:T(8,128)(2,1)} %pad_maximum_fusion.3), channel_id=1, source_target_pairs={{0,8},{8,0},{16,24},{24,16},{32,40},{40,32},{48,56},{56,48},{64,72... | collective-permute-start | bytes 1179656 | tf_op jit(solution)/shard_map/ppermute | solution.py:27
  62.6 13.3 %all-to-all-start.2 = ((bf16[16,64,128]{2,1,0:T(8,128)(2,1)}), bf16[16,64,128]{2,1,0:T(8,128)(2,1)S(1)}, u32[]{:S(2)}, u32[]{:S(2)}) async-start(bf16[16,64,128]{2,1,0:T(8,128)(2,1)} %merged.1), calls=%async_computation.2 | async-start | bytes 524288 | tf_op jit(solution)/shard_map/all_to_all | solution.py:306
  66.2 9.7 %copy-start.1 = (bf16[3,3072,128]{2,1,0:T(8,128)(2,1)S(1)}, bf16[3,3072,128]{2,1,0:T(8,128)(2,1)}, u32[]{:S(2)}) copy-start(bf16[3,3072,128]{2,1,0:T(8,128)(2,1)} %qkv_ref.1) | copy-start | bytes 7077892
  66.2 9.7 %copy-start.5 = (f32[3072]{0:T(1024)S(1)}, f32[3072]{0:T(1024)}, u32[]{:S(2)}) copy-start(f32[3072]{0:T(1024)} %param.16) | copy-start | bytes 36868
  66.2 9.7 %copy-start.6 = (f32[128]{0:T(128)S(1)}, f32[128]{0:T(128)}, u32[]{:S(2)}) copy-start(f32[128]{0:T(128)} %param.18) | copy-start | bytes 1540
  66.2 9.7 %copy-start.7 = (f32[128]{0:T(128)S(1)}, f32[128]{0:T(128)}, u32[]{:S(2)}) copy-start(f32[128]{0:T(128)} %param.19) | copy-start | bytes 1540
  68.4 21.1 %collective-permute-start.2 = (bf16[128,1536]{1,0:T(8,128)(2,1)}, bf16[128,1536]{1,0:T(8,128)(2,1)}, u32[]{:S(2)}, u32[]{:S(2)}) collective-permute-start(bf16[128,1536]{1,0:T(8,128)(2,1)} %get-tuple-element.27), channel_id=1, source_target_pairs={{0,8},{8,0},{16,24},{24,16},{32,40},{40,32},{48,56},{56,48},{64,72... | collective-permute-start | bytes 1179656 | tf_op jit(solution)/shard_map/ppermute | solution.py:27
  72.8 19.5 %collective-permute-start.6 = (bf16[512,768]{1,0:T(8,128)(2,1)S(1)}, bf16[512,768]{1,0:T(8,128)(2,1)}, u32[]{:S(2)}, u32[]{:S(2)}) collective-permute-start(bf16[512,768]{1,0:T(8,128)(2,1)S(1)} %pad_maximum_fusion.1.first_ref), channel_id=1, source_target_pairs={{0,16},{8,24},{16,0},{24,8},{32,48},{40,56},{48,32},{56,40},{64,80... | collective-permute-start | bytes 2359304 | tf_op jit(solution)/shard_map/ppermute | solution.py:27
  75.9 1.0 copy-start.2
  76.9 12.7 %copy-start.8 = (bf16[128,1536]{1,0:T(8,128)(2,1)S(1)}, bf16[128,1536]{1,0:T(8,128)(2,1)}, u32[]{:S(2)}) copy-start(bf16[128,1536]{1,0:T(8,128)(2,1)} %get-tuple-element.26) | copy-start | bytes 1179652
  86.8 5.4 %collective-permute-start.1 = (bf16[256,128]{1,0:T(8,128)(2,1)S(1)}, bf16[256,128]{1,0:T(8,128)(2,1)S(1)}, u32[]{:S(2)}, u32[]{:S(2)}) collective-permute-start(bf16[256,128]{1,0:T(8,128)(2,1)S(1)} %get-tuple-element.17), channel_id=1, source_target_pairs={{0,8},{8,0},{16,24},{24,16},{32,40},{40,32},{48,56},{56,48},{64,72... | collective-permute-start | bytes 196616 | tf_op jit(solution)/shard_map/ppermute | solution.py:27
  94.5 19.7 %all-to-all-start.4 = ((bf16[8,16,768]{2,1,0:T(8,128)(2,1)}), bf16[8,16,768]{2,1,0:T(8,128)(2,1)S(1)}, u32[]{:S(2)}, u32[]{:S(2)}) async-start(bf16[8,16,768]{2,1,0:T(8,128)(2,1)} %bitcast.18), calls=%async_computation.4 | async-start | bytes 393216 | tf_op jit(solution)/shard_map/all_to_all | solution.py:343
  105.6 16.9 %collective-permute-start.8 = (bf16[256,768]{1,0:T(8,128)(2,1)S(1)}, bf16[256,768]{1,0:T(8,128)(2,1)S(1)}, u32[]{:S(2)}, u32[]{:S(2)}) collective-permute-start(bf16[256,768]{1,0:T(8,128)(2,1)S(1)} %get-tuple-element.25), channel_id=1, source_target_pairs={{0,16},{8,24},{16,0},{24,8},{32,48},{40,56},{48,32},{56,40},{64,80... | collective-permute-start | bytes 1179656 | tf_op jit(solution)/shard_map/ppermute | solution.py:27
  114.9 14.4 %all-to-all-start.5 = ((bf16[8,16,768]{2,1,0:T(8,128)(2,1)}), bf16[8,16,768]{2,1,0:T(8,128)(2,1)S(1)}, u32[]{:S(2)}, u32[]{:S(2)}) async-start(bf16[8,16,768]{2,1,0:T(8,128)(2,1)} %grad_block.1), calls=%async_computation.5 | async-start | bytes 393216 | tf_op jit(solution)/shard_map/all_to_all | solution.py:349
  120.6 6.8 %collective-permute-start.7 = (bf16[2,256,128]{2,1,0:T(8,128)(2,1)S(1)}, bf16[2,256,128]{2,1,0:T(8,128)(2,1)S(1)}, u32[]{:S(2)}, u32[]{:S(2)}) collective-permute-start(bf16[2,256,128]{2,1,0:T(8,128)(2,1)S(1)} %pad_maximum_fusion.5.near_ref), channel_id=1, source_target_pairs={{0,16},{8,24},{16,0},{24,8},{32,48},{40,56},{48,32},{56,40},{64,80... | collective-permute-start | bytes 393224 | tf_op jit(solution)/shard_map/ppermute | solution.py:27
  129.2 22.2 %all-to-all-start.6 = ((bf16[16,16,768]{2,1,0:T(8,128)(2,1)}), bf16[16,16,768]{2,1,0:T(8,128)(2,1)S(1)}, u32[]{:S(2)}, u32[]{:S(2)}) async-start(bf16[16,16,768]{2,1,0:T(8,128)(2,1)} %bitcast.20), calls=%async_computation.6 | async-start | bytes 786432 | tf_op jit(solution)/shard_map/all_to_all | solution.py:355
  135.9 8.4 %collective-permute-start.10 = (bf16[128,768]{1,0:T(8,128)(2,1)S(1)}, bf16[128,768]{1,0:T(8,128)(2,1)S(1)}, u32[]{:S(2)}, u32[]{:S(2)}) collective-permute-start(bf16[128,768]{1,0:T(8,128)(2,1)S(1)} %bitcast.27), channel_id=1, source_target_pairs={{0,256},{128,384},{256,0},{384,128},{1,257},{129,385},{257,1},{385... | collective-permute-start | bytes 589832 | tf_op jit(solution)/shard_map/ppermute | solution.py:27
  138.4 11.5 %collective-permute-start.11 = (bf16[128,768]{1,0:T(8,128)(2,1)S(1)}, bf16[128,768]{1,0:T(8,128)(2,1)S(1)}, u32[]{:S(2)}, u32[]{:S(2)}) collective-permute-start(bf16[128,768]{1,0:T(8,128)(2,1)S(1)} %bitcast.28), channel_id=1, source_target_pairs={{0,384},{128,256},{256,128},{384,0},{1,385},{129,257},{257,129},{3... | collective-permute-start | bytes 589832 | tf_op jit(solution)/shard_map/ppermute | solution.py:27
  142.4 7.6 %collective-permute-start.9 = (bf16[128,768]{1,0:T(8,128)(2,1)S(1)}, bf16[128,768]{1,0:T(8,128)(2,1)S(1)}, u32[]{:S(2)}, u32[]{:S(2)}) collective-permute-start(bf16[128,768]{1,0:T(8,128)(2,1)S(1)} %bitcast.29), channel_id=1, source_target_pairs={{0,128},{128,0},{256,384},{384,256},{1,129},{129,1},{257,385},{385... | collective-permute-start | bytes 589832 | tf_op jit(solution)/shard_map/ppermute | solution.py:27

commit v4 on v3

--- a/solution.py
+++ b/solution.py
@@ -144,14 +144,18 @@
         out_ref[i] = total
 
 
-def grad_kernel(place_ref, head_ref, first_ref, second_ref, out_ref, rows_ref, *, masks):
+def grad_kernel(place_ref, head_ref, first_ref, second_ref, out_ref, rows_ref, *, masks, part):
+    low = (2 << len(masks)) // 2 - 1
     seq = place_ref[1]
     half = first_ref.shape[0]
-    part = rows_ref.shape[0] >> len(masks)
+    put = 0
     for slot in range(1 << len(masks)):
         mask = sum(m for bit, m in enumerate(masks) if slot >> bit & 1)
-        start = pl.multiple_of((seq ^ mask) * part, part)
-        rows_ref[slot * part : (slot + 1) * part, :] = head_ref[pl.ds(start, part), :]
+        for upper in range(rows_ref.shape[0] // (part << len(masks))):
+            source = upper * (low + 1) + ((seq ^ mask) & low)
+            start = pl.multiple_of(source * part, part)
+            rows_ref[put : put + part, :] = head_ref[pl.ds(start, part), :]
+            put += part
     out_ref[...] = (
         lax.dot_general(rows_ref[:half, :], first_ref[...], TN, preferred_element_type=F32)
         + lax.dot_general(rows_ref[half:, :], second_ref[...], TN, preferred_element_type=F32)
@@ -173,12 +177,14 @@
         out_ref[:, start : start + columns] = total.astype(BF16)
 
 
-def columns_kernel(place_ref, *refs):
-    out_ref = refs[-1]
-    columns = refs[0].shape[1]
-    for k, ref in enumerate(refs[:-1]):
-        start = pl.multiple_of((place_ref[0] ^ k) * columns, columns)
-        out_ref[:, pl.ds(start, columns)] = ref[...]
+def columns_kernel(place_ref, own_ref, other_ref, out_ref, *, pairs):
+    rows, columns = own_ref.shape[1:]
+    core = place_ref[2]
+    for i in range(own_ref.shape[0]):
+        cols = slice(i // pairs * columns, (i // pairs + 1) * columns)
+        for ref, lane in ((own_ref, core), (other_ref, 1 - core)):
+            start = pl.multiple_of((i % pairs * 2 + lane) * rows, rows)
+            out_ref[pl.ds(start, rows), cols] = ref[i]
 
 
 def head_norm(projected, gain):
@@ -274,7 +280,7 @@
     rows = block * seq_size
     grp = lax.axis_index("grp")
     seq = lax.axis_index("seq")
-    place = jnp.stack([grp, seq]).astype(jnp.int32)
+    place = jnp.stack([grp, seq, lax.axis_index("dp") & 1]).astype(jnp.int32)
 
     frames = video[0]
     frame_count, tokens = frames.shape[:2]
@@ -294,33 +300,43 @@
     )
 
     by_column = jnp.concatenate(
-        [cotangent[0, :, g * columns : (g + 1) * columns] for g in range(grp_size)], axis=0
-    ).reshape(grp_size, block, columns)
+        [cotangent[0, :, g * columns : (g + 1) * columns] for g in range(grp_size)] * 2, axis=0
+    ).reshape(2 * grp_size, block, columns)
     by_column, _ = lax.optimization_barrier((by_column, earlier))
-    near = lax.all_to_all(by_column, "grp", 0, 0, tiled=True).reshape(shared, columns)
+    halves = seq_size // 2
+    apart = [
+        [g * seq_size + h * halves + r for h in range(2) for g in range(grp_size)]
+        for r in range(halves)
+    ]
+    near = lax.all_to_all(
+        by_column, ("grp", "seq"), 0, 0, axis_index_groups=apart, tiled=True
+    ).reshape(2 * shared, columns)
+    near_other = xor_swap(near, "seq", 4)
+
+    side = seq & 1
+    depth = (seq >> 1) & 1
+
+    def halves_of(matrix, choice):
+        size = matrix.shape[1] // 2
+        return [
+            lax.dynamic_slice_in_dim(matrix, c * size, size, 1) for c in (choice, 1 - choice)
+        ]
+
+    weight, _ = lax.optimization_barrier((out_weight, sums))
+    kept, given = halves_of(weight, side)
+    weight_other = xor_swap(given, "seq", 1)
 
     parts = lax.all_to_all(sums.reshape(seq_size, shared, LANES), "seq", 0, 0, tiled=True)
     slab_sums = call(resplit_kernel, [(grp_size, shared, LANES)], parts, name="slab_sums")
+    near_other, weight_other, _ = lax.optimization_barrier((near_other, weight_other, slab_sums))
+    near = jnp.concatenate([near, near_other], axis=0)
+    near_other = xor_swap(near, "seq", 1)
     slab_parts = lax.all_to_all(slab_sums, "grp", 0, 0, tiled=True)
     merged = call(merge_kernel, [(seq_size, shared, LANES)], slab_parts, name="merged")
+    near_other, _ = lax.optimization_barrier((near_other, merged))
+    near = jnp.concatenate([near, near_other], axis=0)
+    far = xor_swap(near, "seq", 2)
     merged = lax.all_to_all(merged, "seq", 0, 0, tiled=True).reshape(groups, LANES)
-
-    masks = (8, 4, 1, 2)
-    for mask in masks[:-1]:
-        near = jnp.concatenate([near, xor_swap(near, "seq", mask)], axis=0)
-    far = xor_swap(near, "seq", masks[-1])
-
-    side = seq & 1
-    depth = (seq >> 1) & 1
-
-    def halved(block, choice, mask):
-        size = block.shape[1] // 2
-        kept = lax.dynamic_slice_in_dim(block, choice * size, size, 1)
-        given = lax.dynamic_slice_in_dim(block, (1 - choice) * size, size, 1)
-        return jnp.concatenate([kept, xor_swap(given, "seq", mask)], axis=0)
-
-    weight, _ = lax.optimization_barrier((out_weight, slab_sums))
-    weight_pair = halved(weight, side, 1)
 
     head_out, own_rows = call(
         functools.partial(attend_kernel, grp_size=grp_size, block=block),
@@ -331,23 +347,30 @@
 
     other_rows = xor_swap(own_rows, "seq", 1)
     local_grad = call(
-        functools.partial(grad_kernel, masks=masks), [(head, columns)], place, head_out, near, far,
-        name="local_grad", places=["smem"], scratch=[pltpu.VMEM((groups, head), BF16)],
-        flops=10**9,
-    )
-    pair_heads, weight_pair, _ = lax.optimization_barrier(
-        (jnp.stack([own_rows, other_rows]), weight_pair, local_grad)
-    )
-    quad_heads = (pair_heads, xor_swap(pair_heads, "seq", 2))
-    weight_quad = halved(weight_pair, depth, 2)
+        functools.partial(grad_kernel, masks=(4, 1, 2), part=shared), [(head, columns)], place,
+        head_out, near, far, name="local_grad", places=["smem"],
+        scratch=[pltpu.VMEM((groups, head), BF16)], flops=10**9,
+    )
     grad_parts = lax.all_to_all(
         local_grad.reshape(dp_size, head // dp_size, columns), "dp", 0, 0, tiled=True
     )
+    other_rows, weight_other, _ = lax.optimization_barrier((other_rows, weight_other, local_grad))
+    pair_heads = jnp.stack([own_rows, other_rows])
+    quad_heads = (pair_heads, xor_swap(pair_heads, "seq", 2))
+    kept, given = halves_of(jnp.concatenate([kept, weight_other], axis=0), depth)
+    weight_quad = jnp.concatenate([kept, xor_swap(given, "seq", 2)], axis=0)
+
+    pairs = dp_size // 2
     grad_block = call(
-        spread_kernel, [(dp_size, head // dp_size, columns)], grad_parts, name="grad_block"
-    )
-    grad_cols = lax.all_to_all(grad_block, "dp", 0, 0, tiled=True).reshape(head, columns)
-
+        spread_kernel, [(grp_size * pairs, head // dp_size, columns)], grad_parts,
+        name="grad_block",
+    )
+    same_core = [
+        [g * dp_size + 2 * p + c for g in range(grp_size) for p in range(pairs)] for c in range(2)
+    ]
+    grad_cols = lax.all_to_all(
+        grad_block, ("grp", "dp"), 0, 0, axis_index_groups=same_core, tiled=True
+    )
     partial = call(
         project_kernel, [(rows, columns)], *quad_heads, weight_quad, name="project", flops=10**9,
     )
@@ -355,9 +378,9 @@
     out_parts = lax.all_to_all(
         partial.reshape(seq_size, block, columns), "seq", 0, 0, tiled=True
     )
-    gathered = [grad_cols] + [xor_swap(grad_cols, "grp", k) for k in range(1, grp_size)]
     out_grad = call(
-        columns_kernel, [(head, width)], place, *gathered, name="grad_columns", places=["smem"]
+        functools.partial(columns_kernel, pairs=pairs), [(head, width)], place, grad_cols,
+        xor_swap(grad_cols, "dp", 1), name="grad_columns", places=["smem"],
     )
     attended = call(attended_kernel, [(block, width)], out_parts, name="attended")
     return (attended[None], out_grad)

time: 155 us -> 169 us (1.090)
  local copies, waits for them, and re-layouts: 7.84 us -> 18 us
  starting transfers between devices: 83.5 us -> 75.3 us
  waiting for transfers between devices: 35.2 us -> 43.2 us
  blocking collectives: 0 us -> 7.03 us
  other arithmetic: 3.86 us -> 1.43 us
    unnamed x24 -> x35, local copies, waits for them, and re-layouts: 3.79 us -> 14 us
    ppermute x11 -> x8, starting transfers between devices: 34.4 us -> 25.5 us  [xor_swap(): return lax.ppermute(block, axis, route)]
    all_to_all x0 -> x1, blocking collectives: none -> 7.03 us  [shards(): slab_parts = lax.all_to_all(slab_sums, 'grp', 0, 0, tiled=True)]
    all_to_all x1, waiting for transfers between devices: 0.01 us -> 5.71 us  [shards(): lax.all_to_all(partial.reshape(seq_size, block, columns), 'seq', 0, 0, ti...]
    all_to_all x1, waiting for transfers between devices: 6.41 us -> 1.01 us  [shards(): lax.all_to_all(local_grad.reshape(dp_size, head // dp_size, columns), 'dp...]
    all_to_all x3 -> x2, starting transfers between devices: 13 us -> 18.1 us  [the longest x1 12.5 us: shards(): lax.all_to_all(by_column, ('grp', 'seq'), 0, 0, axis_index_groups=apart,...]
    all_to_all x1, starting transfers between devices: 10.9 us -> 6.12 us  [shards(): lax.all_to_all(sums.reshape(seq_size, shared, LANES), 'seq', 0, 0, tiled=...]
    all_to_all x1, waiting for transfers between devices: 0.01 us -> 3.97 us  [shards(): lax.all_to_all(merged, 'seq', 0, 0, tiled=True).reshape(groups, LANES)]
  transfers between devices with their start and end apart: 19 -> 15, of which waited for: 8 -> 12; matrix products, arithmetic and copies ran while one was open for 5% -> 8% of each run, Pallas kernels for 12% -> 10%
where the time goes in v4:
time: 169 us; the launch traced here: 166 us
  starting transfers between devices  75.3 us (45%)
  waiting for transfers between devices  43.2 us (26%)
  Pallas kernels  20.3 us (12%)
  local copies, waits for them, and re-layouts  18 us (11%)
  blocking collectives  7.03 us (4%)
    ppermute x8, waiting for transfers between devices, xor_swap(): return lax.ppermute(block, axis, route)  28.7 us
    ppermute x8, starting transfers between devices, xor_swap(): return lax.ppermute(block, axis, route)  25.5 us
    pallas_call x10, Pallas kernels, call(): pl.pallas_call(body, out_shape=outs, in_specs=in_specs, out_specs=(whole,...  20.3 us
    unnamed x35, local copies, waits for them, and re-layouts  14 us
    all_to_all x1, starting transfers between devices, shards(): lax.all_to_all(by_column, ('grp', 'seq'), 0, 0, axis_index_groups=apart,...  12.5 us
    all_to_all x1, starting transfers between devices, shards(): lax.all_to_all(local_grad.reshape(dp_size, head // dp_size, columns), 'dp...  8.45 us
    all_to_all x1, blocking collectives, shards(): slab_parts = lax.all_to_all(slab_sums, 'grp', 0, 0, tiled=True)  7.03 us
    all_to_all x1, starting transfers between devices, shards(): lax.all_to_all(merged, 'seq', 0, 0, tiled=True).reshape(groups, LANES)  6.93 us
  transfers between devices with their start and end apart: 15, of which 12 were waited for; matrix products, arithmetic and copies ran while one was open for 8% of the time, Pallas kernels for 10%

profile of v4, /device:TPU:1, one launch (start us, length us, event | category | flops | bytes accessed | tf_op | source)
XLA Modules:
  0.0 166.2 jit_solution(5866094172557022173)
XLA Ops:
  0.6 0.9 slice_bitcast_fusion
  1.5 4.0 %collective-permute-start = (bf16[2,64,512]{2,1,0:T(8,128)(2,1)S(1)}, bf16[2,64,512]{2,1,0:T(8,128)(2,1)S(1)}, u32[]{:S(2)}, u32[]{:S(2)}) collective-permute-start(bf16[2,64,512]{2,1,0:T(8,128)(2,1)S(1)} %slice_bitcast_fusion), channel_id=1, source_target_pairs={{0,8},{8,16},{16,24},{24,32},{32,40},{40,48},{48,56},{56,64},{64,7... | collective-permute-start | bytes 393224 | tf_op jit(solution)/shard_map/ppermute | solution.py:22
  5.6 1.3 bitcast_dynamic-update-slice_fusion.6
  6.9 1.3 bitcast_dynamic-update-slice_fusion.4
  8.3 1.3 bitcast_dynamic-update-slice_fusion.2
  9.6 1.3 bitcast_dynamic-update-slice_fusion
  11.0 1.3 bitcast_dynamic-update-slice_fusion.7
  12.3 1.3 bitcast_dynamic-update-slice_fusion.5
  13.7 1.3 bitcast_dynamic-update-slice_fusion.3
  15.0 1.3 bitcast_dynamic-update-slice_fusion.1
  16.4 12.5 %all-to-all-start.3 = ((bf16[8,16,768]{2,1,0:T(8,128)(2,1)}), bf16[8,16,768]{2,1,0:T(8,128)(2,1)S(1)}, u32[]{:S(2)}, u32[]{:S(2)}) async-start(bf16[8,16,768]{2,1,0:T(8,128)(2,1)} %bitcast.16), calls=%async_computation.3 | async-start | bytes 393216 | tf_op jit(solution)/shard_map/all_to_all | solution.py:311
  29.6 1.0 copy-done
  30.6 0.9 copy-done.3
  32.4 1.4 late_frames.1
  33.8 1.6 group_sums.1
  35.4 3.2 %all-to-all-done.3 = bf16[8,16,768]{2,1,0:T(8,128)(2,1)S(1)} async-done(((bf16[8,16,768]{2,1,0:T(8,128)(2,1)}), bf16[8,16,768]{2,1,0:T(8,128)(2,1)S(1)}, u32[]{:S(2)}, u32[]{:S(2)}) %all-to-all-start.3) | async-done | bytes 196640 | tf_op jit(solution)/shard_map/all_to_all | solution.py:311
  38.6 6.1 %all-to-all-start = ((bf16[16,64,128]{2,1,0:T(8,128)(2,1)}), bf16[16,64,128]{2,1,0:T(8,128)(2,1)S(1)}, u32[]{:S(2)}, u32[]{:S(2)}) async-start(bf16[16,64,128]{2,1,0:T(8,128)(2,1)} %bitcast.6), calls=%async_computation | async-start | bytes 524288 | tf_op jit(solution)/shard_map/all_to_all | solution.py:329
  44.7 1.0 constant_dynamic-slice_fusion
  45.7 3.3 %collective-permute-start.3 = (bf16[128,1536]{1,0:T(8,128)(2,1)}, bf16[128,1536]{1,0:T(8,128)(2,1)S(1)}, u32[]{:S(2)}, u32[]{:S(2)}) collective-permute-start(bf16[128,1536]{1,0:T(8,128)(2,1)} %get-tuple-element.33), channel_id=1, source_target_pairs={{0,8},{8,0},{16,24},{24,16},{32,40},{40,32},{48,56},{56,48},{64,72... | collective-permute-start | bytes 1179656 | tf_op jit(solution)/shard_map/ppermute | solution.py:27
  48.9 4.0 %collective-permute-start.2 = (bf16[128,768]{1,0:T(8,128)(2,1)S(1)}, bf16[128,768]{1,0:T(8,128)(2,1)S(1)}, u32[]{:S(2)}, u32[]{:S(2)}) collective-permute-start(bf16[128,768]{1,0:T(8,128)(2,1)S(1)} %bitcast.38), channel_id=1, source_target_pairs={{0,32},{8,40},{16,48},{24,56},{32,0},{40,8},{48,16},{56,24},{64,96... | collective-permute-start | bytes 589832 | tf_op jit(solution)/shard_map/ppermute | solution.py:27
  53.8 4.6 %collective-permute-done.3 = bf16[128,1536]{1,0:T(8,128)(2,1)S(1)} collective-permute-done((bf16[128,1536]{1,0:T(8,128)(2,1)}, bf16[128,1536]{1,0:T(8,128)(2,1)S(1)}, u32[]{:S(2)}, u32[]{:S(2)}) %collective-permute-start.3) | collective-permute-done | bytes 393248 | tf_op jit(solution)/shard_map/ppermute | solution.py:27
  59.2 3.3 %collective-permute-done.2 = bf16[128,768]{1,0:T(8,128)(2,1)S(1)} collective-permute-done((bf16[128,768]{1,0:T(8,128)(2,1)S(1)}, bf16[128,768]{1,0:T(8,128)(2,1)S(1)}, u32[]{:S(2)}, u32[]{:S(2)}) %collective-permute-start.2) | collective-permute-done | bytes 196640 | tf_op jit(solution)/shard_map/ppermute | solution.py:27
  62.5 2.7 %collective-permute-start.4 = (bf16[256,768]{1,0:T(8,128)(2,1)S(1)}, bf16[256,768]{1,0:T(8,128)(2,1)}, u32[]{:S(2)}, u32[]{:S(2)}) collective-permute-start(bf16[256,768]{1,0:T(8,128)(2,1)S(1)} %pad_maximum_fusion.2), channel_id=1, source_target_pairs={{0,8},{8,0},{16,24},{24,16},{32,40},{40,32},{48,56},{56,48},{64,72... | collective-permute-start | bytes 1179656 | tf_op jit(solution)/shard_map/ppermute | solution.py:27
  65.2 7.0 %all_to_all.35.parts_ref = bf16[4,64,128]{2,1,0:T(8,128)(2,1)S(1)} all-to-all(bf16[4,64,128]{2,1,0:T(8,128)(2,1)S(1)} %slab_sums.1), channel_id=1, replica_groups=mesh['grp'=4,'seq'=16,'dp'=8] {'grp'}, dimensions={0} | all-to-all | bytes 131072 | tf_op jit(solution)/shard_map/all_to_all | solution.py:334
  72.2 0.9 merged.1
  73.1 6.9 %all-to-all-start.2 = ((bf16[16,64,128]{2,1,0:T(8,128)(2,1)}), bf16[16,64,128]{2,1,0:T(8,128)(2,1)S(1)}, u32[]{:S(2)}, u32[]{:S(2)}) async-start(bf16[16,64,128]{2,1,0:T(8,128)(2,1)} %merged.1), calls=%async_computation.2 | async-start | bytes 524288 | tf_op jit(solution)/shard_map/all_to_all | solution.py:339
  80.0 1.2 pad_maximum_fusion.first_ref
  81.2 3.4 %collective-permute-start.5 = (bf16[512,768]{1,0:T(8,128)(2,1)S(1)}, bf16[512,768]{1,0:T(8,128)(2,1)}, u32[]{:S(2)}, u32[]{:S(2)}) collective-permute-start(bf16[512,768]{1,0:T(8,128)(2,1)S(1)} %pad_maximum_fusion.first_ref), channel_id=1, source_target_pairs={{0,16},{8,24},{16,0},{24,8},{32,48},{40,56},{48,32},{56,40},{64,80... | collective-permute-start | bytes 2359304 | tf_op jit(solution)/shard_map/ppermute | solution.py:27
  84.8 4.0 %all-to-all-done.2 = bf16[16,64,128]{2,1,0:T(8,128)(2,1)S(1)} async-done(((bf16[16,64,128]{2,1,0:T(8,128)(2,1)}), bf16[16,64,128]{2,1,0:T(8,128)(2,1)S(1)}, u32[]{:S(2)}, u32[]{:S(2)}) %all-to-all-start.2) | async-done | bytes 262176 | tf_op jit(solution)/shard_map/all_to_all | solution.py:339
  88.8 1.0 copy-done.2
  89.8 9.9 %attend.1 = (bf16[1024,128]{1,0:T(8,128)(2,1)S(1)}, bf16[256,128]{1,0:T(8,128)(2,1)S(1)}) custom-call(s32[3]{0:T(128)S(1)} %pad_add_fusion.place_ref, bf16[1024,128]{1,0:T(8,128)(2,1)S(1)} %bitcast.31, bf16[64,3072]{1,0:T(8,128)(2,1)S(1)} %copy-done.2, f32[1,3072]{1,0:T(1,128)S(1)} %bitcast.35, bf16[3,3072,128]{2,1,0:T(8,128)(2,1)S(1)} %copy-done.1, ...), custom_call_target="tpu_custom_call" | custom-call | flops 8000000000 | bytes 1000000 | tf_op jit(solution)/shard_map/attend/pallas_call | solution.py:256
  99.7 5.5 %collective-permute-done.5.second_ref = bf16[512,768]{1,0:T(8,128)(2,1)} collective-permute-done((bf16[512,768]{1,0:T(8,128)(2,1)S(1)}, bf16[512,768]{1,0:T(8,128)(2,1)}, u32[]{:S(2)}, u32[]{:S(2)}) %collective-permute-start.5) | collective-permute-done | bytes 786464 | tf_op jit(solution)/shard_map/ppermute | solution.py:27
  105.2 2.3 %local_grad.1 = bf16[128,768]{1,0:T(8,128)(2,1)} custom-call(s32[3]{0:T(128)S(1)} %pad_add_fusion.place_ref, bf16[1024,128]{1,0:T(8,128)(2,1)S(1)} %get-tuple-element.24.head_ref, bf16[512,768]{1,0:T(8,128)(2,1)S(1)} %pad_maximum_fusion.first_ref, bf16[512,768]{1,0:T(8,128)(2,1)} %collective-permute-done.5.second_ref), custom_call_target="tpu_custom_call" | custom-call | flops 1000000000 | bytes 1000000 | tf_op jit(solution)/shard_map/local_grad/pallas_call | solution.py:256
  107.4 8.5 %all-to-all-start.4 = ((bf16[8,16,768]{2,1,0:T(8,128)(2,1)}), bf16[8,16,768]{2,1,0:T(8,128)(2,1)S(1)}, u32[]{:S(2)}, u32[]{:S(2)}) async-start(bf16[8,16,768]{2,1,0:T(8,128)(2,1)} %bitcast.19), calls=%async_computation.4 | async-start | bytes 393216 | tf_op jit(solution)/shard_map/all_to_all | solution.py:354
  115.9 2.9 %collective-permute-start.1 = (bf16[256,128]{1,0:T(8,128)(2,1)S(1)}, bf16[256,128]{1,0:T(8,128)(2,1)S(1)}, u32[]{:S(2)}, u32[]{:S(2)}) collective-permute-start(bf16[256,128]{1,0:T(8,128)(2,1)S(1)} %get-tuple-element.20), channel_id=1, source_target_pairs={{0,8},{8,0},{16,24},{24,16},{32,40},{40,32},{48,56},{56,48},{64,72... | collective-permute-start | bytes 196616 | tf_op jit(solution)/shard_map/ppermute | solution.py:27
  118.8 5.0 %collective-permute-done.1 = bf16[256,128]{1,0:T(8,128)(2,1)S(1)} collective-permute-done((bf16[256,128]{1,0:T(8,128)(2,1)S(1)}, bf16[256,128]{1,0:T(8,128)(2,1)S(1)}, u32[]{:S(2)}, u32[]{:S(2)}) %collective-permute-start.1) | collective-permute-done | bytes 65568 | tf_op jit(solution)/shard_map/ppermute | solution.py:27
  123.8 1.0 all-to-all-done.4.parts_ref
  125.6 5.6 %all-to-all-start.5 = ((bf16[16,16,768]{2,1,0:T(8,128)(2,1)}), bf16[16,16,768]{2,1,0:T(8,128)(2,1)S(1)}, u32[]{:S(2)}, u32[]{:S(2)}) async-start(bf16[16,16,768]{2,1,0:T(8,128)(2,1)} %grad_block.1), calls=%async_computation.5 | async-start | bytes 786432 | tf_op jit(solution)/shard_map/all_to_all | solution.py:371
  131.3 2.7 %collective-permute-start.7 = (bf16[256,768]{1,0:T(8,128)(2,1)S(1)}, bf16[256,768]{1,0:T(8,128)(2,1)S(1)}, u32[]{:S(2)}, u32[]{:S(2)}) collective-permute-start(bf16[256,768]{1,0:T(8,128)(2,1)S(1)} %get-tuple-element.31), channel_id=1, source_target_pairs={{0,16},{8,24},{16,0},{24,8},{32,48},{40,56},{48,32},{56,40},{64,80... | collective-permute-start | bytes 1179656 | tf_op jit(solution)/shard_map/ppermute | solution.py:27
  134.0 2.6 %collective-permute-start.6 = (bf16[2,256,128]{2,1,0:T(8,128)(2,1)S(1)}, bf16[2,256,128]{2,1,0:T(8,128)(2,1)S(1)}, u32[]{:S(2)}, u32[]{:S(2)}) collective-permute-start(bf16[2,256,128]{2,1,0:T(8,128)(2,1)S(1)} %pad_maximum_fusion.3.near_ref), channel_id=1, source_target_pairs={{0,16},{8,24},{16,0},{24,8},{32,48},{40,56},{48,32},{56,40},{64,80... | collective-permute-start | bytes 393224 | tf_op jit(solution)/shard_map/ppermute | solution.py:27
  136.6 6.2 %collective-permute-done.7 = bf16[256,768]{1,0:T(8,128)(2,1)S(1)} collective-permute-done((bf16[256,768]{1,0:T(8,128)(2,1)S(1)}, bf16[256,768]{1,0:T(8,128)(2,1)S(1)}, u32[]{:S(2)}, u32[]{:S(2)}) %collective-permute-start.7) | collective-permute-done | bytes 393248 | tf_op jit(solution)/shard_map/ppermute | solution.py:27
  142.9 2.8 %collective-permute-done.6.far_ref = bf16[2,256,128]{2,1,0:T(8,128)(2,1)S(1)} collective-permute-done((bf16[2,256,128]{2,1,0:T(8,128)(2,1)S(1)}, bf16[2,256,128]{2,1,0:T(8,128)(2,1)S(1)}, u32[]{:S(2)}, u32[]{:S(2)}) %collective-permute-start.6) | collective-permute-done | bytes 131104 | tf_op jit(solution)/shard_map/ppermute | solution.py:27
  145.7 1.1 project.1
  146.8 6.3 %all-to-all-start.6 = ((bf16[16,16,768]{2,1,0:T(8,128)(2,1)}), bf16[16,16,768]{2,1,0:T(8,128)(2,1)S(1)}, u32[]{:S(2)}, u32[]{:S(2)}) async-start(bf16[16,16,768]{2,1,0:T(8,128)(2,1)} %bitcast.20), calls=%async_computation.6 | async-start | bytes 786432 | tf_op jit(solution)/shard_map/all_to_all | solution.py:378
  153.1 4.0 %collective-permute-start.8 = (bf16[16,16,768]{2,1,0:T(8,128)(2,1)S(1)}, bf16[16,16,768]{2,1,0:T(8,128)(2,1)S(1)}, u32[]{:S(2)}, u32[]{:S(2)}) collective-permute-start(bf16[16,16,768]{2,1,0:T(8,128)(2,1)S(1)} %all-to-all-done.5.own_ref), channel_id=1, source_target_pairs={{0,1},{1,0},{2,3},{3,2},{4,5},{5,4},{6,7},{7,6},{8,9},{9,8},{10,11... | collective-permute-start | bytes 1179656 | tf_op jit(solution)/shard_map/ppermute | solution.py:27
  157.0 1.3 collective-permute-done.8.other_ref
  158.3 1.5 grad_columns.1
  159.8 5.7 %all-to-all-done.6.parts_ref = bf16[16,16,768]{2,1,0:T(8,128)(2,1)S(1)} async-done(((bf16[16,16,768]{2,1,0:T(8,128)(2,1)}), bf16[16,16,768]{2,1,0:T(8,128)(2,1)S(1)}, u32[]{:S(2)}, u32[]{:S(2)}) %all-to-all-start.6) | async-done | bytes 393248 | tf_op jit(solution)/shard_map/all_to_all | solution.py:378
  (38 shorter events, 5.0 us)
Async XLA Ops:
  1.5 14.8 %collective-permute-start = (bf16[2,64,512]{2,1,0:T(8,128)(2,1)S(1)}, bf16[2,64,512]{2,1,0:T(8,128)(2,1)S(1)}, u32[]{:S(2)}, u32[]{:S(2)}) collective-permute-start(bf16[2,64,512]{2,1,0:T(8,128)(2,1)S(1)} %slice_bitcast_fusion), channel_id=1, source_target_pairs={{0,8},{8,16},{16,24},{24,32},{32,40},{40,48},{48,56},{56,64},{64,7... | collective-permute-start | bytes 393224 | tf_op jit(solution)/shard_map/ppermute | solution.py:22
  16.4 22.2 %all-to-all-start.3 = ((bf16[8,16,768]{2,1,0:T(8,128)(2,1)}), bf16[8,16,768]{2,1,0:T(8,128)(2,1)S(1)}, u32[]{:S(2)}, u32[]{:S(2)}) async-start(bf16[8,16,768]{2,1,0:T(8,128)(2,1)} %bitcast.16), calls=%async_computation.3 | async-start | bytes 393216 | tf_op jit(solution)/shard_map/all_to_all | solution.py:311
  29.6 1.0 copy-start
  30.6 0.9 copy-start.3
  31.5 0.8 copy-start.4
  33.8 10.9 %copy-start.11 = (bf16[128,3072]{1,0:T(8,128)(2,1)S(1)}, bf16[128,3072]{1,0:T(8,128)(2,1)}, u32[]{:S(2)}) copy-start(bf16[128,3072]{1,0:T(8,128)(2,1)} %param.20) | copy-start | bytes 2359300
  38.6 23.9 %copy-start.8 = (bf16[8,16,768]{2,1,0:T(8,128)(2,1)}, bf16[8,16,768]{2,1,0:T(8,128)(2,1)S(1)}, u32[]{:S(2)}) copy-start(bf16[8,16,768]{2,1,0:T(8,128)(2,1)S(1)} %all-to-all-done.3) | copy-start | bytes 589828
  38.6 15.0 %all-to-all-start = ((bf16[16,64,128]{2,1,0:T(8,128)(2,1)}), bf16[16,64,128]{2,1,0:T(8,128)(2,1)S(1)}, u32[]{:S(2)}, u32[]{:S(2)}) async-start(bf16[16,64,128]{2,1,0:T(8,128)(2,1)} %bitcast.6), calls=%async_computation | async-start | bytes 524288 | tf_op jit(solution)/shard_map/all_to_all | solution.py:329
  45.7 12.7 %collective-permute-start.3 = (bf16[128,1536]{1,0:T(8,128)(2,1)}, bf16[128,1536]{1,0:T(8,128)(2,1)S(1)}, u32[]{:S(2)}, u32[]{:S(2)}) collective-permute-start(bf16[128,1536]{1,0:T(8,128)(2,1)} %get-tuple-element.33), channel_id=1, source_target_pairs={{0,8},{8,0},{16,24},{24,16},{32,40},{40,32},{48,56},{56,48},{64,72... | collective-permute-start | bytes 1179656 | tf_op jit(solution)/shard_map/ppermute | solution.py:27
  48.9 13.5 %collective-permute-start.2 = (bf16[128,768]{1,0:T(8,128)(2,1)S(1)}, bf16[128,768]{1,0:T(8,128)(2,1)S(1)}, u32[]{:S(2)}, u32[]{:S(2)}) collective-permute-start(bf16[128,768]{1,0:T(8,128)(2,1)S(1)} %bitcast.38), channel_id=1, source_target_pairs={{0,32},{8,40},{16,48},{24,56},{32,0},{40,8},{48,16},{56,24},{64,96... | collective-permute-start | bytes 589832 | tf_op jit(solution)/shard_map/ppermute | solution.py:27
  53.8 35.0 %copy-start.1 = (bf16[3,3072,128]{2,1,0:T(8,128)(2,1)S(1)}, bf16[3,3072,128]{2,1,0:T(8,128)(2,1)}, u32[]{:S(2)}) copy-start(bf16[3,3072,128]{2,1,0:T(8,128)(2,1)} %qkv_ref.1) | copy-start | bytes 7077892
  53.8 35.0 %copy-start.5 = (f32[3072]{0:T(1024)S(1)}, f32[3072]{0:T(1024)}, u32[]{:S(2)}) copy-start(f32[3072]{0:T(1024)} %param.16) | copy-start | bytes 36868
  53.8 35.0 %copy-start.6 = (f32[128]{0:T(128)S(1)}, f32[128]{0:T(128)}, u32[]{:S(2)}) copy-start(f32[128]{0:T(128)} %param.18) | copy-start | bytes 1540
  53.8 35.0 %copy-start.7 = (f32[128]{0:T(128)S(1)}, f32[128]{0:T(128)}, u32[]{:S(2)}) copy-start(f32[128]{0:T(128)} %param.19) | copy-start | bytes 1540
  58.4 0.8 copy-start.12
  62.4 10.6 %copy-start.10 = (bf16[128,768]{1,0:T(8,128)(2,1)}, bf16[128,768]{1,0:T(8,128)(2,1)S(1)}, u32[]{:S(2)}) copy-start(bf16[128,768]{1,0:T(8,128)(2,1)S(1)} %collective-permute-done.2) | copy-start | bytes 589828
  62.5 17.6 %collective-permute-start.4 = (bf16[256,768]{1,0:T(8,128)(2,1)S(1)}, bf16[256,768]{1,0:T(8,128)(2,1)}, u32[]{:S(2)}, u32[]{:S(2)}) collective-permute-start(bf16[256,768]{1,0:T(8,128)(2,1)S(1)} %pad_maximum_fusion.2), channel_id=1, source_target_pairs={{0,8},{8,0},{16,24},{24,16},{32,40},{40,32},{48,56},{56,48},{64,72... | collective-permute-start | bytes 1179656 | tf_op jit(solution)/shard_map/ppermute | solution.py:27
  73.1 15.7 %all-to-all-start.2 = ((bf16[16,64,128]{2,1,0:T(8,128)(2,1)}), bf16[16,64,128]{2,1,0:T(8,128)(2,1)S(1)}, u32[]{:S(2)}, u32[]{:S(2)}) async-start(bf16[16,64,128]{2,1,0:T(8,128)(2,1)} %merged.1), calls=%async_computation.2 | async-start | bytes 524288 | tf_op jit(solution)/shard_map/all_to_all | solution.py:339
  81.2 23.9 %collective-permute-start.5 = (bf16[512,768]{1,0:T(8,128)(2,1)S(1)}, bf16[512,768]{1,0:T(8,128)(2,1)}, u32[]{:S(2)}, u32[]{:S(2)}) collective-permute-start(bf16[512,768]{1,0:T(8,128)(2,1)S(1)} %pad_maximum_fusion.first_ref), channel_id=1, source_target_pairs={{0,16},{8,24},{16,0},{24,8},{32,48},{40,56},{48,32},{56,40},{64,80... | collective-permute-start | bytes 2359304 | tf_op jit(solution)/shard_map/ppermute | solution.py:27
  88.8 1.0 copy-start.2
  107.4 23.8 %copy-start.9 = (bf16[128,1536]{1,0:T(8,128)(2,1)S(1)}, bf16[128,1536]{1,0:T(8,128)(2,1)}, u32[]{:S(2)}) copy-start(bf16[128,1536]{1,0:T(8,128)(2,1)} %get-tuple-element.32) | copy-start | bytes 1179652
  107.4 23.8 %copy-start.13 = (bf16[128,1536]{1,0:T(8,128)(2,1)S(1)}, bf16[128,1536]{1,0:T(8,128)(2,1)}, u32[]{:S(2)}) copy-start(bf16[128,1536]{1,0:T(8,128)(2,1)} %copy-done.12) | copy-start | bytes 1179652
  107.4 17.4 %all-to-all-start.4 = ((bf16[8,16,768]{2,1,0:T(8,128)(2,1)}), bf16[8,16,768]{2,1,0:T(8,128)(2,1)S(1)}, u32[]{:S(2)}, u32[]{:S(2)}) async-start(bf16[8,16,768]{2,1,0:T(8,128)(2,1)} %bitcast.19), calls=%async_computation.4 | async-start | bytes 393216 | tf_op jit(solution)/shard_map/all_to_all | solution.py:354
  115.9 7.9 %collective-permute-start.1 = (bf16[256,128]{1,0:T(8,128)(2,1)S(1)}, bf16[256,128]{1,0:T(8,128)(2,1)S(1)}, u32[]{:S(2)}, u32[]{:S(2)}) collective-permute-start(bf16[256,128]{1,0:T(8,128)(2,1)S(1)} %get-tuple-element.20), channel_id=1, source_target_pairs={{0,8},{8,0},{16,24},{24,16},{32,40},{40,32},{48,56},{56,48},{64,72... | collective-permute-start | bytes 196616 | tf_op jit(solution)/shard_map/ppermute | solution.py:27
  125.6 21.2 %all-to-all-start.5 = ((bf16[16,16,768]{2,1,0:T(8,128)(2,1)}), bf16[16,16,768]{2,1,0:T(8,128)(2,1)S(1)}, u32[]{:S(2)}, u32[]{:S(2)}) async-start(bf16[16,16,768]{2,1,0:T(8,128)(2,1)} %grad_block.1), calls=%async_computation.5 | async-start | bytes 786432 | tf_op jit(solution)/shard_map/all_to_all | solution.py:371
  131.3 11.6 %collective-permute-start.7 = (bf16[256,768]{1,0:T(8,128)(2,1)S(1)}, bf16[256,768]{1,0:T(8,128)(2,1)S(1)}, u32[]{:S(2)}, u32[]{:S(2)}) collective-permute-start(bf16[256,768]{1,0:T(8,128)(2,1)S(1)} %get-tuple-element.31), channel_id=1, source_target_pairs={{0,16},{8,24},{16,0},{24,8},{32,48},{40,56},{48,32},{56,40},{64,80... | collective-permute-start | bytes 1179656 | tf_op jit(solution)/shard_map/ppermute | solution.py:27
  134.0 11.7 %collective-permute-start.6 = (bf16[2,256,128]{2,1,0:T(8,128)(2,1)S(1)}, bf16[2,256,128]{2,1,0:T(8,128)(2,1)S(1)}, u32[]{:S(2)}, u32[]{:S(2)}) collective-permute-start(bf16[2,256,128]{2,1,0:T(8,128)(2,1)S(1)} %pad_maximum_fusion.3.near_ref), channel_id=1, source_target_pairs={{0,16},{8,24},{16,0},{24,8},{32,48},{40,56},{48,32},{56,40},{64,80... | collective-permute-start | bytes 393224 | tf_op jit(solution)/shard_map/ppermute | solution.py:27
  146.8 18.7 %all-to-all-start.6 = ((bf16[16,16,768]{2,1,0:T(8,128)(2,1)}), bf16[16,16,768]{2,1,0:T(8,128)(2,1)S(1)}, u32[]{:S(2)}, u32[]{:S(2)}) async-start(bf16[16,16,768]{2,1,0:T(8,128)(2,1)} %bitcast.20), calls=%async_computation.6 | async-start | bytes 786432 | tf_op jit(solution)/shard_map/all_to_all | solution.py:378
  153.1 5.3 %collective-permute-start.8 = (bf16[16,16,768]{2,1,0:T(8,128)(2,1)S(1)}, bf16[16,16,768]{2,1,0:T(8,128)(2,1)S(1)}, u32[]{:S(2)}, u32[]{:S(2)}) collective-permute-start(bf16[16,16,768]{2,1,0:T(8,128)(2,1)S(1)} %all-to-all-done.5.own_ref), channel_id=1, source_target_pairs={{0,1},{1,0},{2,3},{3,2},{4,5},{5,4},{6,7},{7,6},{8,9},{9,8},{10,11... | collective-permute-start | bytes 1179656 | tf_op jit(solution)/shard_map/ppermute | solution.py:27

commit v5 on v4

--- a/solution.py
+++ b/solution.py
@@ -144,37 +144,89 @@
         out_ref[i] = total
 
 
-def grad_kernel(place_ref, head_ref, first_ref, second_ref, out_ref, rows_ref, *, masks, part):
-    low = (2 << len(masks)) // 2 - 1
+def split_kernel(rows_ref, out_ref):
+    columns = out_ref.shape[2]
+    for i in range(out_ref.shape[0]):
+        out_ref[i] = rows_ref[:, i * columns : (i + 1) * columns]
+
+
+def grad_kernel(
+    place_ref, head_ref, given_ref, first_ref, second_ref, out_ref, rows_ref, *, masks, part,
+):
     seq = place_ref[1]
+    head = head_ref.shape[1]
     half = first_ref.shape[0]
-    put = 0
     for slot in range(1 << len(masks)):
         mask = sum(m for bit, m in enumerate(masks) if slot >> bit & 1)
-        for upper in range(rows_ref.shape[0] // (part << len(masks))):
-            source = upper * (low + 1) + ((seq ^ mask) & low)
-            start = pl.multiple_of(source * part, part)
-            rows_ref[put : put + part, :] = head_ref[pl.ds(start, part), :]
-            put += part
-    out_ref[...] = (
+        source = seq ^ mask
+        start = pl.multiple_of(source * part, part)
+        given = pl.multiple_of((source >> 1) * part, part)
+        here = slice(slot * part, (slot + 1) * part)
+        rows_ref[here, :head] = head_ref[pl.ds(start, part), :]
+        rows_ref[here, head:] = given_ref[pl.ds(given, part), :]
+    total = (
         lax.dot_general(rows_ref[:half, :], first_ref[...], TN, preferred_element_type=F32)
         + lax.dot_general(rows_ref[half:, :], second_ref[...], TN, preferred_element_type=F32)
     ).astype(BF16)
-
-
-def project_kernel(near_ref, far_ref, weight_ref, out_ref):
-    heads = jnp.concatenate([near_ref[0], near_ref[1], far_ref[0], far_ref[1]], axis=1)
-    out_ref[...] = jnp.dot(heads, weight_ref[...], preferred_element_type=F32).astype(BF16)
+    side = seq & 1
+    out_ref[side] = total[:head, :]
+    out_ref[1 - side] = total[head:, :]
+
+
+def pair_kernel(place_ref, own_ref, given_ref, out_ref, *, part):
+    grp = place_ref[0]
+    side = place_ref[1] & 1
+    rows = own_ref.shape[0]
+    slabs = (given_ref.shape[0] - rows // 2) // part
+    block = rows // (2 * slabs)
+    out_ref[0] = own_ref[...]
+    for i in range(slabs):
+        near = pl.multiple_of((2 * i + side) * block, block)
+        far = pl.multiple_of((2 * i + 1 - side) * block, block)
+        start = pl.multiple_of(i * part + grp * block, block)
+        out_ref[1, pl.ds(near, block), :] = given_ref[pl.ds(start, block), :]
+        first = slabs * part + i * block
+        out_ref[1, pl.ds(far, block), :] = given_ref[first : first + block, :]
+
+
+def weights_kernel(place_ref, weight_ref, partner_ref, kept_ref, given_ref):
+    columns = kept_ref.shape[1]
+    size = weight_ref.shape[0]
+    side = place_ref[1] & 1
+    depth = (place_ref[1] >> 1) & 1
+    for i, (ref, first) in enumerate([(weight_ref, 2 * side), (partner_ref, 0)]):
+        keep = pl.multiple_of((first + depth) * columns, columns)
+        give = pl.multiple_of((first + 1 - depth) * columns, columns)
+        kept_ref[i * size : (i + 1) * size, :] = ref[:, pl.ds(keep, columns)]
+        given_ref[i * size : (i + 1) * size, :] = ref[:, pl.ds(give, columns)]
+
+
+def project_kernel(place_ref, near_ref, far_ref, near_weight_ref, far_weight_ref, *refs):
+    out_refs, sum_ref = refs[:4], refs[4]
+    near = jnp.concatenate([near_ref[0], near_ref[1]], axis=1)
+    far = jnp.concatenate([far_ref[0], far_ref[1]], axis=1)
+    sum_ref[...] = (
+        jnp.dot(near, near_weight_ref[...], preferred_element_type=F32)
+        + jnp.dot(far, far_weight_ref[...], preferred_element_type=F32)
+    ).astype(BF16)
+    part = sum_ref.shape[0] // 4
+    for k, ref in enumerate(out_refs):
+        start = pl.multiple_of(((place_ref[1] >> 2) ^ k) * part, part)
+        ref[...] = sum_ref[pl.ds(start, part), :]
+
+
+def total_kernel(*refs):
+    total = refs[0][...].astype(F32)
+    for ref in refs[1:-1]:
+        total = total + ref[...].astype(F32)
+    refs[-1][...] = total.astype(BF16)
 
 
 def attended_kernel(parts_ref, out_ref):
     columns = parts_ref.shape[2]
-    for t in range(4):
-        total = parts_ref[t].astype(F32)
-        for i in range(t + 4, parts_ref.shape[0], 4):
-            total = total + parts_ref[i].astype(F32)
+    for t in range(parts_ref.shape[0]):
         start = (2 * (t & 1) + (t >> 1)) * columns
-        out_ref[:, start : start + columns] = total.astype(BF16)
+        out_ref[:, start : start + columns] = parts_ref[t]
 
 
 def columns_kernel(place_ref, own_ref, other_ref, out_ref, *, pairs):
@@ -194,7 +246,7 @@
 
 def attend_kernel(
     place_ref, merged_ref, embed_ref, norm_ref, qkv_ref, qgain_ref, kgain_ref, out_ref, own_ref,
-    kv_ref, q_ref, k_ref, v_ref, *, grp_size, block,
+    give_ref,    kv_ref, q_ref, k_ref, v_ref, *, grp_size, block,
 ):
     latents, width = embed_ref.shape
     head = q_ref.shape[1]
@@ -241,9 +293,18 @@
         mixed = jnp.dot(weights.astype(BF16), v_ref[...], preferred_element_type=F32)
         out_ref[here, :] = (mixed / denominator).astype(BF16)
     grp = place_ref[0]
-    for i in range(total // (block * grp_size)):
-        start = pl.multiple_of((i * grp_size + grp) * block, block)
+    side = place_ref[1] & 1
+    part = block * grp_size
+    slabs = total // (2 * part)
+    for i in range(2 * slabs):
+        start = pl.multiple_of(i * part + grp * block, block)
         own_ref[i * block : (i + 1) * block, :] = out_ref[pl.ds(start, block), :]
+    for i in range(slabs):
+        start = pl.multiple_of((2 * i + 1 - side) * part, part)
+        give_ref[i * part : (i + 1) * part, :] = out_ref[pl.ds(start, part), :]
+        start = pl.multiple_of((2 * i + side) * part + grp * block, block)
+        first = slabs * part + i * block
+        give_ref[first : first + block, :] = out_ref[pl.ds(start, block), :]
 
 
 def call(body, shapes, *args, name, scratch=(), places=(), flops=10**8, moved=10**6):
@@ -299,66 +360,61 @@
         first, earlier, taps, latent_rhs, late, labels, name="group_sums", flops=10**9,
     )
 
-    by_column = jnp.concatenate(
-        [cotangent[0, :, g * columns : (g + 1) * columns] for g in range(grp_size)] * 2, axis=0
-    ).reshape(2 * grp_size, block, columns)
-    by_column, _ = lax.optimization_barrier((by_column, earlier))
-    halves = seq_size // 2
-    apart = [
-        [g * seq_size + h * halves + r for h in range(2) for g in range(grp_size)]
-        for r in range(halves)
-    ]
-    near = lax.all_to_all(
-        by_column, ("grp", "seq"), 0, 0, axis_index_groups=apart, tiled=True
-    ).reshape(2 * shared, columns)
-    near_other = xor_swap(near, "seq", 4)
-
-    side = seq & 1
-    depth = (seq >> 1) & 1
-
-    def halves_of(matrix, choice):
-        size = matrix.shape[1] // 2
-        return [
-            lax.dynamic_slice_in_dim(matrix, c * size, size, 1) for c in (choice, 1 - choice)
-        ]
-
-    weight, _ = lax.optimization_barrier((out_weight, sums))
-    kept, given = halves_of(weight, side)
-    weight_other = xor_swap(given, "seq", 1)
+    by_column = call(
+        split_kernel, [(grp_size, block, columns)], cotangent[0], name="split_columns"
+    )
+    near = lax.all_to_all(by_column, "grp", 0, 0, tiled=True).reshape(shared, columns)
+    near, _ = lax.optimization_barrier((near, sums))
+    near_other = xor_swap(near, "seq", 8)
 
     parts = lax.all_to_all(sums.reshape(seq_size, shared, LANES), "seq", 0, 0, tiled=True)
     slab_sums = call(resplit_kernel, [(grp_size, shared, LANES)], parts, name="slab_sums")
-    near_other, weight_other, _ = lax.optimization_barrier((near_other, weight_other, slab_sums))
+    near_other, _ = lax.optimization_barrier((near_other, slab_sums))
     near = jnp.concatenate([near, near_other], axis=0)
-    near_other = xor_swap(near, "seq", 1)
+    near_other = xor_swap(near, "seq", 4)
     slab_parts = lax.all_to_all(slab_sums, "grp", 0, 0, tiled=True)
     merged = call(merge_kernel, [(seq_size, shared, LANES)], slab_parts, name="merged")
     near_other, _ = lax.optimization_barrier((near_other, merged))
     near = jnp.concatenate([near, near_other], axis=0)
     far = xor_swap(near, "seq", 2)
+    weight, _ = lax.optimization_barrier((out_weight, merged))
+    given = lax.dynamic_slice_in_dim(weight, (1 - (seq & 1)) * (width // 2), width // 2, 1)
+    weight_other = xor_swap(given, "seq", 1)
     merged = lax.all_to_all(merged, "seq", 0, 0, tiled=True).reshape(groups, LANES)
 
-    head_out, own_rows = call(
+    head_out, own_rows, given_rows = call(
         functools.partial(attend_kernel, grp_size=grp_size, block=block),
-        [(groups, head), (rows, head)], place, merged, embed_weight, norm_gain[None],
-        qkv_weight, q_gain[None], k_gain[None], name="attend", flops=8 * 10**9, places=["smem"],
+        [(groups, head), (rows, head), (groups // 2 + rows // 2, head)], place, merged,
+        embed_weight, norm_gain[None], qkv_weight, q_gain[None], k_gain[None], name="attend",
+        flops=8 * 10**9, places=["smem"],
         scratch=[pltpu.VMEM((width, 2 * head), BF16)] + [pltpu.VMEM((groups, head), BF16)] * 3,
     )
 
-    other_rows = xor_swap(own_rows, "seq", 1)
+    side_rows = xor_swap(given_rows, "seq", 1)
+    weight_other, _ = lax.optimization_barrier((weight_other, own_rows))
+    near_weight, given = call(
+        weights_kernel, [(2 * head, columns)] * 2, place, out_weight, weight_other,
+        name="weights", places=["smem"],
+    )
+    far_weight = xor_swap(given, "seq", 2)
     local_grad = call(
-        functools.partial(grad_kernel, masks=(4, 1, 2), part=shared), [(head, columns)], place,
-        head_out, near, far, name="local_grad", places=["smem"],
-        scratch=[pltpu.VMEM((groups, head), BF16)], flops=10**9,
-    )
+        functools.partial(grad_kernel, masks=(8, 4, 2), part=shared), [(2, head, columns)],
+        place, head_out, side_rows, near, far, name="local_grad", places=["smem"],
+        scratch=[pltpu.VMEM((groups // 2, 2 * head), BF16)], flops=10**9,
+    )
+    both_sides = [
+        [(2 * z + y) * dp_size + d for y in range(2) for d in range(dp_size)]
+        for z in range(seq_size // 2)
+    ]
     grad_parts = lax.all_to_all(
-        local_grad.reshape(dp_size, head // dp_size, columns), "dp", 0, 0, tiled=True
-    )
-    other_rows, weight_other, _ = lax.optimization_barrier((other_rows, weight_other, local_grad))
-    pair_heads = jnp.stack([own_rows, other_rows])
-    quad_heads = (pair_heads, xor_swap(pair_heads, "seq", 2))
-    kept, given = halves_of(jnp.concatenate([kept, weight_other], axis=0), depth)
-    weight_quad = jnp.concatenate([kept, xor_swap(given, "seq", 2)], axis=0)
+        local_grad.reshape(2 * dp_size, head // dp_size, columns), ("seq", "dp"), 0, 0,
+        axis_index_groups=both_sides, tiled=True,
+    )
+    pair_heads = call(
+        functools.partial(pair_kernel, part=shared), [(2, rows, head)], place, own_rows,
+        side_rows, name="pair_heads", places=["smem"],
+    )
+    far_heads = xor_swap(pair_heads, "seq", 2)
 
     pairs = dp_size // 2
     grad_block = call(
@@ -371,12 +427,17 @@
     grad_cols = lax.all_to_all(
         grad_block, ("grp", "dp"), 0, 0, axis_index_groups=same_core, tiled=True
     )
-    partial = call(
-        project_kernel, [(rows, columns)], *quad_heads, weight_quad, name="project", flops=10**9,
-    )
-    partial, _ = lax.optimization_barrier((partial, grad_cols))
+    partials = call(
+        project_kernel, [(rows // 4, columns)] * 4, place, pair_heads, far_heads, near_weight,
+        far_weight, name="project", flops=10**9, places=["smem"],
+        scratch=[pltpu.VMEM((rows, columns), BF16)],
+    )
+    partials = [partials[0]] + [xor_swap(partials[k], "seq", 4 * k) for k in range(1, 4)]
+    projected = call(total_kernel, [(rows // 4, columns)], *partials, name="projected")
+    projected, _ = lax.optimization_barrier((projected, grad_cols))
+    quads = [list(range(k, k + 4)) for k in range(0, seq_size, 4)]
     out_parts = lax.all_to_all(
-        partial.reshape(seq_size, block, columns), "seq", 0, 0, tiled=True
+        projected.reshape(4, block, columns), "seq", 0, 0, axis_index_groups=quads, tiled=True
     )
     out_grad = call(
         functools.partial(columns_kernel, pairs=pairs), [(head, width)], place, grad_cols,

time: 169 us -> 174 us (1.030)
  local copies, waits for them, and re-layouts: 18 us -> 6.21 us
  waiting for transfers between devices: 43.2 us -> 54.1 us
  starting transfers between devices: 75.3 us -> 81.6 us
    ppermute x8 -> x11, starting transfers between devices: 25.5 us -> 38.2 us  [xor_swap(): return lax.ppermute(block, axis, route)]
    all_to_all x3, starting transfers between devices: 27.2 us -> 16.9 us  [the longest x1 9.59 us: shards(): lax.all_to_all(local_grad.reshape(2 * dp_size, head // dp_size, columns),...]
    unnamed x35 -> x22, local copies, waits for them, and re-layouts: 14 us -> 4.48 us
    all_to_all x1, waiting for transfers between devices: 0.01 us -> 8.05 us  [shards(): lax.all_to_all(grad_block, ('grp', 'dp'), 0, 0, axis_index_groups=same_co...]
    all_to_all x1, waiting for transfers between devices: 0.63 us -> 8.13 us  [shards(): lax.all_to_all(sums.reshape(seq_size, shared, LANES), 'seq', 0, 0, tiled=...]
    ppermute x8 -> x11, waiting for transfers between devices: 28.7 us -> 22.8 us  [xor_swap(): return lax.ppermute(block, axis, route)]
    all_to_all x3, waiting for transfers between devices: 9.89 us -> 15.1 us  [the longest x1 11.3 us: shards(): lax.all_to_all(local_grad.reshape(2 * dp_size, head // dp_size, columns),...]
    all_to_all x1, starting transfers between devices: 6.12 us -> 11.1 us  [shards(): lax.all_to_all(sums.reshape(seq_size, shared, LANES), 'seq', 0, 0, tiled=...]
  transfers between devices with their start and end apart: 15 -> 18, of which waited for: 12 -> 8; matrix products, arithmetic and copies ran while one was open for 8% -> 1% of each run, Pallas kernels for 10% -> 10%
where the time goes in v5:
time: 174 us; the launch traced here: 172 us
  starting transfers between devices  81.6 us (47%)
  waiting for transfers between devices  54.1 us (31%)
  Pallas kernels  22 us (13%)
  blocking collectives  7.11 us (4%)
  local copies, waits for them, and re-layouts  6.21 us (4%)
    ppermute x11, starting transfers between devices, xor_swap(): return lax.ppermute(block, axis, route)  38.2 us
    ppermute x11, waiting for transfers between devices, xor_swap(): return lax.ppermute(block, axis, route)  22.8 us
    pallas_call x14, Pallas kernels, call(): pl.pallas_call(body, out_shape=outs, in_specs=in_specs, out_specs=(whole,...  22 us
    all_to_all x1, waiting for transfers between devices, shards(): lax.all_to_all(local_grad.reshape(2 * dp_size, head // dp_size, columns),...  11.3 us
    all_to_all x1, starting transfers between devices, shards(): lax.all_to_all(sums.reshape(seq_size, shared, LANES), 'seq', 0, 0, tiled=...  11.1 us
    all_to_all x1, starting transfers between devices, shards(): lax.all_to_all(local_grad.reshape(2 * dp_size, head // dp_size, columns),...  9.59 us
    all_to_all x1, waiting for transfers between devices, shards(): lax.all_to_all(sums.reshape(seq_size, shared, LANES), 'seq', 0, 0, tiled=...  8.13 us
    all_to_all x1, waiting for transfers between devices, shards(): lax.all_to_all(grad_block, ('grp', 'dp'), 0, 0, axis_index_groups=same_co...  8.05 us
  transfers between devices with their start and end apart: 18, of which 8 were waited for; matrix products, arithmetic and copies ran while one was open for 1% of the time, Pallas kernels for 10%

profile of v5, /device:TPU:1, one launch (start us, length us, event | category | flops | bytes accessed | tf_op | source)
XLA Modules:
  0.0 172.0 jit_solution(2393419621342403243)
XLA Ops:
  0.6 0.9 slice_bitcast_fusion
  1.5 4.0 %collective-permute-start = (bf16[2,64,512]{2,1,0:T(8,128)(2,1)S(1)}, bf16[2,64,512]{2,1,0:T(8,128)(2,1)S(1)}, u32[]{:S(2)}, u32[]{:S(2)}) collective-permute-start(bf16[2,64,512]{2,1,0:T(8,128)(2,1)S(1)} %slice_bitcast_fusion), channel_id=1, source_target_pairs={{0,8},{8,16},{16,24},{24,32},{32,40},{40,48},{48,56},{56,64},{64,7... | collective-permute-start | bytes 393224 | tf_op jit(solution)/shard_map/ppermute | solution.py:22
  5.6 0.8 reshape_squeeze.3.labels_ref
  6.4 1.0 copy-done.1
  7.4 0.9 copy-done.4
  8.3 0.8 copy-done.6
  9.1 1.4 late_frames.1
  10.6 1.6 group_sums.1
  12.2 11.1 %all-to-all-start = ((bf16[16,64,128]{2,1,0:T(8,128)(2,1)}), bf16[16,64,128]{2,1,0:T(8,128)(2,1)S(1)}, u32[]{:S(2)}, u32[]{:S(2)}) async-start(bf16[16,64,128]{2,1,0:T(8,128)(2,1)} %bitcast.6), calls=%async_computation | async-start | bytes 524288 | tf_op jit(solution)/shard_map/all_to_all | solution.py:370
  23.3 0.6 split_columns.1
  23.9 8.1 %all-to-all-done.parts_ref = bf16[16,64,128]{2,1,0:T(8,128)(2,1)S(1)} async-done(((bf16[16,64,128]{2,1,0:T(8,128)(2,1)}), bf16[16,64,128]{2,1,0:T(8,128)(2,1)S(1)}, u32[]{:S(2)}, u32[]{:S(2)}) %all-to-all-start) | async-done | bytes 262176 | tf_op jit(solution)/shard_map/all_to_all | solution.py:370
  32.0 4.0 %all-to-all-start.3 = ((bf16[4,16,768]{2,1,0:T(8,128)(2,1)}), bf16[4,16,768]{2,1,0:T(8,128)(2,1)S(1)}, u32[]{:S(2)}, u32[]{:S(2)}) async-start(bf16[4,16,768]{2,1,0:T(8,128)(2,1)} %split_columns.1), calls=%async_computation.3 | async-start | bytes 196608 | tf_op jit(solution)/shard_map/all_to_all | solution.py:366
  36.0 0.8 slab_sums.1
  36.9 3.8 %all-to-all-done.3 = bf16[4,16,768]{2,1,0:T(8,128)(2,1)S(1)} async-done(((bf16[4,16,768]{2,1,0:T(8,128)(2,1)}), bf16[4,16,768]{2,1,0:T(8,128)(2,1)S(1)}, u32[]{:S(2)}, u32[]{:S(2)}) %all-to-all-start.3) | async-done | bytes 98336 | tf_op jit(solution)/shard_map/all_to_all | solution.py:366
  40.7 3.3 %all-to-all-start.1 = ((bf16[4,64,128]{2,1,0:T(8,128)(2,1)}), bf16[4,64,128]{2,1,0:T(8,128)(2,1)S(1)}, u32[]{:S(2)}, u32[]{:S(2)}) async-start(bf16[4,64,128]{2,1,0:T(8,128)(2,1)} %slab_sums.1), calls=%async_computation.1 | async-start | bytes 131072 | tf_op jit(solution)/shard_map/all_to_all | solution.py:375
  44.0 5.3 %collective-permute-start.8 = (bf16[64,768]{1,0:T(8,128)(2,1)S(1)}, bf16[64,768]{1,0:T(8,128)(2,1)S(1)}, u32[]{:S(2)}, u32[]{:S(2)}) collective-permute-start(bf16[64,768]{1,0:T(8,128)(2,1)S(1)} %bitcast.25), channel_id=1, source_target_pairs={{0,64},{8,72},{16,80},{24,88},{32,96},{40,104},{48,112},{56,120},{... | collective-permute-start | bytes 294920 | tf_op jit(solution)/shard_map/ppermute | solution.py:27
  49.3 0.9 merged.1
  50.2 6.5 %all-to-all-start.2 = ((bf16[16,64,128]{2,1,0:T(8,128)(2,1)}), bf16[16,64,128]{2,1,0:T(8,128)(2,1)S(1)}, u32[]{:S(2)}, u32[]{:S(2)}) async-start(bf16[16,64,128]{2,1,0:T(8,128)(2,1)} %merged.1), calls=%async_computation.2 | async-start | bytes 524288 | tf_op jit(solution)/shard_map/all_to_all | solution.py:383
  56.8 0.1 pad_add_fusion.place_ref
  56.9 4.2 %collective-permute-start.9 = (bf16[128,768]{1,0:T(8,128)(2,1)S(1)}, bf16[128,768]{1,0:T(8,128)(2,1)S(1)}, u32[]{:S(2)}, u32[]{:S(2)}) collective-permute-start(bf16[128,768]{1,0:T(8,128)(2,1)S(1)} %pad_maximum_fusion), channel_id=1, source_target_pairs={{0,32},{8,40},{16,48},{24,56},{32,0},{40,8},{48,16},{56,24},{64,96... | collective-permute-start | bytes 589832 | tf_op jit(solution)/shard_map/ppermute | solution.py:27
  61.1 13.1 %collective-permute-done.9 = bf16[128,768]{1,0:T(8,128)(2,1)S(1)} collective-permute-done((bf16[128,768]{1,0:T(8,128)(2,1)S(1)}, bf16[128,768]{1,0:T(8,128)(2,1)S(1)}, u32[]{:S(2)}, u32[]{:S(2)}) %collective-permute-start.9) | collective-permute-done | bytes 196640 | tf_op jit(solution)/shard_map/ppermute | solution.py:27
  74.2 1.9 %collective-permute-start.10 = (bf16[256,768]{1,0:T(8,128)(2,1)S(1)}, bf16[256,768]{1,0:T(8,128)(2,1)S(1)}, u32[]{:S(2)}, u32[]{:S(2)}) collective-permute-start(bf16[256,768]{1,0:T(8,128)(2,1)S(1)} %constant_dynamic-update-slice_fusion.first_ref), channel_id=1, source_target_pairs={{0,16},{8,24},{16,0},{24,8},{32,48},{40,56},{48,32},{56,40},{64,80... | collective-permute-start | bytes 1179656 | tf_op jit(solution)/shard_map/ppermute | solution.py:27
  76.2 1.7 copy-done.2
  77.8 9.8 %attend.1 = (bf16[1024,128]{1,0:T(8,128)(2,1)S(1)}, bf16[256,128]{1,0:T(8,128)(2,1)S(1)}, bf16[640,128]{1,0:T(8,128)(2,1)S(1)}) custom-call(s32[3]{0:T(128)S(1)} %pad_add_fusion.place_ref, bf16[1024,128]{1,0:T(8,128)(2,1)S(1)} %bitcast.18, bf16[64,3072]{1,0:T(8,128)(2,1)S(1)} %copy-done.3, f32[1,3072]{1,0:T(1,128)S(1)} %bitcast.22, ...), custom_call_target="tpu_custom_call" | custom-call | flops 8000000000 | bytes 1000000 | tf_op jit(solution)/shard_map/attend/pallas_call | solution.py:317
  87.6 2.8 %collective-permute-start.1 = (bf16[640,128]{1,0:T(8,128)(2,1)S(1)}, bf16[640,128]{1,0:T(8,128)(2,1)S(1)}, u32[]{:S(2)}, u32[]{:S(2)}) collective-permute-start(bf16[640,128]{1,0:T(8,128)(2,1)S(1)} %get-tuple-element.26), channel_id=1, source_target_pairs={{0,8},{8,0},{16,24},{24,16},{32,40},{40,32},{48,56},{56,48},{64,72... | collective-permute-start | bytes 491528 | tf_op jit(solution)/shard_map/ppermute | solution.py:27
  90.4 3.4 %collective-permute-done.1.given_ref = bf16[640,128]{1,0:T(8,128)(2,1)S(1)} collective-permute-done((bf16[640,128]{1,0:T(8,128)(2,1)S(1)}, bf16[640,128]{1,0:T(8,128)(2,1)S(1)}, u32[]{:S(2)}, u32[]{:S(2)}) %collective-permute-start.1) | collective-permute-done | bytes 163872 | tf_op jit(solution)/shard_map/ppermute | solution.py:27
  93.8 1.7 local_grad.1
  95.5 9.6 %all-to-all-start.4 = ((bf16[16,16,768]{2,1,0:T(8,128)(2,1)}), bf16[16,16,768]{2,1,0:T(8,128)(2,1)S(1)}, u32[]{:S(2)}, u32[]{:S(2)}) async-start(bf16[16,16,768]{2,1,0:T(8,128)(2,1)} %bitcast.13), calls=%async_computation.4 | async-start | bytes 786432 | tf_op jit(solution)/shard_map/all_to_all | solution.py:409
  105.2 3.3 %collective-permute-start.3 = (bf16[128,1536]{1,0:T(8,128)(2,1)S(1)}, bf16[128,1536]{1,0:T(8,128)(2,1)S(1)}, u32[]{:S(2)}, u32[]{:S(2)}) collective-permute-start(bf16[128,1536]{1,0:T(8,128)(2,1)S(1)} %constant_dynamic-slice_fusion), channel_id=1, source_target_pairs={{0,8},{8,0},{16,24},{24,16},{32,40},{40,32},{48,56},{56,48},{64,72... | collective-permute-start | bytes 1179656 | tf_op jit(solution)/shard_map/ppermute | solution.py:27
  108.5 11.3 %all-to-all-done.4.parts_ref = bf16[16,16,768]{2,1,0:T(8,128)(2,1)S(1)} async-done(((bf16[16,16,768]{2,1,0:T(8,128)(2,1)}), bf16[16,16,768]{2,1,0:T(8,128)(2,1)S(1)}, u32[]{:S(2)}, u32[]{:S(2)}) %all-to-all-start.4) | async-done | bytes 393248 | tf_op jit(solution)/shard_map/all_to_all | solution.py:409
  119.8 0.8 grad_block.1
  120.6 4.8 %all-to-all-start.5 = ((bf16[16,16,768]{2,1,0:T(8,128)(2,1)}), bf16[16,16,768]{2,1,0:T(8,128)(2,1)S(1)}, u32[]{:S(2)}, u32[]{:S(2)}) async-start(bf16[16,16,768]{2,1,0:T(8,128)(2,1)} %grad_block.1), calls=%async_computation.5 | async-start | bytes 786432 | tf_op jit(solution)/shard_map/all_to_all | solution.py:427
  125.4 0.6 weights.1
  126.0 3.6 %collective-permute-start.4 = (bf16[256,768]{1,0:T(8,128)(2,1)S(1)}, bf16[256,768]{1,0:T(8,128)(2,1)S(1)}, u32[]{:S(2)}, u32[]{:S(2)}) collective-permute-start(bf16[256,768]{1,0:T(8,128)(2,1)S(1)} %get-tuple-element.30), channel_id=1, source_target_pairs={{0,16},{8,24},{16,0},{24,8},{32,48},{40,56},{48,32},{56,40},{64,80... | collective-permute-start | bytes 1179656 | tf_op jit(solution)/shard_map/ppermute | solution.py:27
  129.7 0.6 pair_heads.1.near_ref
  130.2 1.9 %collective-permute-start.2 = (bf16[2,256,128]{2,1,0:T(8,128)(2,1)S(1)}, bf16[2,256,128]{2,1,0:T(8,128)(2,1)S(1)}, u32[]{:S(2)}, u32[]{:S(2)}) collective-permute-start(bf16[2,256,128]{2,1,0:T(8,128)(2,1)S(1)} %pair_heads.1.near_ref), channel_id=1, source_target_pairs={{0,16},{8,24},{16,0},{24,8},{32,48},{40,56},{48,32},{56,40},{64,80... | collective-permute-start | bytes 393224 | tf_op jit(solution)/shard_map/ppermute | solution.py:27
  132.2 8.1 %all-to-all-done.5.own_ref = bf16[16,16,768]{2,1,0:T(8,128)(2,1)S(1)} async-done(((bf16[16,16,768]{2,1,0:T(8,128)(2,1)}), bf16[16,16,768]{2,1,0:T(8,128)(2,1)S(1)}, u32[]{:S(2)}, u32[]{:S(2)}) %all-to-all-start.5) | async-done | bytes 393248 | tf_op jit(solution)/shard_map/all_to_all | solution.py:427
  140.2 3.7 %collective-permute-start.11 = (bf16[16,16,768]{2,1,0:T(8,128)(2,1)S(1)}, bf16[16,16,768]{2,1,0:T(8,128)(2,1)S(1)}, u32[]{:S(2)}, u32[]{:S(2)}) collective-permute-start(bf16[16,16,768]{2,1,0:T(8,128)(2,1)S(1)} %all-to-all-done.5.own_ref), channel_id=1, source_target_pairs={{0,1},{1,0},{2,3},{3,2},{4,5},{5,4},{6,7},{7,6},{8,9},{9,8},{10,11... | collective-permute-start | bytes 1179656 | tf_op jit(solution)/shard_map/ppermute | solution.py:27
  143.9 0.9 project.1
  144.9 4.1 %collective-permute-start.5 = (bf16[64,768]{1,0:T(8,128)(2,1)S(1)}, bf16[64,768]{1,0:T(8,128)(2,1)S(1)}, u32[]{:S(2)}, u32[]{:S(2)}) collective-permute-start(bf16[64,768]{1,0:T(8,128)(2,1)S(1)} %get-tuple-element.32), channel_id=1, source_target_pairs={{0,32},{8,40},{16,48},{24,56},{32,0},{40,8},{48,16},{56,24},{64,96... | collective-permute-start | bytes 294920 | tf_op jit(solution)/shard_map/ppermute | solution.py:27
  149.0 5.4 %collective-permute-start.6 = (bf16[64,768]{1,0:T(8,128)(2,1)S(1)}, bf16[64,768]{1,0:T(8,128)(2,1)S(1)}, u32[]{:S(2)}, u32[]{:S(2)}) collective-permute-start(bf16[64,768]{1,0:T(8,128)(2,1)S(1)} %get-tuple-element.33), channel_id=1, source_target_pairs={{0,64},{8,72},{16,80},{24,88},{32,96},{40,104},{48,112},{56,120},{... | collective-permute-start | bytes 294920 | tf_op jit(solution)/shard_map/ppermute | solution.py:27
  154.5 1.9 %collective-permute-start.7 = (bf16[64,768]{1,0:T(8,128)(2,1)S(1)}, bf16[64,768]{1,0:T(8,128)(2,1)S(1)}, u32[]{:S(2)}, u32[]{:S(2)}) collective-permute-start(bf16[64,768]{1,0:T(8,128)(2,1)S(1)} %get-tuple-element.34), channel_id=1, source_target_pairs={{0,96},{8,104},{16,112},{24,120},{32,64},{40,72},{48,80},{56,88},{... | collective-permute-start | bytes 294920 | tf_op jit(solution)/shard_map/ppermute | solution.py:27
  156.4 2.5 %collective-permute-done.6.refs_2_ = bf16[64,768]{1,0:T(8,128)(2,1)S(1)} collective-permute-done((bf16[64,768]{1,0:T(8,128)(2,1)S(1)}, bf16[64,768]{1,0:T(8,128)(2,1)S(1)}, u32[]{:S(2)}, u32[]{:S(2)}) %collective-permute-start.6) | collective-permute-done | bytes 98336 | tf_op jit(solution)/shard_map/ppermute | solution.py:27
  158.9 3.8 %collective-permute-done.7.refs_3_ = bf16[64,768]{1,0:T(8,128)(2,1)S(1)} collective-permute-done((bf16[64,768]{1,0:T(8,128)(2,1)S(1)}, bf16[64,768]{1,0:T(8,128)(2,1)S(1)}, u32[]{:S(2)}, u32[]{:S(2)}) %collective-permute-start.7) | collective-permute-done | bytes 98336 | tf_op jit(solution)/shard_map/ppermute | solution.py:27
  162.7 0.1 projected.1
  162.8 7.1 %all_to_all.35.parts_ref = bf16[4,16,768]{2,1,0:T(8,128)(2,1)S(1)} all-to-all(bf16[4,16,768]{2,1,0:T(8,128)(2,1)S(1)} %bitcast.17), channel_id=1, replica_groups={{0,8,16,24},{32,40,48,56},{64,72,80,88},{96,104,112,120},{1,9,17,25},{3..., dimensions={0} | all-to-all | bytes 196608 | tf_op jit(solution)/shard_map/all_to_all | solution.py:439
  169.9 0.6 attended.1
  170.5 1.5 grad_columns.1
  (31 shorter events, 0.1 us)
Async XLA Ops:
  1.5 9.0 %collective-permute-start = (bf16[2,64,512]{2,1,0:T(8,128)(2,1)S(1)}, bf16[2,64,512]{2,1,0:T(8,128)(2,1)S(1)}, u32[]{:S(2)}, u32[]{:S(2)}) collective-permute-start(bf16[2,64,512]{2,1,0:T(8,128)(2,1)S(1)} %slice_bitcast_fusion), channel_id=1, source_target_pairs={{0,8},{8,16},{16,24},{24,32},{32,40},{40,48},{48,56},{56,64},{64,7... | collective-permute-start | bytes 393224 | tf_op jit(solution)/shard_map/ppermute | solution.py:22
  6.4 1.0 copy-start.1
  7.4 0.9 copy-start.4
  8.3 0.8 copy-start.6
  10.5 12.7 %copy-start.5 = (bf16[1,16,3072]{2,1,0:T(8,128)(2,1)S(1)}, bf16[1,16,3072]{2,1,0:T(8,128)(2,1)}, u32[]{:S(2)}) copy-start(bf16[1,16,3072]{2,1,0:T(8,128)(2,1)} %param.21) | copy-start | bytes 294916
  12.2 64.0 %copy-start.3 = (bf16[64,3072]{1,0:T(8,128)(2,1)S(1)}, bf16[64,3072]{1,0:T(8,128)(2,1)}, u32[]{:S(2)}) copy-start(bf16[64,3072]{1,0:T(8,128)(2,1)} %embed_ref.1) | copy-start | bytes 1179652
  12.2 64.0 %copy-start.7 = (f32[3072]{0:T(1024)S(1)}, f32[3072]{0:T(1024)}, u32[]{:S(2)}) copy-start(f32[3072]{0:T(1024)} %param.16) | copy-start | bytes 36868
  12.2 64.0 %copy-start.8 = (f32[128]{0:T(128)S(1)}, f32[128]{0:T(128)}, u32[]{:S(2)}) copy-start(f32[128]{0:T(128)} %param.18) | copy-start | bytes 1540
  12.2 64.0 %copy-start.9 = (f32[128]{0:T(128)S(1)}, f32[128]{0:T(128)}, u32[]{:S(2)}) copy-start(f32[128]{0:T(128)} %param.19) | copy-start | bytes 1540
  12.2 19.9 %all-to-all-start = ((bf16[16,64,128]{2,1,0:T(8,128)(2,1)}), bf16[16,64,128]{2,1,0:T(8,128)(2,1)S(1)}, u32[]{:S(2)}, u32[]{:S(2)}) async-start(bf16[16,64,128]{2,1,0:T(8,128)(2,1)} %bitcast.6), calls=%async_computation | async-start | bytes 524288 | tf_op jit(solution)/shard_map/all_to_all | solution.py:370
  32.0 8.7 %all-to-all-start.3 = ((bf16[4,16,768]{2,1,0:T(8,128)(2,1)}), bf16[4,16,768]{2,1,0:T(8,128)(2,1)S(1)}, u32[]{:S(2)}, u32[]{:S(2)}) async-start(bf16[4,16,768]{2,1,0:T(8,128)(2,1)} %split_columns.1), calls=%async_computation.3 | async-start | bytes 196608 | tf_op jit(solution)/shard_map/all_to_all | solution.py:366
  40.7 8.6 %all-to-all-start.1 = ((bf16[4,64,128]{2,1,0:T(8,128)(2,1)}), bf16[4,64,128]{2,1,0:T(8,128)(2,1)S(1)}, u32[]{:S(2)}, u32[]{:S(2)}) async-start(bf16[4,64,128]{2,1,0:T(8,128)(2,1)} %slab_sums.1), calls=%async_computation.1 | async-start | bytes 131072 | tf_op jit(solution)/shard_map/all_to_all | solution.py:375
  44.0 12.9 %collective-permute-start.8 = (bf16[64,768]{1,0:T(8,128)(2,1)S(1)}, bf16[64,768]{1,0:T(8,128)(2,1)S(1)}, u32[]{:S(2)}, u32[]{:S(2)}) collective-permute-start(bf16[64,768]{1,0:T(8,128)(2,1)S(1)} %bitcast.25), channel_id=1, source_target_pairs={{0,64},{8,72},{16,80},{24,88},{32,96},{40,104},{48,112},{56,120},{... | collective-permute-start | bytes 294920 | tf_op jit(solution)/shard_map/ppermute | solution.py:27
  50.2 25.9 %all-to-all-start.2 = ((bf16[16,64,128]{2,1,0:T(8,128)(2,1)}), bf16[16,64,128]{2,1,0:T(8,128)(2,1)S(1)}, u32[]{:S(2)}, u32[]{:S(2)}) async-start(bf16[16,64,128]{2,1,0:T(8,128)(2,1)} %merged.1), calls=%async_computation.2 | async-start | bytes 524288 | tf_op jit(solution)/shard_map/all_to_all | solution.py:383
  56.9 17.3 %collective-permute-start.9 = (bf16[128,768]{1,0:T(8,128)(2,1)S(1)}, bf16[128,768]{1,0:T(8,128)(2,1)S(1)}, u32[]{:S(2)}, u32[]{:S(2)}) collective-permute-start(bf16[128,768]{1,0:T(8,128)(2,1)S(1)} %pad_maximum_fusion), channel_id=1, source_target_pairs={{0,32},{8,40},{16,48},{24,56},{32,0},{40,8},{48,16},{56,24},{64,96... | collective-permute-start | bytes 589832 | tf_op jit(solution)/shard_map/ppermute | solution.py:27
  74.2 16.2 %collective-permute-start.10 = (bf16[256,768]{1,0:T(8,128)(2,1)S(1)}, bf16[256,768]{1,0:T(8,128)(2,1)S(1)}, u32[]{:S(2)}, u32[]{:S(2)}) collective-permute-start(bf16[256,768]{1,0:T(8,128)(2,1)S(1)} %constant_dynamic-update-slice_fusion.first_ref), channel_id=1, source_target_pairs={{0,16},{8,24},{16,0},{24,8},{32,48},{40,56},{48,32},{56,40},{64,80... | collective-permute-start | bytes 1179656 | tf_op jit(solution)/shard_map/ppermute | solution.py:27
  76.1 1.7 copy-start.2
  87.6 17.5 %copy-start = (bf16[128,3072]{1,0:T(8,128)(2,1)S(1)}, bf16[128,3072]{1,0:T(8,128)(2,1)}, u32[]{:S(2)}) copy-start(bf16[128,3072]{1,0:T(8,128)(2,1)} %weight_ref.1) | copy-start | bytes 2359300
  87.6 6.2 %collective-permute-start.1 = (bf16[640,128]{1,0:T(8,128)(2,1)S(1)}, bf16[640,128]{1,0:T(8,128)(2,1)S(1)}, u32[]{:S(2)}, u32[]{:S(2)}) collective-permute-start(bf16[640,128]{1,0:T(8,128)(2,1)S(1)} %get-tuple-element.26), channel_id=1, source_target_pairs={{0,8},{8,0},{16,24},{24,16},{32,40},{40,32},{48,56},{56,48},{64,72... | collective-permute-start | bytes 491528 | tf_op jit(solution)/shard_map/ppermute | solution.py:27
  95.5 24.2 %all-to-all-start.4 = ((bf16[16,16,768]{2,1,0:T(8,128)(2,1)}), bf16[16,16,768]{2,1,0:T(8,128)(2,1)S(1)}, u32[]{:S(2)}, u32[]{:S(2)}) async-start(bf16[16,16,768]{2,1,0:T(8,128)(2,1)} %bitcast.13), calls=%async_computation.4 | async-start | bytes 786432 | tf_op jit(solution)/shard_map/all_to_all | solution.py:409
  105.2 20.2 %collective-permute-start.3 = (bf16[128,1536]{1,0:T(8,128)(2,1)S(1)}, bf16[128,1536]{1,0:T(8,128)(2,1)S(1)}, u32[]{:S(2)}, u32[]{:S(2)}) collective-permute-start(bf16[128,1536]{1,0:T(8,128)(2,1)S(1)} %constant_dynamic-slice_fusion), channel_id=1, source_target_pairs={{0,8},{8,0},{16,24},{24,16},{32,40},{40,32},{48,56},{56,48},{64,72... | collective-permute-start | bytes 1179656 | tf_op jit(solution)/shard_map/ppermute | solution.py:27
  120.6 19.7 %all-to-all-start.5 = ((bf16[16,16,768]{2,1,0:T(8,128)(2,1)}), bf16[16,16,768]{2,1,0:T(8,128)(2,1)S(1)}, u32[]{:S(2)}, u32[]{:S(2)}) async-start(bf16[16,16,768]{2,1,0:T(8,128)(2,1)} %grad_block.1), calls=%async_computation.5 | async-start | bytes 786432 | tf_op jit(solution)/shard_map/all_to_all | solution.py:427
  126.0 17.9 %collective-permute-start.4 = (bf16[256,768]{1,0:T(8,128)(2,1)S(1)}, bf16[256,768]{1,0:T(8,128)(2,1)S(1)}, u32[]{:S(2)}, u32[]{:S(2)}) collective-permute-start(bf16[256,768]{1,0:T(8,128)(2,1)S(1)} %get-tuple-element.30), channel_id=1, source_target_pairs={{0,16},{8,24},{16,0},{24,8},{32,48},{40,56},{48,32},{56,40},{64,80... | collective-permute-start | bytes 1179656 | tf_op jit(solution)/shard_map/ppermute | solution.py:27
  130.2 13.7 %collective-permute-start.2 = (bf16[2,256,128]{2,1,0:T(8,128)(2,1)S(1)}, bf16[2,256,128]{2,1,0:T(8,128)(2,1)S(1)}, u32[]{:S(2)}, u32[]{:S(2)}) collective-permute-start(bf16[2,256,128]{2,1,0:T(8,128)(2,1)S(1)} %pair_heads.1.near_ref), channel_id=1, source_target_pairs={{0,16},{8,24},{16,0},{24,8},{32,48},{40,56},{48,32},{56,40},{64,80... | collective-permute-start | bytes 393224 | tf_op jit(solution)/shard_map/ppermute | solution.py:27
  140.2 30.3 %collective-permute-start.11 = (bf16[16,16,768]{2,1,0:T(8,128)(2,1)S(1)}, bf16[16,16,768]{2,1,0:T(8,128)(2,1)S(1)}, u32[]{:S(2)}, u32[]{:S(2)}) collective-permute-start(bf16[16,16,768]{2,1,0:T(8,128)(2,1)S(1)} %all-to-all-done.5.own_ref), channel_id=1, source_target_pairs={{0,1},{1,0},{2,3},{3,2},{4,5},{5,4},{6,7},{7,6},{8,9},{9,8},{10,11... | collective-permute-start | bytes 1179656 | tf_op jit(solution)/shard_map/ppermute | solution.py:27
  144.9 11.5 %collective-permute-start.5 = (bf16[64,768]{1,0:T(8,128)(2,1)S(1)}, bf16[64,768]{1,0:T(8,128)(2,1)S(1)}, u32[]{:S(2)}, u32[]{:S(2)}) collective-permute-start(bf16[64,768]{1,0:T(8,128)(2,1)S(1)} %get-tuple-element.32), channel_id=1, source_target_pairs={{0,32},{8,40},{16,48},{24,56},{32,0},{40,8},{48,16},{56,24},{64,96... | collective-permute-start | bytes 294920 | tf_op jit(solution)/shard_map/ppermute | solution.py:27
  149.0 9.9 %collective-permute-start.6 = (bf16[64,768]{1,0:T(8,128)(2,1)S(1)}, bf16[64,768]{1,0:T(8,128)(2,1)S(1)}, u32[]{:S(2)}, u32[]{:S(2)}) collective-permute-start(bf16[64,768]{1,0:T(8,128)(2,1)S(1)} %get-tuple-element.33), channel_id=1, source_target_pairs={{0,64},{8,72},{16,80},{24,88},{32,96},{40,104},{48,112},{56,120},{... | collective-permute-start | bytes 294920 | tf_op jit(solution)/shard_map/ppermute | solution.py:27
  154.5 8.3 %collective-permute-start.7 = (bf16[64,768]{1,0:T(8,128)(2,1)S(1)}, bf16[64,768]{1,0:T(8,128)(2,1)S(1)}, u32[]{:S(2)}, u32[]{:S(2)}) collective-permute-start(bf16[64,768]{1,0:T(8,128)(2,1)S(1)} %get-tuple-element.34), channel_id=1, source_target_pairs={{0,96},{8,104},{16,112},{24,120},{32,64},{40,72},{48,80},{56,88},{... | collective-permute-start | bytes 294920 | tf_op jit(solution)/shard_map/ppermute | solution.py:27

commit v6 on v5

--- a/solution.py
+++ b/solution.py
@@ -96,7 +96,9 @@
         windows.append([padded[2 - k : 4 - k].reshape(-1, channels) for k in range(3)])
     first = latent_rows(windows, conv_ref, latent_ref)
     rows = jnp.concatenate([first, late_ref[...]], axis=0)
-    labels = labels_ref[...]
+    labels = jnp.concatenate(
+        [labels_ref[i : i + 1, :] for i in range(labels_ref.shape[0])], axis=1
+    )
     total = out_ref.shape[0]
     block = total // (grp * seq)
     step = 256
@@ -347,7 +349,6 @@
     frame_count, tokens = frames.shape[:2]
     earlier = shifted_frames(frames[frame_count - 2 :], "seq", 1)
     latent_t = latent_weight.T
-    labels = assign[0].reshape(1, -1)
     late, first, taps, latent_rhs = call(
         late_kernel,
         [((frame_count - 2) * tokens, LANES), (2,) + frames.shape[1:], conv_weight.shape,
@@ -355,26 +356,25 @@
         frames, conv_weight, latent_t, name="late_frames", flops=10**9, places=["hbm"] * 3,
         scratch=[pltpu.VMEM(frames.shape, BF16), pltpu.SemaphoreType.DMA((4,))],
     )
+    by_column = call(
+        split_kernel, [(grp_size, block, columns)], cotangent[0], name="split_columns"
+    )
+    near = lax.all_to_all(by_column, "grp", 0, 0, tiled=True).reshape(shared, columns)
+    late, near = lax.optimization_barrier((late, near))
     sums = call(
         functools.partial(sums_kernel, grp=grp_size, seq=seq_size), [(groups, LANES)],
-        first, earlier, taps, latent_rhs, late, labels, name="group_sums", flops=10**9,
-    )
-
-    by_column = call(
-        split_kernel, [(grp_size, block, columns)], cotangent[0], name="split_columns"
-    )
-    near = lax.all_to_all(by_column, "grp", 0, 0, tiled=True).reshape(shared, columns)
-    near, _ = lax.optimization_barrier((near, sums))
+        first, earlier, taps, latent_rhs, late, assign[0], name="group_sums", flops=10**9,
+    )
     near_other = xor_swap(near, "seq", 8)
 
     parts = lax.all_to_all(sums.reshape(seq_size, shared, LANES), "seq", 0, 0, tiled=True)
     slab_sums = call(resplit_kernel, [(grp_size, shared, LANES)], parts, name="slab_sums")
-    near_other, _ = lax.optimization_barrier((near_other, slab_sums))
     near = jnp.concatenate([near, near_other], axis=0)
+    near, slab_sums = lax.optimization_barrier((near, slab_sums))
     near_other = xor_swap(near, "seq", 4)
     slab_parts = lax.all_to_all(slab_sums, "grp", 0, 0, tiled=True)
     merged = call(merge_kernel, [(seq_size, shared, LANES)], slab_parts, name="merged")
-    near_other, _ = lax.optimization_barrier((near_other, merged))
+    near_other, merged = lax.optimization_barrier((near_other, merged))
     near = jnp.concatenate([near, near_other], axis=0)
     far = xor_swap(near, "seq", 2)
     weight, _ = lax.optimization_barrier((out_weight, merged))
@@ -390,8 +390,8 @@
         scratch=[pltpu.VMEM((width, 2 * head), BF16)] + [pltpu.VMEM((groups, head), BF16)] * 3,
     )
 
+    given_rows, weight_other = lax.optimization_barrier((given_rows, weight_other))
     side_rows = xor_swap(given_rows, "seq", 1)
-    weight_other, _ = lax.optimization_barrier((weight_other, own_rows))
     near_weight, given = call(
         weights_kernel, [(2 * head, columns)] * 2, place, out_weight, weight_other,
         name="weights", places=["smem"],
@@ -416,21 +416,22 @@
     )
     far_heads = xor_swap(pair_heads, "seq", 2)
 
+    partials = call(
+        project_kernel, [(rows // 4, columns)] * 4, place, pair_heads, far_heads, near_weight,
+        far_weight, name="project", flops=10**9, places=["smem"],
+        scratch=[pltpu.VMEM((rows, columns), BF16)],
+    )
     pairs = dp_size // 2
     grad_block = call(
         spread_kernel, [(grp_size * pairs, head // dp_size, columns)], grad_parts,
         name="grad_block",
     )
+    grad_block, *partials = lax.optimization_barrier((grad_block, *partials))
     same_core = [
         [g * dp_size + 2 * p + c for g in range(grp_size) for p in range(pairs)] for c in range(2)
     ]
     grad_cols = lax.all_to_all(
         grad_block, ("grp", "dp"), 0, 0, axis_index_groups=same_core, tiled=True
-    )
-    partials = call(
-        project_kernel, [(rows // 4, columns)] * 4, place, pair_heads, far_heads, near_weight,
-        far_weight, name="project", flops=10**9, places=["smem"],
-        scratch=[pltpu.VMEM((rows, columns), BF16)],
     )
     partials = [partials[0]] + [xor_swap(partials[k], "seq", 4 * k) for k in range(1, 4)]
     projected = call(total_kernel, [(rows // 4, columns)], *partials, name="projected")

time: 174 us -> 174 us (level)
  blocking collectives: 7.11 us -> 30.4 us
  waiting for transfers between devices: 54.1 us -> 32.3 us
    all_to_all x0 -> x1, blocking collectives: none -> 22.3 us  [shards(): lax.all_to_all(grad_block, ('grp', 'dp'), 0, 0, axis_index_groups=same_co...]
    all_to_all x1, waiting for transfers between devices: 11.3 us -> 0.01 us  [shards(): lax.all_to_all(local_grad.reshape(2 * dp_size, head // dp_size, columns),...]
    all_to_all x1, waiting for transfers between devices: 8.13 us -> 0.01 us  [shards(): lax.all_to_all(sums.reshape(seq_size, shared, LANES), 'seq', 0, 0, tiled=...]
    all_to_all x1 -> x0, waiting for transfers between devices: 8.05 us -> none  [shards(): lax.all_to_all(grad_block, ('grp', 'dp'), 0, 0, axis_index_groups=same_co...]
    all_to_all x1 -> x0, starting transfers between devices: 4.82 us -> none  [shards(): lax.all_to_all(grad_block, ('grp', 'dp'), 0, 0, axis_index_groups=same_co...]
    all_to_all x1, waiting for transfers between devices: 0.01 us -> 4.48 us  [shards(): slab_parts = lax.all_to_all(slab_sums, 'grp', 0, 0, tiled=True)]
    all_to_all x1, starting transfers between devices: 9.59 us -> 13.1 us  [shards(): lax.all_to_all(local_grad.reshape(2 * dp_size, head // dp_size, columns),...]
    all_to_all x1, waiting for transfers between devices: 3.82 us -> 0.47 us  [shards(): lax.all_to_all(by_column, 'grp', 0, 0, tiled=True).reshape(shared, columns)]
  transfers between devices with their start and end apart: 18 -> 17, of which waited for: 8 -> 9; matrix products, arithmetic and copies ran while one was open for 1% -> 0% of each run, Pallas kernels for 10% -> 9%
where the time goes in v6:
time: 174 us; the launch traced here: 173 us
  starting transfers between devices  81.6 us (47%)
  waiting for transfers between devices  32.3 us (19%)
  blocking collectives  30.4 us (17%)
  Pallas kernels  21.2 us (12%)
  local copies, waits for them, and re-layouts  6.33 us (4%)
    ppermute x11, starting transfers between devices, xor_swap(): return lax.ppermute(block, axis, route)  40 us
    ppermute x11, waiting for transfers between devices, xor_swap(): return lax.ppermute(block, axis, route)  25.2 us
    all_to_all x1, blocking collectives, shards(): lax.all_to_all(grad_block, ('grp', 'dp'), 0, 0, axis_index_groups=same_co...  22.3 us
    pallas_call x14, Pallas kernels, call(): pl.pallas_call(body, out_shape=outs, in_specs=in_specs, out_specs=(whole,...  21.2 us
    all_to_all x1, starting transfers between devices, shards(): lax.all_to_all(local_grad.reshape(2 * dp_size, head // dp_size, columns),...  13.1 us
    all_to_all x1, starting transfers between devices, shards(): lax.all_to_all(sums.reshape(seq_size, shared, LANES), 'seq', 0, 0, tiled=...  11.1 us
    all_to_all x1, blocking collectives, shards(): lax.all_to_all(projected.reshape(4, block, columns), 'seq', 0, 0, axis_in...  8.12 us
    unnamed x23, local copies, waits for them, and re-layouts  5.36 us
  transfers between devices with their start and end apart: 17, of which 9 were waited for; matrix products, arithmetic and copies ran while one was open for 0% of the time, Pallas kernels for 9%

profile of v6, /device:TPU:1, one launch (start us, length us, event | category | flops | bytes accessed | tf_op | source)
XLA Modules:
  0.0 172.9 jit_solution(4163114291923753015)
XLA Ops:
  0.6 0.9 slice_bitcast_fusion
  1.6 4.0 %collective-permute-start.1 = (bf16[2,64,512]{2,1,0:T(8,128)(2,1)S(1)}, bf16[2,64,512]{2,1,0:T(8,128)(2,1)S(1)}, u32[]{:S(2)}, u32[]{:S(2)}) collective-permute-start(bf16[2,64,512]{2,1,0:T(8,128)(2,1)S(1)} %slice_bitcast_fusion), channel_id=1, source_target_pairs={{0,8},{8,16},{16,24},{24,32},{32,40},{40,48},{48,56},{56,64},{64,7... | collective-permute-start | bytes 393224 | tf_op jit(solution)/shard_map/ppermute | solution.py:22
  5.6 0.9 copy-done.4
  6.5 0.6 split_columns.1
  7.2 4.0 %all-to-all-start = ((bf16[4,16,768]{2,1,0:T(8,128)(2,1)}), bf16[4,16,768]{2,1,0:T(8,128)(2,1)S(1)}, u32[]{:S(2)}, u32[]{:S(2)}) async-start(bf16[4,16,768]{2,1,0:T(8,128)(2,1)} %split_columns.1), calls=%async_computation | async-start | bytes 196608 | tf_op jit(solution)/shard_map/all_to_all | solution.py:362
  11.2 1.0 copy-done.1
  12.2 0.9 copy-done.5
  13.1 0.8 copy-done.6
  13.9 1.4 late_frames.1
  15.3 0.5 all-to-all-done
  15.8 1.6 group_sums.1
  17.4 11.1 %all-to-all-start.1 = ((bf16[16,64,128]{2,1,0:T(8,128)(2,1)}), bf16[16,64,128]{2,1,0:T(8,128)(2,1)S(1)}, u32[]{:S(2)}, u32[]{:S(2)}) async-start(bf16[16,64,128]{2,1,0:T(8,128)(2,1)} %bitcast.9), calls=%async_computation.1 | async-start | bytes 524288 | tf_op jit(solution)/shard_map/all_to_all | solution.py:370
  28.5 7.2 %collective-permute-start = (bf16[64,768]{1,0:T(8,128)(2,1)S(1)}, bf16[64,768]{1,0:T(8,128)(2,1)S(1)}, u32[]{:S(2)}, u32[]{:S(2)}) collective-permute-start(bf16[64,768]{1,0:T(8,128)(2,1)S(1)} %bitcast.27), channel_id=1, source_target_pairs={{0,64},{8,72},{16,80},{24,88},{32,96},{40,104},{48,112},{56,120},{... | collective-permute-start | bytes 294920 | tf_op jit(solution)/shard_map/ppermute | solution.py:27
  35.7 6.9 %collective-permute-done = bf16[64,768]{1,0:T(8,128)(2,1)S(1)} collective-permute-done((bf16[64,768]{1,0:T(8,128)(2,1)S(1)}, bf16[64,768]{1,0:T(8,128)(2,1)S(1)}, u32[]{:S(2)}, u32[]{:S(2)}) %collective-permute-start) | collective-permute-done | bytes 98336 | tf_op jit(solution)/shard_map/ppermute | solution.py:27
  42.6 0.8 slab_sums.1
  43.5 2.6 %collective-permute-start.2 = (bf16[128,768]{1,0:T(8,128)(2,1)S(1)}, bf16[128,768]{1,0:T(8,128)(2,1)S(1)}, u32[]{:S(2)}, u32[]{:S(2)}) collective-permute-start(bf16[128,768]{1,0:T(8,128)(2,1)S(1)} %pad_maximum_fusion), channel_id=1, source_target_pairs={{0,32},{8,40},{16,48},{24,56},{32,0},{40,8},{48,16},{56,24},{64,96... | collective-permute-start | bytes 589832 | tf_op jit(solution)/shard_map/ppermute | solution.py:27
  46.1 4.3 %all-to-all-start.2 = ((bf16[4,64,128]{2,1,0:T(8,128)(2,1)}), bf16[4,64,128]{2,1,0:T(8,128)(2,1)S(1)}, u32[]{:S(2)}, u32[]{:S(2)}) async-start(bf16[4,64,128]{2,1,0:T(8,128)(2,1)} %slab_sums.1), calls=%async_computation.2 | async-start | bytes 131072 | tf_op jit(solution)/shard_map/all_to_all | solution.py:375
  50.4 4.5 %all-to-all-done.2.parts_ref = bf16[4,64,128]{2,1,0:T(8,128)(2,1)S(1)} async-done(((bf16[4,64,128]{2,1,0:T(8,128)(2,1)}), bf16[4,64,128]{2,1,0:T(8,128)(2,1)S(1)}, u32[]{:S(2)}, u32[]{:S(2)}) %all-to-all-start.2) | async-done | bytes 65568 | tf_op jit(solution)/shard_map/all_to_all | solution.py:375
  54.8 0.9 merged.1
  55.7 0.4 collective-permute-done.2
  56.1 5.1 %all-to-all-start.3 = ((bf16[16,64,128]{2,1,0:T(8,128)(2,1)}), bf16[16,64,128]{2,1,0:T(8,128)(2,1)S(1)}, u32[]{:S(2)}, u32[]{:S(2)}) async-start(bf16[16,64,128]{2,1,0:T(8,128)(2,1)} %merged.1), calls=%async_computation.3 | async-start | bytes 524288 | tf_op jit(solution)/shard_map/all_to_all | solution.py:383
  61.2 0.1 pad_add_fusion.place_ref
  61.4 3.3 %collective-permute-start.3 = (bf16[128,1536]{1,0:T(8,128)(2,1)S(1)}, bf16[128,1536]{1,0:T(8,128)(2,1)S(1)}, u32[]{:S(2)}, u32[]{:S(2)}) collective-permute-start(bf16[128,1536]{1,0:T(8,128)(2,1)S(1)} %constant_dynamic-slice_fusion), channel_id=1, source_target_pairs={{0,8},{8,0},{16,24},{24,16},{32,40},{40,32},{48,56},{56,48},{64,72... | collective-permute-start | bytes 1179656 | tf_op jit(solution)/shard_map/ppermute | solution.py:27
  64.7 3.1 %collective-permute-start.5 = (bf16[256,768]{1,0:T(8,128)(2,1)S(1)}, bf16[256,768]{1,0:T(8,128)(2,1)S(1)}, u32[]{:S(2)}, u32[]{:S(2)}) collective-permute-start(bf16[256,768]{1,0:T(8,128)(2,1)S(1)} %constant_dynamic-update-slice_fusion.first_ref), channel_id=1, source_target_pairs={{0,16},{8,24},{16,0},{24,8},{32,48},{40,56},{48,32},{56,40},{64,80... | collective-permute-start | bytes 1179656 | tf_op jit(solution)/shard_map/ppermute | solution.py:27
  67.8 2.2 %all-to-all-done.3 = bf16[16,64,128]{2,1,0:T(8,128)(2,1)S(1)} async-done(((bf16[16,64,128]{2,1,0:T(8,128)(2,1)}), bf16[16,64,128]{2,1,0:T(8,128)(2,1)S(1)}, u32[]{:S(2)}, u32[]{:S(2)}) %all-to-all-start.3) | async-done | bytes 262176 | tf_op jit(solution)/shard_map/all_to_all | solution.py:383
  70.0 1.7 copy-done.2
  71.7 9.8 %attend.1 = (bf16[1024,128]{1,0:T(8,128)(2,1)S(1)}, bf16[256,128]{1,0:T(8,128)(2,1)S(1)}, bf16[640,128]{1,0:T(8,128)(2,1)S(1)}) custom-call(s32[3]{0:T(128)S(1)} %pad_add_fusion.place_ref, bf16[1024,128]{1,0:T(8,128)(2,1)S(1)} %bitcast.19, bf16[64,3072]{1,0:T(8,128)(2,1)S(1)} %copy-done.3, f32[1,3072]{1,0:T(1,128)S(1)} %bitcast.23, ...), custom_call_target="tpu_custom_call" | custom-call | flops 8000000000 | bytes 1000000 | tf_op jit(solution)/shard_map/attend/pallas_call | solution.py:319
  81.5 3.3 %collective-permute-start.4 = (bf16[640,128]{1,0:T(8,128)(2,1)S(1)}, bf16[640,128]{1,0:T(8,128)(2,1)S(1)}, u32[]{:S(2)}, u32[]{:S(2)}) collective-permute-start(bf16[640,128]{1,0:T(8,128)(2,1)S(1)} %get-tuple-element.42), channel_id=1, source_target_pairs={{0,8},{8,0},{16,24},{24,16},{32,40},{40,32},{48,56},{56,48},{64,72... | collective-permute-start | bytes 491528 | tf_op jit(solution)/shard_map/ppermute | solution.py:27
  84.8 2.8 %collective-permute-done.4.given_ref = bf16[640,128]{1,0:T(8,128)(2,1)S(1)} collective-permute-done((bf16[640,128]{1,0:T(8,128)(2,1)S(1)}, bf16[640,128]{1,0:T(8,128)(2,1)S(1)}, u32[]{:S(2)}, u32[]{:S(2)}) %collective-permute-start.4) | collective-permute-done | bytes 163872 | tf_op jit(solution)/shard_map/ppermute | solution.py:27
  87.5 1.7 local_grad.1
  89.2 13.1 %all-to-all-start.4 = ((bf16[16,16,768]{2,1,0:T(8,128)(2,1)}), bf16[16,16,768]{2,1,0:T(8,128)(2,1)S(1)}, u32[]{:S(2)}, u32[]{:S(2)}) async-start(bf16[16,16,768]{2,1,0:T(8,128)(2,1)} %bitcast.14), calls=%async_computation.4 | async-start | bytes 786432 | tf_op jit(solution)/shard_map/all_to_all | solution.py:409
  102.4 0.6 weights.1
  103.0 2.1 %collective-permute-start.7 = (bf16[256,768]{1,0:T(8,128)(2,1)S(1)}, bf16[256,768]{1,0:T(8,128)(2,1)S(1)}, u32[]{:S(2)}, u32[]{:S(2)}) collective-permute-start(bf16[256,768]{1,0:T(8,128)(2,1)S(1)} %get-tuple-element.47), channel_id=1, source_target_pairs={{0,16},{8,24},{16,0},{24,8},{32,48},{40,56},{48,32},{56,40},{64,80... | collective-permute-start | bytes 1179656 | tf_op jit(solution)/shard_map/ppermute | solution.py:27
  105.0 0.6 pair_heads.1.near_ref
  105.6 3.2 %collective-permute-start.6 = (bf16[2,256,128]{2,1,0:T(8,128)(2,1)S(1)}, bf16[2,256,128]{2,1,0:T(8,128)(2,1)S(1)}, u32[]{:S(2)}, u32[]{:S(2)}) collective-permute-start(bf16[2,256,128]{2,1,0:T(8,128)(2,1)S(1)} %pair_heads.1.near_ref), channel_id=1, source_target_pairs={{0,16},{8,24},{16,0},{24,8},{32,48},{40,56},{48,32},{56,40},{64,80... | collective-permute-start | bytes 393224 | tf_op jit(solution)/shard_map/ppermute | solution.py:27
  108.9 9.5 %collective-permute-done.6.far_ref = bf16[2,256,128]{2,1,0:T(8,128)(2,1)S(1)} collective-permute-done((bf16[2,256,128]{2,1,0:T(8,128)(2,1)S(1)}, bf16[2,256,128]{2,1,0:T(8,128)(2,1)S(1)}, u32[]{:S(2)}, u32[]{:S(2)}) %collective-permute-start.6) | collective-permute-done | bytes 131104 | tf_op jit(solution)/shard_map/ppermute | solution.py:27
  118.3 0.9 project.1
  119.3 0.1 grad_block.1
  119.4 22.3 %all_to_all.35.own_ref = bf16[16,16,768]{2,1,0:T(8,128)(2,1)S(1)} all-to-all(bf16[16,16,768]{2,1,0:T(8,128)(2,1)S(1)} %grad_block.1), channel_id=1, replica_groups={{0,2,4,6,128,130,132,134,256,258,260,262,384,386,388,390},{1,3,5,7,129,..., dimensions={0} | all-to-all | bytes 786432 | tf_op jit(solution)/shard_map/all_to_all | solution.py:433
  141.7 4.0 %collective-permute-start.11 = (bf16[16,16,768]{2,1,0:T(8,128)(2,1)S(1)}, bf16[16,16,768]{2,1,0:T(8,128)(2,1)S(1)}, u32[]{:S(2)}, u32[]{:S(2)}) collective-permute-start(bf16[16,16,768]{2,1,0:T(8,128)(2,1)S(1)} %all_to_all.35.own_ref), channel_id=1, source_target_pairs={{0,1},{1,0},{2,3},{3,2},{4,5},{5,4},{6,7},{7,6},{8,9},{9,8},{10,11... | collective-permute-start | bytes 1179656 | tf_op jit(solution)/shard_map/ppermute | solution.py:27
  145.6 2.6 %collective-permute-start.8 = (bf16[64,768]{1,0:T(8,128)(2,1)S(1)}, bf16[64,768]{1,0:T(8,128)(2,1)S(1)}, u32[]{:S(2)}, u32[]{:S(2)}) collective-permute-start(bf16[64,768]{1,0:T(8,128)(2,1)S(1)} %get-tuple-element.53), channel_id=1, source_target_pairs={{0,32},{8,40},{16,48},{24,56},{32,0},{40,8},{48,16},{56,24},{64,96... | collective-permute-start | bytes 294920 | tf_op jit(solution)/shard_map/ppermute | solution.py:27
  148.2 4.3 %collective-permute-start.9 = (bf16[64,768]{1,0:T(8,128)(2,1)S(1)}, bf16[64,768]{1,0:T(8,128)(2,1)S(1)}, u32[]{:S(2)}, u32[]{:S(2)}) collective-permute-start(bf16[64,768]{1,0:T(8,128)(2,1)S(1)} %get-tuple-element.54), channel_id=1, source_target_pairs={{0,64},{8,72},{16,80},{24,88},{32,96},{40,104},{48,112},{56,120},{... | collective-permute-start | bytes 294920 | tf_op jit(solution)/shard_map/ppermute | solution.py:27
  152.5 4.5 %collective-permute-start.10 = (bf16[64,768]{1,0:T(8,128)(2,1)S(1)}, bf16[64,768]{1,0:T(8,128)(2,1)S(1)}, u32[]{:S(2)}, u32[]{:S(2)}) collective-permute-start(bf16[64,768]{1,0:T(8,128)(2,1)S(1)} %get-tuple-element.55), channel_id=1, source_target_pairs={{0,96},{8,104},{16,112},{24,120},{32,64},{40,72},{48,80},{56,88},{... | collective-permute-start | bytes 294920 | tf_op jit(solution)/shard_map/ppermute | solution.py:27
  157.1 1.2 collective-permute-done.9.refs_2_
  158.3 4.3 %collective-permute-done.10.refs_3_ = bf16[64,768]{1,0:T(8,128)(2,1)S(1)} collective-permute-done((bf16[64,768]{1,0:T(8,128)(2,1)S(1)}, bf16[64,768]{1,0:T(8,128)(2,1)S(1)}, u32[]{:S(2)}, u32[]{:S(2)}) %collective-permute-start.10) | collective-permute-done | bytes 98336 | tf_op jit(solution)/shard_map/ppermute | solution.py:27
  162.6 8.1 %all_to_all.36.parts_ref = bf16[4,16,768]{2,1,0:T(8,128)(2,1)S(1)} all-to-all(bf16[4,16,768]{2,1,0:T(8,128)(2,1)S(1)} %bitcast.18), channel_id=1, replica_groups={{0,8,16,24},{32,40,48,56},{64,72,80,88},{96,104,112,120},{1,9,17,25},{3..., dimensions={0} | all-to-all | bytes 196608 | tf_op jit(solution)/shard_map/all_to_all | solution.py:440
  170.8 0.6 attended.1
  171.4 1.5 grad_columns.1
  (30 shorter events, 0.2 us)
Async XLA Ops:
  0.6 15.2 %copy-start.8 = (s32[1,8,64]{2,1,0:T(8,128)S(1)}, s32[1,8,64]{2,1,0:T(8,128)}, u32[]{:S(2)}) copy-start(s32[1,8,64]{2,1,0:T(8,128)} %param.14) | copy-start | bytes 6148
  1.6 14.3 %collective-permute-start.1 = (bf16[2,64,512]{2,1,0:T(8,128)(2,1)S(1)}, bf16[2,64,512]{2,1,0:T(8,128)(2,1)S(1)}, u32[]{:S(2)}, u32[]{:S(2)}) collective-permute-start(bf16[2,64,512]{2,1,0:T(8,128)(2,1)S(1)} %slice_bitcast_fusion), channel_id=1, source_target_pairs={{0,8},{8,16},{16,24},{24,32},{32,40},{40,48},{48,56},{56,64},{64,7... | collective-permute-start | bytes 393224 | tf_op jit(solution)/shard_map/ppermute | solution.py:22
  5.6 0.9 copy-start.4
  7.2 8.7 %all-to-all-start = ((bf16[4,16,768]{2,1,0:T(8,128)(2,1)}), bf16[4,16,768]{2,1,0:T(8,128)(2,1)S(1)}, u32[]{:S(2)}, u32[]{:S(2)}) async-start(bf16[4,16,768]{2,1,0:T(8,128)(2,1)} %split_columns.1), calls=%async_computation | async-start | bytes 196608 | tf_op jit(solution)/shard_map/all_to_all | solution.py:362
  11.2 1.0 copy-start.1
  12.2 0.9 copy-start.5
  13.1 0.8 copy-start.6
  15.8 45.5 %copy-start = (bf16[128,3072]{1,0:T(8,128)(2,1)S(1)}, bf16[128,3072]{1,0:T(8,128)(2,1)}, u32[]{:S(2)}) copy-start(bf16[128,3072]{1,0:T(8,128)(2,1)} %weight_ref.1) | copy-start | bytes 2359300
  17.4 52.6 %copy-start.3 = (bf16[64,3072]{1,0:T(8,128)(2,1)S(1)}, bf16[64,3072]{1,0:T(8,128)(2,1)}, u32[]{:S(2)}) copy-start(bf16[64,3072]{1,0:T(8,128)(2,1)} %embed_ref.1) | copy-start | bytes 1179652
  17.4 52.6 %copy-start.7 = (f32[3072]{0:T(1024)S(1)}, f32[3072]{0:T(1024)}, u32[]{:S(2)}) copy-start(f32[3072]{0:T(1024)} %param.16) | copy-start | bytes 36868
  17.4 52.6 %copy-start.9 = (f32[128]{0:T(128)S(1)}, f32[128]{0:T(128)}, u32[]{:S(2)}) copy-start(f32[128]{0:T(128)} %param.18) | copy-start | bytes 1540
  17.4 52.6 %copy-start.10 = (f32[128]{0:T(128)S(1)}, f32[128]{0:T(128)}, u32[]{:S(2)}) copy-start(f32[128]{0:T(128)} %param.19) | copy-start | bytes 1540
  17.4 25.2 %all-to-all-start.1 = ((bf16[16,64,128]{2,1,0:T(8,128)(2,1)}), bf16[16,64,128]{2,1,0:T(8,128)(2,1)S(1)}, u32[]{:S(2)}, u32[]{:S(2)}) async-start(bf16[16,64,128]{2,1,0:T(8,128)(2,1)} %bitcast.9), calls=%async_computation.1 | async-start | bytes 524288 | tf_op jit(solution)/shard_map/all_to_all | solution.py:370
  28.5 14.1 %collective-permute-start = (bf16[64,768]{1,0:T(8,128)(2,1)S(1)}, bf16[64,768]{1,0:T(8,128)(2,1)S(1)}, u32[]{:S(2)}, u32[]{:S(2)}) collective-permute-start(bf16[64,768]{1,0:T(8,128)(2,1)S(1)} %bitcast.27), channel_id=1, source_target_pairs={{0,64},{8,72},{16,80},{24,88},{32,96},{40,104},{48,112},{56,120},{... | collective-permute-start | bytes 294920 | tf_op jit(solution)/shard_map/ppermute | solution.py:27
  43.5 12.7 %collective-permute-start.2 = (bf16[128,768]{1,0:T(8,128)(2,1)S(1)}, bf16[128,768]{1,0:T(8,128)(2,1)S(1)}, u32[]{:S(2)}, u32[]{:S(2)}) collective-permute-start(bf16[128,768]{1,0:T(8,128)(2,1)S(1)} %pad_maximum_fusion), channel_id=1, source_target_pairs={{0,32},{8,40},{16,48},{24,56},{32,0},{40,8},{48,16},{56,24},{64,96... | collective-permute-start | bytes 589832 | tf_op jit(solution)/shard_map/ppermute | solution.py:27
  46.1 8.8 %all-to-all-start.2 = ((bf16[4,64,128]{2,1,0:T(8,128)(2,1)}), bf16[4,64,128]{2,1,0:T(8,128)(2,1)S(1)}, u32[]{:S(2)}, u32[]{:S(2)}) async-start(bf16[4,64,128]{2,1,0:T(8,128)(2,1)} %slab_sums.1), calls=%async_computation.2 | async-start | bytes 131072 | tf_op jit(solution)/shard_map/all_to_all | solution.py:375
  56.1 13.8 %all-to-all-start.3 = ((bf16[16,64,128]{2,1,0:T(8,128)(2,1)}), bf16[16,64,128]{2,1,0:T(8,128)(2,1)S(1)}, u32[]{:S(2)}, u32[]{:S(2)}) async-start(bf16[16,64,128]{2,1,0:T(8,128)(2,1)} %merged.1), calls=%async_computation.3 | async-start | bytes 524288 | tf_op jit(solution)/shard_map/all_to_all | solution.py:383
  61.4 20.1 %collective-permute-start.3 = (bf16[128,1536]{1,0:T(8,128)(2,1)S(1)}, bf16[128,1536]{1,0:T(8,128)(2,1)S(1)}, u32[]{:S(2)}, u32[]{:S(2)}) collective-permute-start(bf16[128,1536]{1,0:T(8,128)(2,1)S(1)} %constant_dynamic-slice_fusion), channel_id=1, source_target_pairs={{0,8},{8,0},{16,24},{24,16},{32,40},{40,32},{48,56},{56,48},{64,72... | collective-permute-start | bytes 1179656 | tf_op jit(solution)/shard_map/ppermute | solution.py:27
  64.7 20.1 %collective-permute-start.5 = (bf16[256,768]{1,0:T(8,128)(2,1)S(1)}, bf16[256,768]{1,0:T(8,128)(2,1)S(1)}, u32[]{:S(2)}, u32[]{:S(2)}) collective-permute-start(bf16[256,768]{1,0:T(8,128)(2,1)S(1)} %constant_dynamic-update-slice_fusion.first_ref), channel_id=1, source_target_pairs={{0,16},{8,24},{16,0},{24,8},{32,48},{40,56},{48,32},{56,40},{64,80... | collective-permute-start | bytes 1179656 | tf_op jit(solution)/shard_map/ppermute | solution.py:27
  70.0 1.7 copy-start.2
  81.5 6.1 %collective-permute-start.4 = (bf16[640,128]{1,0:T(8,128)(2,1)S(1)}, bf16[640,128]{1,0:T(8,128)(2,1)S(1)}, u32[]{:S(2)}, u32[]{:S(2)}) collective-permute-start(bf16[640,128]{1,0:T(8,128)(2,1)S(1)} %get-tuple-element.42), channel_id=1, source_target_pairs={{0,8},{8,0},{16,24},{24,16},{32,40},{40,32},{48,56},{56,48},{64,72... | collective-permute-start | bytes 491528 | tf_op jit(solution)/shard_map/ppermute | solution.py:27
  89.2 30.0 %all-to-all-start.4 = ((bf16[16,16,768]{2,1,0:T(8,128)(2,1)}), bf16[16,16,768]{2,1,0:T(8,128)(2,1)S(1)}, u32[]{:S(2)}, u32[]{:S(2)}) async-start(bf16[16,16,768]{2,1,0:T(8,128)(2,1)} %bitcast.14), calls=%async_computation.4 | async-start | bytes 786432 | tf_op jit(solution)/shard_map/all_to_all | solution.py:409
  103.0 15.4 %collective-permute-start.7 = (bf16[256,768]{1,0:T(8,128)(2,1)S(1)}, bf16[256,768]{1,0:T(8,128)(2,1)S(1)}, u32[]{:S(2)}, u32[]{:S(2)}) collective-permute-start(bf16[256,768]{1,0:T(8,128)(2,1)S(1)} %get-tuple-element.47), channel_id=1, source_target_pairs={{0,16},{8,24},{16,0},{24,8},{32,48},{40,56},{48,32},{56,40},{64,80... | collective-permute-start | bytes 1179656 | tf_op jit(solution)/shard_map/ppermute | solution.py:27
  105.6 12.7 %collective-permute-start.6 = (bf16[2,256,128]{2,1,0:T(8,128)(2,1)S(1)}, bf16[2,256,128]{2,1,0:T(8,128)(2,1)S(1)}, u32[]{:S(2)}, u32[]{:S(2)}) collective-permute-start(bf16[2,256,128]{2,1,0:T(8,128)(2,1)S(1)} %pair_heads.1.near_ref), channel_id=1, source_target_pairs={{0,16},{8,24},{16,0},{24,8},{32,48},{40,56},{48,32},{56,40},{64,80... | collective-permute-start | bytes 393224 | tf_op jit(solution)/shard_map/ppermute | solution.py:27
  141.7 29.7 %collective-permute-start.11 = (bf16[16,16,768]{2,1,0:T(8,128)(2,1)S(1)}, bf16[16,16,768]{2,1,0:T(8,128)(2,1)S(1)}, u32[]{:S(2)}, u32[]{:S(2)}) collective-permute-start(bf16[16,16,768]{2,1,0:T(8,128)(2,1)S(1)} %all_to_all.35.own_ref), channel_id=1, source_target_pairs={{0,1},{1,0},{2,3},{3,2},{4,5},{5,4},{6,7},{7,6},{8,9},{9,8},{10,11... | collective-permute-start | bytes 1179656 | tf_op jit(solution)/shard_map/ppermute | solution.py:27
  145.6 11.4 %collective-permute-start.8 = (bf16[64,768]{1,0:T(8,128)(2,1)S(1)}, bf16[64,768]{1,0:T(8,128)(2,1)S(1)}, u32[]{:S(2)}, u32[]{:S(2)}) collective-permute-start(bf16[64,768]{1,0:T(8,128)(2,1)S(1)} %get-tuple-element.53), channel_id=1, source_target_pairs={{0,32},{8,40},{16,48},{24,56},{32,0},{40,8},{48,16},{56,24},{64,96... | collective-permute-start | bytes 294920 | tf_op jit(solution)/shard_map/ppermute | solution.py:27
  148.2 10.0 %collective-permute-start.9 = (bf16[64,768]{1,0:T(8,128)(2,1)S(1)}, bf16[64,768]{1,0:T(8,128)(2,1)S(1)}, u32[]{:S(2)}, u32[]{:S(2)}) collective-permute-start(bf16[64,768]{1,0:T(8,128)(2,1)S(1)} %get-tuple-element.54), channel_id=1, source_target_pairs={{0,64},{8,72},{16,80},{24,88},{32,96},{40,104},{48,112},{56,120},{... | collective-permute-start | bytes 294920 | tf_op jit(solution)/shard_map/ppermute | solution.py:27
  152.5 10.1 %collective-permute-start.10 = (bf16[64,768]{1,0:T(8,128)(2,1)S(1)}, bf16[64,768]{1,0:T(8,128)(2,1)S(1)}, u32[]{:S(2)}, u32[]{:S(2)}) collective-permute-start(bf16[64,768]{1,0:T(8,128)(2,1)S(1)} %get-tuple-element.55), channel_id=1, source_target_pairs={{0,96},{8,104},{16,112},{24,120},{32,64},{40,72},{48,80},{56,88},{... | collective-permute-start | bytes 294920 | tf_op jit(solution)/shard_map/ppermute | solution.py:27

commit v7 on v3

--- a/solution.py
+++ b/solution.py
@@ -20,6 +20,11 @@
     devices = range(lax.axis_size(axis))
     route = [(i - distance, i) for i in devices if i - distance in devices]
     return lax.ppermute(block, axis, route)
+
+
+def ring_step(block, distance):
+    size = lax.axis_size("seq")
+    return lax.ppermute(block, "seq", [(i, (i + 2 * distance) % size) for i in range(size)])
 
 
 def xor_swap(block, axis, mask):
@@ -96,7 +101,9 @@
         windows.append([padded[2 - k : 4 - k].reshape(-1, channels) for k in range(3)])
     first = latent_rows(windows, conv_ref, latent_ref)
     rows = jnp.concatenate([first, late_ref[...]], axis=0)
-    labels = labels_ref[...]
+    labels = jnp.concatenate(
+        [labels_ref[i : i + 1, :] for i in range(labels_ref.shape[0])], axis=1
+    )
     total = out_ref.shape[0]
     block = total // (grp * seq)
     step = 256
@@ -138,47 +145,52 @@
         out_ref[i] = rows
 
 
-def spread_kernel(parts_ref, out_ref):
-    total = add_up(parts_ref).astype(BF16)
+def total_kernel(parts_ref, out_ref):
+    out_ref[...] = add_up(parts_ref).astype(BF16)
+
+
+def split_kernel(rows_ref, out_ref):
+    columns = out_ref.shape[2]
+    parts = rows_ref.shape[1] // columns
     for i in range(out_ref.shape[0]):
-        out_ref[i] = total
-
-
-def grad_kernel(place_ref, head_ref, first_ref, second_ref, out_ref, rows_ref, *, masks):
-    seq = place_ref[1]
-    half = first_ref.shape[0]
-    part = rows_ref.shape[0] >> len(masks)
-    for slot in range(1 << len(masks)):
-        mask = sum(m for bit, m in enumerate(masks) if slot >> bit & 1)
-        start = pl.multiple_of((seq ^ mask) * part, part)
-        rows_ref[slot * part : (slot + 1) * part, :] = head_ref[pl.ds(start, part), :]
-    out_ref[...] = (
-        lax.dot_general(rows_ref[:half, :], first_ref[...], TN, preferred_element_type=F32)
-        + lax.dot_general(rows_ref[half:, :], second_ref[...], TN, preferred_element_type=F32)
-    ).astype(BF16)
-
-
-def project_kernel(near_ref, far_ref, weight_ref, out_ref):
-    heads = jnp.concatenate([near_ref[0], near_ref[1], far_ref[0], far_ref[1]], axis=1)
-    out_ref[...] = jnp.dot(heads, weight_ref[...], preferred_element_type=F32).astype(BF16)
-
-
-def attended_kernel(parts_ref, out_ref):
-    columns = parts_ref.shape[2]
-    for t in range(4):
-        total = parts_ref[t].astype(F32)
-        for i in range(t + 4, parts_ref.shape[0], 4):
-            total = total + parts_ref[i].astype(F32)
-        start = (2 * (t & 1) + (t >> 1)) * columns
-        out_ref[:, start : start + columns] = total.astype(BF16)
+        start = i % parts * columns
+        out_ref[i] = rows_ref[:, start : start + columns]
+
+
+def grad_kernel(place_ref, head_ref, *refs, offsets):
+    slab = place_ref[1] >> 1
+    part = refs[0].shape[0]
+    slabs = head_ref.shape[0] // part
+    total = None
+    for offset, ref in zip(offsets, refs):
+        start = pl.multiple_of(((slab + offset) & (slabs - 1)) * part, part)
+        term = lax.dot_general(
+            head_ref[pl.ds(start, part), :], ref[...], TN, preferred_element_type=F32
+        )
+        total = term if total is None else total + term
+    refs[-1][...] = total.astype(BF16)
+
+
+def project_kernel(own_ref, weight_ref, out_ref):
+    step = 768
+    for start in range(0, weight_ref.shape[1], step):
+        cols = slice(start, start + step)
+        out_ref[:, cols] = jnp.dot(
+            own_ref[...], weight_ref[:, cols], preferred_element_type=F32
+        ).astype(BF16)
 
 
 def columns_kernel(place_ref, *refs):
     out_ref = refs[-1]
+    grp, high, core = place_ref[0], place_ref[2] >> 1, place_ref[2] & 1
     columns = refs[0].shape[1]
-    for k, ref in enumerate(refs[:-1]):
-        start = pl.multiple_of((place_ref[0] ^ k) * columns, columns)
-        out_ref[:, pl.ds(start, columns)] = ref[...]
+    rows = refs[0].shape[0] // 8
+    for j, ref in enumerate(refs[:-1]):
+        left = pl.multiple_of((grp ^ j) * columns, columns)
+        for k in range(8):
+            lane = core ^ (k & 1)
+            top = pl.multiple_of(((high ^ (k >> 1)) * 2 + lane) * rows, rows)
+            out_ref[pl.ds(top, rows), pl.ds(left, columns)] = ref[k * rows : (k + 1) * rows, :]
 
 
 def head_norm(projected, gain):
@@ -188,7 +200,7 @@
 
 def attend_kernel(
     place_ref, merged_ref, embed_ref, norm_ref, qkv_ref, qgain_ref, kgain_ref, out_ref, own_ref,
-    kv_ref, q_ref, k_ref, v_ref, *, grp_size, block,
+       kv_ref, q_ref, k_ref, v_ref, *, grp_size, block,
 ):
     latents, width = embed_ref.shape
     head = q_ref.shape[1]
@@ -234,9 +246,8 @@
         denominator = jnp.sum(weights, axis=-1, keepdims=True)
         mixed = jnp.dot(weights.astype(BF16), v_ref[...], preferred_element_type=F32)
         out_ref[here, :] = (mixed / denominator).astype(BF16)
-    grp = place_ref[0]
     for i in range(total // (block * grp_size)):
-        start = pl.multiple_of((i * grp_size + grp) * block, block)
+        start = pl.multiple_of((i * grp_size + place_ref[0]) * block, block)
         own_ref[i * block : (i + 1) * block, :] = out_ref[pl.ds(start, block), :]
 
 
@@ -274,13 +285,12 @@
     rows = block * seq_size
     grp = lax.axis_index("grp")
     seq = lax.axis_index("seq")
-    place = jnp.stack([grp, seq]).astype(jnp.int32)
+    place = jnp.stack([grp, seq, lax.axis_index("dp")]).astype(jnp.int32)
 
     frames = video[0]
     frame_count, tokens = frames.shape[:2]
     earlier = shifted_frames(frames[frame_count - 2 :], "seq", 1)
     latent_t = latent_weight.T
-    labels = assign[0].reshape(1, -1)
     late, first, taps, latent_rhs = call(
         late_kernel,
         [((frame_count - 2) * tokens, LANES), (2,) + frames.shape[1:], conv_weight.shape,
@@ -288,78 +298,73 @@
         frames, conv_weight, latent_t, name="late_frames", flops=10**9, places=["hbm"] * 3,
         scratch=[pltpu.VMEM(frames.shape, BF16), pltpu.SemaphoreType.DMA((4,))],
     )
+    by_column = call(
+        split_kernel, [(2 * grp_size, block, columns)], cotangent[0], name="split_columns"
+    )
+    corners = [
+        [g * seq_size + 2 * z + y for y in range(2) for g in range(grp_size)]
+        for z in range(seq_size // 2)
+    ]
+    near = lax.all_to_all(
+        by_column, ("grp", "seq"), 0, 0, axis_index_groups=corners, tiled=True
+    ).reshape(2 * shared, columns)
+    late, near = lax.optimization_barrier((late, near))
     sums = call(
         functools.partial(sums_kernel, grp=grp_size, seq=seq_size), [(groups, LANES)],
-        first, earlier, taps, latent_rhs, late, labels, name="group_sums", flops=10**9,
-    )
-
-    by_column = jnp.concatenate(
-        [cotangent[0, :, g * columns : (g + 1) * columns] for g in range(grp_size)], axis=0
-    ).reshape(grp_size, block, columns)
-    by_column, _ = lax.optimization_barrier((by_column, earlier))
-    near = lax.all_to_all(by_column, "grp", 0, 0, tiled=True).reshape(shared, columns)
-
+        first, earlier, taps, latent_rhs, late, assign[0], name="group_sums", flops=10**9,
+    )
+    near, sums = lax.optimization_barrier((near, sums))
+    up, down = ring_step(near, 1), ring_step(near, -1)
     parts = lax.all_to_all(sums.reshape(seq_size, shared, LANES), "seq", 0, 0, tiled=True)
+    grad_rows = [near, up, down]
     slab_sums = call(resplit_kernel, [(grp_size, shared, LANES)], parts, name="slab_sums")
+    up, down, slab_sums = lax.optimization_barrier((up, down, slab_sums))
     slab_parts = lax.all_to_all(slab_sums, "grp", 0, 0, tiled=True)
+    up, down = ring_step(up, 1), ring_step(down, -1)
+    grad_rows += [up, down]
     merged = call(merge_kernel, [(seq_size, shared, LANES)], slab_parts, name="merged")
-    merged = lax.all_to_all(merged, "seq", 0, 0, tiled=True).reshape(groups, LANES)
-
-    masks = (8, 4, 1, 2)
-    for mask in masks[:-1]:
-        near = jnp.concatenate([near, xor_swap(near, "seq", mask)], axis=0)
-    far = xor_swap(near, "seq", masks[-1])
-
-    side = seq & 1
-    depth = (seq >> 1) & 1
-
-    def halved(block, choice, mask):
-        size = block.shape[1] // 2
-        kept = lax.dynamic_slice_in_dim(block, choice * size, size, 1)
-        given = lax.dynamic_slice_in_dim(block, (1 - choice) * size, size, 1)
-        return jnp.concatenate([kept, xor_swap(given, "seq", mask)], axis=0)
-
-    weight, _ = lax.optimization_barrier((out_weight, slab_sums))
-    weight_pair = halved(weight, side, 1)
+    up, down, merged = lax.optimization_barrier((up, down, merged))
+    merged = lax.all_to_all(merged, "seq", 0, 0, tiled=True)
+    up, down = ring_step(up, 1), ring_step(down, -1)
+    grad_rows += [up, down]
+    up, down, merged = lax.optimization_barrier((up, down, merged))
+    grad_rows += [ring_step(up, 1)]
+    offsets = (0, -1, 1, -2, 2, -3, 3, -4)
 
     head_out, own_rows = call(
         functools.partial(attend_kernel, grp_size=grp_size, block=block),
-        [(groups, head), (rows, head)], place, merged, embed_weight, norm_gain[None],
-        qkv_weight, q_gain[None], k_gain[None], name="attend", flops=8 * 10**9, places=["smem"],
+        [(groups, head), (rows, head)], place, merged.reshape(groups, LANES), embed_weight,
+        norm_gain[None], qkv_weight, q_gain[None], k_gain[None], name="attend",
+        flops=8 * 10**9, places=["smem"],
         scratch=[pltpu.VMEM((width, 2 * head), BF16)] + [pltpu.VMEM((groups, head), BF16)] * 3,
     )
-
-    other_rows = xor_swap(own_rows, "seq", 1)
     local_grad = call(
-        functools.partial(grad_kernel, masks=masks), [(head, columns)], place, head_out, near, far,
-        name="local_grad", places=["smem"], scratch=[pltpu.VMEM((groups, head), BF16)],
-        flops=10**9,
-    )
-    pair_heads, weight_pair, _ = lax.optimization_barrier(
-        (jnp.stack([own_rows, other_rows]), weight_pair, local_grad)
-    )
-    quad_heads = (pair_heads, xor_swap(pair_heads, "seq", 2))
-    weight_quad = halved(weight_pair, depth, 2)
+        functools.partial(grad_kernel, offsets=offsets), [(head, columns)], place, head_out,
+        *grad_rows, name="local_grad", places=["smem"], flops=10**9,
+    )
     grad_parts = lax.all_to_all(
         local_grad.reshape(dp_size, head // dp_size, columns), "dp", 0, 0, tiled=True
     )
+    partial = call(
+        project_kernel, [(rows, width)], own_rows, out_weight, name="project", flops=10**9,
+    )
     grad_block = call(
-        spread_kernel, [(dp_size, head // dp_size, columns)], grad_parts, name="grad_block"
-    )
-    grad_cols = lax.all_to_all(grad_block, "dp", 0, 0, tiled=True).reshape(head, columns)
-
-    partial = call(
-        project_kernel, [(rows, columns)], *quad_heads, weight_quad, name="project", flops=10**9,
-    )
-    partial, _ = lax.optimization_barrier((partial, grad_cols))
+        total_kernel, [(head // dp_size, columns)], grad_parts, name="grad_block"
+    )
+    partial, grad_block = lax.optimization_barrier((partial, grad_block))
     out_parts = lax.all_to_all(
-        partial.reshape(seq_size, block, columns), "seq", 0, 0, tiled=True
-    )
-    gathered = [grad_cols] + [xor_swap(grad_cols, "grp", k) for k in range(1, grp_size)]
+        partial.reshape(seq_size, block, width), "seq", 0, 0, tiled=True
+    )
+    both = jnp.concatenate([grad_block, xor_swap(grad_block, "dp", 1)], axis=0)
+    grad_cols = jnp.concatenate(
+        [both] + [xor_swap(both, "dp", 2 * k) for k in range(1, dp_size // 2)], axis=0
+    )
     out_grad = call(
-        columns_kernel, [(head, width)], place, *gathered, name="grad_columns", places=["smem"]
-    )
-    attended = call(attended_kernel, [(block, width)], out_parts, name="attended")
+        columns_kernel, [(head, width)], place, grad_cols,
+        *[xor_swap(grad_cols, "grp", k) for k in range(1, grp_size)], name="grad_columns",
+        places=["smem"],
+    )
+    attended = call(total_kernel, [(block, width)], out_parts, name="attended")
     return (attended[None], out_grad)
 
 

time: 155 us -> 169 us (1.090)
  the two profiles are of different devices: /device:TPU:1 before, /device:TPU:168 now
where the time goes in v7:
time: 169 us; the launch traced here: 168 us
  starting transfers between devices  87.9 us (52%)
  waiting for transfers between devices  42.2 us (25%)
  Pallas kernels  20.4 us (12%)
  blocking collectives  9.94 us (6%)
  local copies, waits for them, and re-layouts  6.28 us (4%)
    ppermute x7, waiting for transfers between devices, xor_swap(): return lax.ppermute(block, axis, route)  27.3 us
    ppermute x7, starting transfers between devices, xor_swap(): return lax.ppermute(block, axis, route)  23.9 us
    ppermute x7, starting transfers between devices, ring_step(): lax.ppermute(block, 'seq', [(i, (i + 2 * distance) % size) for i in range...  22.9 us
    pallas_call x11, Pallas kernels, call(): pl.pallas_call(body, out_shape=outs, in_specs=in_specs, out_specs=(whole,...  20.4 us
    all_to_all x1, blocking collectives, shards(): slab_parts = lax.all_to_all(slab_sums, 'grp', 0, 0, tiled=True)  9.94 us
    all_to_all x1, starting transfers between devices, shards(): lax.all_to_all(sums.reshape(seq_size, shared, LANES), 'seq', 0, 0, tiled=...  9.65 us
    all_to_all x1, starting transfers between devices, shards(): merged = lax.all_to_all(merged, 'seq', 0, 0, tiled=True)  9.58 us
    ppermute x7, waiting for transfers between devices, ring_step(): lax.ppermute(block, 'seq', [(i, (i + 2 * distance) % size) for i in range...  8.2 us
  transfers between devices with their start and end apart: 20, of which 11 were waited for; matrix products, arithmetic and copies ran while one was open for 1% of the time, Pallas kernels for 9%

profile of v7, /device:TPU:168, one launch (start us, length us, event | category | flops | bytes accessed | tf_op | source)
XLA Modules:
  0.0 167.7 jit_solution(17962321300268529882)
XLA Ops:
  0.6 0.9 copy-done.4
  1.5 0.7 split_columns.1
  2.2 5.8 %all-to-all-start = ((bf16[8,16,768]{2,1,0:T(8,128)(2,1)}), bf16[8,16,768]{2,1,0:T(8,128)(2,1)S(1)}, u32[]{:S(2)}, u32[]{:S(2)}) async-start(bf16[8,16,768]{2,1,0:T(8,128)(2,1)} %split_columns.1), calls=%async_computation | async-start | bytes 393216 | tf_op jit(solution)/shard_map/all_to_all | solution.py:308
  8.0 0.9 slice_bitcast_fusion
  8.9 3.7 %collective-permute-start = (bf16[2,64,512]{2,1,0:T(8,128)(2,1)S(1)}, bf16[2,64,512]{2,1,0:T(8,128)(2,1)S(1)}, u32[]{:S(2)}, u32[]{:S(2)}) collective-permute-start(bf16[2,64,512]{2,1,0:T(8,128)(2,1)S(1)} %slice_bitcast_fusion), channel_id=1, source_target_pairs={{0,8},{8,16},{16,24},{24,32},{32,40},{40,48},{48,56},{56,64},{64,7... | collective-permute-start | bytes 393224 | tf_op jit(solution)/shard_map/ppermute | solution.py:22
  12.6 1.0 copy-done
  13.7 0.9 copy-done.5
  14.6 0.8 copy-done.6
  15.4 1.4 late_frames.1
  16.8 1.6 group_sums.1
  18.4 9.7 %all-to-all-start.1 = ((bf16[16,64,128]{2,1,0:T(8,128)(2,1)}), bf16[16,64,128]{2,1,0:T(8,128)(2,1)S(1)}, u32[]{:S(2)}, u32[]{:S(2)}) async-start(bf16[16,64,128]{2,1,0:T(8,128)(2,1)} %bitcast.9), calls=%async_computation.1 | async-start | bytes 524288 | tf_op jit(solution)/shard_map/all_to_all | solution.py:318
  28.1 2.5 %collective-permute-start.2 = (bf16[128,768]{1,0:T(8,128)(2,1)S(1)}, bf16[128,768]{1,0:T(8,128)(2,1)S(1)}, u32[]{:S(2)}, u32[]{:S(2)}) collective-permute-start(bf16[128,768]{1,0:T(8,128)(2,1)S(1)} %bitcast.19), channel_id=1, source_target_pairs={{0,112},{8,120},{16,0},{24,8},{32,16},{40,24},{48,32},{56,40},{64,... | collective-permute-start | bytes 589832 | tf_op jit(solution)/shard_map/ppermute | solution.py:27
  30.6 3.4 %collective-permute-start.1 = (bf16[128,768]{1,0:T(8,128)(2,1)S(1)}, bf16[128,768]{1,0:T(8,128)(2,1)S(1)}, u32[]{:S(2)}, u32[]{:S(2)}) collective-permute-start(bf16[128,768]{1,0:T(8,128)(2,1)S(1)} %bitcast.20), channel_id=1, source_target_pairs={{0,16},{8,24},{16,32},{24,40},{32,48},{40,56},{48,64},{56,72},{64,... | collective-permute-start | bytes 589832 | tf_op jit(solution)/shard_map/ppermute | solution.py:27
  33.9 2.6 %all-to-all-done.1.parts_ref = bf16[16,64,128]{2,1,0:T(8,128)(2,1)S(1)} async-done(((bf16[16,64,128]{2,1,0:T(8,128)(2,1)}), bf16[16,64,128]{2,1,0:T(8,128)(2,1)S(1)}, u32[]{:S(2)}, u32[]{:S(2)}) %all-to-all-start.1) | async-done | bytes 262176 | tf_op jit(solution)/shard_map/all_to_all | solution.py:318
  36.5 0.2 slab_sums.1
  36.7 2.5 %collective-permute-done.2.refs_2_ = bf16[128,768]{1,0:T(8,128)(2,1)S(1)} collective-permute-done((bf16[128,768]{1,0:T(8,128)(2,1)S(1)}, bf16[128,768]{1,0:T(8,128)(2,1)S(1)}, u32[]{:S(2)}, u32[]{:S(2)}) %collective-permute-start.2) | collective-permute-done | bytes 196640 | tf_op jit(solution)/shard_map/ppermute | solution.py:27
  39.3 4.0 %collective-permute-start.3 = (bf16[128,768]{1,0:T(8,128)(2,1)S(1)}, bf16[128,768]{1,0:T(8,128)(2,1)S(1)}, u32[]{:S(2)}, u32[]{:S(2)}) collective-permute-start(bf16[128,768]{1,0:T(8,128)(2,1)S(1)} %collective-permute-done.1.refs_1_), channel_id=1, source_target_pairs={{0,16},{8,24},{16,32},{24,40},{32,48},{40,56},{48,64},{56,72},{64,... | collective-permute-start | bytes 589832 | tf_op jit(solution)/shard_map/ppermute | solution.py:27
  43.3 1.9 %collective-permute-start.4 = (bf16[128,768]{1,0:T(8,128)(2,1)S(1)}, bf16[128,768]{1,0:T(8,128)(2,1)S(1)}, u32[]{:S(2)}, u32[]{:S(2)}) collective-permute-start(bf16[128,768]{1,0:T(8,128)(2,1)S(1)} %collective-permute-done.2.refs_2_), channel_id=1, source_target_pairs={{0,112},{8,120},{16,0},{24,8},{32,16},{40,24},{48,32},{56,40},{64,... | collective-permute-start | bytes 589832 | tf_op jit(solution)/shard_map/ppermute | solution.py:27
  45.2 9.9 %all_to_all.30.parts_ref = bf16[4,64,128]{2,1,0:T(8,128)(2,1)S(1)} all-to-all(bf16[4,64,128]{2,1,0:T(8,128)(2,1)S(1)} %slab_sums.1), channel_id=1, replica_groups=mesh['grp'=4,'seq'=16,'dp'=8] {'grp'}, dimensions={0} | all-to-all | bytes 131072 | tf_op jit(solution)/shard_map/all_to_all | solution.py:322
  55.1 0.9 merged.1
  56.0 9.6 %all-to-all-start.3 = ((bf16[16,64,128]{2,1,0:T(8,128)(2,1)}), bf16[16,64,128]{2,1,0:T(8,128)(2,1)S(1)}, u32[]{:S(2)}, u32[]{:S(2)}) async-start(bf16[16,64,128]{2,1,0:T(8,128)(2,1)} %merged.1), calls=%async_computation.3 | async-start | bytes 524288 | tf_op jit(solution)/shard_map/all_to_all | solution.py:327
  65.6 3.4 %collective-permute-start.5 = (bf16[128,768]{1,0:T(8,128)(2,1)S(1)}, bf16[128,768]{1,0:T(8,128)(2,1)S(1)}, u32[]{:S(2)}, u32[]{:S(2)}) collective-permute-start(bf16[128,768]{1,0:T(8,128)(2,1)S(1)} %collective-permute-done.3.refs_3_), channel_id=1, source_target_pairs={{0,16},{8,24},{16,32},{24,40},{32,48},{40,56},{48,64},{56,72},{64,... | collective-permute-start | bytes 589832 | tf_op jit(solution)/shard_map/ppermute | solution.py:27
  69.0 2.5 %collective-permute-start.6 = (bf16[128,768]{1,0:T(8,128)(2,1)S(1)}, bf16[128,768]{1,0:T(8,128)(2,1)S(1)}, u32[]{:S(2)}, u32[]{:S(2)}) collective-permute-start(bf16[128,768]{1,0:T(8,128)(2,1)S(1)} %collective-permute-done.4.refs_4_), channel_id=1, source_target_pairs={{0,112},{8,120},{16,0},{24,8},{32,16},{40,24},{48,32},{56,40},{64,... | collective-permute-start | bytes 589832 | tf_op jit(solution)/shard_map/ppermute | solution.py:27
  71.6 2.0 %collective-permute-done.5.refs_5_ = bf16[128,768]{1,0:T(8,128)(2,1)S(1)} collective-permute-done((bf16[128,768]{1,0:T(8,128)(2,1)S(1)}, bf16[128,768]{1,0:T(8,128)(2,1)S(1)}, u32[]{:S(2)}, u32[]{:S(2)}) %collective-permute-start.5) | collective-permute-done | bytes 196640 | tf_op jit(solution)/shard_map/ppermute | solution.py:27
  73.5 3.7 %collective-permute-done.6.refs_6_ = bf16[128,768]{1,0:T(8,128)(2,1)S(1)} collective-permute-done((bf16[128,768]{1,0:T(8,128)(2,1)S(1)}, bf16[128,768]{1,0:T(8,128)(2,1)S(1)}, u32[]{:S(2)}, u32[]{:S(2)}) %collective-permute-start.6) | collective-permute-done | bytes 196640 | tf_op jit(solution)/shard_map/ppermute | solution.py:27
  77.2 5.3 %collective-permute-start.7 = (bf16[128,768]{1,0:T(8,128)(2,1)S(1)}, bf16[128,768]{1,0:T(8,128)(2,1)S(1)}, u32[]{:S(2)}, u32[]{:S(2)}) collective-permute-start(bf16[128,768]{1,0:T(8,128)(2,1)S(1)} %collective-permute-done.5.refs_5_), channel_id=1, source_target_pairs={{0,16},{8,24},{16,32},{24,40},{32,48},{40,56},{48,64},{56,72},{64,... | collective-permute-start | bytes 589832 | tf_op jit(solution)/shard_map/ppermute | solution.py:27
  82.6 1.7 copy-done.1
  84.2 9.7 %attend.1 = (bf16[1024,128]{1,0:T(8,128)(2,1)S(1)}, bf16[256,128]{1,0:T(8,128)(2,1)S(1)}) custom-call(s32[3]{0:T(128)S(1)} %pad_add_fusion.place_ref, bf16[1024,128]{1,0:T(8,128)(2,1)S(1)} %bitcast.18, bf16[64,3072]{1,0:T(8,128)(2,1)S(1)} %copy-done.3, f32[1,3072]{1,0:T(1,128)S(1)} %bitcast.25, bf16[3,3072,128]{2,1,0:T(8,128)(2,1)S(1)} %copy-done.1, ...), custom_call_target="tpu_custom_call" | custom-call | flops 8000000000 | bytes 1000000 | tf_op jit(solution)/shard_map/attend/pallas_call | solution.py:261
  94.0 1.8 %local_grad.1 = bf16[128,768]{1,0:T(8,128)(2,1)} custom-call(s32[3]{0:T(128)S(1)} %pad_add_fusion.place_ref, bf16[1024,128]{1,0:T(8,128)(2,1)S(1)} %get-tuple-element.38.head_ref, bf16[128,768]{1,0:T(8,128)(2,1)S(1)} %bitcast.21, bf16[128,768]{1,0:T(8,128)(2,1)S(1)} %collective-permute-done.1.refs_1_, bf16[128,768]{1,0:T(8,128)(2,1)S(1)} %collective-permute-done.2.refs_2_, ...), custom_call_target="tpu_custom_call" | custom-call | flops 1000000000 | bytes 1000000 | tf_op jit(solution)/shard_map/local_grad/pallas_call | solution.py:261
  95.8 7.2 %all-to-all-start.4 = ((bf16[8,16,768]{2,1,0:T(8,128)(2,1)}), bf16[8,16,768]{2,1,0:T(8,128)(2,1)S(1)}, u32[]{:S(2)}, u32[]{:S(2)}) async-start(bf16[8,16,768]{2,1,0:T(8,128)(2,1)} %bitcast.14), calls=%async_computation.4 | async-start | bytes 393216 | tf_op jit(solution)/shard_map/all_to_all | solution.py:345
  103.0 1.8 %project.1 = bf16[256,3072]{1,0:T(8,128)(2,1)} custom-call(bf16[256,128]{1,0:T(8,128)(2,1)S(1)} %get-tuple-element.37.own_ref, bf16[128,3072]{1,0:T(8,128)(2,1)S(1)} %copy-done.2), custom_call_target="tpu_custom_call" | custom-call | flops 1000000000 | bytes 1000000 | tf_op jit(solution)/shard_map/project/pallas_call | solution.py:261
  104.8 4.0 %all-to-all-done.4.parts_ref = bf16[8,16,768]{2,1,0:T(8,128)(2,1)S(1)} async-done(((bf16[8,16,768]{2,1,0:T(8,128)(2,1)}), bf16[8,16,768]{2,1,0:T(8,128)(2,1)S(1)}, u32[]{:S(2)}, u32[]{:S(2)}) %all-to-all-start.4) | async-done | bytes 196640 | tf_op jit(solution)/shard_map/all_to_all | solution.py:345
  108.9 5.1 %all-to-all-start.5 = ((bf16[16,16,3072]{2,1,0:T(8,128)(2,1)}), bf16[16,16,3072]{2,1,0:T(8,128)(2,1)S(1)}, u32[]{:S(2)}, u32[]{:S(2)}) async-start(bf16[16,16,3072]{2,1,0:T(8,128)(2,1)} %bitcast.15), calls=%async_computation.5 | async-start | bytes 3145728 | tf_op jit(solution)/shard_map/all_to_all | solution.py:355
  114.0 1.9 %collective-permute-start.8 = (bf16[16,768]{1,0:T(8,128)(2,1)S(1)}, bf16[16,768]{1,0:T(8,128)(2,1)S(1)}, u32[]{:S(2)}, u32[]{:S(2)}) collective-permute-start(bf16[16,768]{1,0:T(8,128)(2,1)S(1)} %grad_block.1), channel_id=1, source_target_pairs={{0,1},{1,0},{2,3},{3,2},{4,5},{5,4},{6,7},{7,6},{8,9},{9,8},{10,11... | collective-permute-start | bytes 73736 | tf_op jit(solution)/shard_map/ppermute | solution.py:32
  115.9 1.1 collective-permute-done.8
  117.1 3.4 %collective-permute-start.9 = (bf16[32,768]{1,0:T(8,128)(2,1)S(1)}, bf16[32,768]{1,0:T(8,128)(2,1)S(1)}, u32[]{:S(2)}, u32[]{:S(2)}) collective-permute-start(bf16[32,768]{1,0:T(8,128)(2,1)S(1)} %get-tuple-element.42), channel_id=1, source_target_pairs={{0,2},{1,3},{2,0},{3,1},{4,6},{5,7},{6,4},{7,5},{8,10},{9,11},{10,... | collective-permute-start | bytes 147464 | tf_op jit(solution)/shard_map/ppermute | solution.py:32
  120.4 5.8 %collective-permute-start.11 = (bf16[32,768]{1,0:T(8,128)(2,1)S(1)}, bf16[32,768]{1,0:T(8,128)(2,1)S(1)}, u32[]{:S(2)}, u32[]{:S(2)}) collective-permute-start(bf16[32,768]{1,0:T(8,128)(2,1)S(1)} %get-tuple-element.42), channel_id=1, source_target_pairs={{0,6},{1,7},{2,4},{3,5},{4,2},{5,3},{6,0},{7,1},{8,14},{9,15},{10,... | collective-permute-start | bytes 147464 | tf_op jit(solution)/shard_map/ppermute | solution.py:32
  126.2 3.1 %collective-permute-start.10 = (bf16[32,768]{1,0:T(8,128)(2,1)S(1)}, bf16[32,768]{1,0:T(8,128)(2,1)S(1)}, u32[]{:S(2)}, u32[]{:S(2)}) collective-permute-start(bf16[32,768]{1,0:T(8,128)(2,1)S(1)} %get-tuple-element.42), channel_id=1, source_target_pairs={{0,4},{1,5},{2,6},{3,7},{4,0},{5,1},{6,2},{7,3},{8,12},{9,13},{10,... | collective-permute-start | bytes 147464 | tf_op jit(solution)/shard_map/ppermute | solution.py:32
  129.3 16.4 %collective-permute-done.9 = bf16[32,768]{1,0:T(8,128)(2,1)S(1)} collective-permute-done((bf16[32,768]{1,0:T(8,128)(2,1)S(1)}, bf16[32,768]{1,0:T(8,128)(2,1)S(1)}, u32[]{:S(2)}, u32[]{:S(2)}) %collective-permute-start.9) | collective-permute-done | bytes 49184 | tf_op jit(solution)/shard_map/ppermute | solution.py:32
  145.7 4.4 %collective-permute-done.10 = bf16[32,768]{1,0:T(8,128)(2,1)S(1)} collective-permute-done((bf16[32,768]{1,0:T(8,128)(2,1)S(1)}, bf16[32,768]{1,0:T(8,128)(2,1)S(1)}, u32[]{:S(2)}, u32[]{:S(2)}) %collective-permute-start.10) | collective-permute-done | bytes 49184 | tf_op jit(solution)/shard_map/ppermute | solution.py:32
  150.1 3.0 %collective-permute-start.14 = (bf16[128,768]{1,0:T(8,128)(2,1)S(1)}, bf16[128,768]{1,0:T(8,128)(2,1)S(1)}, u32[]{:S(2)}, u32[]{:S(2)}) collective-permute-start(bf16[128,768]{1,0:T(8,128)(2,1)S(1)} %constant_dynamic-update-slice_fusion.2.refs_0_), channel_id=1, source_target_pairs={{0,384},{128,256},{256,128},{384,0},{1,385},{129,257},{257,129},{3... | collective-permute-start | bytes 589832 | tf_op jit(solution)/shard_map/ppermute | solution.py:32
  153.2 3.5 %collective-permute-start.13 = (bf16[128,768]{1,0:T(8,128)(2,1)S(1)}, bf16[128,768]{1,0:T(8,128)(2,1)S(1)}, u32[]{:S(2)}, u32[]{:S(2)}) collective-permute-start(bf16[128,768]{1,0:T(8,128)(2,1)S(1)} %constant_dynamic-update-slice_fusion.2.refs_0_), channel_id=1, source_target_pairs={{0,256},{128,384},{256,0},{384,128},{1,257},{129,385},{257,1},{385... | collective-permute-start | bytes 589832 | tf_op jit(solution)/shard_map/ppermute | solution.py:32
  156.6 3.3 %collective-permute-start.12 = (bf16[128,768]{1,0:T(8,128)(2,1)S(1)}, bf16[128,768]{1,0:T(8,128)(2,1)S(1)}, u32[]{:S(2)}, u32[]{:S(2)}) collective-permute-start(bf16[128,768]{1,0:T(8,128)(2,1)S(1)} %constant_dynamic-update-slice_fusion.2.refs_0_), channel_id=1, source_target_pairs={{0,128},{128,0},{256,384},{384,256},{1,129},{129,1},{257,385},{385... | collective-permute-start | bytes 589832 | tf_op jit(solution)/shard_map/ppermute | solution.py:32
  160.0 1.8 %collective-permute-done.14.refs_3_ = bf16[128,768]{1,0:T(8,128)(2,1)S(1)} collective-permute-done((bf16[128,768]{1,0:T(8,128)(2,1)S(1)}, bf16[128,768]{1,0:T(8,128)(2,1)S(1)}, u32[]{:S(2)}, u32[]{:S(2)}) %collective-permute-start.14) | collective-permute-done | bytes 196640 | tf_op jit(solution)/shard_map/ppermute | solution.py:32
  161.8 1.9 %collective-permute-done.13.refs_2_ = bf16[128,768]{1,0:T(8,128)(2,1)S(1)} collective-permute-done((bf16[128,768]{1,0:T(8,128)(2,1)S(1)}, bf16[128,768]{1,0:T(8,128)(2,1)S(1)}, u32[]{:S(2)}, u32[]{:S(2)}) %collective-permute-start.13) | collective-permute-done | bytes 196640 | tf_op jit(solution)/shard_map/ppermute | solution.py:32
  163.7 1.6 collective-permute-done.12.refs_1_
  165.4 1.5 grad_columns.1
  166.9 0.8 attended.1
  (33 shorter events, 0.2 us)
Async XLA Ops:
  0.6 0.9 copy-start.4
  2.2 14.6 %all-to-all-start = ((bf16[8,16,768]{2,1,0:T(8,128)(2,1)}), bf16[8,16,768]{2,1,0:T(8,128)(2,1)S(1)}, u32[]{:S(2)}, u32[]{:S(2)}) async-start(bf16[8,16,768]{2,1,0:T(8,128)(2,1)} %split_columns.1), calls=%async_computation | async-start | bytes 393216 | tf_op jit(solution)/shard_map/all_to_all | solution.py:308
  8.9 7.9 %collective-permute-start = (bf16[2,64,512]{2,1,0:T(8,128)(2,1)S(1)}, bf16[2,64,512]{2,1,0:T(8,128)(2,1)S(1)}, u32[]{:S(2)}, u32[]{:S(2)}) collective-permute-start(bf16[2,64,512]{2,1,0:T(8,128)(2,1)S(1)} %slice_bitcast_fusion), channel_id=1, source_target_pairs={{0,8},{8,16},{16,24},{24,32},{32,40},{40,48},{48,56},{56,64},{64,7... | collective-permute-start | bytes 393224 | tf_op jit(solution)/shard_map/ppermute | solution.py:22
  12.6 1.0 copy-start
  13.7 0.9 copy-start.5
  14.6 0.8 copy-start.6
  15.4 1.4 copy-start.8
  18.4 64.1 %copy-start.3 = (bf16[64,3072]{1,0:T(8,128)(2,1)S(1)}, bf16[64,3072]{1,0:T(8,128)(2,1)}, u32[]{:S(2)}) copy-start(bf16[64,3072]{1,0:T(8,128)(2,1)} %embed_ref.1) | copy-start | bytes 1179652
  18.4 64.1 %copy-start.7 = (f32[3072]{0:T(1024)S(1)}, f32[3072]{0:T(1024)}, u32[]{:S(2)}) copy-start(f32[3072]{0:T(1024)} %param.16) | copy-start | bytes 36868
  18.4 64.1 %copy-start.9 = (f32[128]{0:T(128)S(1)}, f32[128]{0:T(128)}, u32[]{:S(2)}) copy-start(f32[128]{0:T(128)} %param.18) | copy-start | bytes 1540
  18.4 64.1 %copy-start.10 = (f32[128]{0:T(128)S(1)}, f32[128]{0:T(128)}, u32[]{:S(2)}) copy-start(f32[128]{0:T(128)} %param.19) | copy-start | bytes 1540
  18.4 18.1 %all-to-all-start.1 = ((bf16[16,64,128]{2,1,0:T(8,128)(2,1)}), bf16[16,64,128]{2,1,0:T(8,128)(2,1)S(1)}, u32[]{:S(2)}, u32[]{:S(2)}) async-start(bf16[16,64,128]{2,1,0:T(8,128)(2,1)} %bitcast.9), calls=%async_computation.1 | async-start | bytes 524288 | tf_op jit(solution)/shard_map/all_to_all | solution.py:318
  28.1 11.2 %collective-permute-start.2 = (bf16[128,768]{1,0:T(8,128)(2,1)S(1)}, bf16[128,768]{1,0:T(8,128)(2,1)S(1)}, u32[]{:S(2)}, u32[]{:S(2)}) collective-permute-start(bf16[128,768]{1,0:T(8,128)(2,1)S(1)} %bitcast.19), channel_id=1, source_target_pairs={{0,112},{8,120},{16,0},{24,8},{32,16},{40,24},{48,32},{56,40},{64,... | collective-permute-start | bytes 589832 | tf_op jit(solution)/shard_map/ppermute | solution.py:27
  30.6 8.7 %collective-permute-start.1 = (bf16[128,768]{1,0:T(8,128)(2,1)S(1)}, bf16[128,768]{1,0:T(8,128)(2,1)S(1)}, u32[]{:S(2)}, u32[]{:S(2)}) collective-permute-start(bf16[128,768]{1,0:T(8,128)(2,1)S(1)} %bitcast.20), channel_id=1, source_target_pairs={{0,16},{8,24},{16,32},{24,40},{32,48},{40,56},{48,64},{56,72},{64,... | collective-permute-start | bytes 589832 | tf_op jit(solution)/shard_map/ppermute | solution.py:27
  39.3 16.8 %collective-permute-start.3 = (bf16[128,768]{1,0:T(8,128)(2,1)S(1)}, bf16[128,768]{1,0:T(8,128)(2,1)S(1)}, u32[]{:S(2)}, u32[]{:S(2)}) collective-permute-start(bf16[128,768]{1,0:T(8,128)(2,1)S(1)} %collective-permute-done.1.refs_1_), channel_id=1, source_target_pairs={{0,16},{8,24},{16,32},{24,40},{32,48},{40,56},{48,64},{56,72},{64,... | collective-permute-start | bytes 589832 | tf_op jit(solution)/shard_map/ppermute | solution.py:27
  43.3 12.8 %collective-permute-start.4 = (bf16[128,768]{1,0:T(8,128)(2,1)S(1)}, bf16[128,768]{1,0:T(8,128)(2,1)S(1)}, u32[]{:S(2)}, u32[]{:S(2)}) collective-permute-start(bf16[128,768]{1,0:T(8,128)(2,1)S(1)} %collective-permute-done.2.refs_2_), channel_id=1, source_target_pairs={{0,112},{8,120},{16,0},{24,8},{32,16},{40,24},{48,32},{56,40},{64,... | collective-permute-start | bytes 589832 | tf_op jit(solution)/shard_map/ppermute | solution.py:27
  56.0 21.2 %all-to-all-start.3 = ((bf16[16,64,128]{2,1,0:T(8,128)(2,1)}), bf16[16,64,128]{2,1,0:T(8,128)(2,1)S(1)}, u32[]{:S(2)}, u32[]{:S(2)}) async-start(bf16[16,64,128]{2,1,0:T(8,128)(2,1)} %merged.1), calls=%async_computation.3 | async-start | bytes 524288 | tf_op jit(solution)/shard_map/all_to_all | solution.py:327
  65.6 7.9 %collective-permute-start.5 = (bf16[128,768]{1,0:T(8,128)(2,1)S(1)}, bf16[128,768]{1,0:T(8,128)(2,1)S(1)}, u32[]{:S(2)}, u32[]{:S(2)}) collective-permute-start(bf16[128,768]{1,0:T(8,128)(2,1)S(1)} %collective-permute-done.3.refs_3_), channel_id=1, source_target_pairs={{0,16},{8,24},{16,32},{24,40},{32,48},{40,56},{48,64},{56,72},{64,... | collective-permute-start | bytes 589832 | tf_op jit(solution)/shard_map/ppermute | solution.py:27
  69.0 8.2 %collective-permute-start.6 = (bf16[128,768]{1,0:T(8,128)(2,1)S(1)}, bf16[128,768]{1,0:T(8,128)(2,1)S(1)}, u32[]{:S(2)}, u32[]{:S(2)}) collective-permute-start(bf16[128,768]{1,0:T(8,128)(2,1)S(1)} %collective-permute-done.4.refs_4_), channel_id=1, source_target_pairs={{0,112},{8,120},{16,0},{24,8},{32,16},{40,24},{48,32},{56,40},{64,... | collective-permute-start | bytes 589832 | tf_op jit(solution)/shard_map/ppermute | solution.py:27
  77.2 16.8 %collective-permute-start.7 = (bf16[128,768]{1,0:T(8,128)(2,1)S(1)}, bf16[128,768]{1,0:T(8,128)(2,1)S(1)}, u32[]{:S(2)}, u32[]{:S(2)}) collective-permute-start(bf16[128,768]{1,0:T(8,128)(2,1)S(1)} %collective-permute-done.5.refs_5_), channel_id=1, source_target_pairs={{0,16},{8,24},{16,32},{24,40},{32,48},{40,56},{48,64},{56,72},{64,... | collective-permute-start | bytes 589832 | tf_op jit(solution)/shard_map/ppermute | solution.py:27
  82.6 1.7 copy-start.1
  94.0 9.0 %copy-start.2 = (bf16[128,3072]{1,0:T(8,128)(2,1)S(1)}, bf16[128,3072]{1,0:T(8,128)(2,1)}, u32[]{:S(2)}) copy-start(bf16[128,3072]{1,0:T(8,128)(2,1)} %weight_ref.1) | copy-start | bytes 2359300
  95.8 13.0 %all-to-all-start.4 = ((bf16[8,16,768]{2,1,0:T(8,128)(2,1)}), bf16[8,16,768]{2,1,0:T(8,128)(2,1)S(1)}, u32[]{:S(2)}, u32[]{:S(2)}) async-start(bf16[8,16,768]{2,1,0:T(8,128)(2,1)} %bitcast.14), calls=%async_computation.4 | async-start | bytes 393216 | tf_op jit(solution)/shard_map/all_to_all | solution.py:345
  108.9 58.0 %all-to-all-start.5 = ((bf16[16,16,3072]{2,1,0:T(8,128)(2,1)}), bf16[16,16,3072]{2,1,0:T(8,128)(2,1)S(1)}, u32[]{:S(2)}, u32[]{:S(2)}) async-start(bf16[16,16,3072]{2,1,0:T(8,128)(2,1)} %bitcast.15), calls=%async_computation.5 | async-start | bytes 3145728 | tf_op jit(solution)/shard_map/all_to_all | solution.py:355
  114.0 3.1 %collective-permute-start.8 = (bf16[16,768]{1,0:T(8,128)(2,1)S(1)}, bf16[16,768]{1,0:T(8,128)(2,1)S(1)}, u32[]{:S(2)}, u32[]{:S(2)}) collective-permute-start(bf16[16,768]{1,0:T(8,128)(2,1)S(1)} %grad_block.1), channel_id=1, source_target_pairs={{0,1},{1,0},{2,3},{3,2},{4,5},{5,4},{6,7},{7,6},{8,9},{9,8},{10,11... | collective-permute-start | bytes 73736 | tf_op jit(solution)/shard_map/ppermute | solution.py:32
  117.1 28.7 %collective-permute-start.9 = (bf16[32,768]{1,0:T(8,128)(2,1)S(1)}, bf16[32,768]{1,0:T(8,128)(2,1)S(1)}, u32[]{:S(2)}, u32[]{:S(2)}) collective-permute-start(bf16[32,768]{1,0:T(8,128)(2,1)S(1)} %get-tuple-element.42), channel_id=1, source_target_pairs={{0,2},{1,3},{2,0},{3,1},{4,6},{5,7},{6,4},{7,5},{8,10},{9,11},{10,... | collective-permute-start | bytes 147464 | tf_op jit(solution)/shard_map/ppermute | solution.py:32
  120.4 29.7 %collective-permute-start.11 = (bf16[32,768]{1,0:T(8,128)(2,1)S(1)}, bf16[32,768]{1,0:T(8,128)(2,1)S(1)}, u32[]{:S(2)}, u32[]{:S(2)}) collective-permute-start(bf16[32,768]{1,0:T(8,128)(2,1)S(1)} %get-tuple-element.42), channel_id=1, source_target_pairs={{0,6},{1,7},{2,4},{3,5},{4,2},{5,3},{6,0},{7,1},{8,14},{9,15},{10,... | collective-permute-start | bytes 147464 | tf_op jit(solution)/shard_map/ppermute | solution.py:32
  126.2 23.9 %collective-permute-start.10 = (bf16[32,768]{1,0:T(8,128)(2,1)S(1)}, bf16[32,768]{1,0:T(8,128)(2,1)S(1)}, u32[]{:S(2)}, u32[]{:S(2)}) collective-permute-start(bf16[32,768]{1,0:T(8,128)(2,1)S(1)} %get-tuple-element.42), channel_id=1, source_target_pairs={{0,4},{1,5},{2,6},{3,7},{4,0},{5,1},{6,2},{7,3},{8,12},{9,13},{10,... | collective-permute-start | bytes 147464 | tf_op jit(solution)/shard_map/ppermute | solution.py:32
  150.1 11.7 %collective-permute-start.14 = (bf16[128,768]{1,0:T(8,128)(2,1)S(1)}, bf16[128,768]{1,0:T(8,128)(2,1)S(1)}, u32[]{:S(2)}, u32[]{:S(2)}) collective-permute-start(bf16[128,768]{1,0:T(8,128)(2,1)S(1)} %constant_dynamic-update-slice_fusion.2.refs_0_), channel_id=1, source_target_pairs={{0,384},{128,256},{256,128},{384,0},{1,385},{129,257},{257,129},{3... | collective-permute-start | bytes 589832 | tf_op jit(solution)/shard_map/ppermute | solution.py:32
  153.2 10.5 %collective-permute-start.13 = (bf16[128,768]{1,0:T(8,128)(2,1)S(1)}, bf16[128,768]{1,0:T(8,128)(2,1)S(1)}, u32[]{:S(2)}, u32[]{:S(2)}) collective-permute-start(bf16[128,768]{1,0:T(8,128)(2,1)S(1)} %constant_dynamic-update-slice_fusion.2.refs_0_), channel_id=1, source_target_pairs={{0,256},{128,384},{256,0},{384,128},{1,257},{129,385},{257,1},{385... | collective-permute-start | bytes 589832 | tf_op jit(solution)/shard_map/ppermute | solution.py:32
  156.6 8.7 %collective-permute-start.12 = (bf16[128,768]{1,0:T(8,128)(2,1)S(1)}, bf16[128,768]{1,0:T(8,128)(2,1)S(1)}, u32[]{:S(2)}, u32[]{:S(2)}) collective-permute-start(bf16[128,768]{1,0:T(8,128)(2,1)S(1)} %constant_dynamic-update-slice_fusion.2.refs_0_), channel_id=1, source_target_pairs={{0,128},{128,0},{256,384},{384,256},{1,129},{129,1},{257,385},{385... | collective-permute-start | bytes 589832 | tf_op jit(solution)/shard_map/ppermute | solution.py:32

commit v8 on v6

--- a/solution.py
+++ b/solution.py
@@ -120,17 +120,23 @@
     return total
 
 
-def resplit_kernel(parts_ref, out_ref):
+def resplit_kernel(parts_ref, cot_ref, out_ref):
     total, counts = join_pairs(add_up(parts_ref))
     lane = lane_index(total.shape[0])
     doubled = jnp.where(lane < HALF, total, pltpu.roll(total, HALF, 1))
     pairs = split_pairs(jnp.where(lane < LANES - 2, doubled, counts))
     for i in range(out_ref.shape[0]):
-        out_ref[i] = pairs
+        out_ref[i, : pairs.shape[0], :] = pairs
+    block, width = cot_ref.shape
+    pieces = width // LANES // out_ref.shape[0]
+    for i in range(width // LANES):
+        start = pairs.shape[0] + i % pieces * block
+        here = cot_ref[:, i * LANES : (i + 1) * LANES]
+        out_ref[i // pieces, start : start + block, :] = here
 
 
 def merge_kernel(parts_ref, out_ref):
-    total, counts = join_pairs(add_up(parts_ref))
+    total, counts = join_pairs(add_up(parts_ref)[: out_ref.shape[1], :])
     lane = lane_index(total.shape[0])
     merged = jnp.where(lane < HALF, total / counts, 0.0)
     high = counts.astype(BF16).astype(F32)
@@ -146,31 +152,30 @@
         out_ref[i] = total
 
 
-def split_kernel(rows_ref, out_ref):
-    columns = out_ref.shape[2]
-    for i in range(out_ref.shape[0]):
-        out_ref[i] = rows_ref[:, i * columns : (i + 1) * columns]
-
-
-def grad_kernel(
-    place_ref, head_ref, given_ref, first_ref, second_ref, out_ref, rows_ref, *, masks, part,
-):
-    seq = place_ref[1]
+def near_kernel(parts_ref, out_ref):
+    rows, columns = out_ref.shape[1:]
+    block = rows // parts_ref.shape[0]
+    first = parts_ref.shape[1] - columns // LANES * block
+    for g in range(parts_ref.shape[0]):
+        for b in range(columns // LANES):
+            start = first + b * block
+            piece = parts_ref[g, start : start + block, :]
+            for i in range(out_ref.shape[0]):
+                cols = slice(b * LANES, (b + 1) * LANES)
+                out_ref[i, g * block : (g + 1) * block, cols] = piece
+
+
+def grad_kernel(place_ref, head_ref, given_ref, cot_ref, out_ref, rows_ref):
+    side = place_ref[1] & 1
     head = head_ref.shape[1]
-    half = first_ref.shape[0]
-    for slot in range(1 << len(masks)):
-        mask = sum(m for bit, m in enumerate(masks) if slot >> bit & 1)
-        source = seq ^ mask
-        start = pl.multiple_of(source * part, part)
-        given = pl.multiple_of((source >> 1) * part, part)
-        here = slice(slot * part, (slot + 1) * part)
+    slabs, part = cot_ref.shape[:2]
+    for slab in range(slabs):
+        start = pl.multiple_of((2 * slab + side) * part, part)
+        here = slice(slab * part, (slab + 1) * part)
         rows_ref[here, :head] = head_ref[pl.ds(start, part), :]
-        rows_ref[here, head:] = given_ref[pl.ds(given, part), :]
-    total = (
-        lax.dot_general(rows_ref[:half, :], first_ref[...], TN, preferred_element_type=F32)
-        + lax.dot_general(rows_ref[half:, :], second_ref[...], TN, preferred_element_type=F32)
-    ).astype(BF16)
-    side = seq & 1
+        rows_ref[here, head:] = given_ref[here, :]
+    cot = cot_ref[...].reshape(slabs * part, cot_ref.shape[2])
+    total = lax.dot_general(rows_ref[...], cot, TN, preferred_element_type=F32).astype(BF16)
     out_ref[side] = total[:head, :]
     out_ref[1 - side] = total[head:, :]
 
@@ -203,42 +208,31 @@
         given_ref[i * size : (i + 1) * size, :] = ref[:, pl.ds(give, columns)]
 
 
-def project_kernel(place_ref, near_ref, far_ref, near_weight_ref, far_weight_ref, *refs):
-    out_refs, sum_ref = refs[:4], refs[4]
+def project_kernel(near_ref, far_ref, near_weight_ref, far_weight_ref, out_ref):
     near = jnp.concatenate([near_ref[0], near_ref[1]], axis=1)
     far = jnp.concatenate([far_ref[0], far_ref[1]], axis=1)
-    sum_ref[...] = (
+    out_ref[...] = (
         jnp.dot(near, near_weight_ref[...], preferred_element_type=F32)
         + jnp.dot(far, far_weight_ref[...], preferred_element_type=F32)
     ).astype(BF16)
-    part = sum_ref.shape[0] // 4
-    for k, ref in enumerate(out_refs):
-        start = pl.multiple_of(((place_ref[1] >> 2) ^ k) * part, part)
-        ref[...] = sum_ref[pl.ds(start, part), :]
-
-
-def total_kernel(*refs):
-    total = refs[0][...].astype(F32)
-    for ref in refs[1:-1]:
-        total = total + ref[...].astype(F32)
-    refs[-1][...] = total.astype(BF16)
 
 
 def attended_kernel(parts_ref, out_ref):
     columns = parts_ref.shape[2]
-    for t in range(parts_ref.shape[0]):
+    for t in range(4):
+        total = parts_ref[t].astype(F32)
+        for i in range(t + 4, parts_ref.shape[0], 4):
+            total = total + parts_ref[i].astype(F32)
         start = (2 * (t & 1) + (t >> 1)) * columns
-        out_ref[:, start : start + columns] = parts_ref[t]
-
-
-def columns_kernel(place_ref, own_ref, other_ref, out_ref, *, pairs):
-    rows, columns = own_ref.shape[1:]
-    core = place_ref[2]
-    for i in range(own_ref.shape[0]):
-        cols = slice(i // pairs * columns, (i // pairs + 1) * columns)
-        for ref, lane in ((own_ref, core), (other_ref, 1 - core)):
-            start = pl.multiple_of((i % pairs * 2 + lane) * rows, rows)
-            out_ref[pl.ds(start, rows), cols] = ref[i]
+        out_ref[:, start : start + columns] = total.astype(BF16)
+
+
+def columns_kernel(place_ref, *refs):
+    out_ref = refs[-1]
+    columns = refs[0].shape[1]
+    for k, ref in enumerate(refs[:-1]):
+        start = pl.multiple_of((place_ref[0] ^ k) * columns, columns)
+        out_ref[:, pl.ds(start, columns)] = ref[...]
 
 
 def head_norm(projected, gain):
@@ -356,31 +350,24 @@
         frames, conv_weight, latent_t, name="late_frames", flops=10**9, places=["hbm"] * 3,
         scratch=[pltpu.VMEM(frames.shape, BF16), pltpu.SemaphoreType.DMA((4,))],
     )
-    by_column = call(
-        split_kernel, [(grp_size, block, columns)], cotangent[0], name="split_columns"
-    )
-    near = lax.all_to_all(by_column, "grp", 0, 0, tiled=True).reshape(shared, columns)
-    late, near = lax.optimization_barrier((late, near))
     sums = call(
         functools.partial(sums_kernel, grp=grp_size, seq=seq_size), [(groups, LANES)],
         first, earlier, taps, latent_rhs, late, assign[0], name="group_sums", flops=10**9,
     )
-    near_other = xor_swap(near, "seq", 8)
 
     parts = lax.all_to_all(sums.reshape(seq_size, shared, LANES), "seq", 0, 0, tiled=True)
-    slab_sums = call(resplit_kernel, [(grp_size, shared, LANES)], parts, name="slab_sums")
-    near = jnp.concatenate([near, near_other], axis=0)
-    near, slab_sums = lax.optimization_barrier((near, slab_sums))
-    near_other = xor_swap(near, "seq", 4)
+    carried = shared + columns // LANES * block
+    slab_sums = call(
+        resplit_kernel, [(grp_size, carried, LANES)], parts, cotangent[0], name="slab_sums"
+    )
     slab_parts = lax.all_to_all(slab_sums, "grp", 0, 0, tiled=True)
     merged = call(merge_kernel, [(seq_size, shared, LANES)], slab_parts, name="merged")
-    near_other, merged = lax.optimization_barrier((near_other, merged))
-    near = jnp.concatenate([near, near_other], axis=0)
-    far = xor_swap(near, "seq", 2)
-    weight, _ = lax.optimization_barrier((out_weight, merged))
-    given = lax.dynamic_slice_in_dim(weight, (1 - (seq & 1)) * (width // 2), width // 2, 1)
-    weight_other = xor_swap(given, "seq", 1)
     merged = lax.all_to_all(merged, "seq", 0, 0, tiled=True).reshape(groups, LANES)
+    slabs = seq_size // 2
+    near = call(near_kernel, [(slabs, shared, columns)], slab_parts, name="near_rows")
+    near, merged = lax.optimization_barrier((near, merged))
+    same_side = [list(range(k, seq_size, 2)) for k in range(2)]
+    grad_rows = lax.all_to_all(near, "seq", 0, 0, axis_index_groups=same_side, tiled=True)
 
     head_out, own_rows, given_rows = call(
         functools.partial(attend_kernel, grp_size=grp_size, block=block),
@@ -390,21 +377,18 @@
         scratch=[pltpu.VMEM((width, 2 * head), BF16)] + [pltpu.VMEM((groups, head), BF16)] * 3,
     )
 
-    given_rows, weight_other = lax.optimization_barrier((given_rows, weight_other))
     side_rows = xor_swap(given_rows, "seq", 1)
-    near_weight, given = call(
-        weights_kernel, [(2 * head, columns)] * 2, place, out_weight, weight_other,
-        name="weights", places=["smem"],
-    )
-    far_weight = xor_swap(given, "seq", 2)
+    side_rows, weight = lax.optimization_barrier((side_rows, out_weight))
+    given = lax.dynamic_slice_in_dim(weight, (1 - (seq & 1)) * (width // 2), width // 2, 1)
+    weight_other = xor_swap(given, "seq", 1)
     local_grad = call(
-        functools.partial(grad_kernel, masks=(8, 4, 2), part=shared), [(2, head, columns)],
-        place, head_out, side_rows, near, far, name="local_grad", places=["smem"],
+        grad_kernel, [(2, head, columns)], place, head_out, side_rows, grad_rows,
+        name="local_grad", places=["smem"],
         scratch=[pltpu.VMEM((groups // 2, 2 * head), BF16)], flops=10**9,
     )
     both_sides = [
         [(2 * z + y) * dp_size + d for y in range(2) for d in range(dp_size)]
-        for z in range(seq_size // 2)
+        for z in range(slabs)
     ]
     grad_parts = lax.all_to_all(
         local_grad.reshape(2 * dp_size, head // dp_size, columns), ("seq", "dp"), 0, 0,
@@ -415,34 +399,26 @@
         side_rows, name="pair_heads", places=["smem"],
     )
     far_heads = xor_swap(pair_heads, "seq", 2)
-
-    partials = call(
-        project_kernel, [(rows // 4, columns)] * 4, place, pair_heads, far_heads, near_weight,
-        far_weight, name="project", flops=10**9, places=["smem"],
-        scratch=[pltpu.VMEM((rows, columns), BF16)],
-    )
-    pairs = dp_size // 2
+    near_weight, given = call(
+        weights_kernel, [(2 * head, columns)] * 2, place, weight, weight_other, name="weights",
+        places=["smem"],
+    )
+    far_weight = xor_swap(given, "seq", 2)
     grad_block = call(
-        spread_kernel, [(grp_size * pairs, head // dp_size, columns)], grad_parts,
-        name="grad_block",
-    )
-    grad_block, *partials = lax.optimization_barrier((grad_block, *partials))
-    same_core = [
-        [g * dp_size + 2 * p + c for g in range(grp_size) for p in range(pairs)] for c in range(2)
-    ]
-    grad_cols = lax.all_to_all(
-        grad_block, ("grp", "dp"), 0, 0, axis_index_groups=same_core, tiled=True
-    )
-    partials = [partials[0]] + [xor_swap(partials[k], "seq", 4 * k) for k in range(1, 4)]
-    projected = call(total_kernel, [(rows // 4, columns)], *partials, name="projected")
-    projected, _ = lax.optimization_barrier((projected, grad_cols))
-    quads = [list(range(k, k + 4)) for k in range(0, seq_size, 4)]
+        spread_kernel, [(dp_size, head // dp_size, columns)], grad_parts, name="grad_block"
+    )
+    grad_cols = lax.all_to_all(grad_block, "dp", 0, 0, tiled=True).reshape(head, columns)
+    partial = call(
+        project_kernel, [(rows, columns)], pair_heads, far_heads, near_weight, far_weight,
+        name="project", flops=10**9,
+    )
+    partial, grad_cols = lax.optimization_barrier((partial, grad_cols))
     out_parts = lax.all_to_all(
-        projected.reshape(4, block, columns), "seq", 0, 0, axis_index_groups=quads, tiled=True
-    )
+        partial.reshape(seq_size, block, columns), "seq", 0, 0, tiled=True
+    )
+    gathered = [grad_cols] + [xor_swap(grad_cols, "grp", k) for k in range(1, grp_size)]
     out_grad = call(
-        functools.partial(columns_kernel, pairs=pairs), [(head, width)], place, grad_cols,
-        xor_swap(grad_cols, "dp", 1), name="grad_columns", places=["smem"],
+        columns_kernel, [(head, width)], place, *gathered, name="grad_columns", places=["smem"]
     )
     attended = call(attended_kernel, [(block, width)], out_parts, name="attended")
     return (attended[None], out_grad)

time: 174 us -> 157 us (0.902)
  starting transfers between devices: 81.6 us -> 58.4 us
  waiting for transfers between devices: 32.3 us -> 39.7 us
    ppermute x11 -> x7, starting transfers between devices: 40 us -> 20.9 us  [xor_swap(): return lax.ppermute(block, axis, route)]
    all_to_all x1, waiting for transfers between devices: 2.2 us -> 7.98 us  [shards(): lax.all_to_all(merged, 'seq', 0, 0, tiled=True).reshape(groups, LANES)]
    ppermute x11 -> x7, waiting for transfers between devices: 25.2 us -> 28.6 us  [xor_swap(): return lax.ppermute(block, axis, route)]
    all_to_all x3, starting transfers between devices: 19.4 us -> 16.5 us  [the longest x1 6.89 us: shards(): lax.all_to_all(grad_block, 'dp', 0, 0, tiled=True).reshape(head, columns)]
    all_to_all x3, waiting for transfers between devices: 4.95 us -> 3.12 us  [the longest x1 1.88 us: shards(): lax.all_to_all(near, 'seq', 0, 0, axis_index_groups=same_side, tiled=True)]
    unnamed x23 -> x22, local copies, waits for them, and re-layouts: 5.36 us -> 4.47 us
    pallas_call x14 -> x13, Pallas kernels: 21.2 us -> 21.1 us  [call(): pl.pallas_call(body, out_shape=outs, in_specs=in_specs, out_specs=(whole,...]
  transfers between devices with their start and end apart: 17 -> 13, of which waited for: 9 -> 8; matrix products, arithmetic and copies ran while one was open for 0% -> 0% of each run, Pallas kernels for 9% -> 11%
where the time goes in v8:
time: 157 us; the launch traced here: 154 us
  starting transfers between devices  58.4 us (37%)
  waiting for transfers between devices  39.7 us (25%)
  blocking collectives  28.9 us (18%)
  Pallas kernels  21.1 us (13%)
  local copies, waits for them, and re-layouts  5.43 us (3%)
    ppermute x7, waiting for transfers between devices, xor_swap(): return lax.ppermute(block, axis, route)  28.6 us
    pallas_call x13, Pallas kernels, call(): pl.pallas_call(body, out_shape=outs, in_specs=in_specs, out_specs=(whole,...  21.1 us
    ppermute x7, starting transfers between devices, xor_swap(): return lax.ppermute(block, axis, route)  20.9 us
    all_to_all x1, blocking collectives, shards(): lax.all_to_all(sums.reshape(seq_size, shared, LANES), 'seq', 0, 0, tiled=...  20.1 us
    all_to_all x1, starting transfers between devices, shards(): lax.all_to_all(local_grad.reshape(2 * dp_size, head // dp_size, columns),...  11.4 us
    all_to_all x1, blocking collectives, shards(): slab_parts = lax.all_to_all(slab_sums, 'grp', 0, 0, tiled=True)  8.82 us
    all_to_all x1, waiting for transfers between devices, shards(): lax.all_to_all(merged, 'seq', 0, 0, tiled=True).reshape(groups, LANES)  7.98 us
    all_to_all x1, starting transfers between devices, shards(): lax.all_to_all(grad_block, 'dp', 0, 0, tiled=True).reshape(head, columns)  6.89 us
  transfers between devices with their start and end apart: 13, of which 8 were waited for; matrix products, arithmetic and copies ran while one was open for 0% of the time, Pallas kernels for 11%

profile of v8, /device:TPU:1, one launch (start us, length us, event | category | flops | bytes accessed | tf_op | source)
XLA Modules:
  0.0 154.5 jit_solution(4002422041863483915)
XLA Ops:
  0.6 0.9 slice_bitcast_fusion
  1.6 4.0 %collective-permute-start = (bf16[2,64,512]{2,1,0:T(8,128)(2,1)S(1)}, bf16[2,64,512]{2,1,0:T(8,128)(2,1)S(1)}, u32[]{:S(2)}, u32[]{:S(2)}) collective-permute-start(bf16[2,64,512]{2,1,0:T(8,128)(2,1)S(1)} %slice_bitcast_fusion), channel_id=1, source_target_pairs={{0,8},{8,16},{16,24},{24,32},{32,40},{40,48},{48,56},{56,64},{64,7... | collective-permute-start | bytes 393224 | tf_op jit(solution)/shard_map/ppermute | solution.py:22
  5.6 0.0 copy-start.2
  5.6 1.0 copy-done.2
  6.7 0.9 copy-done.5
  7.5 0.8 copy-done.6
  8.4 1.4 late_frames.1
  9.8 0.0 copy-start.1
  9.8 0.9 group_sums.1
  10.7 0.0 copy-start.4
  10.7 0.0 copy-start.7
  10.7 0.0 copy-start.9
  10.7 0.0 copy-start.10
  10.8 20.1 %all_to_all.35.parts_ref = bf16[16,64,128]{2,1,0:T(8,128)(2,1)S(1)} all-to-all(bf16[16,64,128]{2,1,0:T(8,128)(2,1)S(1)} %bitcast.23), channel_id=1, replica_groups=mesh['grp'=4,'seq'=16,'dp'=8] {'seq'}, dimensions={0} | all-to-all | bytes 524288 | tf_op jit(solution)/shard_map/all_to_all | solution.py:358
  30.8 0.2 slab_sums.1
  31.0 8.8 %all_to_all.36.parts_ref = bf16[4,160,128]{2,1,0:T(8,128)(2,1)S(1)} all-to-all(bf16[4,160,128]{2,1,0:T(8,128)(2,1)S(1)} %slab_sums.1), channel_id=1, replica_groups=mesh['grp'=4,'seq'=16,'dp'=8] {'grp'}, dimensions={0} | all-to-all | bytes 327680 | tf_op jit(solution)/shard_map/all_to_all | solution.py:363
  39.8 0.9 merged.1
  40.7 5.5 %all-to-all-start.2 = ((bf16[16,64,128]{2,1,0:T(8,128)(2,1)}), bf16[16,64,128]{2,1,0:T(8,128)(2,1)S(1)}, u32[]{:S(2)}, u32[]{:S(2)}) async-start(bf16[16,64,128]{2,1,0:T(8,128)(2,1)} %merged.1), calls=%async_computation.2 | async-start | bytes 524288 | tf_op jit(solution)/shard_map/all_to_all | solution.py:365
  46.2 1.0 near_rows.1
  47.2 8.0 %all-to-all-done.2 = bf16[16,64,128]{2,1,0:T(8,128)(2,1)S(1)} async-done(((bf16[16,64,128]{2,1,0:T(8,128)(2,1)}), bf16[16,64,128]{2,1,0:T(8,128)(2,1)S(1)}, u32[]{:S(2)}, u32[]{:S(2)}) %all-to-all-start.2) | async-done | bytes 262176 | tf_op jit(solution)/shard_map/all_to_all | solution.py:365
  55.2 3.5 %all-to-all-start.3 = ((bf16[8,64,768]{2,1,0:T(8,128)(2,1)}), bf16[8,64,768]{2,1,0:T(8,128)(2,1)S(1)}, u32[]{:S(2)}, u32[]{:S(2)}) async-start(bf16[8,64,768]{2,1,0:T(8,128)(2,1)} %near_rows.1), calls=%async_computation.3 | async-start | bytes 1572864 | tf_op jit(solution)/shard_map/all_to_all | solution.py:370
  58.8 0.1 pad_add_fusion.place_ref
  58.9 1.7 %copy-done.3 = bf16[3,3072,128]{2,1,0:T(8,128)(2,1)S(1)} copy-done((bf16[3,3072,128]{2,1,0:T(8,128)(2,1)S(1)}, bf16[3,3072,128]{2,1,0:T(8,128)(2,1)}, u32[]{:S(2)}) %copy-start.3) | copy-done | bytes 2359320
  60.5 9.8 %attend.1 = (bf16[1024,128]{1,0:T(8,128)(2,1)S(1)}, bf16[256,128]{1,0:T(8,128)(2,1)S(1)}, bf16[640,128]{1,0:T(8,128)(2,1)S(1)}) custom-call(s32[3]{0:T(128)S(1)} %pad_add_fusion.place_ref, bf16[1024,128]{1,0:T(8,128)(2,1)S(1)} %bitcast.22, bf16[64,3072]{1,0:T(8,128)(2,1)S(1)} %copy-done.4, f32[1,3072]{1,0:T(1,128)S(1)} %bitcast.27, ...), custom_call_target="tpu_custom_call" | custom-call | flops 8000000000 | bytes 1000000 | tf_op jit(solution)/shard_map/attend/pallas_call | solution.py:313
  70.4 3.4 %collective-permute-start.1 = (bf16[640,128]{1,0:T(8,128)(2,1)S(1)}, bf16[640,128]{1,0:T(8,128)(2,1)S(1)}, u32[]{:S(2)}, u32[]{:S(2)}) collective-permute-start(bf16[640,128]{1,0:T(8,128)(2,1)S(1)} %get-tuple-element.23), channel_id=1, source_target_pairs={{0,8},{8,0},{16,24},{24,16},{32,40},{40,32},{48,56},{56,48},{64,72... | collective-permute-start | bytes 491528 | tf_op jit(solution)/shard_map/ppermute | solution.py:27
  73.8 3.0 %collective-permute-done.1.given_ref = bf16[640,128]{1,0:T(8,128)(2,1)S(1)} collective-permute-done((bf16[640,128]{1,0:T(8,128)(2,1)S(1)}, bf16[640,128]{1,0:T(8,128)(2,1)S(1)}, u32[]{:S(2)}, u32[]{:S(2)}) %collective-permute-start.1) | collective-permute-done | bytes 163872 | tf_op jit(solution)/shard_map/ppermute | solution.py:27
  76.8 1.9 %all-to-all-done.3.cot_ref = bf16[8,64,768]{2,1,0:T(8,128)(2,1)S(1)} async-done(((bf16[8,64,768]{2,1,0:T(8,128)(2,1)}), bf16[8,64,768]{2,1,0:T(8,128)(2,1)S(1)}, u32[]{:S(2)}, u32[]{:S(2)}) %all-to-all-start.3) | async-done | bytes 786464 | tf_op jit(solution)/shard_map/all_to_all | solution.py:370
  78.7 1.7 %local_grad.1 = bf16[2,128,768]{2,1,0:T(8,128)(2,1)} custom-call(s32[3]{0:T(128)S(1)} %pad_add_fusion.place_ref, bf16[1024,128]{1,0:T(8,128)(2,1)S(1)} %get-tuple-element.28.head_ref, bf16[640,128]{1,0:T(8,128)(2,1)S(1)} %collective-permute-done.1.given_ref, bf16[8,64,768]{2,1,0:T(8,128)(2,1)S(1)} %all-to-all-done.3.cot_ref), custom_call_target="tpu_custom_call" | custom-call | flops 1000000000 | bytes 1000000 | tf_op jit(solution)/shard_map/local_grad/pallas_call | solution.py:313
  80.4 11.4 %all-to-all-start.4 = ((bf16[16,16,768]{2,1,0:T(8,128)(2,1)}), bf16[16,16,768]{2,1,0:T(8,128)(2,1)S(1)}, u32[]{:S(2)}, u32[]{:S(2)}) async-start(bf16[16,16,768]{2,1,0:T(8,128)(2,1)} %bitcast.13), calls=%async_computation.4 | async-start | bytes 786432 | tf_op jit(solution)/shard_map/all_to_all | solution.py:393
  91.9 3.3 %collective-permute-start.3 = (bf16[128,1536]{1,0:T(8,128)(2,1)S(1)}, bf16[128,1536]{1,0:T(8,128)(2,1)S(1)}, u32[]{:S(2)}, u32[]{:S(2)}) collective-permute-start(bf16[128,1536]{1,0:T(8,128)(2,1)S(1)} %constant_dynamic-slice_fusion), channel_id=1, source_target_pairs={{0,8},{8,0},{16,24},{24,16},{32,40},{40,32},{48,56},{56,48},{64,72... | collective-permute-start | bytes 1179656 | tf_op jit(solution)/shard_map/ppermute | solution.py:27
  95.2 15.9 %collective-permute-done.3.partner_ref = bf16[128,1536]{1,0:T(8,128)(2,1)S(1)} collective-permute-done((bf16[128,1536]{1,0:T(8,128)(2,1)S(1)}, bf16[128,1536]{1,0:T(8,128)(2,1)S(1)}, u32[]{:S(2)}, u32[]{:S(2)}) %collective-permute-start.3) | collective-permute-done | bytes 393248 | tf_op jit(solution)/shard_map/ppermute | solution.py:27
  111.0 0.6 weights.1
  111.6 2.3 %collective-permute-start.4 = (bf16[256,768]{1,0:T(8,128)(2,1)S(1)}, bf16[256,768]{1,0:T(8,128)(2,1)S(1)}, u32[]{:S(2)}, u32[]{:S(2)}) collective-permute-start(bf16[256,768]{1,0:T(8,128)(2,1)S(1)} %get-tuple-element.27), channel_id=1, source_target_pairs={{0,16},{8,24},{16,0},{24,8},{32,48},{40,56},{48,32},{56,40},{64,80... | collective-permute-start | bytes 1179656 | tf_op jit(solution)/shard_map/ppermute | solution.py:27
  113.9 0.7 grad_block.1
  114.7 6.9 %all-to-all-start.5 = ((bf16[8,16,768]{2,1,0:T(8,128)(2,1)}), bf16[8,16,768]{2,1,0:T(8,128)(2,1)S(1)}, u32[]{:S(2)}, u32[]{:S(2)}) async-start(bf16[8,16,768]{2,1,0:T(8,128)(2,1)} %grad_block.1), calls=%async_computation.5 | async-start | bytes 393216 | tf_op jit(solution)/shard_map/all_to_all | solution.py:410
  121.6 0.6 pair_heads.1.near_ref
  122.2 3.0 %collective-permute-start.2 = (bf16[2,256,128]{2,1,0:T(8,128)(2,1)S(1)}, bf16[2,256,128]{2,1,0:T(8,128)(2,1)S(1)}, u32[]{:S(2)}, u32[]{:S(2)}) collective-permute-start(bf16[2,256,128]{2,1,0:T(8,128)(2,1)S(1)} %pair_heads.1.near_ref), channel_id=1, source_target_pairs={{0,16},{8,24},{16,0},{24,8},{32,48},{40,56},{48,32},{56,40},{64,80... | collective-permute-start | bytes 393224 | tf_op jit(solution)/shard_map/ppermute | solution.py:27
  125.1 4.0 %collective-permute-done.2.far_ref = bf16[2,256,128]{2,1,0:T(8,128)(2,1)S(1)} collective-permute-done((bf16[2,256,128]{2,1,0:T(8,128)(2,1)S(1)}, bf16[2,256,128]{2,1,0:T(8,128)(2,1)S(1)}, u32[]{:S(2)}, u32[]{:S(2)}) %collective-permute-start.2) | collective-permute-done | bytes 131104 | tf_op jit(solution)/shard_map/ppermute | solution.py:27
  129.2 1.1 project.1
  130.3 1.2 all-to-all-done.5
  131.5 6.0 %all-to-all-start.6 = ((bf16[16,16,768]{2,1,0:T(8,128)(2,1)}), bf16[16,16,768]{2,1,0:T(8,128)(2,1)S(1)}, u32[]{:S(2)}, u32[]{:S(2)}) async-start(bf16[16,16,768]{2,1,0:T(8,128)(2,1)} %bitcast.15), calls=%async_computation.6 | async-start | bytes 786432 | tf_op jit(solution)/shard_map/all_to_all | solution.py:416
  137.6 2.8 %collective-permute-start.7 = (bf16[128,768]{1,0:T(8,128)(2,1)S(1)}, bf16[128,768]{1,0:T(8,128)(2,1)S(1)}, u32[]{:S(2)}, u32[]{:S(2)}) collective-permute-start(bf16[128,768]{1,0:T(8,128)(2,1)S(1)} %bitcast.18), channel_id=1, source_target_pairs={{0,384},{128,256},{256,128},{384,0},{1,385},{129,257},{257,129},{3... | collective-permute-start | bytes 589832 | tf_op jit(solution)/shard_map/ppermute | solution.py:27
  140.4 3.1 %collective-permute-start.6 = (bf16[128,768]{1,0:T(8,128)(2,1)S(1)}, bf16[128,768]{1,0:T(8,128)(2,1)S(1)}, u32[]{:S(2)}, u32[]{:S(2)}) collective-permute-start(bf16[128,768]{1,0:T(8,128)(2,1)S(1)} %bitcast.19), channel_id=1, source_target_pairs={{0,256},{128,384},{256,0},{384,128},{1,257},{129,385},{257,1},{385... | collective-permute-start | bytes 589832 | tf_op jit(solution)/shard_map/ppermute | solution.py:27
  143.5 3.1 %collective-permute-start.5 = (bf16[128,768]{1,0:T(8,128)(2,1)S(1)}, bf16[128,768]{1,0:T(8,128)(2,1)S(1)}, u32[]{:S(2)}, u32[]{:S(2)}) collective-permute-start(bf16[128,768]{1,0:T(8,128)(2,1)S(1)} %bitcast.20), channel_id=1, source_target_pairs={{0,128},{128,0},{256,384},{384,256},{1,129},{129,1},{257,385},{385... | collective-permute-start | bytes 589832 | tf_op jit(solution)/shard_map/ppermute | solution.py:27
  146.6 1.8 %collective-permute-done.6.refs_2_ = bf16[128,768]{1,0:T(8,128)(2,1)S(1)} collective-permute-done((bf16[128,768]{1,0:T(8,128)(2,1)S(1)}, bf16[128,768]{1,0:T(8,128)(2,1)S(1)}, u32[]{:S(2)}, u32[]{:S(2)}) %collective-permute-start.6) | collective-permute-done | bytes 196640 | tf_op jit(solution)/shard_map/ppermute | solution.py:27
  148.4 3.9 %collective-permute-done.5.refs_1_ = bf16[128,768]{1,0:T(8,128)(2,1)S(1)} collective-permute-done((bf16[128,768]{1,0:T(8,128)(2,1)S(1)}, bf16[128,768]{1,0:T(8,128)(2,1)S(1)}, u32[]{:S(2)}, u32[]{:S(2)}) %collective-permute-start.5) | collective-permute-done | bytes 196640 | tf_op jit(solution)/shard_map/ppermute | solution.py:27
  152.3 1.5 grad_columns.1
  153.8 0.7 attended.1
  (18 shorter events, 0.1 us)
Async XLA Ops:
  0.6 9.2 %copy-start.8 = (s32[1,8,64]{2,1,0:T(8,128)S(1)}, s32[1,8,64]{2,1,0:T(8,128)}, u32[]{:S(2)}) copy-start(s32[1,8,64]{2,1,0:T(8,128)} %param.14) | copy-start | bytes 6148
  1.6 8.2 %collective-permute-start = (bf16[2,64,512]{2,1,0:T(8,128)(2,1)S(1)}, bf16[2,64,512]{2,1,0:T(8,128)(2,1)S(1)}, u32[]{:S(2)}, u32[]{:S(2)}) collective-permute-start(bf16[2,64,512]{2,1,0:T(8,128)(2,1)S(1)} %slice_bitcast_fusion), channel_id=1, source_target_pairs={{0,8},{8,16},{16,24},{24,32},{32,40},{40,48},{48,56},{56,64},{64,7... | collective-permute-start | bytes 393224 | tf_op jit(solution)/shard_map/ppermute | solution.py:22
  5.6 1.0 copy-start.2
  6.7 0.9 copy-start.5
  7.5 0.8 copy-start.6
  9.8 21.0 %copy-start.1 = (bf16[1,16,3072]{2,1,0:T(8,128)(2,1)S(1)}, bf16[1,16,3072]{2,1,0:T(8,128)(2,1)}, u32[]{:S(2)}) copy-start(bf16[1,16,3072]{2,1,0:T(8,128)(2,1)} %param.21) | copy-start | bytes 294916
  10.7 48.1 %copy-start.4 = (bf16[64,3072]{1,0:T(8,128)(2,1)S(1)}, bf16[64,3072]{1,0:T(8,128)(2,1)}, u32[]{:S(2)}) copy-start(bf16[64,3072]{1,0:T(8,128)(2,1)} %embed_ref.1) | copy-start | bytes 1179652
  10.7 48.1 %copy-start.7 = (f32[3072]{0:T(1024)S(1)}, f32[3072]{0:T(1024)}, u32[]{:S(2)}) copy-start(f32[3072]{0:T(1024)} %param.16) | copy-start | bytes 36868
  10.7 48.1 %copy-start.9 = (f32[128]{0:T(128)S(1)}, f32[128]{0:T(128)}, u32[]{:S(2)}) copy-start(f32[128]{0:T(128)} %param.18) | copy-start | bytes 1540
  10.7 48.1 %copy-start.10 = (f32[128]{0:T(128)S(1)}, f32[128]{0:T(128)}, u32[]{:S(2)}) copy-start(f32[128]{0:T(128)} %param.19) | copy-start | bytes 1540
  40.7 14.5 %all-to-all-start.2 = ((bf16[16,64,128]{2,1,0:T(8,128)(2,1)}), bf16[16,64,128]{2,1,0:T(8,128)(2,1)S(1)}, u32[]{:S(2)}, u32[]{:S(2)}) async-start(bf16[16,64,128]{2,1,0:T(8,128)(2,1)} %merged.1), calls=%async_computation.2 | async-start | bytes 524288 | tf_op jit(solution)/shard_map/all_to_all | solution.py:365
  55.2 23.5 %all-to-all-start.3 = ((bf16[8,64,768]{2,1,0:T(8,128)(2,1)}), bf16[8,64,768]{2,1,0:T(8,128)(2,1)S(1)}, u32[]{:S(2)}, u32[]{:S(2)}) async-start(bf16[8,64,768]{2,1,0:T(8,128)(2,1)} %near_rows.1), calls=%async_computation.3 | async-start | bytes 1572864 | tf_op jit(solution)/shard_map/all_to_all | solution.py:370
  58.9 1.7 %copy-start.3 = (bf16[3,3072,128]{2,1,0:T(8,128)(2,1)S(1)}, bf16[3,3072,128]{2,1,0:T(8,128)(2,1)}, u32[]{:S(2)}) copy-start(bf16[3,3072,128]{2,1,0:T(8,128)(2,1)} %qkv_ref.1) | copy-start | bytes 7077892
  70.4 21.5 %copy-start = (bf16[128,3072]{1,0:T(8,128)(2,1)S(1)}, bf16[128,3072]{1,0:T(8,128)(2,1)}, u32[]{:S(2)}) copy-start(bf16[128,3072]{1,0:T(8,128)(2,1)} %weight_ref) | copy-start | bytes 2359300
  70.4 6.4 %collective-permute-start.1 = (bf16[640,128]{1,0:T(8,128)(2,1)S(1)}, bf16[640,128]{1,0:T(8,128)(2,1)S(1)}, u32[]{:S(2)}, u32[]{:S(2)}) collective-permute-start(bf16[640,128]{1,0:T(8,128)(2,1)S(1)} %get-tuple-element.23), channel_id=1, source_target_pairs={{0,8},{8,0},{16,24},{24,16},{32,40},{40,32},{48,56},{56,48},{64,72... | collective-permute-start | bytes 491528 | tf_op jit(solution)/shard_map/ppermute | solution.py:27
  80.4 33.5 %all-to-all-start.4 = ((bf16[16,16,768]{2,1,0:T(8,128)(2,1)}), bf16[16,16,768]{2,1,0:T(8,128)(2,1)S(1)}, u32[]{:S(2)}, u32[]{:S(2)}) async-start(bf16[16,16,768]{2,1,0:T(8,128)(2,1)} %bitcast.13), calls=%async_computation.4 | async-start | bytes 786432 | tf_op jit(solution)/shard_map/all_to_all | solution.py:393
  91.9 19.2 %collective-permute-start.3 = (bf16[128,1536]{1,0:T(8,128)(2,1)S(1)}, bf16[128,1536]{1,0:T(8,128)(2,1)S(1)}, u32[]{:S(2)}, u32[]{:S(2)}) collective-permute-start(bf16[128,1536]{1,0:T(8,128)(2,1)S(1)} %constant_dynamic-slice_fusion), channel_id=1, source_target_pairs={{0,8},{8,0},{16,24},{24,16},{32,40},{40,32},{48,56},{56,48},{64,72... | collective-permute-start | bytes 1179656 | tf_op jit(solution)/shard_map/ppermute | solution.py:27
  111.6 17.6 %collective-permute-start.4 = (bf16[256,768]{1,0:T(8,128)(2,1)S(1)}, bf16[256,768]{1,0:T(8,128)(2,1)S(1)}, u32[]{:S(2)}, u32[]{:S(2)}) collective-permute-start(bf16[256,768]{1,0:T(8,128)(2,1)S(1)} %get-tuple-element.27), channel_id=1, source_target_pairs={{0,16},{8,24},{16,0},{24,8},{32,48},{40,56},{48,32},{56,40},{64,80... | collective-permute-start | bytes 1179656 | tf_op jit(solution)/shard_map/ppermute | solution.py:27
  114.7 16.9 %all-to-all-start.5 = ((bf16[8,16,768]{2,1,0:T(8,128)(2,1)}), bf16[8,16,768]{2,1,0:T(8,128)(2,1)S(1)}, u32[]{:S(2)}, u32[]{:S(2)}) async-start(bf16[8,16,768]{2,1,0:T(8,128)(2,1)} %grad_block.1), calls=%async_computation.5 | async-start | bytes 393216 | tf_op jit(solution)/shard_map/all_to_all | solution.py:410
  122.2 7.0 %collective-permute-start.2 = (bf16[2,256,128]{2,1,0:T(8,128)(2,1)S(1)}, bf16[2,256,128]{2,1,0:T(8,128)(2,1)S(1)}, u32[]{:S(2)}, u32[]{:S(2)}) collective-permute-start(bf16[2,256,128]{2,1,0:T(8,128)(2,1)S(1)} %pair_heads.1.near_ref), channel_id=1, source_target_pairs={{0,16},{8,24},{16,0},{24,8},{32,48},{40,56},{48,32},{56,40},{64,80... | collective-permute-start | bytes 393224 | tf_op jit(solution)/shard_map/ppermute | solution.py:27
  131.5 22.2 %all-to-all-start.6 = ((bf16[16,16,768]{2,1,0:T(8,128)(2,1)}), bf16[16,16,768]{2,1,0:T(8,128)(2,1)S(1)}, u32[]{:S(2)}, u32[]{:S(2)}) async-start(bf16[16,16,768]{2,1,0:T(8,128)(2,1)} %bitcast.15), calls=%async_computation.6 | async-start | bytes 786432 | tf_op jit(solution)/shard_map/all_to_all | solution.py:416
  137.6 9.0 %collective-permute-start.7 = (bf16[128,768]{1,0:T(8,128)(2,1)S(1)}, bf16[128,768]{1,0:T(8,128)(2,1)S(1)}, u32[]{:S(2)}, u32[]{:S(2)}) collective-permute-start(bf16[128,768]{1,0:T(8,128)(2,1)S(1)} %bitcast.18), channel_id=1, source_target_pairs={{0,384},{128,256},{256,128},{384,0},{1,385},{129,257},{257,129},{3... | collective-permute-start | bytes 589832 | tf_op jit(solution)/shard_map/ppermute | solution.py:27
  140.4 8.0 %collective-permute-start.6 = (bf16[128,768]{1,0:T(8,128)(2,1)S(1)}, bf16[128,768]{1,0:T(8,128)(2,1)S(1)}, u32[]{:S(2)}, u32[]{:S(2)}) collective-permute-start(bf16[128,768]{1,0:T(8,128)(2,1)S(1)} %bitcast.19), channel_id=1, source_target_pairs={{0,256},{128,384},{256,0},{384,128},{1,257},{129,385},{257,1},{385... | collective-permute-start | bytes 589832 | tf_op jit(solution)/shard_map/ppermute | solution.py:27
  143.5 8.8 %collective-permute-start.5 = (bf16[128,768]{1,0:T(8,128)(2,1)S(1)}, bf16[128,768]{1,0:T(8,128)(2,1)S(1)}, u32[]{:S(2)}, u32[]{:S(2)}) collective-permute-start(bf16[128,768]{1,0:T(8,128)(2,1)S(1)} %bitcast.20), channel_id=1, source_target_pairs={{0,128},{128,0},{256,384},{384,256},{1,129},{129,1},{257,385},{385... | collective-permute-start | bytes 589832 | tf_op jit(solution)/shard_map/ppermute | solution.py:27

commit v9 on v8

--- a/solution.py
+++ b/solution.py
@@ -180,51 +180,39 @@
     out_ref[1 - side] = total[head:, :]
 
 
-def pair_kernel(place_ref, own_ref, given_ref, out_ref, *, part):
+def project_kernel(
+    place_ref, own_ref, given_ref, weight_ref, partner_ref, out_ref, heads_ref, *, part,
+):
     grp = place_ref[0]
     side = place_ref[1] & 1
-    rows = own_ref.shape[0]
+    rows, head = own_ref.shape
     slabs = (given_ref.shape[0] - rows // 2) // part
     block = rows // (2 * slabs)
-    out_ref[0] = own_ref[...]
+    heads_ref[:, :head] = own_ref[...]
     for i in range(slabs):
         near = pl.multiple_of((2 * i + side) * block, block)
         far = pl.multiple_of((2 * i + 1 - side) * block, block)
         start = pl.multiple_of(i * part + grp * block, block)
-        out_ref[1, pl.ds(near, block), :] = given_ref[pl.ds(start, block), :]
+        heads_ref[pl.ds(near, block), head:] = given_ref[pl.ds(start, block), :]
         first = slabs * part + i * block
-        out_ref[1, pl.ds(far, block), :] = given_ref[first : first + block, :]
-
-
-def weights_kernel(place_ref, weight_ref, partner_ref, kept_ref, given_ref):
-    columns = kept_ref.shape[1]
-    size = weight_ref.shape[0]
-    side = place_ref[1] & 1
-    depth = (place_ref[1] >> 1) & 1
-    for i, (ref, first) in enumerate([(weight_ref, 2 * side), (partner_ref, 0)]):
-        keep = pl.multiple_of((first + depth) * columns, columns)
-        give = pl.multiple_of((first + 1 - depth) * columns, columns)
-        kept_ref[i * size : (i + 1) * size, :] = ref[:, pl.ds(keep, columns)]
-        given_ref[i * size : (i + 1) * size, :] = ref[:, pl.ds(give, columns)]
-
-
-def project_kernel(near_ref, far_ref, near_weight_ref, far_weight_ref, out_ref):
-    near = jnp.concatenate([near_ref[0], near_ref[1]], axis=1)
-    far = jnp.concatenate([far_ref[0], far_ref[1]], axis=1)
-    out_ref[...] = (
-        jnp.dot(near, near_weight_ref[...], preferred_element_type=F32)
-        + jnp.dot(far, far_weight_ref[...], preferred_element_type=F32)
-    ).astype(BF16)
+        heads_ref[pl.ds(far, block), head:] = given_ref[first : first + block, :]
+    step = 768
+    for start in range(0, out_ref.shape[1], step):
+        here = slice(start, start + step)
+        kept = pl.multiple_of(side * out_ref.shape[1] + start, step)
+        weights = jnp.concatenate([weight_ref[:, pl.ds(kept, step)], partner_ref[:, here]], axis=0)
+        out_ref[:, here] = jnp.dot(
+            heads_ref[...], weights, preferred_element_type=F32
+        ).astype(BF16)
 
 
 def attended_kernel(parts_ref, out_ref):
     columns = parts_ref.shape[2]
-    for t in range(4):
-        total = parts_ref[t].astype(F32)
-        for i in range(t + 4, parts_ref.shape[0], 4):
+    for side in range(2):
+        total = parts_ref[side].astype(F32)
+        for i in range(side + 2, parts_ref.shape[0], 2):
             total = total + parts_ref[i].astype(F32)
-        start = (2 * (t & 1) + (t >> 1)) * columns
-        out_ref[:, start : start + columns] = total.astype(BF16)
+        out_ref[:, side * columns : (side + 1) * columns] = total.astype(BF16)
 
 
 def columns_kernel(place_ref, *refs):
@@ -362,6 +350,9 @@
     )
     slab_parts = lax.all_to_all(slab_sums, "grp", 0, 0, tiled=True)
     merged = call(merge_kernel, [(seq_size, shared, LANES)], slab_parts, name="merged")
+    merged, weight = lax.optimization_barrier((merged, out_weight))
+    given = lax.dynamic_slice_in_dim(weight, (1 - (seq & 1)) * (width // 2), width // 2, 1)
+    weight_other = xor_swap(given, "seq", 1)
     merged = lax.all_to_all(merged, "seq", 0, 0, tiled=True).reshape(groups, LANES)
     slabs = seq_size // 2
     near = call(near_kernel, [(slabs, shared, columns)], slab_parts, name="near_rows")
@@ -377,10 +368,8 @@
         scratch=[pltpu.VMEM((width, 2 * head), BF16)] + [pltpu.VMEM((groups, head), BF16)] * 3,
     )
 
+    given_rows, weight_other = lax.optimization_barrier((given_rows, weight_other))
     side_rows = xor_swap(given_rows, "seq", 1)
-    side_rows, weight = lax.optimization_barrier((side_rows, out_weight))
-    given = lax.dynamic_slice_in_dim(weight, (1 - (seq & 1)) * (width // 2), width // 2, 1)
-    weight_other = xor_swap(given, "seq", 1)
     local_grad = call(
         grad_kernel, [(2, head, columns)], place, head_out, side_rows, grad_rows,
         name="local_grad", places=["smem"],
@@ -394,27 +383,19 @@
         local_grad.reshape(2 * dp_size, head // dp_size, columns), ("seq", "dp"), 0, 0,
         axis_index_groups=both_sides, tiled=True,
     )
-    pair_heads = call(
-        functools.partial(pair_kernel, part=shared), [(2, rows, head)], place, own_rows,
-        side_rows, name="pair_heads", places=["smem"],
-    )
-    far_heads = xor_swap(pair_heads, "seq", 2)
-    near_weight, given = call(
-        weights_kernel, [(2 * head, columns)] * 2, place, weight, weight_other, name="weights",
-        places=["smem"],
-    )
-    far_weight = xor_swap(given, "seq", 2)
+    partial = call(
+        functools.partial(project_kernel, part=shared), [(rows, width // 2)], place, own_rows,
+        side_rows, out_weight, weight_other, name="project", flops=10**9, places=["smem"],
+        scratch=[pltpu.VMEM((rows, 2 * head), BF16)],
+    )
     grad_block = call(
         spread_kernel, [(dp_size, head // dp_size, columns)], grad_parts, name="grad_block"
     )
+    grad_block, partial = lax.optimization_barrier((grad_block, partial))
     grad_cols = lax.all_to_all(grad_block, "dp", 0, 0, tiled=True).reshape(head, columns)
-    partial = call(
-        project_kernel, [(rows, columns)], pair_heads, far_heads, near_weight, far_weight,
-        name="project", flops=10**9,
-    )
     partial, grad_cols = lax.optimization_barrier((partial, grad_cols))
     out_parts = lax.all_to_all(
-        partial.reshape(seq_size, block, columns), "seq", 0, 0, tiled=True
+        partial.reshape(seq_size, block, width // 2), "seq", 0, 0, tiled=True
     )
     gathered = [grad_cols] + [xor_swap(grad_cols, "grp", k) for k in range(1, grp_size)]
     out_grad = call(

time: 157 us -> 151 us (0.962)
  starting transfers between devices: 58.4 us -> 46.9 us
  blocking collectives: 28.9 us -> 40.3 us
  waiting for transfers between devices: 39.7 us -> 34.7 us
    ppermute x7 -> x5, waiting for transfers between devices: 28.6 us -> 8.48 us  [xor_swap(): return lax.ppermute(block, axis, route)]
    all_to_all x1, waiting for transfers between devices: 0.01 us -> 12.8 us  [shards(): lax.all_to_all(local_grad.reshape(2 * dp_size, head // dp_size, columns),...]
    all_to_all x0 -> x1, blocking collectives: none -> 11.3 us  [shards(): lax.all_to_all(grad_block, 'dp', 0, 0, tiled=True).reshape(head, columns)]
    ppermute x7 -> x5, starting transfers between devices: 20.9 us -> 14.2 us  [xor_swap(): return lax.ppermute(block, axis, route)]
    all_to_all x2 -> x1, starting transfers between devices: 12.9 us -> 7.22 us  [shards(): lax.all_to_all(partial.reshape(seq_size, block, width // 2), 'seq', 0, 0,...]
    all_to_all x2 -> x1, waiting for transfers between devices: 1.23 us -> 5.47 us  [shards(): lax.all_to_all(partial.reshape(seq_size, block, width // 2), 'seq', 0, 0,...]
    all_to_all x1, waiting for transfers between devices: 1.88 us -> 0.01 us  [shards(): lax.all_to_all(near, 'seq', 0, 0, axis_index_groups=same_side, tiled=True)]
    pallas_call x13 -> x11, Pallas kernels: 21.1 us -> 20 us  [call(): pl.pallas_call(body, out_shape=outs, in_specs=in_specs, out_specs=(whole,...]
  transfers between devices with their start and end apart: 13 -> 10, of which waited for: 8 -> 6; matrix products, arithmetic and copies ran while one was open for 0% -> 0% of each run, Pallas kernels for 11% -> 10%
where the time goes in v9:
time: 151 us; the launch traced here: 148 us
  starting transfers between devices  46.9 us (31%)
  blocking collectives  40.3 us (27%)
  waiting for transfers between devices  34.7 us (23%)
  Pallas kernels  20 us (13%)
  local copies, waits for them, and re-layouts  5.42 us (4%)
    all_to_all x1, blocking collectives, shards(): lax.all_to_all(sums.reshape(seq_size, shared, LANES), 'seq', 0, 0, tiled=...  20.1 us
    pallas_call x11, Pallas kernels, call(): pl.pallas_call(body, out_shape=outs, in_specs=in_specs, out_specs=(whole,...  20 us
    ppermute x5, starting transfers between devices, xor_swap(): return lax.ppermute(block, axis, route)  14.2 us
    all_to_all x1, waiting for transfers between devices, shards(): lax.all_to_all(local_grad.reshape(2 * dp_size, head // dp_size, columns),...  12.8 us
    all_to_all x1, starting transfers between devices, shards(): lax.all_to_all(local_grad.reshape(2 * dp_size, head // dp_size, columns),...  12.4 us
    all_to_all x1, blocking collectives, shards(): lax.all_to_all(grad_block, 'dp', 0, 0, tiled=True).reshape(head, columns)  11.3 us
    all_to_all x1, blocking collectives, shards(): slab_parts = lax.all_to_all(slab_sums, 'grp', 0, 0, tiled=True)  8.95 us
    ppermute x5, waiting for transfers between devices, xor_swap(): return lax.ppermute(block, axis, route)  8.48 us
  transfers between devices with their start and end apart: 10, of which 6 were waited for; matrix products, arithmetic and copies ran while one was open for 0% of the time, Pallas kernels for 10%

profile of v9, /device:TPU:1, one launch (start us, length us, event | category | flops | bytes accessed | tf_op | source)
XLA Modules:
  0.0 148.3 jit_solution(5996078666094152593)
XLA Ops:
  0.6 0.9 slice_bitcast_fusion
  1.6 4.0 %collective-permute-start = (bf16[2,64,512]{2,1,0:T(8,128)(2,1)S(1)}, bf16[2,64,512]{2,1,0:T(8,128)(2,1)S(1)}, u32[]{:S(2)}, u32[]{:S(2)}) collective-permute-start(bf16[2,64,512]{2,1,0:T(8,128)(2,1)S(1)} %slice_bitcast_fusion), channel_id=1, source_target_pairs={{0,8},{8,16},{16,24},{24,32},{32,40},{40,48},{48,56},{56,64},{64,7... | collective-permute-start | bytes 393224 | tf_op jit(solution)/shard_map/ppermute | solution.py:22
  5.6 0.0 copy-start.2
  5.6 1.0 copy-done.2
  6.7 0.9 copy-done.5
  7.5 0.8 copy-done.6
  8.4 1.4 late_frames.1
  9.8 0.0 copy-start.1
  9.8 0.0 collective-permute-done.earlier_ref
  9.8 0.9 group_sums.1
  10.7 0.0 copy-start
  10.7 20.1 %all_to_all.35.parts_ref = bf16[16,64,128]{2,1,0:T(8,128)(2,1)S(1)} all-to-all(bf16[16,64,128]{2,1,0:T(8,128)(2,1)S(1)} %bitcast.23), channel_id=1, replica_groups=mesh['grp'=4,'seq'=16,'dp'=8] {'seq'}, dimensions={0} | all-to-all | bytes 524288 | tf_op jit(solution)/shard_map/all_to_all | solution.py:346
  30.8 0.2 slab_sums.1
  31.0 0.0 copy-start.4
  31.0 0.0 copy-start.7
  31.0 0.0 copy-start.9
  31.0 0.0 copy-start.10
  31.0 8.9 %all_to_all.36.parts_ref = bf16[4,160,128]{2,1,0:T(8,128)(2,1)S(1)} all-to-all(bf16[4,160,128]{2,1,0:T(8,128)(2,1)S(1)} %slab_sums.1), channel_id=1, replica_groups=mesh['grp'=4,'seq'=16,'dp'=8] {'grp'}, dimensions={0} | all-to-all | bytes 327680 | tf_op jit(solution)/shard_map/all_to_all | solution.py:351
  40.0 0.9 merged.1
  40.9 5.5 %all-to-all-start.2 = ((bf16[16,64,128]{2,1,0:T(8,128)(2,1)}), bf16[16,64,128]{2,1,0:T(8,128)(2,1)S(1)}, u32[]{:S(2)}, u32[]{:S(2)}) async-start(bf16[16,64,128]{2,1,0:T(8,128)(2,1)} %merged.1), calls=%async_computation.2 | async-start | bytes 524288 | tf_op jit(solution)/shard_map/all_to_all | solution.py:356
  46.4 1.0 near_rows.1
  47.4 8.0 %all-to-all-done.2 = bf16[16,64,128]{2,1,0:T(8,128)(2,1)S(1)} async-done(((bf16[16,64,128]{2,1,0:T(8,128)(2,1)}), bf16[16,64,128]{2,1,0:T(8,128)(2,1)S(1)}, u32[]{:S(2)}, u32[]{:S(2)}) %all-to-all-start.2) | async-done | bytes 262176 | tf_op jit(solution)/shard_map/all_to_all | solution.py:356
  55.4 3.5 %all-to-all-start.3 = ((bf16[8,64,768]{2,1,0:T(8,128)(2,1)}), bf16[8,64,768]{2,1,0:T(8,128)(2,1)S(1)}, u32[]{:S(2)}, u32[]{:S(2)}) async-start(bf16[8,64,768]{2,1,0:T(8,128)(2,1)} %near_rows.1), calls=%async_computation.3 | async-start | bytes 1572864 | tf_op jit(solution)/shard_map/all_to_all | solution.py:361
  58.9 0.1 pad_add_fusion.place_ref
  59.0 3.3 %collective-permute-start.1 = (bf16[128,1536]{1,0:T(8,128)(2,1)S(1)}, bf16[128,1536]{1,0:T(8,128)(2,1)S(1)}, u32[]{:S(2)}, u32[]{:S(2)}) collective-permute-start(bf16[128,1536]{1,0:T(8,128)(2,1)S(1)} %constant_dynamic-slice_fusion), channel_id=1, source_target_pairs={{0,8},{8,0},{16,24},{24,16},{32,40},{40,32},{48,56},{56,48},{64,72... | collective-permute-start | bytes 1179656 | tf_op jit(solution)/shard_map/ppermute | solution.py:27
  62.4 0.0 copy-start.3
  62.4 1.7 %copy-done.3 = bf16[3,3072,128]{2,1,0:T(8,128)(2,1)S(1)} copy-done((bf16[3,3072,128]{2,1,0:T(8,128)(2,1)S(1)}, bf16[3,3072,128]{2,1,0:T(8,128)(2,1)}, u32[]{:S(2)}) %copy-start.3) | copy-done | bytes 2359320
  64.0 9.8 %attend.1 = (bf16[1024,128]{1,0:T(8,128)(2,1)S(1)}, bf16[256,128]{1,0:T(8,128)(2,1)S(1)}, bf16[640,128]{1,0:T(8,128)(2,1)S(1)}) custom-call(s32[3]{0:T(128)S(1)} %pad_add_fusion.place_ref, bf16[1024,128]{1,0:T(8,128)(2,1)S(1)} %bitcast.22, bf16[64,3072]{1,0:T(8,128)(2,1)S(1)} %copy-done.4, f32[1,3072]{1,0:T(1,128)S(1)} %bitcast.27, ...), custom_call_target="tpu_custom_call" | custom-call | flops 8000000000 | bytes 1000000 | tf_op jit(solution)/shard_map/attend/pallas_call | solution.py:301
  73.8 0.0 collective-permute-done.1.partner_ref
  73.9 2.0 %collective-permute-start.2 = (bf16[640,128]{1,0:T(8,128)(2,1)S(1)}, bf16[640,128]{1,0:T(8,128)(2,1)S(1)}, u32[]{:S(2)}, u32[]{:S(2)}) collective-permute-start(bf16[640,128]{1,0:T(8,128)(2,1)S(1)} %get-tuple-element.28), channel_id=1, source_target_pairs={{0,8},{8,0},{16,24},{24,16},{32,40},{40,32},{48,56},{56,48},{64,72... | collective-permute-start | bytes 491528 | tf_op jit(solution)/shard_map/ppermute | solution.py:27
  75.8 4.1 %collective-permute-done.2.given_ref = bf16[640,128]{1,0:T(8,128)(2,1)S(1)} collective-permute-done((bf16[640,128]{1,0:T(8,128)(2,1)S(1)}, bf16[640,128]{1,0:T(8,128)(2,1)S(1)}, u32[]{:S(2)}, u32[]{:S(2)}) %collective-permute-start.2) | collective-permute-done | bytes 163872 | tf_op jit(solution)/shard_map/ppermute | solution.py:27
  79.9 0.0 all-to-all-done.3.cot_ref
  79.9 1.7 %local_grad.1 = bf16[2,128,768]{2,1,0:T(8,128)(2,1)} custom-call(s32[3]{0:T(128)S(1)} %pad_add_fusion.place_ref, bf16[1024,128]{1,0:T(8,128)(2,1)S(1)} %get-tuple-element.25.head_ref, bf16[640,128]{1,0:T(8,128)(2,1)S(1)} %collective-permute-done.2.given_ref, bf16[8,64,768]{2,1,0:T(8,128)(2,1)S(1)} %all-to-all-done.3.cot_ref), custom_call_target="tpu_custom_call" | custom-call | flops 1000000000 | bytes 1000000 | tf_op jit(solution)/shard_map/local_grad/pallas_call | solution.py:301
  81.7 12.4 %all-to-all-start.4 = ((bf16[16,16,768]{2,1,0:T(8,128)(2,1)}), bf16[16,16,768]{2,1,0:T(8,128)(2,1)S(1)}, u32[]{:S(2)}, u32[]{:S(2)}) async-start(bf16[16,16,768]{2,1,0:T(8,128)(2,1)} %bitcast.13), calls=%async_computation.4 | async-start | bytes 786432 | tf_op jit(solution)/shard_map/all_to_all | solution.py:382
  94.0 1.8 %project.1 = bf16[256,1536]{1,0:T(8,128)(2,1)} custom-call(s32[3]{0:T(128)S(1)} %pad_add_fusion.place_ref, bf16[256,128]{1,0:T(8,128)(2,1)S(1)} %get-tuple-element.30.own_ref, bf16[640,128]{1,0:T(8,128)(2,1)S(1)} %collective-permute-done.2.given_ref, bf16[128,3072]{1,0:T(8,128)(2,1)S(1)} %copy-done, bf16[128,1536]{1,0:T(8,128)(2,1)S(1)} %collective-permute-done.1.partner_ref), custom_call_target="tpu_custom_call" | custom-call | flops 1000000000 | bytes 1000000 | tf_op jit(solution)/shard_map/project/pallas_call | solution.py:301
  95.8 12.8 %all-to-all-done.4.parts_ref = bf16[16,16,768]{2,1,0:T(8,128)(2,1)S(1)} async-done(((bf16[16,16,768]{2,1,0:T(8,128)(2,1)}), bf16[16,16,768]{2,1,0:T(8,128)(2,1)S(1)}, u32[]{:S(2)}, u32[]{:S(2)}) %all-to-all-start.4) | async-done | bytes 393248 | tf_op jit(solution)/shard_map/all_to_all | solution.py:382
  108.6 0.1 grad_block.1
  108.7 11.3 %all_to_all.37 = bf16[8,16,768]{2,1,0:T(8,128)(2,1)S(1)} all-to-all(bf16[8,16,768]{2,1,0:T(8,128)(2,1)S(1)} %grad_block.1), channel_id=1, replica_groups=mesh['grp'=4,'seq'=16,'dp'=8] {'dp'}, dimensions={0} | all-to-all | bytes 393216 | tf_op jit(solution)/shard_map/all_to_all | solution.py:395
  119.9 7.2 %all-to-all-start.6 = ((bf16[16,16,1536]{2,1,0:T(8,128)(2,1)}), bf16[16,16,1536]{2,1,0:T(8,128)(2,1)S(1)}, u32[]{:S(2)}, u32[]{:S(2)}) async-start(bf16[16,16,1536]{2,1,0:T(8,128)(2,1)} %bitcast.15), calls=%async_computation.6 | async-start | bytes 1572864 | tf_op jit(solution)/shard_map/all_to_all | solution.py:397
  127.2 2.8 %collective-permute-start.5 = (bf16[128,768]{1,0:T(8,128)(2,1)S(1)}, bf16[128,768]{1,0:T(8,128)(2,1)S(1)}, u32[]{:S(2)}, u32[]{:S(2)}) collective-permute-start(bf16[128,768]{1,0:T(8,128)(2,1)S(1)} %bitcast.18), channel_id=1, source_target_pairs={{0,384},{128,256},{256,128},{384,0},{1,385},{129,257},{257,129},{3... | collective-permute-start | bytes 589832 | tf_op jit(solution)/shard_map/ppermute | solution.py:27
  130.0 3.1 %collective-permute-start.4 = (bf16[128,768]{1,0:T(8,128)(2,1)S(1)}, bf16[128,768]{1,0:T(8,128)(2,1)S(1)}, u32[]{:S(2)}, u32[]{:S(2)}) collective-permute-start(bf16[128,768]{1,0:T(8,128)(2,1)S(1)} %bitcast.19), channel_id=1, source_target_pairs={{0,256},{128,384},{256,0},{384,128},{1,257},{129,385},{257,1},{385... | collective-permute-start | bytes 589832 | tf_op jit(solution)/shard_map/ppermute | solution.py:27
  133.1 3.1 %collective-permute-start.3 = (bf16[128,768]{1,0:T(8,128)(2,1)S(1)}, bf16[128,768]{1,0:T(8,128)(2,1)S(1)}, u32[]{:S(2)}, u32[]{:S(2)}) collective-permute-start(bf16[128,768]{1,0:T(8,128)(2,1)S(1)} %bitcast.20), channel_id=1, source_target_pairs={{0,128},{128,0},{256,384},{384,256},{1,129},{129,1},{257,385},{385... | collective-permute-start | bytes 589832 | tf_op jit(solution)/shard_map/ppermute | solution.py:27
  136.2 0.0 collective-permute-done.5.refs_3_
  136.2 2.0 %collective-permute-done.4.refs_2_ = bf16[128,768]{1,0:T(8,128)(2,1)S(1)} collective-permute-done((bf16[128,768]{1,0:T(8,128)(2,1)S(1)}, bf16[128,768]{1,0:T(8,128)(2,1)S(1)}, u32[]{:S(2)}, u32[]{:S(2)}) %collective-permute-start.4) | collective-permute-done | bytes 196640 | tf_op jit(solution)/shard_map/ppermute | solution.py:27
  138.2 2.4 %collective-permute-done.3.refs_1_ = bf16[128,768]{1,0:T(8,128)(2,1)S(1)} collective-permute-done((bf16[128,768]{1,0:T(8,128)(2,1)S(1)}, bf16[128,768]{1,0:T(8,128)(2,1)S(1)}, u32[]{:S(2)}, u32[]{:S(2)}) %collective-permute-start.3) | collective-permute-done | bytes 196640 | tf_op jit(solution)/shard_map/ppermute | solution.py:27
  140.6 1.5 grad_columns.1
  142.1 5.5 %all-to-all-done.6.parts_ref = bf16[16,16,1536]{2,1,0:T(8,128)(2,1)S(1)} async-done(((bf16[16,16,1536]{2,1,0:T(8,128)(2,1)}), bf16[16,16,1536]{2,1,0:T(8,128)(2,1)S(1)}, u32[]{:S(2)}, u32[]{:S(2)}) %all-to-all-start.6) | async-done | bytes 786464 | tf_op jit(solution)/shard_map/all_to_all | solution.py:397
  147.5 0.7 attended.1
  (11 shorter events, 0.0 us)
Async XLA Ops:
  0.6 9.2 %copy-start.8 = (s32[1,8,64]{2,1,0:T(8,128)S(1)}, s32[1,8,64]{2,1,0:T(8,128)}, u32[]{:S(2)}) copy-start(s32[1,8,64]{2,1,0:T(8,128)} %param.14) | copy-start | bytes 6148
  1.6 8.2 %collective-permute-start = (bf16[2,64,512]{2,1,0:T(8,128)(2,1)S(1)}, bf16[2,64,512]{2,1,0:T(8,128)(2,1)S(1)}, u32[]{:S(2)}, u32[]{:S(2)}) collective-permute-start(bf16[2,64,512]{2,1,0:T(8,128)(2,1)S(1)} %slice_bitcast_fusion), channel_id=1, source_target_pairs={{0,8},{8,16},{16,24},{24,32},{32,40},{40,48},{48,56},{56,64},{64,7... | collective-permute-start | bytes 393224 | tf_op jit(solution)/shard_map/ppermute | solution.py:22
  5.6 1.0 copy-start.2
  6.7 0.9 copy-start.5
  7.5 0.8 copy-start.6
  9.8 21.0 %copy-start.1 = (bf16[1,16,3072]{2,1,0:T(8,128)(2,1)S(1)}, bf16[1,16,3072]{2,1,0:T(8,128)(2,1)}, u32[]{:S(2)}) copy-start(bf16[1,16,3072]{2,1,0:T(8,128)(2,1)} %param.21) | copy-start | bytes 294916
  10.7 48.3 %copy-start = (bf16[128,3072]{1,0:T(8,128)(2,1)S(1)}, bf16[128,3072]{1,0:T(8,128)(2,1)}, u32[]{:S(2)}) copy-start(bf16[128,3072]{1,0:T(8,128)(2,1)} %weight_ref.1) | copy-start | bytes 2359300
  31.0 31.3 %copy-start.4 = (bf16[64,3072]{1,0:T(8,128)(2,1)S(1)}, bf16[64,3072]{1,0:T(8,128)(2,1)}, u32[]{:S(2)}) copy-start(bf16[64,3072]{1,0:T(8,128)(2,1)} %embed_ref.1) | copy-start | bytes 1179652
  31.0 31.3 %copy-start.7 = (f32[3072]{0:T(1024)S(1)}, f32[3072]{0:T(1024)}, u32[]{:S(2)}) copy-start(f32[3072]{0:T(1024)} %param.16) | copy-start | bytes 36868
  31.0 31.3 %copy-start.9 = (f32[128]{0:T(128)S(1)}, f32[128]{0:T(128)}, u32[]{:S(2)}) copy-start(f32[128]{0:T(128)} %param.18) | copy-start | bytes 1540
  31.0 31.3 %copy-start.10 = (f32[128]{0:T(128)S(1)}, f32[128]{0:T(128)}, u32[]{:S(2)}) copy-start(f32[128]{0:T(128)} %param.19) | copy-start | bytes 1540
  40.9 14.5 %all-to-all-start.2 = ((bf16[16,64,128]{2,1,0:T(8,128)(2,1)}), bf16[16,64,128]{2,1,0:T(8,128)(2,1)S(1)}, u32[]{:S(2)}, u32[]{:S(2)}) async-start(bf16[16,64,128]{2,1,0:T(8,128)(2,1)} %merged.1), calls=%async_computation.2 | async-start | bytes 524288 | tf_op jit(solution)/shard_map/all_to_all | solution.py:356
  55.4 24.6 %all-to-all-start.3 = ((bf16[8,64,768]{2,1,0:T(8,128)(2,1)}), bf16[8,64,768]{2,1,0:T(8,128)(2,1)S(1)}, u32[]{:S(2)}, u32[]{:S(2)}) async-start(bf16[8,64,768]{2,1,0:T(8,128)(2,1)} %near_rows.1), calls=%async_computation.3 | async-start | bytes 1572864 | tf_op jit(solution)/shard_map/all_to_all | solution.py:361
  59.0 14.8 %collective-permute-start.1 = (bf16[128,1536]{1,0:T(8,128)(2,1)S(1)}, bf16[128,1536]{1,0:T(8,128)(2,1)S(1)}, u32[]{:S(2)}, u32[]{:S(2)}) collective-permute-start(bf16[128,1536]{1,0:T(8,128)(2,1)S(1)} %constant_dynamic-slice_fusion), channel_id=1, source_target_pairs={{0,8},{8,0},{16,24},{24,16},{32,40},{40,32},{48,56},{56,48},{64,72... | collective-permute-start | bytes 1179656 | tf_op jit(solution)/shard_map/ppermute | solution.py:27
  62.4 1.7 %copy-start.3 = (bf16[3,3072,128]{2,1,0:T(8,128)(2,1)S(1)}, bf16[3,3072,128]{2,1,0:T(8,128)(2,1)}, u32[]{:S(2)}) copy-start(bf16[3,3072,128]{2,1,0:T(8,128)(2,1)} %qkv_ref.1) | copy-start | bytes 7077892
  73.9 6.1 %collective-permute-start.2 = (bf16[640,128]{1,0:T(8,128)(2,1)S(1)}, bf16[640,128]{1,0:T(8,128)(2,1)S(1)}, u32[]{:S(2)}, u32[]{:S(2)}) collective-permute-start(bf16[640,128]{1,0:T(8,128)(2,1)S(1)} %get-tuple-element.28), channel_id=1, source_target_pairs={{0,8},{8,0},{16,24},{24,16},{32,40},{40,32},{48,56},{56,48},{64,72... | collective-permute-start | bytes 491528 | tf_op jit(solution)/shard_map/ppermute | solution.py:27
  81.7 27.0 %all-to-all-start.4 = ((bf16[16,16,768]{2,1,0:T(8,128)(2,1)}), bf16[16,16,768]{2,1,0:T(8,128)(2,1)S(1)}, u32[]{:S(2)}, u32[]{:S(2)}) async-start(bf16[16,16,768]{2,1,0:T(8,128)(2,1)} %bitcast.13), calls=%async_computation.4 | async-start | bytes 786432 | tf_op jit(solution)/shard_map/all_to_all | solution.py:382
  119.9 27.6 %all-to-all-start.6 = ((bf16[16,16,1536]{2,1,0:T(8,128)(2,1)}), bf16[16,16,1536]{2,1,0:T(8,128)(2,1)S(1)}, u32[]{:S(2)}, u32[]{:S(2)}) async-start(bf16[16,16,1536]{2,1,0:T(8,128)(2,1)} %bitcast.15), calls=%async_computation.6 | async-start | bytes 1572864 | tf_op jit(solution)/shard_map/all_to_all | solution.py:397
  127.2 9.0 %collective-permute-start.5 = (bf16[128,768]{1,0:T(8,128)(2,1)S(1)}, bf16[128,768]{1,0:T(8,128)(2,1)S(1)}, u32[]{:S(2)}, u32[]{:S(2)}) collective-permute-start(bf16[128,768]{1,0:T(8,128)(2,1)S(1)} %bitcast.18), channel_id=1, source_target_pairs={{0,384},{128,256},{256,128},{384,0},{1,385},{129,257},{257,129},{3... | collective-permute-start | bytes 589832 | tf_op jit(solution)/shard_map/ppermute | solution.py:27
  130.0 8.3 %collective-permute-start.4 = (bf16[128,768]{1,0:T(8,128)(2,1)S(1)}, bf16[128,768]{1,0:T(8,128)(2,1)S(1)}, u32[]{:S(2)}, u32[]{:S(2)}) collective-permute-start(bf16[128,768]{1,0:T(8,128)(2,1)S(1)} %bitcast.19), channel_id=1, source_target_pairs={{0,256},{128,384},{256,0},{384,128},{1,257},{129,385},{257,1},{385... | collective-permute-start | bytes 589832 | tf_op jit(solution)/shard_map/ppermute | solution.py:27
  133.1 7.5 %collective-permute-start.3 = (bf16[128,768]{1,0:T(8,128)(2,1)S(1)}, bf16[128,768]{1,0:T(8,128)(2,1)S(1)}, u32[]{:S(2)}, u32[]{:S(2)}) collective-permute-start(bf16[128,768]{1,0:T(8,128)(2,1)S(1)} %bitcast.20), channel_id=1, source_target_pairs={{0,128},{128,0},{256,384},{384,256},{1,129},{129,1},{257,385},{385... | collective-permute-start | bytes 589832 | tf_op jit(solution)/shard_map/ppermute | solution.py:27

commit v10 on v9

--- a/solution.py
+++ b/solution.py
@@ -223,21 +223,31 @@
         out_ref[:, pl.ds(start, columns)] = ref[...]
 
 
+def qkv_kernel(qkv_ref, q_ref, kv_ref, sems):
+    head = q_ref.shape[1]
+    copies = [
+        pltpu.make_async_copy(qkv_ref.at[i], ref, sems.at[i])
+        for i, ref in enumerate((q_ref, kv_ref.at[:, :head], kv_ref.at[:, head:]))
+    ]
+    for copy in copies:
+        copy.start()
+    for copy in copies:
+        copy.wait()
+
+
 def head_norm(projected, gain):
     square_mean = jnp.mean(projected * projected, axis=-1, keepdims=True)
     return (projected * lax.rsqrt(square_mean + 1e-06) * gain).astype(BF16)
 
 
 def attend_kernel(
-    place_ref, merged_ref, embed_ref, norm_ref, qkv_ref, qgain_ref, kgain_ref, out_ref, own_ref,
-    give_ref,    kv_ref, q_ref, k_ref, v_ref, *, grp_size, block,
+    place_ref, merged_ref, embed_ref, norm_ref, qw_ref, kv_ref, qgain_ref, kgain_ref, out_ref, own_ref,
+    give_ref, normed_ref, q_ref, k_ref, v_ref, *, grp_size, block,
 ):
     latents, width = embed_ref.shape
     head = q_ref.shape[1]
     total = out_ref.shape[0]
     step = 256
-    kv_ref[:, :head] = qkv_ref[1]
-    kv_ref[:, head:] = qkv_ref[2]
     pick = (lane_index(16) >= LANES - 2).astype(F32).astype(BF16)
     count_row = lax.dot_general(pick, merged_ref[...], NT, preferred_element_type=F32)[0:1, :]
     bias = jnp.log(count_row)
@@ -259,12 +269,14 @@
         factors = jnp.where(lane < latents, rows, tail).astype(BF16)
         center = jnp.dot(factors, embed, preferred_element_type=F32)
         spread = jnp.mean(center * center, axis=-1, keepdims=True)
-        normed = (center * lax.rsqrt(spread + 1e-06) * norm_ref[...]).astype(BF16)
-        q_part = jnp.dot(normed, qkv_ref[0], preferred_element_type=F32)
-        kv_part = jnp.dot(normed, kv_ref[...], preferred_element_type=F32)
-        q_ref[here, :] = head_norm(q_part, qgain_ref[...])
-        k_ref[here, :] = head_norm(kv_part[:, :head], kgain_ref[...])
-        v_ref[here, :] = kv_part[:, head:].astype(BF16)
+        scaled = center * lax.rsqrt(spread + 1e-06) * norm_ref[...]
+        normed_ref[here, :] = scaled.astype(BF16)
+    q_part = jnp.dot(normed_ref[...], qw_ref[...], preferred_element_type=F32)
+    q_ref[...] = head_norm(q_part, qgain_ref[...])
+    kv_part = jnp.dot(normed_ref[...], kv_ref[...], preferred_element_type=F32)
+    k_ref[...] = head_norm(kv_part[:, :head], kgain_ref[...])
+    v_ref[...] = kv_part[:, head:].astype(BF16)
+    step = 512
     scale = 1.0 / math.sqrt(head)
     for start in range(0, total, step):
         here = slice(start, start + step)
@@ -343,16 +355,24 @@
         first, earlier, taps, latent_rhs, late, assign[0], name="group_sums", flops=10**9,
     )
 
+    sums, weight, qkv = lax.optimization_barrier((sums, out_weight, qkv_weight))
+    given = lax.dynamic_slice_in_dim(weight, (1 - (seq & 1)) * (width // 2), width // 2, 1)
+    weight_other = xor_swap(given, "seq", 1)
+    q_weight, kv_weight = call(
+        qkv_kernel, [(width, head), (width, 2 * head)], qkv, name="qkv_layout", places=["hbm"],
+        moved=10**7,
+        scratch=[pltpu.SemaphoreType.DMA((3,))],
+    )
     parts = lax.all_to_all(sums.reshape(seq_size, shared, LANES), "seq", 0, 0, tiled=True)
     carried = shared + columns // LANES * block
     slab_sums = call(
         resplit_kernel, [(grp_size, carried, LANES)], parts, cotangent[0], name="slab_sums"
     )
+    slab_sums, weight_other, q_weight, kv_weight = lax.optimization_barrier(
+        (slab_sums, weight_other, q_weight, kv_weight)
+    )
     slab_parts = lax.all_to_all(slab_sums, "grp", 0, 0, tiled=True)
     merged = call(merge_kernel, [(seq_size, shared, LANES)], slab_parts, name="merged")
-    merged, weight = lax.optimization_barrier((merged, out_weight))
-    given = lax.dynamic_slice_in_dim(weight, (1 - (seq & 1)) * (width // 2), width // 2, 1)
-    weight_other = xor_swap(given, "seq", 1)
     merged = lax.all_to_all(merged, "seq", 0, 0, tiled=True).reshape(groups, LANES)
     slabs = seq_size // 2
     near = call(near_kernel, [(slabs, shared, columns)], slab_parts, name="near_rows")
@@ -363,12 +383,11 @@
     head_out, own_rows, given_rows = call(
         functools.partial(attend_kernel, grp_size=grp_size, block=block),
         [(groups, head), (rows, head), (groups // 2 + rows // 2, head)], place, merged,
-        embed_weight, norm_gain[None], qkv_weight, q_gain[None], k_gain[None], name="attend",
+        embed_weight, norm_gain[None], q_weight, kv_weight, q_gain[None], k_gain[None], name="attend",
         flops=8 * 10**9, places=["smem"],
-        scratch=[pltpu.VMEM((width, 2 * head), BF16)] + [pltpu.VMEM((groups, head), BF16)] * 3,
-    )
-
-    given_rows, weight_other = lax.optimization_barrier((given_rows, weight_other))
+        scratch=[pltpu.VMEM((groups, width), BF16)] + [pltpu.VMEM((groups, head), BF16)] * 3,
+    )
+
     side_rows = xor_swap(given_rows, "seq", 1)
     local_grad = call(
         grad_kernel, [(2, head, columns)], place, head_out, side_rows, grad_rows,

time: 151 us -> 154 us (1.020)
  blocking collectives: 40.3 us -> 20.1 us
  starting transfers between devices: 46.9 us -> 60.6 us
  waiting for transfers between devices: 34.7 us -> 40.4 us
  local copies, waits for them, and re-layouts: 5.42 us -> 9.6 us
    all_to_all x1 -> x0, blocking collectives: 20.1 us -> none  [shards(): lax.all_to_all(sums.reshape(seq_size, shared, LANES), 'seq', 0, 0, tiled=...]
    all_to_all x0 -> x1, starting transfers between devices: none -> 11.2 us  [shards(): lax.all_to_all(sums.reshape(seq_size, shared, LANES), 'seq', 0, 0, tiled=...]
    unnamed x22 -> x34, local copies, waits for them, and re-layouts: 4.47 us -> 7.9 us
    ppermute x5, waiting for transfers between devices: 8.48 us -> 11.8 us  [xor_swap(): return lax.ppermute(block, axis, route)]
    all_to_all x0 -> x1, waiting for transfers between devices: none -> 2.57 us  [shards(): lax.all_to_all(sums.reshape(seq_size, shared, LANES), 'seq', 0, 0, tiled=...]
    pallas_call x11 -> x12, Pallas kernels: 20 us -> 20.4 us  [call(): pl.pallas_call(body, out_shape=outs, in_specs=in_specs, out_specs=(whole,...]
  transfers between devices with their start and end apart: 10 -> 11, of which waited for: 6 -> 9; matrix products, arithmetic and copies ran while one was open for 0% -> 1% of each run, Pallas kernels for 10% -> 10%
where the time goes in v10:
time: 154 us; the launch traced here: 152 us
  starting transfers between devices  60.6 us (39%)
  waiting for transfers between devices  40.4 us (26%)
  Pallas kernels  20.4 us (13%)
  blocking collectives  20.1 us (13%)
  local copies, waits for them, and re-layouts  9.6 us (6%)
    pallas_call x12, Pallas kernels, call(): pl.pallas_call(body, out_shape=outs, in_specs=in_specs, out_specs=(whole,...  20.4 us
    ppermute x5, starting transfers between devices, xor_swap(): return lax.ppermute(block, axis, route)  15.5 us
    all_to_all x1, starting transfers between devices, shards(): lax.all_to_all(local_grad.reshape(2 * dp_size, head // dp_size, columns),...  13.6 us
    all_to_all x1, waiting for transfers between devices, shards(): lax.all_to_all(local_grad.reshape(2 * dp_size, head // dp_size, columns),...  12.3 us
    ppermute x5, waiting for transfers between devices, xor_swap(): return lax.ppermute(block, axis, route)  11.8 us
    all_to_all x1, blocking collectives, shards(): lax.all_to_all(grad_block, 'dp', 0, 0, tiled=True).reshape(head, columns)  11.3 us
    all_to_all x1, starting transfers between devices, shards(): lax.all_to_all(sums.reshape(seq_size, shared, LANES), 'seq', 0, 0, tiled=...  11.2 us
    all_to_all x1, blocking collectives, shards(): slab_parts = lax.all_to_all(slab_sums, 'grp', 0, 0, tiled=True)  8.81 us
  transfers between devices with their start and end apart: 11, of which 9 were waited for; matrix products, arithmetic and copies ran while one was open for 1% of the time, Pallas kernels for 10%

profile of v10, /device:TPU:1, one launch (start us, length us, event | category | flops | bytes accessed | tf_op | source)
XLA Modules:
  0.0 152.0 jit_solution(15756199077488705021)
XLA Ops:
  0.6 0.9 slice_bitcast_fusion
  1.6 4.0 %collective-permute-start = (bf16[2,64,512]{2,1,0:T(8,128)(2,1)S(1)}, bf16[2,64,512]{2,1,0:T(8,128)(2,1)S(1)}, u32[]{:S(2)}, u32[]{:S(2)}) collective-permute-start(bf16[2,64,512]{2,1,0:T(8,128)(2,1)S(1)} %slice_bitcast_fusion), channel_id=1, source_target_pairs={{0,8},{8,16},{16,24},{24,32},{32,40},{40,48},{48,56},{56,64},{64,7... | collective-permute-start | bytes 393224 | tf_op jit(solution)/shard_map/ppermute | solution.py:22
  5.6 0.0 copy-start.3
  5.6 1.0 copy-done.3
  6.7 0.9 copy-done.9
  7.6 0.8 copy-done.10
  8.4 1.4 late_frames.1
  9.8 0.0 copy-start.1
  9.8 0.0 copy-start
  9.8 1.6 %group_sums.1 = bf16[1024,128]{1,0:T(8,128)(2,1)} custom-call(bf16[2,64,512]{2,1,0:T(8,128)(2,1)S(1)} %get-tuple-element.24.video_ref, bf16[2,64,512]{2,1,0:T(8,128)(2,1)S(1)} %collective-permute-done.earlier_ref, bf16[3,128,128]{2,1,0:T(8,128)(2,1)S(1)} %get-tuple-element.25.conv_ref, bf16[64,512]{1,0:T(8,128)(2,1)S(1)} %get-tuple-element.26.latent_ref, ...), custom_call_target="tpu_custom_call" | custom-call | flops 1000000000 | bytes 1000000 | tf_op jit(solution)/shard_map/group_sums/pallas_call | solution.py:313
  11.4 11.2 %all-to-all-start = ((bf16[16,64,128]{2,1,0:T(8,128)(2,1)}), bf16[16,64,128]{2,1,0:T(8,128)(2,1)S(1)}, u32[]{:S(2)}, u32[]{:S(2)}) async-start(bf16[16,64,128]{2,1,0:T(8,128)(2,1)} %bitcast.7), calls=%async_computation | async-start | bytes 524288 | tf_op jit(solution)/shard_map/all_to_all | solution.py:366
  22.6 0.8 constant_dynamic-slice_fusion
  23.4 3.3 %collective-permute-start.1 = (bf16[128,1536]{1,0:T(8,128)(2,1)}, bf16[128,1536]{1,0:T(8,128)(2,1)}, u32[]{:S(2)}, u32[]{:S(2)}) collective-permute-start(bf16[128,1536]{1,0:T(8,128)(2,1)} %constant_dynamic-slice_fusion), channel_id=1, source_target_pairs={{0,8},{8,0},{16,24},{24,16},{32,40},{40,32},{48,56},{56,48},{64,72... | collective-permute-start | bytes 1179656 | tf_op jit(solution)/shard_map/ppermute | solution.py:27
  26.7 0.4 qkv_layout.1
  27.0 1.2 copy-done.4
  28.2 0.9 copy-done.6
  29.1 2.6 %all-to-all-done.parts_ref = bf16[16,64,128]{2,1,0:T(8,128)(2,1)S(1)} async-done(((bf16[16,64,128]{2,1,0:T(8,128)(2,1)}), bf16[16,64,128]{2,1,0:T(8,128)(2,1)S(1)}, u32[]{:S(2)}, u32[]{:S(2)}) %all-to-all-start) | async-done | bytes 262176 | tf_op jit(solution)/shard_map/all_to_all | solution.py:366
  31.7 0.2 slab_sums.1
  31.9 4.3 %collective-permute-done.1.partner_ref = bf16[128,1536]{1,0:T(8,128)(2,1)} collective-permute-done((bf16[128,1536]{1,0:T(8,128)(2,1)}, bf16[128,1536]{1,0:T(8,128)(2,1)}, u32[]{:S(2)}, u32[]{:S(2)}) %collective-permute-start.1) | collective-permute-done | bytes 393248 | tf_op jit(solution)/shard_map/ppermute | solution.py:27
  36.2 8.8 %all_to_all.35.parts_ref = bf16[4,160,128]{2,1,0:T(8,128)(2,1)S(1)} all-to-all(bf16[4,160,128]{2,1,0:T(8,128)(2,1)S(1)} %slab_sums.1), channel_id=1, replica_groups=mesh['grp'=4,'seq'=16,'dp'=8] {'grp'}, dimensions={0} | all-to-all | bytes 327680 | tf_op jit(solution)/shard_map/all_to_all | solution.py:374
  45.0 0.9 merged.1
  45.9 6.0 %all-to-all-start.2 = ((bf16[16,64,128]{2,1,0:T(8,128)(2,1)}), bf16[16,64,128]{2,1,0:T(8,128)(2,1)S(1)}, u32[]{:S(2)}, u32[]{:S(2)}) async-start(bf16[16,64,128]{2,1,0:T(8,128)(2,1)} %merged.1), calls=%async_computation.2 | async-start | bytes 524288 | tf_op jit(solution)/shard_map/all_to_all | solution.py:376
  51.9 1.0 near_rows.1
  52.9 7.6 %all-to-all-done.2 = bf16[16,64,128]{2,1,0:T(8,128)(2,1)S(1)} async-done(((bf16[16,64,128]{2,1,0:T(8,128)(2,1)}), bf16[16,64,128]{2,1,0:T(8,128)(2,1)S(1)}, u32[]{:S(2)}, u32[]{:S(2)}) %all-to-all-start.2) | async-done | bytes 262176 | tf_op jit(solution)/shard_map/all_to_all | solution.py:376
  60.6 3.5 %all-to-all-start.3 = ((bf16[8,64,768]{2,1,0:T(8,128)(2,1)}), bf16[8,64,768]{2,1,0:T(8,128)(2,1)S(1)}, u32[]{:S(2)}, u32[]{:S(2)}) async-start(bf16[8,64,768]{2,1,0:T(8,128)(2,1)} %near_rows.1), calls=%async_computation.3 | async-start | bytes 1572864 | tf_op jit(solution)/shard_map/all_to_all | solution.py:381
  64.1 0.1 pad_add_fusion.place_ref
  64.2 1.4 copy-done.5
  65.6 8.7 %attend.1 = (bf16[1024,128]{1,0:T(8,128)(2,1)S(1)}, bf16[256,128]{1,0:T(8,128)(2,1)S(1)}, bf16[640,128]{1,0:T(8,128)(2,1)S(1)}) custom-call(s32[3]{0:T(128)S(1)} %pad_add_fusion.place_ref, bf16[1024,128]{1,0:T(8,128)(2,1)S(1)} %bitcast.22, bf16[64,3072]{1,0:T(8,128)(2,1)S(1)} %copy-done.8, f32[1,3072]{1,0:T(1,128)S(1)} %bitcast.26, ...), custom_call_target="tpu_custom_call" | custom-call | flops 8000000000 | bytes 1000000 | tf_op jit(solution)/shard_map/attend/pallas_call | solution.py:313
  74.3 0.7 copy-done.15
  75.0 3.3 %collective-permute-start.2 = (bf16[640,128]{1,0:T(8,128)(2,1)S(1)}, bf16[640,128]{1,0:T(8,128)(2,1)S(1)}, u32[]{:S(2)}, u32[]{:S(2)}) collective-permute-start(bf16[640,128]{1,0:T(8,128)(2,1)S(1)} %get-tuple-element.38), channel_id=1, source_target_pairs={{0,8},{8,0},{16,24},{24,16},{32,40},{40,32},{48,56},{56,48},{64,72... | collective-permute-start | bytes 491528 | tf_op jit(solution)/shard_map/ppermute | solution.py:27
  78.3 3.1 %collective-permute-done.2.given_ref = bf16[640,128]{1,0:T(8,128)(2,1)S(1)} collective-permute-done((bf16[640,128]{1,0:T(8,128)(2,1)S(1)}, bf16[640,128]{1,0:T(8,128)(2,1)S(1)}, u32[]{:S(2)}, u32[]{:S(2)}) %collective-permute-start.2) | collective-permute-done | bytes 163872 | tf_op jit(solution)/shard_map/ppermute | solution.py:27
  81.4 0.6 all-to-all-done.3.cot_ref
  81.9 0.9 copy-done.16
  82.9 1.7 %local_grad.1 = bf16[2,128,768]{2,1,0:T(8,128)(2,1)} custom-call(s32[3]{0:T(128)S(1)} %pad_add_fusion.place_ref, bf16[1024,128]{1,0:T(8,128)(2,1)S(1)} %copy-done.16, bf16[640,128]{1,0:T(8,128)(2,1)S(1)} %collective-permute-done.2.given_ref, bf16[8,64,768]{2,1,0:T(8,128)(2,1)S(1)} %all-to-all-done.3.cot_ref), custom_call_target="tpu_custom_call" | custom-call | flops 1000000000 | bytes 1000000 | tf_op jit(solution)/shard_map/local_grad/pallas_call | solution.py:313
  84.6 13.6 %all-to-all-start.4 = ((bf16[16,16,768]{2,1,0:T(8,128)(2,1)}), bf16[16,16,768]{2,1,0:T(8,128)(2,1)S(1)}, u32[]{:S(2)}, u32[]{:S(2)}) async-start(bf16[16,16,768]{2,1,0:T(8,128)(2,1)} %bitcast.13), calls=%async_computation.4 | async-start | bytes 786432 | tf_op jit(solution)/shard_map/all_to_all | solution.py:401
  98.2 2.3 %project.1 = bf16[256,1536]{1,0:T(8,128)(2,1)} custom-call(s32[3]{0:T(128)S(1)} %pad_add_fusion.place_ref, bf16[256,128]{1,0:T(8,128)(2,1)S(1)} %get-tuple-element.40.own_ref, bf16[640,128]{1,0:T(8,128)(2,1)S(1)} %collective-permute-done.2.given_ref, bf16[128,3072]{1,0:T(8,128)(2,1)S(1)} %copy-done.1, bf16[128,1536]{1,0:T(8,128)(2,1)} %collective-permute-done.1.partner_ref), custom_call_target="tpu_custom_call" | custom-call | flops 1000000000 | bytes 1000000 | tf_op jit(solution)/shard_map/project/pallas_call | solution.py:313
  100.4 12.3 %all-to-all-done.4.parts_ref = bf16[16,16,768]{2,1,0:T(8,128)(2,1)S(1)} async-done(((bf16[16,16,768]{2,1,0:T(8,128)(2,1)}), bf16[16,16,768]{2,1,0:T(8,128)(2,1)S(1)}, u32[]{:S(2)}, u32[]{:S(2)}) %all-to-all-start.4) | async-done | bytes 393248 | tf_op jit(solution)/shard_map/all_to_all | solution.py:401
  112.8 0.1 grad_block.1
  112.8 11.3 %all_to_all.36 = bf16[8,16,768]{2,1,0:T(8,128)(2,1)S(1)} all-to-all(bf16[8,16,768]{2,1,0:T(8,128)(2,1)S(1)} %grad_block.1), channel_id=1, replica_groups=mesh['grp'=4,'seq'=16,'dp'=8] {'dp'}, dimensions={0} | all-to-all | bytes 393216 | tf_op jit(solution)/shard_map/all_to_all | solution.py:414
  124.1 6.8 %all-to-all-start.6 = ((bf16[16,16,1536]{2,1,0:T(8,128)(2,1)}), bf16[16,16,1536]{2,1,0:T(8,128)(2,1)S(1)}, u32[]{:S(2)}, u32[]{:S(2)}) async-start(bf16[16,16,1536]{2,1,0:T(8,128)(2,1)} %bitcast.15), calls=%async_computation.6 | async-start | bytes 1572864 | tf_op jit(solution)/shard_map/all_to_all | solution.py:416
  130.9 2.8 %collective-permute-start.5 = (bf16[128,768]{1,0:T(8,128)(2,1)S(1)}, bf16[128,768]{1,0:T(8,128)(2,1)S(1)}, u32[]{:S(2)}, u32[]{:S(2)}) collective-permute-start(bf16[128,768]{1,0:T(8,128)(2,1)S(1)} %bitcast.18), channel_id=1, source_target_pairs={{0,384},{128,256},{256,128},{384,0},{1,385},{129,257},{257,129},{3... | collective-permute-start | bytes 589832 | tf_op jit(solution)/shard_map/ppermute | solution.py:27
  133.7 3.1 %collective-permute-start.4 = (bf16[128,768]{1,0:T(8,128)(2,1)S(1)}, bf16[128,768]{1,0:T(8,128)(2,1)S(1)}, u32[]{:S(2)}, u32[]{:S(2)}) collective-permute-start(bf16[128,768]{1,0:T(8,128)(2,1)S(1)} %bitcast.19), channel_id=1, source_target_pairs={{0,256},{128,384},{256,0},{384,128},{1,257},{129,385},{257,1},{385... | collective-permute-start | bytes 589832 | tf_op jit(solution)/shard_map/ppermute | solution.py:27
  136.8 3.1 %collective-permute-start.3 = (bf16[128,768]{1,0:T(8,128)(2,1)S(1)}, bf16[128,768]{1,0:T(8,128)(2,1)S(1)}, u32[]{:S(2)}, u32[]{:S(2)}) collective-permute-start(bf16[128,768]{1,0:T(8,128)(2,1)S(1)} %bitcast.20), channel_id=1, source_target_pairs={{0,128},{128,0},{256,384},{384,256},{1,129},{129,1},{257,385},{385... | collective-permute-start | bytes 589832 | tf_op jit(solution)/shard_map/ppermute | solution.py:27
  139.9 2.0 %collective-permute-done.4.refs_2_ = bf16[128,768]{1,0:T(8,128)(2,1)S(1)} collective-permute-done((bf16[128,768]{1,0:T(8,128)(2,1)S(1)}, bf16[128,768]{1,0:T(8,128)(2,1)S(1)}, u32[]{:S(2)}, u32[]{:S(2)}) %collective-permute-start.4) | collective-permute-done | bytes 196640 | tf_op jit(solution)/shard_map/ppermute | solution.py:27
  142.0 2.4 %collective-permute-done.3.refs_1_ = bf16[128,768]{1,0:T(8,128)(2,1)S(1)} collective-permute-done((bf16[128,768]{1,0:T(8,128)(2,1)S(1)}, bf16[128,768]{1,0:T(8,128)(2,1)S(1)}, u32[]{:S(2)}, u32[]{:S(2)}) %collective-permute-start.3) | collective-permute-done | bytes 196640 | tf_op jit(solution)/shard_map/ppermute | solution.py:27
  144.3 1.5 grad_columns.1
  145.8 5.5 %all-to-all-done.6.parts_ref = bf16[16,16,1536]{2,1,0:T(8,128)(2,1)S(1)} async-done(((bf16[16,16,1536]{2,1,0:T(8,128)(2,1)}), bf16[16,16,1536]{2,1,0:T(8,128)(2,1)S(1)}, u32[]{:S(2)}, u32[]{:S(2)}) %all-to-all-start.6) | async-done | bytes 786464 | tf_op jit(solution)/shard_map/all_to_all | solution.py:416
  151.3 0.7 attended.1
  (25 shorter events, 0.1 us)
Async XLA Ops:
  0.6 9.2 %copy-start.12 = (s32[1,8,64]{2,1,0:T(8,128)S(1)}, s32[1,8,64]{2,1,0:T(8,128)}, u32[]{:S(2)}) copy-start(s32[1,8,64]{2,1,0:T(8,128)} %param.14) | copy-start | bytes 6148
  1.6 8.3 %collective-permute-start = (bf16[2,64,512]{2,1,0:T(8,128)(2,1)S(1)}, bf16[2,64,512]{2,1,0:T(8,128)(2,1)S(1)}, u32[]{:S(2)}, u32[]{:S(2)}) collective-permute-start(bf16[2,64,512]{2,1,0:T(8,128)(2,1)S(1)} %slice_bitcast_fusion), channel_id=1, source_target_pairs={{0,8},{8,16},{16,24},{24,32},{32,40},{40,48},{48,56},{56,64},{64,7... | collective-permute-start | bytes 393224 | tf_op jit(solution)/shard_map/ppermute | solution.py:22
  5.6 1.0 copy-start.3
  6.7 0.9 copy-start.9
  7.6 0.8 copy-start.10
  9.8 12.8 %copy-start.1 = (bf16[128,3072]{1,0:T(8,128)(2,1)S(1)}, bf16[128,3072]{1,0:T(8,128)(2,1)}, u32[]{:S(2)}) copy-start(bf16[128,3072]{1,0:T(8,128)(2,1)} %weight_ref.1) | copy-start | bytes 2359300
  9.8 16.8 %copy-start = (bf16[3,3072,128]{2,1,0:T(8,128)(2,1)S(1)}, bf16[3,3072,128]{2,1,0:T(8,128)(2,1)}, u32[]{:S(2)}) copy-start(bf16[3,3072,128]{2,1,0:T(8,128)(2,1)} %qkv_ref) | copy-start | bytes 7077892
  11.4 20.2 %copy-start.2 = (bf16[1,16,3072]{2,1,0:T(8,128)(2,1)S(1)}, bf16[1,16,3072]{2,1,0:T(8,128)(2,1)}, u32[]{:S(2)}) copy-start(bf16[1,16,3072]{2,1,0:T(8,128)(2,1)} %param.21) | copy-start | bytes 294916
  11.4 20.2 %all-to-all-start = ((bf16[16,64,128]{2,1,0:T(8,128)(2,1)}), bf16[16,64,128]{2,1,0:T(8,128)(2,1)S(1)}, u32[]{:S(2)}, u32[]{:S(2)}) async-start(bf16[16,64,128]{2,1,0:T(8,128)(2,1)} %bitcast.7), calls=%async_computation | async-start | bytes 524288 | tf_op jit(solution)/shard_map/all_to_all | solution.py:366
  23.4 12.8 %collective-permute-start.1 = (bf16[128,1536]{1,0:T(8,128)(2,1)}, bf16[128,1536]{1,0:T(8,128)(2,1)}, u32[]{:S(2)}, u32[]{:S(2)}) collective-permute-start(bf16[128,1536]{1,0:T(8,128)(2,1)} %constant_dynamic-slice_fusion), channel_id=1, source_target_pairs={{0,8},{8,0},{16,24},{24,16},{32,40},{40,32},{48,56},{56,48},{64,72... | collective-permute-start | bytes 1179656 | tf_op jit(solution)/shard_map/ppermute | solution.py:27
  27.0 1.2 copy-start.4
  28.2 0.9 copy-start.6
  29.1 35.1 %copy-start.8 = (bf16[64,3072]{1,0:T(8,128)(2,1)S(1)}, bf16[64,3072]{1,0:T(8,128)(2,1)}, u32[]{:S(2)}) copy-start(bf16[64,3072]{1,0:T(8,128)(2,1)} %embed_ref.1) | copy-start | bytes 1179652
  29.1 35.1 %copy-start.11 = (f32[3072]{0:T(1024)S(1)}, f32[3072]{0:T(1024)}, u32[]{:S(2)}) copy-start(f32[3072]{0:T(1024)} %param.16) | copy-start | bytes 36868
  29.1 35.1 %copy-start.13 = (f32[128]{0:T(128)S(1)}, f32[128]{0:T(128)}, u32[]{:S(2)}) copy-start(f32[128]{0:T(128)} %param.18) | copy-start | bytes 1540
  29.1 35.1 %copy-start.14 = (f32[128]{0:T(128)S(1)}, f32[128]{0:T(128)}, u32[]{:S(2)}) copy-start(f32[128]{0:T(128)} %param.19) | copy-start | bytes 1540
  31.7 32.6 %copy-start.7 = (bf16[3072,128]{1,0:T(8,128)(2,1)S(1)}, bf16[3072,128]{1,0:T(8,128)(2,1)}, u32[]{:S(2)}) copy-start(bf16[3072,128]{1,0:T(8,128)(2,1)} %copy-done.6) | copy-start | bytes 2359300
  45.9 14.7 %all-to-all-start.2 = ((bf16[16,64,128]{2,1,0:T(8,128)(2,1)}), bf16[16,64,128]{2,1,0:T(8,128)(2,1)S(1)}, u32[]{:S(2)}, u32[]{:S(2)}) async-start(bf16[16,64,128]{2,1,0:T(8,128)(2,1)} %merged.1), calls=%async_computation.2 | async-start | bytes 524288 | tf_op jit(solution)/shard_map/all_to_all | solution.py:376
  60.6 21.4 %all-to-all-start.3 = ((bf16[8,64,768]{2,1,0:T(8,128)(2,1)}), bf16[8,64,768]{2,1,0:T(8,128)(2,1)S(1)}, u32[]{:S(2)}, u32[]{:S(2)}) async-start(bf16[8,64,768]{2,1,0:T(8,128)(2,1)} %near_rows.1), calls=%async_computation.3 | async-start | bytes 1572864 | tf_op jit(solution)/shard_map/all_to_all | solution.py:381
  64.2 1.4 copy-start.5
  74.3 0.7 copy-start.15
  75.0 6.3 %collective-permute-start.2 = (bf16[640,128]{1,0:T(8,128)(2,1)S(1)}, bf16[640,128]{1,0:T(8,128)(2,1)S(1)}, u32[]{:S(2)}, u32[]{:S(2)}) collective-permute-start(bf16[640,128]{1,0:T(8,128)(2,1)S(1)} %get-tuple-element.38), channel_id=1, source_target_pairs={{0,8},{8,0},{16,24},{24,16},{32,40},{40,32},{48,56},{56,48},{64,72... | collective-permute-start | bytes 491528 | tf_op jit(solution)/shard_map/ppermute | solution.py:27
  81.9 1.0 copy-start.16
  84.6 28.2 %all-to-all-start.4 = ((bf16[16,16,768]{2,1,0:T(8,128)(2,1)}), bf16[16,16,768]{2,1,0:T(8,128)(2,1)S(1)}, u32[]{:S(2)}, u32[]{:S(2)}) async-start(bf16[16,16,768]{2,1,0:T(8,128)(2,1)} %bitcast.13), calls=%async_computation.4 | async-start | bytes 786432 | tf_op jit(solution)/shard_map/all_to_all | solution.py:401
  124.1 27.2 %all-to-all-start.6 = ((bf16[16,16,1536]{2,1,0:T(8,128)(2,1)}), bf16[16,16,1536]{2,1,0:T(8,128)(2,1)S(1)}, u32[]{:S(2)}, u32[]{:S(2)}) async-start(bf16[16,16,1536]{2,1,0:T(8,128)(2,1)} %bitcast.15), calls=%async_computation.6 | async-start | bytes 1572864 | tf_op jit(solution)/shard_map/all_to_all | solution.py:416
  130.9 9.0 %collective-permute-start.5 = (bf16[128,768]{1,0:T(8,128)(2,1)S(1)}, bf16[128,768]{1,0:T(8,128)(2,1)S(1)}, u32[]{:S(2)}, u32[]{:S(2)}) collective-permute-start(bf16[128,768]{1,0:T(8,128)(2,1)S(1)} %bitcast.18), channel_id=1, source_target_pairs={{0,384},{128,256},{256,128},{384,0},{1,385},{129,257},{257,129},{3... | collective-permute-start | bytes 589832 | tf_op jit(solution)/shard_map/ppermute | solution.py:27
  133.7 8.3 %collective-permute-start.4 = (bf16[128,768]{1,0:T(8,128)(2,1)S(1)}, bf16[128,768]{1,0:T(8,128)(2,1)S(1)}, u32[]{:S(2)}, u32[]{:S(2)}) collective-permute-start(bf16[128,768]{1,0:T(8,128)(2,1)S(1)} %bitcast.19), channel_id=1, source_target_pairs={{0,256},{128,384},{256,0},{384,128},{1,257},{129,385},{257,1},{385... | collective-permute-start | bytes 589832 | tf_op jit(solution)/shard_map/ppermute | solution.py:27
  136.8 7.5 %collective-permute-start.3 = (bf16[128,768]{1,0:T(8,128)(2,1)S(1)}, bf16[128,768]{1,0:T(8,128)(2,1)S(1)}, u32[]{:S(2)}, u32[]{:S(2)}) collective-permute-start(bf16[128,768]{1,0:T(8,128)(2,1)S(1)} %bitcast.20), channel_id=1, source_target_pairs={{0,128},{128,0},{256,384},{384,256},{1,129},{129,1},{257,385},{385... | collective-permute-start | bytes 589832 | tf_op jit(solution)/shard_map/ppermute | solution.py:27

commit v11 on v9

--- a/solution.py
+++ b/solution.py
@@ -230,12 +230,12 @@
 
 def attend_kernel(
     place_ref, merged_ref, embed_ref, norm_ref, qkv_ref, qgain_ref, kgain_ref, out_ref, own_ref,
-    give_ref,    kv_ref, q_ref, k_ref, v_ref, *, grp_size, block,
+    give_ref, normed_ref, kv_ref, q_ref, k_ref, v_ref, *, grp_size, block,
 ):
     latents, width = embed_ref.shape
     head = q_ref.shape[1]
     total = out_ref.shape[0]
-    step = 256
+    step = 512
     kv_ref[:, :head] = qkv_ref[1]
     kv_ref[:, head:] = qkv_ref[2]
     pick = (lane_index(16) >= LANES - 2).astype(F32).astype(BF16)
@@ -259,12 +259,13 @@
         factors = jnp.where(lane < latents, rows, tail).astype(BF16)
         center = jnp.dot(factors, embed, preferred_element_type=F32)
         spread = jnp.mean(center * center, axis=-1, keepdims=True)
-        normed = (center * lax.rsqrt(spread + 1e-06) * norm_ref[...]).astype(BF16)
-        q_part = jnp.dot(normed, qkv_ref[0], preferred_element_type=F32)
-        kv_part = jnp.dot(normed, kv_ref[...], preferred_element_type=F32)
-        q_ref[here, :] = head_norm(q_part, qgain_ref[...])
-        k_ref[here, :] = head_norm(kv_part[:, :head], kgain_ref[...])
-        v_ref[here, :] = kv_part[:, head:].astype(BF16)
+        scaled = center * lax.rsqrt(spread + 1e-06) * norm_ref[...]
+        normed_ref[here, :] = scaled.astype(BF16)
+    q_part = jnp.dot(normed_ref[...], qkv_ref[0], preferred_element_type=F32)
+    q_ref[...] = head_norm(q_part, qgain_ref[...])
+    kv_part = jnp.dot(normed_ref[...], kv_ref[...], preferred_element_type=F32)
+    k_ref[...] = head_norm(kv_part[:, :head], kgain_ref[...])
+    v_ref[...] = kv_part[:, head:].astype(BF16)
     scale = 1.0 / math.sqrt(head)
     for start in range(0, total, step):
         here = slice(start, start + step)
@@ -365,7 +366,8 @@
         [(groups, head), (rows, head), (groups // 2 + rows // 2, head)], place, merged,
         embed_weight, norm_gain[None], qkv_weight, q_gain[None], k_gain[None], name="attend",
         flops=8 * 10**9, places=["smem"],
-        scratch=[pltpu.VMEM((width, 2 * head), BF16)] + [pltpu.VMEM((groups, head), BF16)] * 3,
+        scratch=[pltpu.VMEM((groups, width), BF16), pltpu.VMEM((width, 2 * head), BF16)]
+        + [pltpu.VMEM((groups, head), BF16)] * 3,
     )
 
     given_rows, weight_other = lax.optimization_barrier((given_rows, weight_other))

time: 151 us -> 150 us (level)
  no operation moved by 1% of the time
where the time goes in v11:
time: 150 us; the launch traced here: 147 us
  starting transfers between devices  46.9 us (31%)
  blocking collectives  40.3 us (27%)
  waiting for transfers between devices  34.7 us (23%)
  Pallas kernels  19.1 us (13%)
  local copies, waits for them, and re-layouts  5.42 us (4%)
    all_to_all x1, blocking collectives, shards(): lax.all_to_all(sums.reshape(seq_size, shared, LANES), 'seq', 0, 0, tiled=...  20.1 us
    pallas_call x11, Pallas kernels, call(): pl.pallas_call(body, out_shape=outs, in_specs=in_specs, out_specs=(whole,...  19.1 us
    ppermute x5, starting transfers between devices, xor_swap(): return lax.ppermute(block, axis, route)  14.2 us
    all_to_all x1, waiting for transfers between devices, shards(): lax.all_to_all(local_grad.reshape(2 * dp_size, head // dp_size, columns),...  12.8 us
    all_to_all x1, starting transfers between devices, shards(): lax.all_to_all(local_grad.reshape(2 * dp_size, head // dp_size, columns),...  12.4 us
    all_to_all x1, blocking collectives, shards(): lax.all_to_all(grad_block, 'dp', 0, 0, tiled=True).reshape(head, columns)  11.3 us
    all_to_all x1, blocking collectives, shards(): slab_parts = lax.all_to_all(slab_sums, 'grp', 0, 0, tiled=True)  8.95 us
    ppermute x5, waiting for transfers between devices, xor_swap(): return lax.ppermute(block, axis, route)  8.5 us
  transfers between devices with their start and end apart: 10, of which 6 were waited for; matrix products, arithmetic and copies ran while one was open for 0% of the time, Pallas kernels for 10%

profile of v11, /device:TPU:1, one launch (start us, length us, event | category | flops | bytes accessed | tf_op | source)
XLA Modules:
  0.0 147.4 jit_solution(3448984618896655203)
XLA Ops:
  0.6 0.9 slice_bitcast_fusion
  1.6 4.0 %collective-permute-start = (bf16[2,64,512]{2,1,0:T(8,128)(2,1)S(1)}, bf16[2,64,512]{2,1,0:T(8,128)(2,1)S(1)}, u32[]{:S(2)}, u32[]{:S(2)}) collective-permute-start(bf16[2,64,512]{2,1,0:T(8,128)(2,1)S(1)} %slice_bitcast_fusion), channel_id=1, source_target_pairs={{0,8},{8,16},{16,24},{24,32},{32,40},{40,48},{48,56},{56,64},{64,7... | collective-permute-start | bytes 393224 | tf_op jit(solution)/shard_map/ppermute | solution.py:22
  5.6 0.0 copy-start.2
  5.6 1.0 copy-done.2
  6.7 0.9 copy-done.5
  7.5 0.8 copy-done.6
  8.4 1.4 late_frames.1
  9.8 0.0 copy-start.1
  9.8 0.0 collective-permute-done.earlier_ref
  9.8 0.9 group_sums.1
  10.7 0.0 copy-start
  10.7 20.1 %all_to_all.35.parts_ref = bf16[16,64,128]{2,1,0:T(8,128)(2,1)S(1)} all-to-all(bf16[16,64,128]{2,1,0:T(8,128)(2,1)S(1)} %bitcast.23), channel_id=1, replica_groups=mesh['grp'=4,'seq'=16,'dp'=8] {'seq'}, dimensions={0} | all-to-all | bytes 524288 | tf_op jit(solution)/shard_map/all_to_all | solution.py:347
  30.8 0.2 slab_sums.1
  31.0 0.0 copy-start.4
  31.0 0.0 copy-start.7
  31.0 0.0 copy-start.9
  31.0 0.0 copy-start.10
  31.0 8.9 %all_to_all.36.parts_ref = bf16[4,160,128]{2,1,0:T(8,128)(2,1)S(1)} all-to-all(bf16[4,160,128]{2,1,0:T(8,128)(2,1)S(1)} %slab_sums.1), channel_id=1, replica_groups=mesh['grp'=4,'seq'=16,'dp'=8] {'grp'}, dimensions={0} | all-to-all | bytes 327680 | tf_op jit(solution)/shard_map/all_to_all | solution.py:352
  40.0 0.9 merged.1
  40.9 5.5 %all-to-all-start.2 = ((bf16[16,64,128]{2,1,0:T(8,128)(2,1)}), bf16[16,64,128]{2,1,0:T(8,128)(2,1)S(1)}, u32[]{:S(2)}, u32[]{:S(2)}) async-start(bf16[16,64,128]{2,1,0:T(8,128)(2,1)} %merged.1), calls=%async_computation.2 | async-start | bytes 524288 | tf_op jit(solution)/shard_map/all_to_all | solution.py:357
  46.4 1.0 near_rows.1
  47.4 8.0 %all-to-all-done.2 = bf16[16,64,128]{2,1,0:T(8,128)(2,1)S(1)} async-done(((bf16[16,64,128]{2,1,0:T(8,128)(2,1)}), bf16[16,64,128]{2,1,0:T(8,128)(2,1)S(1)}, u32[]{:S(2)}, u32[]{:S(2)}) %all-to-all-start.2) | async-done | bytes 262176 | tf_op jit(solution)/shard_map/all_to_all | solution.py:357
  55.4 3.5 %all-to-all-start.3 = ((bf16[8,64,768]{2,1,0:T(8,128)(2,1)}), bf16[8,64,768]{2,1,0:T(8,128)(2,1)S(1)}, u32[]{:S(2)}, u32[]{:S(2)}) async-start(bf16[8,64,768]{2,1,0:T(8,128)(2,1)} %near_rows.1), calls=%async_computation.3 | async-start | bytes 1572864 | tf_op jit(solution)/shard_map/all_to_all | solution.py:362
  58.9 0.1 pad_add_fusion.place_ref
  59.0 3.3 %collective-permute-start.1 = (bf16[128,1536]{1,0:T(8,128)(2,1)S(1)}, bf16[128,1536]{1,0:T(8,128)(2,1)S(1)}, u32[]{:S(2)}, u32[]{:S(2)}) collective-permute-start(bf16[128,1536]{1,0:T(8,128)(2,1)S(1)} %constant_dynamic-slice_fusion), channel_id=1, source_target_pairs={{0,8},{8,0},{16,24},{24,16},{32,40},{40,32},{48,56},{56,48},{64,72... | collective-permute-start | bytes 1179656 | tf_op jit(solution)/shard_map/ppermute | solution.py:27
  62.4 0.0 copy-start.3
  62.4 1.7 %copy-done.3 = bf16[3,3072,128]{2,1,0:T(8,128)(2,1)S(1)} copy-done((bf16[3,3072,128]{2,1,0:T(8,128)(2,1)S(1)}, bf16[3,3072,128]{2,1,0:T(8,128)(2,1)}, u32[]{:S(2)}) %copy-start.3) | copy-done | bytes 2359320
  64.0 8.9 %attend.1 = (bf16[1024,128]{1,0:T(8,128)(2,1)S(1)}, bf16[256,128]{1,0:T(8,128)(2,1)S(1)}, bf16[640,128]{1,0:T(8,128)(2,1)S(1)}) custom-call(s32[3]{0:T(128)S(1)} %pad_add_fusion.place_ref, bf16[1024,128]{1,0:T(8,128)(2,1)S(1)} %bitcast.22, bf16[64,3072]{1,0:T(8,128)(2,1)S(1)} %copy-done.4, f32[1,3072]{1,0:T(1,128)S(1)} %bitcast.27, ...), custom_call_target="tpu_custom_call" | custom-call | flops 8000000000 | bytes 1000000 | tf_op jit(solution)/shard_map/attend/pallas_call | solution.py:302
  72.9 0.0 collective-permute-done.1.partner_ref
  72.9 2.0 %collective-permute-start.2 = (bf16[640,128]{1,0:T(8,128)(2,1)S(1)}, bf16[640,128]{1,0:T(8,128)(2,1)S(1)}, u32[]{:S(2)}, u32[]{:S(2)}) collective-permute-start(bf16[640,128]{1,0:T(8,128)(2,1)S(1)} %get-tuple-element.28), channel_id=1, source_target_pairs={{0,8},{8,0},{16,24},{24,16},{32,40},{40,32},{48,56},{56,48},{64,72... | collective-permute-start | bytes 491528 | tf_op jit(solution)/shard_map/ppermute | solution.py:27
  74.9 4.1 %collective-permute-done.2.given_ref = bf16[640,128]{1,0:T(8,128)(2,1)S(1)} collective-permute-done((bf16[640,128]{1,0:T(8,128)(2,1)S(1)}, bf16[640,128]{1,0:T(8,128)(2,1)S(1)}, u32[]{:S(2)}, u32[]{:S(2)}) %collective-permute-start.2) | collective-permute-done | bytes 163872 | tf_op jit(solution)/shard_map/ppermute | solution.py:27
  79.0 0.0 all-to-all-done.3.cot_ref
  79.0 1.7 %local_grad.1 = bf16[2,128,768]{2,1,0:T(8,128)(2,1)} custom-call(s32[3]{0:T(128)S(1)} %pad_add_fusion.place_ref, bf16[1024,128]{1,0:T(8,128)(2,1)S(1)} %get-tuple-element.25.head_ref, bf16[640,128]{1,0:T(8,128)(2,1)S(1)} %collective-permute-done.2.given_ref, bf16[8,64,768]{2,1,0:T(8,128)(2,1)S(1)} %all-to-all-done.3.cot_ref), custom_call_target="tpu_custom_call" | custom-call | flops 1000000000 | bytes 1000000 | tf_op jit(solution)/shard_map/local_grad/pallas_call | solution.py:302
  80.7 12.4 %all-to-all-start.4 = ((bf16[16,16,768]{2,1,0:T(8,128)(2,1)}), bf16[16,16,768]{2,1,0:T(8,128)(2,1)S(1)}, u32[]{:S(2)}, u32[]{:S(2)}) async-start(bf16[16,16,768]{2,1,0:T(8,128)(2,1)} %bitcast.13), calls=%async_computation.4 | async-start | bytes 786432 | tf_op jit(solution)/shard_map/all_to_all | solution.py:384
  93.1 1.8 %project.1 = bf16[256,1536]{1,0:T(8,128)(2,1)} custom-call(s32[3]{0:T(128)S(1)} %pad_add_fusion.place_ref, bf16[256,128]{1,0:T(8,128)(2,1)S(1)} %get-tuple-element.30.own_ref, bf16[640,128]{1,0:T(8,128)(2,1)S(1)} %collective-permute-done.2.given_ref, bf16[128,3072]{1,0:T(8,128)(2,1)S(1)} %copy-done, bf16[128,1536]{1,0:T(8,128)(2,1)S(1)} %collective-permute-done.1.partner_ref), custom_call_target="tpu_custom_call" | custom-call | flops 1000000000 | bytes 1000000 | tf_op jit(solution)/shard_map/project/pallas_call | solution.py:302
  94.9 12.8 %all-to-all-done.4.parts_ref = bf16[16,16,768]{2,1,0:T(8,128)(2,1)S(1)} async-done(((bf16[16,16,768]{2,1,0:T(8,128)(2,1)}), bf16[16,16,768]{2,1,0:T(8,128)(2,1)S(1)}, u32[]{:S(2)}, u32[]{:S(2)}) %all-to-all-start.4) | async-done | bytes 393248 | tf_op jit(solution)/shard_map/all_to_all | solution.py:384
  107.7 0.1 grad_block.1
  107.8 11.3 %all_to_all.37 = bf16[8,16,768]{2,1,0:T(8,128)(2,1)S(1)} all-to-all(bf16[8,16,768]{2,1,0:T(8,128)(2,1)S(1)} %grad_block.1), channel_id=1, replica_groups=mesh['grp'=4,'seq'=16,'dp'=8] {'dp'}, dimensions={0} | all-to-all | bytes 393216 | tf_op jit(solution)/shard_map/all_to_all | solution.py:397
  119.0 7.2 %all-to-all-start.6 = ((bf16[16,16,1536]{2,1,0:T(8,128)(2,1)}), bf16[16,16,1536]{2,1,0:T(8,128)(2,1)S(1)}, u32[]{:S(2)}, u32[]{:S(2)}) async-start(bf16[16,16,1536]{2,1,0:T(8,128)(2,1)} %bitcast.15), calls=%async_computation.6 | async-start | bytes 1572864 | tf_op jit(solution)/shard_map/all_to_all | solution.py:399
  126.3 2.8 %collective-permute-start.5 = (bf16[128,768]{1,0:T(8,128)(2,1)S(1)}, bf16[128,768]{1,0:T(8,128)(2,1)S(1)}, u32[]{:S(2)}, u32[]{:S(2)}) collective-permute-start(bf16[128,768]{1,0:T(8,128)(2,1)S(1)} %bitcast.18), channel_id=1, source_target_pairs={{0,384},{128,256},{256,128},{384,0},{1,385},{129,257},{257,129},{3... | collective-permute-start | bytes 589832 | tf_op jit(solution)/shard_map/ppermute | solution.py:27
  129.1 3.1 %collective-permute-start.4 = (bf16[128,768]{1,0:T(8,128)(2,1)S(1)}, bf16[128,768]{1,0:T(8,128)(2,1)S(1)}, u32[]{:S(2)}, u32[]{:S(2)}) collective-permute-start(bf16[128,768]{1,0:T(8,128)(2,1)S(1)} %bitcast.19), channel_id=1, source_target_pairs={{0,256},{128,384},{256,0},{384,128},{1,257},{129,385},{257,1},{385... | collective-permute-start | bytes 589832 | tf_op jit(solution)/shard_map/ppermute | solution.py:27
  132.2 3.1 %collective-permute-start.3 = (bf16[128,768]{1,0:T(8,128)(2,1)S(1)}, bf16[128,768]{1,0:T(8,128)(2,1)S(1)}, u32[]{:S(2)}, u32[]{:S(2)}) collective-permute-start(bf16[128,768]{1,0:T(8,128)(2,1)S(1)} %bitcast.20), channel_id=1, source_target_pairs={{0,128},{128,0},{256,384},{384,256},{1,129},{129,1},{257,385},{385... | collective-permute-start | bytes 589832 | tf_op jit(solution)/shard_map/ppermute | solution.py:27
  135.3 0.0 collective-permute-done.5.refs_3_
  135.3 2.0 %collective-permute-done.4.refs_2_ = bf16[128,768]{1,0:T(8,128)(2,1)S(1)} collective-permute-done((bf16[128,768]{1,0:T(8,128)(2,1)S(1)}, bf16[128,768]{1,0:T(8,128)(2,1)S(1)}, u32[]{:S(2)}, u32[]{:S(2)}) %collective-permute-start.4) | collective-permute-done | bytes 196640 | tf_op jit(solution)/shard_map/ppermute | solution.py:27
  137.3 2.3 %collective-permute-done.3.refs_1_ = bf16[128,768]{1,0:T(8,128)(2,1)S(1)} collective-permute-done((bf16[128,768]{1,0:T(8,128)(2,1)S(1)}, bf16[128,768]{1,0:T(8,128)(2,1)S(1)}, u32[]{:S(2)}, u32[]{:S(2)}) %collective-permute-start.3) | collective-permute-done | bytes 196640 | tf_op jit(solution)/shard_map/ppermute | solution.py:27
  139.7 1.5 %grad_columns.1 = bf16[128,3072]{1,0:T(8,128)(2,1)} custom-call(s32[3]{0:T(128)S(1)} %pad_add_fusion.place_ref, bf16[128,768]{1,0:T(8,128)(2,1)S(1)} %bitcast.21, bf16[128,768]{1,0:T(8,128)(2,1)S(1)} %collective-permute-done.3.refs_1_, bf16[128,768]{1,0:T(8,128)(2,1)S(1)} %collective-permute-done.4.refs_2_, bf16[128,768]{1,0:T(8,128)(2,1)S(1)} %collective-permute-done.5.refs_3_), custom_call_target="tpu_custom_call" | custom-call | flops 100000000 | bytes 1000000 | tf_op jit(solution)/shard_map/grad_columns/pallas_call | solution.py:302
  141.2 5.5 %all-to-all-done.6.parts_ref = bf16[16,16,1536]{2,1,0:T(8,128)(2,1)S(1)} async-done(((bf16[16,16,1536]{2,1,0:T(8,128)(2,1)}), bf16[16,16,1536]{2,1,0:T(8,128)(2,1)S(1)}, u32[]{:S(2)}, u32[]{:S(2)}) %all-to-all-start.6) | async-done | bytes 786464 | tf_op jit(solution)/shard_map/all_to_all | solution.py:399
  146.6 0.7 attended.1
  (11 shorter events, 0.0 us)
Async XLA Ops:
  0.6 9.2 %copy-start.8 = (s32[1,8,64]{2,1,0:T(8,128)S(1)}, s32[1,8,64]{2,1,0:T(8,128)}, u32[]{:S(2)}) copy-start(s32[1,8,64]{2,1,0:T(8,128)} %param.14) | copy-start | bytes 6148
  1.6 8.2 %collective-permute-start = (bf16[2,64,512]{2,1,0:T(8,128)(2,1)S(1)}, bf16[2,64,512]{2,1,0:T(8,128)(2,1)S(1)}, u32[]{:S(2)}, u32[]{:S(2)}) collective-permute-start(bf16[2,64,512]{2,1,0:T(8,128)(2,1)S(1)} %slice_bitcast_fusion), channel_id=1, source_target_pairs={{0,8},{8,16},{16,24},{24,32},{32,40},{40,48},{48,56},{56,64},{64,7... | collective-permute-start | bytes 393224 | tf_op jit(solution)/shard_map/ppermute | solution.py:22
  5.6 1.0 copy-start.2
  6.7 0.9 copy-start.5
  7.5 0.8 copy-start.6
  9.8 21.0 %copy-start.1 = (bf16[1,16,3072]{2,1,0:T(8,128)(2,1)S(1)}, bf16[1,16,3072]{2,1,0:T(8,128)(2,1)}, u32[]{:S(2)}) copy-start(bf16[1,16,3072]{2,1,0:T(8,128)(2,1)} %param.21) | copy-start | bytes 294916
  10.7 48.3 %copy-start = (bf16[128,3072]{1,0:T(8,128)(2,1)S(1)}, bf16[128,3072]{1,0:T(8,128)(2,1)}, u32[]{:S(2)}) copy-start(bf16[128,3072]{1,0:T(8,128)(2,1)} %weight_ref.1) | copy-start | bytes 2359300
  31.0 31.3 %copy-start.4 = (bf16[64,3072]{1,0:T(8,128)(2,1)S(1)}, bf16[64,3072]{1,0:T(8,128)(2,1)}, u32[]{:S(2)}) copy-start(bf16[64,3072]{1,0:T(8,128)(2,1)} %embed_ref.1) | copy-start | bytes 1179652
  31.0 31.3 %copy-start.7 = (f32[3072]{0:T(1024)S(1)}, f32[3072]{0:T(1024)}, u32[]{:S(2)}) copy-start(f32[3072]{0:T(1024)} %param.16) | copy-start | bytes 36868
  31.0 31.3 %copy-start.9 = (f32[128]{0:T(128)S(1)}, f32[128]{0:T(128)}, u32[]{:S(2)}) copy-start(f32[128]{0:T(128)} %param.18) | copy-start | bytes 1540
  31.0 31.3 %copy-start.10 = (f32[128]{0:T(128)S(1)}, f32[128]{0:T(128)}, u32[]{:S(2)}) copy-start(f32[128]{0:T(128)} %param.19) | copy-start | bytes 1540
  40.9 14.5 %all-to-all-start.2 = ((bf16[16,64,128]{2,1,0:T(8,128)(2,1)}), bf16[16,64,128]{2,1,0:T(8,128)(2,1)S(1)}, u32[]{:S(2)}, u32[]{:S(2)}) async-start(bf16[16,64,128]{2,1,0:T(8,128)(2,1)} %merged.1), calls=%async_computation.2 | async-start | bytes 524288 | tf_op jit(solution)/shard_map/all_to_all | solution.py:357
  55.4 23.7 %all-to-all-start.3 = ((bf16[8,64,768]{2,1,0:T(8,128)(2,1)}), bf16[8,64,768]{2,1,0:T(8,128)(2,1)S(1)}, u32[]{:S(2)}, u32[]{:S(2)}) async-start(bf16[8,64,768]{2,1,0:T(8,128)(2,1)} %near_rows.1), calls=%async_computation.3 | async-start | bytes 1572864 | tf_op jit(solution)/shard_map/all_to_all | solution.py:362
  59.0 13.9 %collective-permute-start.1 = (bf16[128,1536]{1,0:T(8,128)(2,1)S(1)}, bf16[128,1536]{1,0:T(8,128)(2,1)S(1)}, u32[]{:S(2)}, u32[]{:S(2)}) collective-permute-start(bf16[128,1536]{1,0:T(8,128)(2,1)S(1)} %constant_dynamic-slice_fusion), channel_id=1, source_target_pairs={{0,8},{8,0},{16,24},{24,16},{32,40},{40,32},{48,56},{56,48},{64,72... | collective-permute-start | bytes 1179656 | tf_op jit(solution)/shard_map/ppermute | solution.py:27
  62.4 1.7 %copy-start.3 = (bf16[3,3072,128]{2,1,0:T(8,128)(2,1)S(1)}, bf16[3,3072,128]{2,1,0:T(8,128)(2,1)}, u32[]{:S(2)}) copy-start(bf16[3,3072,128]{2,1,0:T(8,128)(2,1)} %qkv_ref.1) | copy-start | bytes 7077892
  72.9 6.1 %collective-permute-start.2 = (bf16[640,128]{1,0:T(8,128)(2,1)S(1)}, bf16[640,128]{1,0:T(8,128)(2,1)S(1)}, u32[]{:S(2)}, u32[]{:S(2)}) collective-permute-start(bf16[640,128]{1,0:T(8,128)(2,1)S(1)} %get-tuple-element.28), channel_id=1, source_target_pairs={{0,8},{8,0},{16,24},{24,16},{32,40},{40,32},{48,56},{56,48},{64,72... | collective-permute-start | bytes 491528 | tf_op jit(solution)/shard_map/ppermute | solution.py:27
  80.7 27.0 %all-to-all-start.4 = ((bf16[16,16,768]{2,1,0:T(8,128)(2,1)}), bf16[16,16,768]{2,1,0:T(8,128)(2,1)S(1)}, u32[]{:S(2)}, u32[]{:S(2)}) async-start(bf16[16,16,768]{2,1,0:T(8,128)(2,1)} %bitcast.13), calls=%async_computation.4 | async-start | bytes 786432 | tf_op jit(solution)/shard_map/all_to_all | solution.py:384
  119.0 27.6 %all-to-all-start.6 = ((bf16[16,16,1536]{2,1,0:T(8,128)(2,1)}), bf16[16,16,1536]{2,1,0:T(8,128)(2,1)S(1)}, u32[]{:S(2)}, u32[]{:S(2)}) async-start(bf16[16,16,1536]{2,1,0:T(8,128)(2,1)} %bitcast.15), calls=%async_computation.6 | async-start | bytes 1572864 | tf_op jit(solution)/shard_map/all_to_all | solution.py:399
  126.3 9.0 %collective-permute-start.5 = (bf16[128,768]{1,0:T(8,128)(2,1)S(1)}, bf16[128,768]{1,0:T(8,128)(2,1)S(1)}, u32[]{:S(2)}, u32[]{:S(2)}) collective-permute-start(bf16[128,768]{1,0:T(8,128)(2,1)S(1)} %bitcast.18), channel_id=1, source_target_pairs={{0,384},{128,256},{256,128},{384,0},{1,385},{129,257},{257,129},{3... | collective-permute-start | bytes 589832 | tf_op jit(solution)/shard_map/ppermute | solution.py:27
  129.1 8.3 %collective-permute-start.4 = (bf16[128,768]{1,0:T(8,128)(2,1)S(1)}, bf16[128,768]{1,0:T(8,128)(2,1)S(1)}, u32[]{:S(2)}, u32[]{:S(2)}) collective-permute-start(bf16[128,768]{1,0:T(8,128)(2,1)S(1)} %bitcast.19), channel_id=1, source_target_pairs={{0,256},{128,384},{256,0},{384,128},{1,257},{129,385},{257,1},{385... | collective-permute-start | bytes 589832 | tf_op jit(solution)/shard_map/ppermute | solution.py:27
  132.2 7.5 %collective-permute-start.3 = (bf16[128,768]{1,0:T(8,128)(2,1)S(1)}, bf16[128,768]{1,0:T(8,128)(2,1)S(1)}, u32[]{:S(2)}, u32[]{:S(2)}) collective-permute-start(bf16[128,768]{1,0:T(8,128)(2,1)S(1)} %bitcast.20), channel_id=1, source_target_pairs={{0,128},{128,0},{256,384},{384,256},{1,129},{129,1},{257,385},{385... | collective-permute-start | bytes 589832 | tf_op jit(solution)/shard_map/ppermute | solution.py:27
